TPU v7x, 32 devices: a whole 2x2x4 slice. The times are simulated.
32 devices in a mesh: dp: 2 (over x), expert: 16 (over z, y, core).
Axes of the slice: x: 2, y: 2, z: 4, core: 2. Of those that a mesh axis runs over, the one named last changes fastest.
Arguments:
- grad_out: bfloat16 [4096, 2048], P(('dp', 'expert')), may hold values from -6 to 6
- gates: bfloat16 [4096, 6], P(('dp', 'expert')), may hold values from 0.049804688 to 0.59765625
- routes: int32 [4096, 6], P(('dp', 'expert')), may hold values from 0 to 15, all different within a row; in each aligned block of 128 rows (0 to 127, 128 to 255, ...) at most 64 rows name the same one
- hidden: bfloat16 [2, 16, 1024, 704], P('dp', 'expert'), may hold values from -0.23925781 to 0.23925781
- down_weight: bfloat16 [16, 704, 2048], P('expert', 'dp'), may hold values from -0.125 to 0.125
Outputs:
- grad_weight: bfloat16 [16, 704, 2048], P('expert', 'dp')
- grad_hidden: bfloat16 [2, 16, 1024, 704], P('dp', 'expert')
- grad_gates: float32 [4096, 6], P(('dp', 'expert'))
Inputs may be any that keep to these rules, and one draw needn't show every extreme that they name: `routes`: each row names 6 different experts; within the rows of one device no expert is named more than 64 times, a bound that some block reaches.
All inputs are finite; a program needn't handle non-finite values.
Results may differ from a plain program's by a relative error of at most 0.017.
Values may be sent and summed in bfloat16 or wider, within the bound.
No kernel may reach another device: no remote copies, remote signals or barrier semaphores. Data moves between devices by JAX's collectives and lax.ppermute only.
A program may use at most 64 MiB of HBM per device.

v0:
```python
import jax
import jax.numpy as jnp
from jax import lax
from jax.sharding import PartitionSpec as P


def shards(grad_out, gates, routes, hidden, down_weight):
    owners = lax.axis_size("expert")
    token_count, chosen = routes.shape
    width = grad_out.shape[1]
    slots = hidden.shape[2]
    capacity = slots // owners
    flat = routes.reshape(-1)
    onehot = (flat[:, None] == jnp.arange(owners, dtype=jnp.int32)[None, :]).astype(jnp.int32)
    before = jnp.cumsum(onehot, axis=0) - onehot
    slot = jnp.sum(before * onehot, axis=1)
    target = flat * capacity + slot
    send_rows = (
        jnp.zeros((owners * capacity, width), grad_out.dtype)
        .at[target]
        .set(jnp.repeat(grad_out, chosen, axis=0))
    )
    send_gate = jnp.zeros((owners * capacity,), gates.dtype).at[target].set(gates.reshape(-1))
    send_rows = send_rows.reshape(owners, capacity, width)
    send_gate = send_gate.reshape(owners, capacity)
    saved = hidden[0, 0]
    local_weight = down_weight[0]
    contract = (((1,), (1,)), ((), ()))
    rows, gate_slots = (
        lax.all_to_all(send_rows, "expert", split_axis=0, concat_axis=0, tiled=True),
        lax.all_to_all(send_gate, "expert", split_axis=0, concat_axis=0, tiled=True),
    )
    rows = rows.reshape(slots, width)
    whole_weight = lax.all_gather(local_weight, "dp", axis=0, tiled=True)
    raw = lax.dot_general(rows, whole_weight, contract, preferred_element_type=jnp.float32)
    factor = gate_slots.reshape(slots, 1).astype(jnp.float32)
    grad_hidden = (factor * raw).astype(jnp.bfloat16)
    slot_grads = jnp.sum(raw * saved.astype(jnp.float32), axis=1)
    returned = lax.all_to_all(
        slot_grads.reshape(owners, capacity), "expert", split_axis=0, concat_axis=0, tiled=True
    )
    grad_gates = returned.reshape(-1)[target].reshape(token_count, chosen)
    scaled = (factor * rows.astype(jnp.float32)).astype(jnp.bfloat16)
    summed = lax.psum_scatter(
        lax.dot_general(
            saved, scaled, (((0,), (0,)), ((), ())), preferred_element_type=jnp.float32
        ).astype(jnp.bfloat16),
        "dp",
        scatter_dimension=0,
        tiled=True,
    )
    return (summed[None], grad_hidden[None, None], grad_gates)


def solution(mesh):
    return jax.shard_map(
        shards,
        mesh=mesh,
        in_specs=(
            P(("dp", "expert"), None),
            P(("dp", "expert"), None),
            P(("dp", "expert"), None),
            P("dp", "expert", None, None),
            P("expert", "dp", None),
        ),
        out_specs=(
            P("expert", "dp", None),
            P("dp", "expert", None, None),
            P(("dp", "expert"), None),
        ),
        check_vma=False,
    )
```

profile of v0, /device:TPU:0, one launch (start us, length us, event | category | flops | bytes accessed | tf_op | source)
XLA Modules:
  0.0 200.7 jit_solution(5764221588993598566)
XLA Ops:
  7.2 0.8 copy.15
  8.2 0.7 broadcast_multiply_fusion
  8.9 1.7 reduce-window.6
  11.2 0.8 copy.18
  12.3 8.6 %scatter_custom_fusion = bf16[1024]{0:T(1024)(128)(2,1)S(1)} fusion(s32[768]{0:T(1024)S(1)} %fusion.11, bf16[768]{0:T(1024)(128)(2,1)S(1)} %reshape.120, bf16[]{:T(256)} %constant.5.clone.1), kind=kCustom, calls=%fused_computation.27 | custom fusion | bytes 2050 | tf_op jit(solution)/shard_map/scatter | solution.py:23
  20.9 0.7 all_to_all.20
  21.6 7.4 %all-to-all-start = ((bf16[16,1,64]{2,1,0:T(2,128)(2,1)}), bf16[16,1,64]{2,1,0:T(2,128)(2,1)S(1)}, u32[]{:S(2)}, u32[]{:S(2)}) async-start(bf16[16,1,64]{2,1,0:T(2,128)(2,1)} %all_to_all.20), calls=%async_computation | async-start | bytes 16384 | tf_op jit(solution)/shard_map/all_to_all | solution.py:31
  29.0 3.6 %broadcast_in_dim.21 = bf16[128,6,2048]{2,1,0:T(8,128)(2,1)} broadcast(bf16[128,2048]{1,0:T(8,128)(2,1)} %param.5), dimensions={0,2} | broadcast | bytes 3670016 | tf_op jit(solution)/shard_map/broadcast_in_dim | solution.py:21
  32.6 4.9 %reshape.128 = bf16[768,2048]{1,0:T(8,128)(2,1)S(1)} reshape(bf16[128,6,2048]{2,1,0:T(8,128)(2,1)} %broadcast_in_dim.21) | data formatting | bytes 6291456 | tf_op jit(solution)/shard_map/reshape | solution.py:21
  37.5 9.4 %scatter_custom_fusion.1 = bf16[1024,2048]{1,0:T(8,128)(2,1)} fusion(s32[768]{0:T(1024)S(1)} %fusion.11, bf16[768,2048]{1,0:T(8,128)(2,1)S(1)} %reshape.128, bf16[]{:T(256)} %constant.5.clone.1), kind=kCustom, calls=%fused_computation.10 | custom fusion | bytes 4194306 | tf_op jit(solution)/shard_map/scatter | solution.py:21
  46.9 6.1 %all-to-all-start.1 = ((bf16[16,64,2048]{2,1,0:T(8,128)(2,1)}), bf16[16,64,2048]{2,1,0:T(8,128)(2,1)}, u32[]{:S(2)}, u32[]{:S(2)}) async-start(bf16[16,64,2048]{2,1,0:T(8,128)(2,1)} %bitcast.40), calls=%async_computation.1 | async-start | bytes 8388608 | tf_op jit(solution)/shard_map/all_to_all | solution.py:30
  53.0 0.7 all-gather.3.cloned.1.call-update
  53.9 76.7 %all-to-all-done.1 = bf16[16,64,2048]{2,1,0:T(8,128)(2,1)} async-done(((bf16[16,64,2048]{2,1,0:T(8,128)(2,1)}), bf16[16,64,2048]{2,1,0:T(8,128)(2,1)}, u32[]{:S(2)}, u32[]{:S(2)}) %all-to-all-start.1) | async-done | bytes 4194336 | tf_op jit(solution)/shard_map/all_to_all | solution.py:30
  130.6 3.0 %multiply_convert_fusion = bf16[16,64,2048]{2,1,0:T(8,128)(2,1)S(1)} fusion(bf16[16,64,2048]{2,1,0:T(8,128)(2,1)} %all-to-all-done.1, f32[16,64]{1,0:T(8,128)S(1)} %bitcast.42), kind=kLoop, calls=%fused_computation.3 | loop fusion | flops 6291456 | bytes 8392704 | tf_op jit(solution)/shard_map/convert_element_type | solution.py:43
  133.7 4.5 %fusion = bf16[704,2048]{1,0:T(8,128)(2,1)} fusion(bf16[1024,2048]{1,0:T(8,128)(2,1)S(1)} %bitcast.41, bf16[1,1,1024,704]{2,3,1,0:T(8,128)(2,1)S(1)} %copy-done), kind=kOutput, calls=%fused_computation.5 | convolution fusion | flops 2954231808 | bytes 8519680 | tf_op jit(solution)/shard_map/dot_general | solution.py:45
  138.4 7.4 %multiply_reduce_fusion = (f32[1024]{0:T(1024)S(1)}, bf16[1,1,1024,704]{2,3,1,0:T(8,128)(2,1)}) fusion(bf16[1,1,1024,704]{2,3,1,0:T(8,128)(2,1)S(1)} %copy-done, f32[1024]{0:T(1024)S(1)} %reshape.107, bf16[1024,2048]{1,0:T(8,128)(2,1)} %bitcast.7, bf16[1,704,2048]{2,1,0:T(8,128)(2,1)} %all-gather.3.cloned.1.call-done), kind=kOutput, calls=%fused_computation.8 | convolution fusion | flops 2956393472 | bytes 9969664 | tf_op jit(solution)/shard_map/dot_general | solution.py:35
  145.8 0.7 all_to_all.18
  146.5 19.6 %all-to-all-start.2 = ((f32[16,1,64]{2,1,0:T(1,128)}), f32[16,1,64]{2,1,0:T(1,128)S(1)}, u32[]{:S(2)}, u32[]{:S(2)}) async-start(f32[16,1,64]{2,1,0:T(1,128)} %all_to_all.18), calls=%async_computation.3 | async-start | bytes 16384 | tf_op jit(solution)/shard_map/all_to_all | solution.py:39
  166.1 6.4 %all-to-all-done.2 = f32[16,1,64]{2,1,0:T(1,128)S(1)} async-done(((f32[16,1,64]{2,1,0:T(1,128)}), f32[16,1,64]{2,1,0:T(1,128)S(1)}, u32[]{:S(2)}, u32[]{:S(2)}) %all-to-all-start.2) | async-done | bytes 4128 | tf_op jit(solution)/shard_map/all_to_all | solution.py:39
  172.5 0.5 broadcast.65
  173.0 0.7 reduce.11
  173.8 3.2 %gather_fusion = f32[768]{0:T(1024)S(1)} fusion(f32[1024]{0:T(1024)S(1)} %reshape.104, s32[1024]{0:T(1024)S(1)} %pad_clamp_fusion), kind=kCustom, calls=%fused_computation | custom fusion | bytes 9216 | tf_op jit(solution)/shard_map/gather | solution.py:42
  177.1 0.7 copy.20
  177.8 16.0 %reduce-scatter.2.cloned.1.call-done = bf16[352,2048]{1,0:T(8,128)(2,1)} async-done(((bf16[704,2048]{1,0:T(8,128)(2,1)}), bf16[352,2048]{1,0:T(8,128)(2,1)}) %reduce-scatter.2.cloned.1.call-update) | async-done | bytes 1441808 | tf_op jit(solution)/shard_map/reduce_scatter | solution.py:44
  (23 shorter events, 1.7 us)
Async XLA Ops:
  21.6 25.3 %all-to-all-start = ((bf16[16,1,64]{2,1,0:T(2,128)(2,1)}), bf16[16,1,64]{2,1,0:T(2,128)(2,1)S(1)}, u32[]{:S(2)}, u32[]{:S(2)}) async-start(bf16[16,1,64]{2,1,0:T(2,128)(2,1)} %all_to_all.20), calls=%async_computation | async-start | bytes 16384 | tf_op jit(solution)/shard_map/all_to_all | solution.py:31
  46.9 83.7 %all-to-all-start.1 = ((bf16[16,64,2048]{2,1,0:T(8,128)(2,1)}), bf16[16,64,2048]{2,1,0:T(8,128)(2,1)}, u32[]{:S(2)}, u32[]{:S(2)}) async-start(bf16[16,64,2048]{2,1,0:T(8,128)(2,1)} %bitcast.40), calls=%async_computation.1 | async-start | bytes 8388608 | tf_op jit(solution)/shard_map/all_to_all | solution.py:30
  53.0 85.4 %all-gather.3.cloned.1.call-start = ((), (), s32[]{:S(2)}) async-start(), calls=%async_computation.5 | async-start | bytes 4325376 | tf_op jit(solution)/shard_map/all_gather | solution.py:34
  53.7 140.1 %reduce-scatter.2.cloned.1.call-start = ((), (), s32[]{:S(2)}) async-start(), calls=%async_computation.4 | async-start | bytes 4325376 | tf_op jit(solution)/shard_map/reduce_scatter | solution.py:44
  130.6 3.1 %copy-start = (bf16[1,1,1024,704]{2,3,1,0:T(8,128)(2,1)S(1)}, bf16[1,1,1024,704]{2,3,1,0:T(8,128)(2,1)}, u32[]{:S(2)}) copy-start(bf16[1,1,1024,704]{2,3,1,0:T(8,128)(2,1)} %param.8) | copy-start | bytes 4325380
  146.5 26.1 %all-to-all-start.2 = ((f32[16,1,64]{2,1,0:T(1,128)}), f32[16,1,64]{2,1,0:T(1,128)S(1)}, u32[]{:S(2)}, u32[]{:S(2)}) async-start(f32[16,1,64]{2,1,0:T(1,128)} %all_to_all.18), calls=%async_computation.3 | async-start | bytes 16384 | tf_op jit(solution)/shard_map/all_to_all | solution.py:39
Sparse Core Ops, SparseCore 0:
  55.3 43.2 all-gather.2
  138.4 55.3 reduce-scatter.1
where the time goes:
time: 201 us
  waiting for transfers between devices  99.8 us (50%)
  local copies, waits for them, and re-layouts  35 us (17%)
  starting transfers between devices  33.3 us (17%)
  between operations  14.2 us (7%)
  matrix products  12 us (6%)
  other arithmetic  6.3 us (3%)
    all_to_all x1, waiting for transfers between devices, shards(): lax.all_to_all(send_rows, 'expert', split_axis=0, concat_axis=0, tiled=True)  76.7 us
    all_to_all x1, starting transfers between devices, shards(): lax.all_to_all(slot_grads.reshape(owners, capacity), 'expert', split_axis...  19.6 us
    reduce_scatter x1, waiting for transfers between devices, shards(): lax.psum_scatter(lax.dot_general(saved, scaled, (((0,), (0,)), ((), ())),...  16 us
    scatter x1, local copies, waits for them, and re-layouts, shards(): send_rows = jnp.zeros((owners * capacity, width), grad_out.dtype).at[targ...  9.4 us
    scatter x1, local copies, waits for them, and re-layouts, shards(): jnp.zeros((owners * capacity,), gates.dtype).at[target]  8.61 us
    dot_general x1, matrix products, shards(): lax.dot_general(rows, whole_weight, contract, preferred_element_type=jnp....  7.43 us
    all_to_all x1, starting transfers between devices, shards(): lax.all_to_all(send_gate, 'expert', split_axis=0, concat_axis=0, tiled=True)  7.39 us
    all_to_all x1, waiting for transfers between devices, shards(): lax.all_to_all(slot_grads.reshape(owners, capacity), 'expert', split_axis...  6.39 us
  transfers between devices with their start and end apart: 5, of which 3 were waited for; matrix products, arithmetic and copies ran while one was open for 19% of the time, Pallas kernels for 0%

commit v1 on v0

--- a/solution.py
+++ b/solution.py
@@ -1,7 +1,308 @@
+import functools
+
 import jax
 import jax.numpy as jnp
 from jax import lax
+from jax.experimental import pallas as pl
+from jax.experimental.pallas import tpu as pltpu
 from jax.sharding import PartitionSpec as P
+
+NZ, NY, NC = 4, 2, 2
+CHUNKS = 2
+LANES = 128
+NT = (((1,), (1,)), ((), ()))
+VMEM = pl.BlockSpec(memory_space=pltpu.VMEM)
+
+
+def params(mib):
+    return pltpu.CompilerParams(vmem_limit_bytes=mib * 2**20)
+
+
+def ring(z):
+    return z ^ (z >> 1)
+
+
+def ring_pairs():
+    size = NY * NC
+    return [
+        (ring(p) * size + rest, ring((p + 1) % NZ) * size + rest)
+        for p in range(NZ)
+        for rest in range(size)
+    ]
+
+
+def swap_pairs(bit):
+    return [(i, i ^ bit) for i in range(NZ * NY * NC)]
+
+
+def pack_kernel(experts, width, routes_ref, gates_ref, grad_ref, *outs):
+    chosen, tokens = routes_ref.shape
+    routes = routes_ref[...]
+    gates = gates_ref[...].astype(jnp.float32)
+    expert = lax.broadcasted_iota(jnp.int32, (experts, tokens), 0)
+    dense = jnp.zeros((experts, tokens), jnp.float32)
+    named = jnp.zeros((experts, tokens), jnp.float32)
+    for k in range(chosen):
+        hit = routes[k : k + 1, :] == expert
+        dense = jnp.where(hit, gates[k : k + 1, :], dense)
+        named = jnp.where(hit, 1.0, named)
+    earlier = (
+        lax.broadcasted_iota(jnp.int32, (tokens, tokens), 0)
+        < lax.broadcasted_iota(jnp.int32, (tokens, tokens), 1)
+    )
+    slots = jnp.dot(
+        named.astype(jnp.bfloat16),
+        jnp.where(earlier, 1.0, 0.0).astype(jnp.bfloat16),
+        preferred_element_type=jnp.float32,
+    )
+    slots = jnp.where(named > 0, slots, -1.0)
+    outs[0][:, :width] = grad_ref[:, :width]
+    outs[0][:, width:] = jnp.zeros((tokens, tokens), jnp.bfloat16)
+    outs[0][:experts, width:] = dense.astype(jnp.bfloat16)
+    outs[0][experts : 2 * experts, width:] = slots.astype(jnp.bfloat16)
+    for c in range(1, len(outs)):
+        outs[c][...] = grad_ref[:, c * width : (c + 1) * width]
+
+
+def pair_place(arrival):
+    index = lax.axis_index("expert")
+    z, y = index >> 2, (index >> 1) & 1
+    z = ring((ring(z) - arrival // NY) & (NZ - 1))
+    return z * NY + (y ^ (arrival % NY))
+
+
+def products(half, width, hs_ref, rows_ref, send_ref, own_ref, n):
+    mine = lax.axis_index("dp")
+    cols = pl.ds(pl.multiple_of(n * 256, 256), 256)
+    block = rows_ref[:, cols]
+    other = hs_ref[pl.ds(pl.multiple_of((1 - mine) * half, 16), half), :]
+    send_ref[:, cols] = jnp.dot(other, block, preferred_element_type=jnp.float32).astype(
+        jnp.bfloat16
+    )
+    own = hs_ref[pl.ds(pl.multiple_of(mine * half, 16), half), :]
+    own_ref[:, cols] = jnp.dot(own, block, preferred_element_type=jnp.float32)
+
+
+def dispatch(xs, pmat_ref, rows_ref, n):
+    cols = pl.ds(pl.multiple_of(n * 256, 256), 256)
+    for a in range(len(xs) // 2):
+        where = pl.ds(pl.multiple_of(pair_place(a) * LANES, LANES), LANES)
+        both = jnp.concatenate([xs[2 * a][:, cols], xs[2 * a + 1][:, cols]], axis=0)
+        rows_ref[where, cols] = jnp.dot(
+            pmat_ref[where, :], both, preferred_element_type=jnp.float32
+        ).astype(jnp.bfloat16)
+
+
+def first_kernel(experts, capacity, half, width, *refs):
+    n_blocks = experts
+    xs = refs[:n_blocks]
+    hidden_ref = refs[n_blocks]
+    rows_ref, send_ref, own_ref, pmat_ref, gslot_ref, hs_ref = refs[n_blocks + 1 :]
+    me = lax.axis_index("expert")
+    core = me & 1
+    tokens = xs[0].shape[0]
+    expert = lax.broadcasted_iota(jnp.int32, (experts, tokens), 0) == me
+    slot = lax.broadcasted_iota(jnp.int32, (LANES, tokens), 0).astype(jnp.float32)
+    for a in range(n_blocks // 2):
+        place = pair_place(a)
+        where = pl.ds(pl.multiple_of(place * LANES, LANES), LANES)
+        halves, gates = [], []
+        for b, x_ref in enumerate((xs[2 * a], xs[2 * a + 1])):
+            ext = x_ref[: 2 * experts, width:].astype(jnp.float32)
+            gate = jnp.sum(jnp.where(expert, ext[:experts], 0.0), axis=0, keepdims=True)
+            number = jnp.sum(jnp.where(expert, ext[experts:], 0.0), axis=0, keepdims=True)
+            offset = ((core ^ b) * capacity).astype(jnp.float32)
+            number = jnp.where(number >= 0, number + offset, -1.0)
+            halves.append(jnp.where(slot == number, 1.0, 0.0).astype(jnp.bfloat16))
+            gates.append(gate)
+        one_hot = jnp.concatenate(halves, axis=1)
+        pmat_ref[where, :] = one_hot
+        gate_pair = jnp.concatenate(gates, axis=1).astype(jnp.bfloat16)
+        gslot = lax.dot_general(
+            jnp.broadcast_to(gate_pair, (16, 2 * tokens)),
+            one_hot,
+            NT,
+            preferred_element_type=jnp.float32,
+        )
+        gslot_ref[:, where] = gslot[:1]
+    hs_ref[...] = (hidden_ref[...].astype(jnp.float32) * gslot_ref[...]).astype(jnp.bfloat16)
+
+    @pl.loop(0, width // 256)
+    def _(n):
+        dispatch(xs, pmat_ref, rows_ref, n)
+        products(half, width, hs_ref, rows_ref, send_ref, own_ref, n)
+
+
+def later_kernel(experts, half, width, *refs):
+    xs = refs[:experts]
+    pmat_ref, hs_ref, rows_ref, send_ref, own_ref = refs[experts:]
+
+    @pl.loop(0, width // 256)
+    def _(n):
+        dispatch(xs, pmat_ref, rows_ref, n)
+        products(half, width, hs_ref, rows_ref, send_ref, own_ref, n)
+
+
+def raw_kernel(half, chunks, *refs):
+    rows = refs[:chunks]
+    own_ref, got_ref, hidden_ref, gslot_ref, pmat_ref, grad_ref, back_ref = refs[chunks:]
+    mine = lax.axis_index("dp")
+    core = lax.axis_index("expert") & 1
+    step = pl.program_id(0)
+    width = rows[0].shape[1]
+    gates = gslot_ref[...]
+    total = jnp.zeros(gates.shape, jnp.float32)
+    for w_ref, d in ((own_ref, mine), (got_ref, 1 - mine)):
+        units = pl.ds(pl.multiple_of(d * half, 16), half)
+        raw = sum(
+            lax.dot_general(
+                w_ref[:, c * width : (c + 1) * width],
+                rows[c][...],
+                NT,
+                preferred_element_type=jnp.float32,
+            )
+            for c in range(chunks)
+        )
+        grad_ref[units, :] = (raw * gates).astype(jnp.bfloat16)
+        total += jnp.sum(
+            raw * hidden_ref[units, :].astype(jnp.float32), axis=0, keepdims=True
+        )
+    for i in range(gates.shape[1] // LANES):
+        part = jnp.broadcast_to(total[:, i * LANES : (i + 1) * LANES], (8, LANES))
+        one_hot = pmat_ref[i * LANES : (i + 1) * LANES, :].astype(jnp.float32)
+        back = jnp.dot(
+            part, one_hot, preferred_element_type=jnp.float32, precision=lax.Precision.HIGHEST
+        )
+        pair = (step * (gates.shape[1] // LANES) + i) * 2
+        back_ref[pl.ds(pair + core, 1), :] = back[:1, :LANES]
+        back_ref[pl.ds(pair + 1 - core, 1), :] = back[:1, LANES:]
+
+
+def gates_kernel(routes_ref, back_ref, out_ref):
+    back = back_ref[...]
+    routes = routes_ref[...]
+    expert = lax.broadcasted_iota(jnp.int32, back.shape, 0)
+    for k in range(out_ref.shape[0]):
+        hit = expert == routes[k : k + 1, :]
+        out_ref[k : k + 1, :] = jnp.sum(jnp.where(hit, back, 0.0), axis=0, keepdims=True)
+
+
+def ring_shards(grad_out, gates, routes, hidden, down_weight):
+    experts = lax.axis_size("expert")
+    tokens, chosen = routes.shape
+    model = grad_out.shape[1]
+    slots, units = hidden.shape[2:]
+    half = down_weight.shape[1]
+    capacity = slots // experts
+    width = model // CHUNKS
+    bf16, f32 = jnp.bfloat16, jnp.float32
+    hidden_t = hidden[0, 0].T
+    routes_t, gates_t = routes.T, gates.T
+    weight = down_weight[0]
+    swap_dp = [(0, 1), (1, 0)]
+
+    chunks = pl.pallas_call(
+        functools.partial(pack_kernel, experts, width),
+        out_shape=[
+            jax.ShapeDtypeStruct((tokens, width + (tokens if c == 0 else 0)), bf16)
+            for c in range(CHUNKS)
+        ],
+        in_specs=[VMEM] * 3,
+        out_specs=[VMEM] * CHUNKS,
+        compiler_params=params(16),
+        name="pack",
+    )(routes_t, gates_t, grad_out)
+
+    got_weight = lax.ppermute(weight, "dp", swap_dp)
+
+    blocks = []
+    for x in chunks:
+        along_z = [x]
+        for _ in range(NZ - 1):
+            along_z.append(lax.ppermute(along_z[-1], "expert", ring_pairs()))
+        arrived = []
+        for block in along_z:
+            for one in (block, lax.ppermute(block, "expert", swap_pairs(2))):
+                arrived += [one, lax.ppermute(one, "expert", swap_pairs(1))]
+        blocks.append(arrived)
+
+    flops = 2 * slots * width * (units + 2 * tokens)
+    rows, send, own = [], [], []
+    shapes = [
+        jax.ShapeDtypeStruct((slots, width), bf16),
+        jax.ShapeDtypeStruct((half, width), bf16),
+        jax.ShapeDtypeStruct((half, width), f32),
+    ]
+    for c in range(CHUNKS):
+        cost = pl.CostEstimate(flops=flops, bytes_accessed=12 * 2**20, transcendentals=0)
+        if c == 0:
+            row, out, keep, pmat, gslot, hs = pl.pallas_call(
+                functools.partial(first_kernel, experts, capacity, half, width),
+                out_shape=shapes
+                + [
+                    jax.ShapeDtypeStruct((slots, 2 * tokens), bf16),
+                    jax.ShapeDtypeStruct((1, slots), f32),
+                    jax.ShapeDtypeStruct((units, slots), bf16),
+                ],
+                in_specs=[VMEM] * (experts + 1),
+                out_specs=[VMEM] * 6,
+                compiler_params=params(40),
+                cost_estimate=cost,
+                name="first_chunk",
+            )(*blocks[0], hidden_t)
+        else:
+            row, out, keep = pl.pallas_call(
+                functools.partial(later_kernel, experts, half, width),
+                out_shape=shapes,
+                in_specs=[VMEM] * (experts + 2),
+                out_specs=[VMEM] * 3,
+                compiler_params=params(40),
+                cost_estimate=cost,
+                name="later_chunk",
+            )(*blocks[c], pmat, hs)
+        rows.append(row)
+        send.append(lax.ppermute(out, "dp", swap_dp))
+        own.append(keep)
+
+    tile = 256
+    grad_hidden, back = pl.pallas_call(
+        functools.partial(raw_kernel, half, CHUNKS),
+        grid=(slots // tile,),
+        out_shape=[
+            jax.ShapeDtypeStruct((units, slots), bf16),
+            jax.ShapeDtypeStruct((experts, tokens), f32),
+        ],
+        in_specs=[pl.BlockSpec((tile, width), lambda i: (i, 0))] * CHUNKS
+        + [pl.BlockSpec((half, model), lambda i: (0, 0))] * 2
+        + [
+            pl.BlockSpec((units, tile), lambda i: (0, i)),
+            pl.BlockSpec((1, tile), lambda i: (0, i)),
+            pl.BlockSpec((tile, 2 * tokens), lambda i: (i, 0)),
+        ],
+        out_specs=[
+            pl.BlockSpec((units, tile), lambda i: (0, i)),
+            pl.BlockSpec((experts, tokens), lambda i: (0, 0)),
+        ],
+        compiler_params=params(40),
+        cost_estimate=pl.CostEstimate(
+            flops=2 * slots * model * units, bytes_accessed=12 * 2**20, transcendentals=0
+        ),
+        name="raw",
+    )(*rows, weight, got_weight, hidden_t, gslot, pmat)
+
+    returned = lax.all_to_all(back, "expert", split_axis=0, concat_axis=0, tiled=True)
+    grad_gates = pl.pallas_call(
+        gates_kernel,
+        out_shape=jax.ShapeDtypeStruct((chosen, tokens), f32),
+        in_specs=[VMEM] * 2,
+        out_specs=VMEM,
+        name="grad_gates",
+    )(routes_t, returned)
+
+    grad_weight = jnp.concatenate(
+        [(mine + theirs.astype(f32)).astype(bf16) for mine, theirs in zip(own, send)], axis=1
+    )
+    return grad_weight[None], grad_hidden.T[None, None], grad_gates.T
 
 
 def shards(grad_out, gates, routes, hidden, down_weight):
@@ -53,8 +354,9 @@
 
 
 def solution(mesh):
+    small = mesh.shape["dp"] == 2 and mesh.shape["expert"] == NZ * NY * NC
     return jax.shard_map(
-        shards,
+        ring_shards if small else shards,
         mesh=mesh,
         in_specs=(
             P(("dp", "expert"), None),

time: 201 us -> 104 us (0.52)
  waiting for transfers between devices: 99.8 us -> 43.1 us
  local copies, waits for them, and re-layouts: 35 us -> 3.78 us
  Pallas kernels: 0 us -> 16.6 us
  between operations: 14.2 us -> 0.73 us
  matrix products: 12 us -> 0 us
  blocking collectives: 0 us -> 11.3 us
  starting transfers between devices: 33.3 us -> 24.5 us
  other arithmetic: 6.3 us -> 3.85 us
    all_to_all x3 -> x0, waiting for transfers between devices: 83.1 us -> none  [the longest x1 76.7 us: shards(): lax.all_to_all(send_rows, 'expert', split_axis=0, concat_axis=0, tiled=True)]
    ppermute x0 -> x33, waiting for transfers between devices: none -> 43.1 us  [the longest x8 22.4 us: ring_shards(): lax.ppermute(block, 'expert', swap_pairs(2))]
    all_to_all x3 -> x0, starting transfers between devices: 33.1 us -> none  [the longest x1 19.6 us: shards(): lax.all_to_all(slot_grads.reshape(owners, capacity), 'expert', split_axis...]
    ppermute x0 -> x33, starting transfers between devices: none -> 24.5 us  [the longest x8 11.3 us: ring_shards(): lax.ppermute(block, 'expert', swap_pairs(2))]
    scatter x2 -> x0, local copies, waits for them, and re-layouts: 18 us -> none  [the longest x1 9.4 us: shards(): send_rows = jnp.zeros((owners * capacity, width), grad_out.dtype).at[targ...]
    pallas_call x0 -> x5, Pallas kernels: none -> 16.6 us  [the longest x1 5.61 us: ring_shards(): pl.pallas_call(functools.partial(raw_kernel, half, CHUNKS), grid=(slots /...]
    reduce_scatter x1 -> x0, waiting for transfers between devices: 16 us -> none  [shards(): lax.psum_scatter(lax.dot_general(saved, scaled, (((0,), (0,)), ((), ())),...]
    dot_general x2 -> x0, matrix products: 12 us -> none  [the longest x1 7.43 us: shards(): lax.dot_general(rows, whole_weight, contract, preferred_element_type=jnp....]
  transfers between devices with their start and end apart: 5 -> 33, of which waited for: 3 -> 15; matrix products, arithmetic and copies ran while one was open for 19% -> 1% of each run, Pallas kernels for 0% -> 16%
where the time goes in v1:
time: 104 us
  waiting for transfers between devices  43.1 us (41%)
  starting transfers between devices  24.5 us (24%)
  Pallas kernels  16.6 us (16%)
  blocking collectives  11.3 us (11%)
  other arithmetic  3.85 us (4%)
  local copies, waits for them, and re-layouts  3.78 us (4%)
    ppermute x8, waiting for transfers between devices, ring_shards(): lax.ppermute(block, 'expert', swap_pairs(2))  22.4 us
    ppermute x6, waiting for transfers between devices, ring_shards(): along_z.append(lax.ppermute(along_z[-1], 'expert', ring_pairs()))  12.5 us
    ppermute x8, starting transfers between devices, ring_shards(): lax.ppermute(block, 'expert', swap_pairs(2))  11.3 us
    all_to_all x1, blocking collectives, ring_shards(): lax.all_to_all(back, 'expert', split_axis=0, concat_axis=0, tiled=True)  11.3 us
    ppermute x2, waiting for transfers between devices, ring_shards(): send.append(lax.ppermute(out, 'dp', swap_dp))  8.18 us
    ppermute x6, starting transfers between devices, ring_shards(): along_z.append(lax.ppermute(along_z[-1], 'expert', ring_pairs()))  7 us
    pallas_call x1, Pallas kernels, ring_shards(): pl.pallas_call(functools.partial(raw_kernel, half, CHUNKS), grid=(slots /...  5.61 us
    pallas_call x1, Pallas kernels, ring_shards(): pl.pallas_call(functools.partial(first_kernel, experts, capacity, half, w...  5.06 us
  transfers between devices with their start and end apart: 33, of which 15 were waited for; matrix products, arithmetic and copies ran while one was open for 1% of the time, Pallas kernels for 16%

profile of v1, /device:TPU:0, one launch (start us, length us, event | category | flops | bytes accessed | tf_op | source)
XLA Modules:
  0.0 103.8 jit_solution(8760857009727349275)
XLA Ops:
  3.2 3.0 %collective-permute-start.19 = (bf16[128,1024]{1,0:T(8,128)(2,1)S(1)}, bf16[128,1024]{1,0:T(8,128)(2,1)S(1)}, u32[]{:S(2)}, u32[]{:S(2)}) collective-permute-start(bf16[128,1024]{1,0:T(8,128)(2,1)S(1)} %get-tuple-element.19.refs_0_), channel_id=1, source_target_pairs={{0,4},{1,5},{2,6},{3,7},{4,12},{5,13},{6,14},{7,15},{12,8},{13,9},... | collective-permute-start | bytes 786440 | tf_op jit(solution)/shard_map/ppermute | solution.py:222
  6.2 2.6 %collective-permute-start.3 = (bf16[128,1152]{1,0:T(8,128)(2,1)S(1)}, bf16[128,1152]{1,0:T(8,128)(2,1)S(1)}, u32[]{:S(2)}, u32[]{:S(2)}) collective-permute-start(bf16[128,1152]{1,0:T(8,128)(2,1)S(1)} %get-tuple-element.16.refs_0_), channel_id=1, source_target_pairs={{0,4},{1,5},{2,6},{3,7},{4,12},{5,13},{6,14},{7,15},{12,8},{13,9},... | collective-permute-start | bytes 884744 | tf_op jit(solution)/shard_map/ppermute | solution.py:222
  10.8 3.5 %collective-permute-done.19.refs_4_ = bf16[128,1024]{1,0:T(8,128)(2,1)S(1)} collective-permute-done((bf16[128,1024]{1,0:T(8,128)(2,1)S(1)}, bf16[128,1024]{1,0:T(8,128)(2,1)S(1)}, u32[]{:S(2)}, u32[]{:S(2)}) %collective-permute-start.19) | collective-permute-done | bytes 262176 | tf_op jit(solution)/shard_map/ppermute | solution.py:222
  14.4 3.7 %collective-permute-done.17.refs_2_ = bf16[128,1024]{1,0:T(8,128)(2,1)S(1)} collective-permute-done((bf16[128,1024]{1,0:T(8,128)(2,1)S(1)}, bf16[128,1024]{1,0:T(8,128)(2,1)S(1)}, u32[]{:S(2)}, u32[]{:S(2)}) %collective-permute-start.17) | collective-permute-done | bytes 262176 | tf_op jit(solution)/shard_map/ppermute | solution.py:225
  18.5 1.5 %collective-permute-start.21 = (bf16[128,1024]{1,0:T(8,128)(2,1)S(1)}, bf16[128,1024]{1,0:T(8,128)(2,1)S(1)}, u32[]{:S(2)}, u32[]{:S(2)}) collective-permute-start(bf16[128,1024]{1,0:T(8,128)(2,1)S(1)} %collective-permute-done.19.refs_4_), channel_id=1, source_target_pairs={{0,2},{1,3},{2,0},{3,1},{4,6},{5,7},{6,4},{7,5},{8,10},{9,11},{10,... | collective-permute-start | bytes 786440 | tf_op jit(solution)/shard_map/ppermute | solution.py:225
  20.7 3.7 %collective-permute-done.1.refs_2_ = bf16[128,1152]{1,0:T(8,128)(2,1)S(1)} collective-permute-done((bf16[128,1152]{1,0:T(8,128)(2,1)S(1)}, bf16[128,1152]{1,0:T(8,128)(2,1)S(1)}, u32[]{:S(2)}, u32[]{:S(2)}) %collective-permute-start.1) | collective-permute-done | bytes 294944 | tf_op jit(solution)/shard_map/ppermute | solution.py:225
  24.4 1.8 %collective-permute-done.23.refs_8_ = bf16[128,1024]{1,0:T(8,128)(2,1)S(1)} collective-permute-done((bf16[128,1024]{1,0:T(8,128)(2,1)S(1)}, bf16[128,1024]{1,0:T(8,128)(2,1)S(1)}, u32[]{:S(2)}, u32[]{:S(2)}) %collective-permute-start.23) | collective-permute-done | bytes 262176 | tf_op jit(solution)/shard_map/ppermute | solution.py:222
  29.5 2.5 %collective-permute-done.7.refs_8_ = bf16[128,1152]{1,0:T(8,128)(2,1)S(1)} collective-permute-done((bf16[128,1152]{1,0:T(8,128)(2,1)S(1)}, bf16[128,1152]{1,0:T(8,128)(2,1)S(1)}, u32[]{:S(2)}, u32[]{:S(2)}) %collective-permute-start.7) | collective-permute-done | bytes 294944 | tf_op jit(solution)/shard_map/ppermute | solution.py:222
  32.9 1.7 %collective-permute-done.5.refs_6_ = bf16[128,1152]{1,0:T(8,128)(2,1)S(1)} collective-permute-done((bf16[128,1152]{1,0:T(8,128)(2,1)S(1)}, bf16[128,1152]{1,0:T(8,128)(2,1)S(1)}, u32[]{:S(2)}, u32[]{:S(2)}) %collective-permute-start.5) | collective-permute-done | bytes 294944 | tf_op jit(solution)/shard_map/ppermute | solution.py:225
  36.1 1.6 %collective-permute-start.32 = (bf16[352,2048]{1,0:T(8,128)(2,1)}, bf16[352,2048]{1,0:T(8,128)(2,1)S(1)}, u32[]{:S(2)}, u32[]{:S(2)}) collective-permute-start(bf16[352,2048]{1,0:T(8,128)(2,1)} %bitcast.22), channel_id=1, source_target_pairs={{0,16},{16,0},{1,17},{17,1},{2,18},{18,2},{3,19},{19,3},{4,20},{20... | collective-permute-start | bytes 4325384 | tf_op jit(solution)/shard_map/ppermute | solution.py:216
  37.6 1.8 %collective-permute-done.27.refs_12_ = bf16[128,1024]{1,0:T(8,128)(2,1)S(1)} collective-permute-done((bf16[128,1024]{1,0:T(8,128)(2,1)S(1)}, bf16[128,1024]{1,0:T(8,128)(2,1)S(1)}, u32[]{:S(2)}, u32[]{:S(2)}) %collective-permute-start.27) | collective-permute-done | bytes 262176 | tf_op jit(solution)/shard_map/ppermute | solution.py:222
  39.5 1.5 %collective-permute-start.9 = (bf16[128,1152]{1,0:T(8,128)(2,1)S(1)}, bf16[128,1152]{1,0:T(8,128)(2,1)S(1)}, u32[]{:S(2)}, u32[]{:S(2)}) collective-permute-start(bf16[128,1152]{1,0:T(8,128)(2,1)S(1)} %collective-permute-done.7.refs_8_), channel_id=1, source_target_pairs={{0,2},{1,3},{2,0},{3,1},{4,6},{5,7},{6,4},{7,5},{8,10},{9,11},{10,... | collective-permute-start | bytes 884744 | tf_op jit(solution)/shard_map/ppermute | solution.py:225
  42.7 2.2 %collective-permute-done.11.refs_12_ = bf16[128,1152]{1,0:T(8,128)(2,1)S(1)} collective-permute-done((bf16[128,1152]{1,0:T(8,128)(2,1)S(1)}, bf16[128,1152]{1,0:T(8,128)(2,1)S(1)}, u32[]{:S(2)}, u32[]{:S(2)}) %collective-permute-start.11) | collective-permute-done | bytes 294944 | tf_op jit(solution)/shard_map/ppermute | solution.py:222
  44.9 1.5 %collective-permute-start.13 = (bf16[128,1152]{1,0:T(8,128)(2,1)S(1)}, bf16[128,1152]{1,0:T(8,128)(2,1)S(1)}, u32[]{:S(2)}, u32[]{:S(2)}) collective-permute-start(bf16[128,1152]{1,0:T(8,128)(2,1)S(1)} %collective-permute-done.11.refs_12_), channel_id=1, source_target_pairs={{0,2},{1,3},{2,0},{3,1},{4,6},{5,7},{6,4},{7,5},{8,10},{9,11},{10,... | collective-permute-start | bytes 884744 | tf_op jit(solution)/shard_map/ppermute | solution.py:225
  46.4 2.1 %collective-permute-done.9.refs_10_ = bf16[128,1152]{1,0:T(8,128)(2,1)S(1)} collective-permute-done((bf16[128,1152]{1,0:T(8,128)(2,1)S(1)}, bf16[128,1152]{1,0:T(8,128)(2,1)S(1)}, u32[]{:S(2)}, u32[]{:S(2)}) %collective-permute-start.9) | collective-permute-done | bytes 294944 | tf_op jit(solution)/shard_map/ppermute | solution.py:225
  48.5 2.0 %collective-permute-start.29 = (bf16[128,1024]{1,0:T(8,128)(2,1)S(1)}, bf16[128,1024]{1,0:T(8,128)(2,1)S(1)}, u32[]{:S(2)}, u32[]{:S(2)}) collective-permute-start(bf16[128,1024]{1,0:T(8,128)(2,1)S(1)} %collective-permute-done.27.refs_12_), channel_id=1, source_target_pairs={{0,2},{1,3},{2,0},{3,1},{4,6},{5,7},{6,4},{7,5},{8,10},{9,11},{10,... | collective-permute-start | bytes 786440 | tf_op jit(solution)/shard_map/ppermute | solution.py:225
  51.0 3.8 %collective-permute-done.13.refs_14_ = bf16[128,1152]{1,0:T(8,128)(2,1)S(1)} collective-permute-done((bf16[128,1152]{1,0:T(8,128)(2,1)S(1)}, bf16[128,1152]{1,0:T(8,128)(2,1)S(1)}, u32[]{:S(2)}, u32[]{:S(2)}) %collective-permute-start.13) | collective-permute-done | bytes 294944 | tf_op jit(solution)/shard_map/ppermute | solution.py:225
  54.8 4.7 %collective-permute-done.29.refs_14_ = bf16[128,1024]{1,0:T(8,128)(2,1)S(1)} collective-permute-done((bf16[128,1024]{1,0:T(8,128)(2,1)S(1)}, bf16[128,1024]{1,0:T(8,128)(2,1)S(1)}, u32[]{:S(2)}, u32[]{:S(2)}) %collective-permute-start.29) | collective-permute-done | bytes 262176 | tf_op jit(solution)/shard_map/ppermute | solution.py:225
  62.0 5.1 %first_chunk.1 = (bf16[1024,1024]{1,0:T(8,128)(2,1)S(1)}, bf16[352,1024]{1,0:T(8,128)(2,1)}, f32[352,1024]{1,0:T(8,128)S(1)}, bf16[1024,256]{1,0:T(8,128)(2,1)S(...) custom-call(bf16[128,1152]{1,0:T(8,128)(2,1)S(1)} %get-tuple-element.16.refs_0_, ...), custom_call_target="tpu_custom_call" | custom-call | flops 2013265920 | bytes 12582912 | tf_op jit(solution)/shard_map/first_chunk/pallas_call | solution.py:239
  67.0 1.7 %collective-permute-start.15 = (bf16[352,1024]{1,0:T(8,128)(2,1)}, bf16[352,1024]{1,0:T(8,128)(2,1)}, u32[]{:S(2)}, u32[]{:S(2)}) collective-permute-start(bf16[352,1024]{1,0:T(8,128)(2,1)} %get-tuple-element.18), channel_id=1, source_target_pairs={{0,16},{16,0},{1,17},{17,1},{2,18},{18,2},{3,19},{19,3},{4,20},{20... | collective-permute-start | bytes 2162696 | tf_op jit(solution)/shard_map/ppermute | solution.py:264
  68.8 4.4 %later_chunk.1 = (bf16[1024,1024]{1,0:T(8,128)(2,1)S(1)}, bf16[352,1024]{1,0:T(8,128)(2,1)}, f32[352,1024]{1,0:T(8,128)S(1)}) custom-call(bf16[128,1024]{1,0:T(8,128)(2,1)S(1)} %get-tuple-element.19.refs_0_, bf16[128,1024]{1,0:T(8,128)(2,1)S(1)} %collective-permute-done.16.refs_1_, bf16[128,1024]{1,0:T(8,128)(2,1)S(1)} %collective-permute-done.17.refs_2_, ...), custom_call_target="tpu_custom_call" | custom-call | flops 2013265920 | bytes 12582912 | tf_op jit(solution)/shard_map/later_chunk/pallas_call | solution.py:254
  73.6 5.6 %raw.1 = (bf16[704,1024]{1,0:T(8,128)(2,1)}, f32[16,128]{1,0:T(8,128)S(1)}) custom-call(bf16[1024,1024]{1,0:T(8,128)(2,1)S(1)} %get-tuple-element.24.refs_0_, bf16[1024,1024]{1,0:T(8,128)(2,1)S(1)} %get-tuple-element.25.refs_1_, bf16[352,2048]{1,0:T(8,128)(2,1)S(1)} %bitcast.23, bf16[352,2048]{1,0:T(8,128)(2,1)S(1)} %collective-permute-done.32.refs_3_, ...), custom_call_target="tpu_custom_call" | custom-call | flops 2952790016 | bytes 12582912 | tf_op jit(solution)/shard_map/raw/pallas_call | solution.py:268
  79.2 11.3 %all_to_all.11 = f32[16,1,128]{2,1,0:T(1,128)} all-to-all(f32[16,1,128]{2,1,0:T(1,128)S(1)} %bitcast.18), channel_id=1, replica_groups=mesh['dp'=2,'expert'=16] {'expert'}, dimensions={0} | all-to-all | bytes 16384 | tf_op jit(solution)/shard_map/all_to_all | solution.py:293
  93.1 8.2 %collective-permute-done.31 = bf16[352,1024]{1,0:T(8,128)(2,1)} collective-permute-done((bf16[352,1024]{1,0:T(8,128)(2,1)}, bf16[352,1024]{1,0:T(8,128)(2,1)}, u32[]{:S(2)}, u32[]{:S(2)}) %collective-permute-start.31) | collective-permute-done | bytes 720928 | tf_op jit(solution)/shard_map/ppermute | solution.py:264
  (63 shorter events, 21.5 us)
Async XLA Ops:
  3.2 11.2 %collective-permute-start.19 = (bf16[128,1024]{1,0:T(8,128)(2,1)S(1)}, bf16[128,1024]{1,0:T(8,128)(2,1)S(1)}, u32[]{:S(2)}, u32[]{:S(2)}) collective-permute-start(bf16[128,1024]{1,0:T(8,128)(2,1)S(1)} %get-tuple-element.19.refs_0_), channel_id=1, source_target_pairs={{0,4},{1,5},{2,6},{3,7},{4,12},{5,13},{6,14},{7,15},{12,8},{13,9},... | collective-permute-start | bytes 786440 | tf_op jit(solution)/shard_map/ppermute | solution.py:222
  6.2 14.5 %collective-permute-start.3 = (bf16[128,1152]{1,0:T(8,128)(2,1)S(1)}, bf16[128,1152]{1,0:T(8,128)(2,1)S(1)}, u32[]{:S(2)}, u32[]{:S(2)}) collective-permute-start(bf16[128,1152]{1,0:T(8,128)(2,1)S(1)} %get-tuple-element.16.refs_0_), channel_id=1, source_target_pairs={{0,4},{1,5},{2,6},{3,7},{4,12},{5,13},{6,14},{7,15},{12,8},{13,9},... | collective-permute-start | bytes 884744 | tf_op jit(solution)/shard_map/ppermute | solution.py:222
  8.8 9.2 %collective-permute-start.17 = (bf16[128,1024]{1,0:T(8,128)(2,1)S(1)}, bf16[128,1024]{1,0:T(8,128)(2,1)S(1)}, u32[]{:S(2)}, u32[]{:S(2)}) collective-permute-start(bf16[128,1024]{1,0:T(8,128)(2,1)S(1)} %get-tuple-element.19.refs_0_), channel_id=1, source_target_pairs={{0,2},{1,3},{2,0},{3,1},{4,6},{5,7},{6,4},{7,5},{8,10},{9,11},{10,... | collective-permute-start | bytes 786440 | tf_op jit(solution)/shard_map/ppermute | solution.py:225
  10.3 8.2 %collective-permute-start.16 = (bf16[128,1024]{1,0:T(8,128)(2,1)S(1)}, bf16[128,1024]{1,0:T(8,128)(2,1)S(1)}, u32[]{:S(2)}, u32[]{:S(2)}) collective-permute-start(bf16[128,1024]{1,0:T(8,128)(2,1)S(1)} %get-tuple-element.19.refs_0_), channel_id=1, source_target_pairs={{0,1},{1,0},{2,3},{3,2},{4,5},{5,4},{6,7},{7,6},{8,9},{9,8},{10,11... | collective-permute-start | bytes 786440 | tf_op jit(solution)/shard_map/ppermute | solution.py:226
  10.3 14.0 %collective-permute-start.1 = (bf16[128,1152]{1,0:T(8,128)(2,1)S(1)}, bf16[128,1152]{1,0:T(8,128)(2,1)S(1)}, u32[]{:S(2)}, u32[]{:S(2)}) collective-permute-start(bf16[128,1152]{1,0:T(8,128)(2,1)S(1)} %get-tuple-element.16.refs_0_), channel_id=1, source_target_pairs={{0,2},{1,3},{2,0},{3,1},{4,6},{5,7},{6,4},{7,5},{8,10},{9,11},{10,... | collective-permute-start | bytes 884744 | tf_op jit(solution)/shard_map/ppermute | solution.py:225
  14.4 10.0 %collective-permute-start = (bf16[128,1152]{1,0:T(8,128)(2,1)S(1)}, bf16[128,1152]{1,0:T(8,128)(2,1)S(1)}, u32[]{:S(2)}, u32[]{:S(2)}) collective-permute-start(bf16[128,1152]{1,0:T(8,128)(2,1)S(1)} %get-tuple-element.16.refs_0_), channel_id=1, source_target_pairs={{0,1},{1,0},{2,3},{3,2},{4,5},{5,4},{6,7},{7,6},{8,9},{9,8},{10,11... | collective-permute-start | bytes 884744 | tf_op jit(solution)/shard_map/ppermute | solution.py:226
  18.5 10.4 %collective-permute-start.21 = (bf16[128,1024]{1,0:T(8,128)(2,1)S(1)}, bf16[128,1024]{1,0:T(8,128)(2,1)S(1)}, u32[]{:S(2)}, u32[]{:S(2)}) collective-permute-start(bf16[128,1024]{1,0:T(8,128)(2,1)S(1)} %collective-permute-done.19.refs_4_), channel_id=1, source_target_pairs={{0,2},{1,3},{2,0},{3,1},{4,6},{5,7},{6,4},{7,5},{8,10},{9,11},{10,... | collective-permute-start | bytes 786440 | tf_op jit(solution)/shard_map/ppermute | solution.py:225
  20.7 8.2 %collective-permute-start.20 = (bf16[128,1024]{1,0:T(8,128)(2,1)S(1)}, bf16[128,1024]{1,0:T(8,128)(2,1)S(1)}, u32[]{:S(2)}, u32[]{:S(2)}) collective-permute-start(bf16[128,1024]{1,0:T(8,128)(2,1)S(1)} %collective-permute-done.19.refs_4_), channel_id=1, source_target_pairs={{0,1},{1,0},{2,3},{3,2},{4,5},{5,4},{6,7},{7,6},{8,9},{9,8},{10,11... | collective-permute-start | bytes 786440 | tf_op jit(solution)/shard_map/ppermute | solution.py:226
  26.2 8.4 %collective-permute-start.5 = (bf16[128,1152]{1,0:T(8,128)(2,1)S(1)}, bf16[128,1152]{1,0:T(8,128)(2,1)S(1)}, u32[]{:S(2)}, u32[]{:S(2)}) collective-permute-start(bf16[128,1152]{1,0:T(8,128)(2,1)S(1)} %collective-permute-done.3.refs_4_), channel_id=1, source_target_pairs={{0,2},{1,3},{2,0},{3,1},{4,6},{5,7},{6,4},{7,5},{8,10},{9,11},{10,... | collective-permute-start | bytes 884744 | tf_op jit(solution)/shard_map/ppermute | solution.py:225
  29.4 10.1 %collective-permute-start.27 = (bf16[128,1024]{1,0:T(8,128)(2,1)S(1)}, bf16[128,1024]{1,0:T(8,128)(2,1)S(1)}, u32[]{:S(2)}, u32[]{:S(2)}) collective-permute-start(bf16[128,1024]{1,0:T(8,128)(2,1)S(1)} %collective-permute-done.23.refs_8_), channel_id=1, source_target_pairs={{0,4},{1,5},{2,6},{3,7},{4,12},{5,13},{6,14},{7,15},{12,8},{13,9},... | collective-permute-start | bytes 786440 | tf_op jit(solution)/shard_map/ppermute | solution.py:222
  32.0 12.9 %collective-permute-start.11 = (bf16[128,1152]{1,0:T(8,128)(2,1)S(1)}, bf16[128,1152]{1,0:T(8,128)(2,1)S(1)}, u32[]{:S(2)}, u32[]{:S(2)}) collective-permute-start(bf16[128,1152]{1,0:T(8,128)(2,1)S(1)} %collective-permute-done.7.refs_8_), channel_id=1, source_target_pairs={{0,4},{1,5},{2,6},{3,7},{4,12},{5,13},{6,14},{7,15},{12,8},{13,9},... | collective-permute-start | bytes 884744 | tf_op jit(solution)/shard_map/ppermute | solution.py:222
  36.1 37.5 %collective-permute-start.32 = (bf16[352,2048]{1,0:T(8,128)(2,1)}, bf16[352,2048]{1,0:T(8,128)(2,1)S(1)}, u32[]{:S(2)}, u32[]{:S(2)}) collective-permute-start(bf16[352,2048]{1,0:T(8,128)(2,1)} %bitcast.22), channel_id=1, source_target_pairs={{0,16},{16,0},{1,17},{17,1},{2,18},{18,2},{3,19},{19,3},{4,20},{20... | collective-permute-start | bytes 4325384 | tf_op jit(solution)/shard_map/ppermute | solution.py:216
  39.5 9.0 %collective-permute-start.9 = (bf16[128,1152]{1,0:T(8,128)(2,1)S(1)}, bf16[128,1152]{1,0:T(8,128)(2,1)S(1)}, u32[]{:S(2)}, u32[]{:S(2)}) collective-permute-start(bf16[128,1152]{1,0:T(8,128)(2,1)S(1)} %collective-permute-done.7.refs_8_), channel_id=1, source_target_pairs={{0,2},{1,3},{2,0},{3,1},{4,6},{5,7},{6,4},{7,5},{8,10},{9,11},{10,... | collective-permute-start | bytes 884744 | tf_op jit(solution)/shard_map/ppermute | solution.py:225
  42.2 8.3 %collective-permute-start.8 = (bf16[128,1152]{1,0:T(8,128)(2,1)S(1)}, bf16[128,1152]{1,0:T(8,128)(2,1)S(1)}, u32[]{:S(2)}, u32[]{:S(2)}) collective-permute-start(bf16[128,1152]{1,0:T(8,128)(2,1)S(1)} %collective-permute-done.7.refs_8_), channel_id=1, source_target_pairs={{0,1},{1,0},{2,3},{3,2},{4,5},{5,4},{6,7},{7,6},{8,9},{9,8},{10,11... | collective-permute-start | bytes 884744 | tf_op jit(solution)/shard_map/ppermute | solution.py:226
  42.2 8.3 %collective-permute-start.6 = (bf16[128,1152]{1,0:T(8,128)(2,1)S(1)}, bf16[128,1152]{1,0:T(8,128)(2,1)S(1)}, u32[]{:S(2)}, u32[]{:S(2)}) collective-permute-start(bf16[128,1152]{1,0:T(8,128)(2,1)S(1)} %collective-permute-done.5.refs_6_), channel_id=1, source_target_pairs={{0,1},{1,0},{2,3},{3,2},{4,5},{5,4},{6,7},{7,6},{8,9},{9,8},{10,11... | collective-permute-start | bytes 884744 | tf_op jit(solution)/shard_map/ppermute | solution.py:226
  44.9 9.9 %collective-permute-start.13 = (bf16[128,1152]{1,0:T(8,128)(2,1)S(1)}, bf16[128,1152]{1,0:T(8,128)(2,1)S(1)}, u32[]{:S(2)}, u32[]{:S(2)}) collective-permute-start(bf16[128,1152]{1,0:T(8,128)(2,1)S(1)} %collective-permute-done.11.refs_12_), channel_id=1, source_target_pairs={{0,2},{1,3},{2,0},{3,1},{4,6},{5,7},{6,4},{7,5},{8,10},{9,11},{10,... | collective-permute-start | bytes 884744 | tf_op jit(solution)/shard_map/ppermute | solution.py:225
  48.5 11.1 %collective-permute-start.29 = (bf16[128,1024]{1,0:T(8,128)(2,1)S(1)}, bf16[128,1024]{1,0:T(8,128)(2,1)S(1)}, u32[]{:S(2)}, u32[]{:S(2)}) collective-permute-start(bf16[128,1024]{1,0:T(8,128)(2,1)S(1)} %collective-permute-done.27.refs_12_), channel_id=1, source_target_pairs={{0,2},{1,3},{2,0},{3,1},{4,6},{5,7},{6,4},{7,5},{8,10},{9,11},{10,... | collective-permute-start | bytes 786440 | tf_op jit(solution)/shard_map/ppermute | solution.py:225
  50.5 9.1 %collective-permute-start.12 = (bf16[128,1152]{1,0:T(8,128)(2,1)S(1)}, bf16[128,1152]{1,0:T(8,128)(2,1)S(1)}, u32[]{:S(2)}, u32[]{:S(2)}) collective-permute-start(bf16[128,1152]{1,0:T(8,128)(2,1)S(1)} %collective-permute-done.11.refs_12_), channel_id=1, source_target_pairs={{0,1},{1,0},{2,3},{3,2},{4,5},{5,4},{6,7},{7,6},{8,9},{9,8},{10,11... | collective-permute-start | bytes 884744 | tf_op jit(solution)/shard_map/ppermute | solution.py:226
  50.5 9.6 %collective-permute-start.10 = (bf16[128,1152]{1,0:T(8,128)(2,1)S(1)}, bf16[128,1152]{1,0:T(8,128)(2,1)S(1)}, u32[]{:S(2)}, u32[]{:S(2)}) collective-permute-start(bf16[128,1152]{1,0:T(8,128)(2,1)S(1)} %collective-permute-done.9.refs_10_), channel_id=1, source_target_pairs={{0,1},{1,0},{2,3},{3,2},{4,5},{5,4},{6,7},{7,6},{8,9},{9,8},{10,11... | collective-permute-start | bytes 884744 | tf_op jit(solution)/shard_map/ppermute | solution.py:226
  59.6 9.2 %collective-permute-start.28 = (bf16[128,1024]{1,0:T(8,128)(2,1)S(1)}, bf16[128,1024]{1,0:T(8,128)(2,1)S(1)}, u32[]{:S(2)}, u32[]{:S(2)}) collective-permute-start(bf16[128,1024]{1,0:T(8,128)(2,1)S(1)} %collective-permute-done.27.refs_12_), channel_id=1, source_target_pairs={{0,1},{1,0},{2,3},{3,2},{4,5},{5,4},{6,7},{7,6},{8,9},{9,8},{10,11... | collective-permute-start | bytes 786440 | tf_op jit(solution)/shard_map/ppermute | solution.py:226
  60.1 8.7 %collective-permute-start.26 = (bf16[128,1024]{1,0:T(8,128)(2,1)S(1)}, bf16[128,1024]{1,0:T(8,128)(2,1)S(1)}, u32[]{:S(2)}, u32[]{:S(2)}) collective-permute-start(bf16[128,1024]{1,0:T(8,128)(2,1)S(1)} %collective-permute-done.25.refs_10_), channel_id=1, source_target_pairs={{0,1},{1,0},{2,3},{3,2},{4,5},{5,4},{6,7},{7,6},{8,9},{9,8},{10,11... | collective-permute-start | bytes 786440 | tf_op jit(solution)/shard_map/ppermute | solution.py:226
  60.2 8.6 %collective-permute-start.30 = (bf16[128,1024]{1,0:T(8,128)(2,1)S(1)}, bf16[128,1024]{1,0:T(8,128)(2,1)S(1)}, u32[]{:S(2)}, u32[]{:S(2)}) collective-permute-start(bf16[128,1024]{1,0:T(8,128)(2,1)S(1)} %collective-permute-done.29.refs_14_), channel_id=1, source_target_pairs={{0,1},{1,0},{2,3},{3,2},{4,5},{5,4},{6,7},{7,6},{8,9},{9,8},{10,11... | collective-permute-start | bytes 786440 | tf_op jit(solution)/shard_map/ppermute | solution.py:226
  67.0 24.7 %collective-permute-start.15 = (bf16[352,1024]{1,0:T(8,128)(2,1)}, bf16[352,1024]{1,0:T(8,128)(2,1)}, u32[]{:S(2)}, u32[]{:S(2)}) collective-permute-start(bf16[352,1024]{1,0:T(8,128)(2,1)} %get-tuple-element.18), channel_id=1, source_target_pairs={{0,16},{16,0},{1,17},{17,1},{2,18},{18,2},{3,19},{19,3},{4,20},{20... | collective-permute-start | bytes 2162696 | tf_op jit(solution)/shard_map/ppermute | solution.py:264
  73.2 28.1 %collective-permute-start.31 = (bf16[352,1024]{1,0:T(8,128)(2,1)}, bf16[352,1024]{1,0:T(8,128)(2,1)}, u32[]{:S(2)}, u32[]{:S(2)}) collective-permute-start(bf16[352,1024]{1,0:T(8,128)(2,1)} %get-tuple-element.23), channel_id=1, source_target_pairs={{0,16},{16,0},{1,17},{17,1},{2,18},{18,2},{3,19},{19,3},{4,20},{20... | collective-permute-start | bytes 2162696 | tf_op jit(solution)/shard_map/ppermute | solution.py:264
  (15 other events, 75.0 us)

commit v2 on v1

--- a/solution.py
+++ b/solution.py
@@ -65,10 +65,7 @@
 
 
 def pair_place(arrival):
-    index = lax.axis_index("expert")
-    z, y = index >> 2, (index >> 1) & 1
-    z = ring((ring(z) - arrival // NY) & (NZ - 1))
-    return z * NY + (y ^ (arrival % NY))
+    return arrival
 
 
 def products(half, width, hs_ref, rows_ref, send_ref, own_ref, n):
@@ -86,7 +83,7 @@
 def dispatch(xs, pmat_ref, rows_ref, n):
     cols = pl.ds(pl.multiple_of(n * 256, 256), 256)
     for a in range(len(xs) // 2):
-        where = pl.ds(pl.multiple_of(pair_place(a) * LANES, LANES), LANES)
+        where = pl.ds(pair_place(a) * LANES, LANES)
         both = jnp.concatenate([xs[2 * a][:, cols], xs[2 * a + 1][:, cols]], axis=0)
         rows_ref[where, cols] = jnp.dot(
             pmat_ref[where, :], both, preferred_element_type=jnp.float32
@@ -95,23 +92,23 @@
 
 def first_kernel(experts, capacity, half, width, *refs):
     n_blocks = experts
-    xs = refs[:n_blocks]
-    hidden_ref = refs[n_blocks]
-    rows_ref, send_ref, own_ref, pmat_ref, gslot_ref, hs_ref = refs[n_blocks + 1 :]
+    xs = [refs[0].at[j] for j in range(n_blocks)]
+    hidden_ref = refs[1]
+    rows_ref, send_ref, own_ref, pmat_ref, gslot_ref, hs_ref = refs[2:]
     me = lax.axis_index("expert")
-    core = me & 1
+    core = 0
     tokens = xs[0].shape[0]
     expert = lax.broadcasted_iota(jnp.int32, (experts, tokens), 0) == me
     slot = lax.broadcasted_iota(jnp.int32, (LANES, tokens), 0).astype(jnp.float32)
     for a in range(n_blocks // 2):
         place = pair_place(a)
-        where = pl.ds(pl.multiple_of(place * LANES, LANES), LANES)
+        where = pl.ds(place * LANES, LANES)
         halves, gates = [], []
         for b, x_ref in enumerate((xs[2 * a], xs[2 * a + 1])):
             ext = x_ref[: 2 * experts, width:].astype(jnp.float32)
             gate = jnp.sum(jnp.where(expert, ext[:experts], 0.0), axis=0, keepdims=True)
             number = jnp.sum(jnp.where(expert, ext[experts:], 0.0), axis=0, keepdims=True)
-            offset = ((core ^ b) * capacity).astype(jnp.float32)
+            offset = float(b * capacity)
             number = jnp.where(number >= 0, number + offset, -1.0)
             halves.append(jnp.where(slot == number, 1.0, 0.0).astype(jnp.bfloat16))
             gates.append(gate)
@@ -134,8 +131,8 @@
 
 
 def later_kernel(experts, half, width, *refs):
-    xs = refs[:experts]
-    pmat_ref, hs_ref, rows_ref, send_ref, own_ref = refs[experts:]
+    xs = [refs[0].at[j] for j in range(experts)]
+    pmat_ref, hs_ref, rows_ref, send_ref, own_ref = refs[1:]
 
     @pl.loop(0, width // 256)
     def _(n):
@@ -147,7 +144,7 @@
     rows = refs[:chunks]
     own_ref, got_ref, hidden_ref, gslot_ref, pmat_ref, grad_ref, back_ref = refs[chunks:]
     mine = lax.axis_index("dp")
-    core = lax.axis_index("expert") & 1
+    core = 0
     step = pl.program_id(0)
     width = rows[0].shape[1]
     gates = gslot_ref[...]
@@ -217,13 +214,7 @@
 
     blocks = []
     for x in chunks:
-        along_z = [x]
-        for _ in range(NZ - 1):
-            along_z.append(lax.ppermute(along_z[-1], "expert", ring_pairs()))
-        arrived = []
-        for block in along_z:
-            for one in (block, lax.ppermute(block, "expert", swap_pairs(2))):
-                arrived += [one, lax.ppermute(one, "expert", swap_pairs(1))]
+        arrived = [lax.all_gather(x, "expert")]
         blocks.append(arrived)
 
     flops = 2 * slots * width * (units + 2 * tokens)
@@ -244,7 +235,7 @@
                     jax.ShapeDtypeStruct((1, slots), f32),
                     jax.ShapeDtypeStruct((units, slots), bf16),
                 ],
-                in_specs=[VMEM] * (experts + 1),
+                in_specs=[VMEM] * 2,
                 out_specs=[VMEM] * 6,
                 compiler_params=params(40),
                 cost_estimate=cost,
@@ -254,7 +245,7 @@
             row, out, keep = pl.pallas_call(
                 functools.partial(later_kernel, experts, half, width),
                 out_shape=shapes,
-                in_specs=[VMEM] * (experts + 2),
+                in_specs=[VMEM] * 3,
                 out_specs=[VMEM] * 3,
                 compiler_params=params(40),
                 cost_estimate=cost,

time: 104 us -> 170 us (1.63)
  waiting for transfers between devices: 43.1 us -> 107 us
  starting transfers between devices: 24.5 us -> 5.11 us
  between operations: 0.73 us -> 14.1 us
  local copies, waits for them, and re-layouts: 3.78 us -> 12.1 us
  blocking collectives: 11.3 us -> 9.44 us
    all_gather x0 -> x2, waiting for transfers between devices: none -> 93.3 us  [ring_shards(): arrived = [lax.all_gather(x, 'expert')]]
    ppermute x30 -> x0, waiting for transfers between devices: 34.9 us -> none  [the longest x8 22.4 us: ring_shards(): lax.ppermute(block, 'expert', swap_pairs(2))]
    ppermute x30 -> x0, starting transfers between devices: 20.9 us -> none  [the longest x8 11.3 us: ring_shards(): lax.ppermute(block, 'expert', swap_pairs(2))]
    unnamed x12 -> x24, local copies, waits for them, and re-layouts: 3.78 us -> 12.1 us
    ppermute x2, waiting for transfers between devices: 8.18 us -> 13 us  [ring_shards(): send.append(lax.ppermute(out, 'dp', swap_dp))]
    all_to_all x1, blocking collectives: 11.3 us -> 9.44 us  [ring_shards(): lax.all_to_all(back, 'expert', split_axis=0, concat_axis=0, tiled=True)]
  transfers between devices with their start and end apart: 33 -> 5, of which waited for: 15 -> 3; matrix products, arithmetic and copies ran while one was open for 1% -> 1% of each run, Pallas kernels for 16% -> 10%
where the time goes in v2:
time: 170 us; the launch traced here: 169 us
  waiting for transfers between devices  107 us (63%)
  Pallas kernels  17.5 us (10%)
  between operations  14.1 us (8%)
  local copies, waits for them, and re-layouts  12.1 us (7%)
  blocking collectives  9.44 us (6%)
  starting transfers between devices  5.11 us (3%)
  other arithmetic  3.85 us (2%)
    all_gather x2, waiting for transfers between devices, ring_shards(): arrived = [lax.all_gather(x, 'expert')]  93.3 us
    ppermute x2, waiting for transfers between devices, ring_shards(): send.append(lax.ppermute(out, 'dp', swap_dp))  13 us
    unnamed x24, local copies, waits for them, and re-layouts  12.1 us
    all_to_all x1, blocking collectives, ring_shards(): lax.all_to_all(back, 'expert', split_axis=0, concat_axis=0, tiled=True)  9.44 us
    pallas_call x1, Pallas kernels, ring_shards(): pl.pallas_call(functools.partial(raw_kernel, half, CHUNKS), grid=(slots /...  6.88 us
    pallas_call x1, Pallas kernels, ring_shards(): pl.pallas_call(functools.partial(first_kernel, experts, capacity, half, w...  4.58 us
    pallas_call x1, Pallas kernels, ring_shards(): pl.pallas_call(functools.partial(later_kernel, experts, half, width), out...  3.83 us
  transfers between devices with their start and end apart: 5, of which 3 were waited for; matrix products, arithmetic and copies ran while one was open for 1% of the time, Pallas kernels for 10%

profile of v2, /device:TPU:0, one launch (start us, length us, event | category | flops | bytes accessed | tf_op | source)
XLA Modules:
  0.0 169.1 jit_solution(8109222146180948887)
XLA Ops:
  7.2 1.0 copy-done
  8.3 0.7 copy-done.1
  8.9 0.7 copy-done.2
  9.6 0.9 pack.1
  10.6 0.7 all-gather.7.cloned.1.call-update
  11.3 3.0 %collective-permute-start.2 = (bf16[352,2048]{1,0:T(8,128)(2,1)}, bf16[352,2048]{1,0:T(8,128)(2,1)}, u32[]{:S(2)}, u32[]{:S(2)}) collective-permute-start(bf16[352,2048]{1,0:T(8,128)(2,1)} %bitcast.26), channel_id=1, source_target_pairs={{0,16},{16,0},{1,17},{17,1},{2,18},{18,2},{3,19},{19,3},{4,20},{20... | collective-permute-start | bytes 4325384 | tf_op jit(solution)/shard_map/ppermute | solution.py:213
  14.3 52.7 %all-gather.5.cloned.1.call-done = bf16[2048,1152]{1,0:T(8,128)(2,1)} async-done(((bf16[128,1152]{1,0:T(8,128)(2,1)}), bf16[2048,1152]{1,0:T(8,128)(2,1)}) %all-gather.5.cloned.1.call-update) | async-done | bytes 4718608 | tf_op jit(solution)/shard_map/all_gather | solution.py:217
  67.0 2.3 %copy-done.3 = bf16[2048,1152]{1,0:T(8,128)(2,1)S(1)} copy-done((bf16[2048,1152]{1,0:T(8,128)(2,1)S(1)}, bf16[2048,1152]{1,0:T(8,128)(2,1)}, u32[]{:S(2)}) %copy-start.3) | copy-done | bytes 4718616
  69.3 1.4 copy-done.5
  70.7 4.6 %first_chunk.1 = (bf16[1024,1024]{1,0:T(8,128)(2,1)S(1)}, bf16[352,1024]{1,0:T(8,128)(2,1)}, f32[352,1024]{1,0:T(8,128)S(1)}, bf16[1024,256]{1,0:T(8,128)(2,1)S(...) custom-call(bf16[16,128,1152]{2,1,0:T(8,128)(2,1)S(1)} %bitcast.22, bf16[704,1024]{1,0:T(8,128)(2,1)S(1)} %bitcast.24), custom_call_target="tpu_custom_call" | custom-call | flops 2013265920 | bytes 12582912 | tf_op jit(solution)/shard_map/first_chunk/pallas_call | solution.py:230
  75.3 1.3 copy-done.8
  76.6 1.1 copy-done.10
  77.7 40.6 %all-gather.7.cloned.1.call-done = bf16[2048,1024]{1,0:T(8,128)(2,1)} async-done(((bf16[128,1024]{1,0:T(8,128)(2,1)}), bf16[2048,1024]{1,0:T(8,128)(2,1)}) %all-gather.7.cloned.1.call-update) | async-done | bytes 4194320 | tf_op jit(solution)/shard_map/all_gather | solution.py:217
  118.3 2.2 %copy-done.4 = bf16[2048,1024]{1,0:T(8,128)(2,1)S(1)} copy-done((bf16[2048,1024]{1,0:T(8,128)(2,1)S(1)}, bf16[2048,1024]{1,0:T(8,128)(2,1)}, u32[]{:S(2)}) %copy-start.4) | copy-done | bytes 4194328
  120.5 1.4 copy-done.11
  121.8 3.8 %later_chunk.1 = (bf16[1024,1024]{1,0:T(8,128)(2,1)S(1)}, bf16[352,1024]{1,0:T(8,128)(2,1)}, f32[352,1024]{1,0:T(8,128)S(1)}) custom-call(bf16[16,128,1024]{2,1,0:T(8,128)(2,1)S(1)} %bitcast.23, bf16[1024,256]{1,0:T(8,128)(2,1)S(1)} %get-tuple-element.20.refs_1_.refs_6_, bf16[704,1024]{1,0:T(8,128)(2,1)S(1)} %copy-done.11), custom_call_target="tpu_custom_call" | custom-call | flops 2013265920 | bytes 12582912 | tf_op jit(solution)/shard_map/later_chunk/pallas_call | solution.py:245
  125.7 1.5 collective-permute-start.1
  127.7 6.9 %raw.1 = (bf16[704,1024]{1,0:T(8,128)(2,1)}, f32[16,128]{1,0:T(8,128)S(1)}) custom-call(bf16[1024,1024]{1,0:T(8,128)(2,1)S(1)} %copy-done.9, bf16[1024,1024]{1,0:T(8,128)(2,1)S(1)} %get-tuple-element.25.refs_1_, bf16[352,2048]{1,0:T(8,128)(2,1)S(1)} %bitcast.27, bf16[352,2048]{1,0:T(8,128)(2,1)} %collective-permute-done.2.refs_3_, ...), custom_call_target="tpu_custom_call" | custom-call | flops 2952790016 | bytes 12582912 | tf_op jit(solution)/shard_map/raw/pallas_call | solution.py:259
  134.6 9.4 %all_to_all.11 = f32[16,1,128]{2,1,0:T(1,128)} all-to-all(f32[16,1,128]{2,1,0:T(1,128)S(1)} %bitcast.20), channel_id=1, replica_groups=mesh['dp'=2,'expert'=16] {'expert'}, dimensions={0} | all-to-all | bytes 16384 | tf_op jit(solution)/shard_map/all_to_all | solution.py:284
  144.0 1.3 grad_gates.1
  145.4 1.3 add_convert_fusion
  146.7 13.0 %collective-permute-done = bf16[352,1024]{1,0:T(8,128)(2,1)} collective-permute-done((bf16[352,1024]{1,0:T(8,128)(2,1)}, bf16[352,1024]{1,0:T(8,128)(2,1)}, u32[]{:S(2)}, u32[]{:S(2)}) %collective-permute-start) | collective-permute-done | bytes 720928 | tf_op jit(solution)/shard_map/ppermute | solution.py:255
  159.7 1.3 add_convert_fusion.1
  161.1 1.2 maximum_bitcast_fusion
  (21 shorter events, 0.7 us)
Async XLA Ops:
  7.2 59.8 %all-gather.5.cloned.1.call-start = ((), (), s32[]{:S(2)}) async-start(), calls=%async_computation.1 | async-start | bytes 5013504 | tf_op jit(solution)/shard_map/all_gather | solution.py:217
  7.2 1.0 copy-start
  8.3 0.7 copy-start.1
  8.9 0.7 copy-start.2
  10.5 107.8 %all-gather.7.cloned.1.call-start = ((), (), s32[]{:S(2)}) async-start(), calls=%async_computation.2 | async-start | bytes 4456448 | tf_op jit(solution)/shard_map/all_gather | solution.py:217
  11.3 116.5 %collective-permute-start.2 = (bf16[352,2048]{1,0:T(8,128)(2,1)}, bf16[352,2048]{1,0:T(8,128)(2,1)}, u32[]{:S(2)}, u32[]{:S(2)}) collective-permute-start(bf16[352,2048]{1,0:T(8,128)(2,1)} %bitcast.26), channel_id=1, source_target_pairs={{0,16},{16,0},{1,17},{17,1},{2,18},{18,2},{3,19},{19,3},{4,20},{20... | collective-permute-start | bytes 4325384 | tf_op jit(solution)/shard_map/ppermute | solution.py:213
  67.0 2.3 %copy-start.3 = (bf16[2048,1152]{1,0:T(8,128)(2,1)S(1)}, bf16[2048,1152]{1,0:T(8,128)(2,1)}, u32[]{:S(2)}) copy-start(bf16[2048,1152]{1,0:T(8,128)(2,1)} %all-gather.5.cloned.1.call-done) | copy-start | bytes 14155780
  69.3 1.4 copy-start.5
  75.3 1.3 copy-start.8
  76.6 1.1 copy-start.10
  118.3 2.2 %copy-start.4 = (bf16[2048,1024]{1,0:T(8,128)(2,1)S(1)}, bf16[2048,1024]{1,0:T(8,128)(2,1)}, u32[]{:S(2)}) copy-start(bf16[2048,1024]{1,0:T(8,128)(2,1)} %all-gather.7.cloned.1.call-done) | copy-start | bytes 12582916
  120.5 1.4 copy-start.11
  121.8 5.9 %copy-start.6 = (bf16[1,1,1024,704]{2,3,1,0:T(8,128)(2,1)S(1)}, bf16[1,1,1024,704]{2,3,1,0:T(8,128)(2,1)}, u32[]{:S(2)}) copy-start(bf16[1,1,1024,704]{2,3,1,0:T(8,128)(2,1)} %param.8) | copy-start | bytes 4325380
  121.8 5.9 %copy-start.7 = (bf16[1,352,2048]{2,1,0:T(8,128)(2,1)S(1)}, bf16[1,352,2048]{2,1,0:T(8,128)(2,1)}, u32[]{:S(2)}) copy-start(bf16[1,352,2048]{2,1,0:T(8,128)(2,1)} %param.9) | copy-start | bytes 4325380
  121.8 5.9 %copy-start.9 = (bf16[1024,1024]{1,0:T(8,128)(2,1)S(1)}, bf16[1024,1024]{1,0:T(8,128)(2,1)}, u32[]{:S(2)}) copy-start(bf16[1024,1024]{1,0:T(8,128)(2,1)} %copy-done.8) | copy-start | bytes 6291460
  125.7 19.7 %collective-permute-start.1 = (bf16[352,1024]{1,0:T(8,128)(2,1)}, bf16[352,1024]{1,0:T(8,128)(2,1)}, u32[]{:S(2)}, u32[]{:S(2)}) collective-permute-start(bf16[352,1024]{1,0:T(8,128)(2,1)} %get-tuple-element.23), channel_id=1, source_target_pairs={{0,16},{16,0},{1,17},{17,1},{2,18},{18,2},{3,19},{19,3},{4,20},{20... | collective-permute-start | bytes 2162696 | tf_op jit(solution)/shard_map/ppermute | solution.py:255
  127.1 32.6 %collective-permute-start = (bf16[352,1024]{1,0:T(8,128)(2,1)}, bf16[352,1024]{1,0:T(8,128)(2,1)}, u32[]{:S(2)}, u32[]{:S(2)}) collective-permute-start(bf16[352,1024]{1,0:T(8,128)(2,1)} %get-tuple-element.18), channel_id=1, source_target_pairs={{0,16},{16,0},{1,17},{17,1},{2,18},{18,2},{3,19},{19,3},{4,20},{20... | collective-permute-start | bytes 2162696 | tf_op jit(solution)/shard_map/ppermute | solution.py:255
Sparse Core Ops, SparseCore 0:
  10.9 56.0 all-gather.4
  69.1 49.1 all-gather.6

commit v3 on v1

--- a/solution.py
+++ b/solution.py
@@ -22,10 +22,10 @@
     return z ^ (z >> 1)
 
 
-def ring_pairs():
+def ring_pairs(step):
     size = NY * NC
     return [
-        (ring(p) * size + rest, ring((p + 1) % NZ) * size + rest)
+        (ring(p) * size + rest, ring((p + step) % NZ) * size + rest)
         for p in range(NZ)
         for rest in range(size)
     ]
@@ -35,8 +35,9 @@
     return [(i, i ^ bit) for i in range(NZ * NY * NC)]
 
 
-def pack_kernel(experts, width, routes_ref, gates_ref, grad_ref, *outs):
+def pack_kernel(experts, routes_ref, gates_ref, grad_ref, out_ref):
     chosen, tokens = routes_ref.shape
+    width = grad_ref.shape[1]
     routes = routes_ref[...]
     gates = gates_ref[...].astype(jnp.float32)
     expert = lax.broadcasted_iota(jnp.int32, (experts, tokens), 0)
@@ -56,12 +57,15 @@
         preferred_element_type=jnp.float32,
     )
     slots = jnp.where(named > 0, slots, -1.0)
-    outs[0][:, :width] = grad_ref[:, :width]
-    outs[0][:, width:] = jnp.zeros((tokens, tokens), jnp.bfloat16)
-    outs[0][:experts, width:] = dense.astype(jnp.bfloat16)
-    outs[0][experts : 2 * experts, width:] = slots.astype(jnp.bfloat16)
-    for c in range(1, len(outs)):
-        outs[c][...] = grad_ref[:, c * width : (c + 1) * width]
+    out_ref[:, :width] = grad_ref[...]
+    out_ref[:, width:] = jnp.zeros((tokens, tokens), jnp.bfloat16)
+    out_ref[:experts, width:] = dense.astype(jnp.bfloat16)
+    out_ref[experts : 2 * experts, width:] = slots.astype(jnp.bfloat16)
+
+
+def later_pack_kernel(grad_ref, after_ref, out_ref):
+    del after_ref
+    out_ref[...] = grad_ref[...]
 
 
 def pair_place(arrival):
@@ -143,25 +147,26 @@
         products(half, width, hs_ref, rows_ref, send_ref, own_ref, n)
 
 
-def raw_kernel(half, chunks, *refs):
-    rows = refs[:chunks]
-    own_ref, got_ref, hidden_ref, gslot_ref, pmat_ref, grad_ref, back_ref = refs[chunks:]
+def raw_part_kernel(half, rows_ref, own_ref, got_ref, raw_ref):
+    mine = lax.axis_index("dp")
+    for w_ref, d in ((own_ref, mine), (got_ref, 1 - mine)):
+        units = pl.ds(pl.multiple_of(d * half, 16), half)
+        raw_ref[units, :] = lax.dot_general(
+            w_ref[...], rows_ref[...], NT, preferred_element_type=jnp.float32
+        )
+
+
+def raw_kernel(half, *refs):
+    rows_ref, own_ref, got_ref, sum_ref, hidden_ref, gslot_ref, pmat_ref, grad_ref, back_ref = refs
     mine = lax.axis_index("dp")
     core = lax.axis_index("expert") & 1
     step = pl.program_id(0)
-    width = rows[0].shape[1]
     gates = gslot_ref[...]
     total = jnp.zeros(gates.shape, jnp.float32)
     for w_ref, d in ((own_ref, mine), (got_ref, 1 - mine)):
         units = pl.ds(pl.multiple_of(d * half, 16), half)
-        raw = sum(
-            lax.dot_general(
-                w_ref[:, c * width : (c + 1) * width],
-                rows[c][...],
-                NT,
-                preferred_element_type=jnp.float32,
-            )
-            for c in range(chunks)
+        raw = sum_ref[units, :] + lax.dot_general(
+            w_ref[...], rows_ref[...], NT, preferred_element_type=jnp.float32
         )
         grad_ref[units, :] = (raw * gates).astype(jnp.bfloat16)
         total += jnp.sum(
@@ -178,6 +183,10 @@
         back_ref[pl.ds(pair + 1 - core, 1), :] = back[:1, LANES:]
 
 
+def finish_kernel(own_ref, got_ref, *refs):
+    refs[-1][...] = (own_ref[...] + got_ref[...].astype(jnp.float32)).astype(jnp.bfloat16)
+
+
 def gates_kernel(routes_ref, back_ref, out_ref):
     back = back_ref[...]
     routes = routes_ref[...]
@@ -195,113 +204,171 @@
     half = down_weight.shape[1]
     capacity = slots // experts
     width = model // CHUNKS
+    tile = 256
     bf16, f32 = jnp.bfloat16, jnp.float32
+    shape = jax.ShapeDtypeStruct
     hidden_t = hidden[0, 0].T
     routes_t, gates_t = routes.T, gates.T
     weight = down_weight[0]
-    swap_dp = [(0, 1), (1, 0)]
-
-    chunks = pl.pallas_call(
-        functools.partial(pack_kernel, experts, width),
-        out_shape=[
-            jax.ShapeDtypeStruct((tokens, width + (tokens if c == 0 else 0)), bf16)
-            for c in range(CHUNKS)
-        ],
-        in_specs=[VMEM] * 3,
-        out_specs=[VMEM] * CHUNKS,
-        compiler_params=params(16),
-        name="pack",
-    )(routes_t, gates_t, grad_out)
-
-    got_weight = lax.ppermute(weight, "dp", swap_dp)
-
-    blocks = []
-    for x in chunks:
-        along_z = [x]
-        for _ in range(NZ - 1):
-            along_z.append(lax.ppermute(along_z[-1], "expert", ring_pairs()))
-        arrived = []
-        for block in along_z:
-            for one in (block, lax.ppermute(block, "expert", swap_pairs(2))):
-                arrived += [one, lax.ppermute(one, "expert", swap_pairs(1))]
-        blocks.append(arrived)
-
-    flops = 2 * slots * width * (units + 2 * tokens)
-    rows, send, own = [], [], []
-    shapes = [
-        jax.ShapeDtypeStruct((slots, width), bf16),
-        jax.ShapeDtypeStruct((half, width), bf16),
-        jax.ShapeDtypeStruct((half, width), f32),
+    columns = [pl.BlockSpec((half, width), lambda i, c=c: (0, c)) for c in range(CHUNKS)]
+
+    def forward(x):
+        return lax.ppermute(x, "expert", ring_pairs(1))
+
+    def backward(x):
+        return lax.ppermute(x, "expert", ring_pairs(-1))
+
+    def across(x):
+        return lax.ppermute(x, "expert", swap_pairs(2))
+
+    def sibling(x):
+        return lax.ppermute(x, "expert", swap_pairs(1))
+
+    def swap(x):
+        return lax.ppermute(x, "dp", [(0, 1), (1, 0)])
+
+    def behind(x, *others):
+        return lax.optimization_barrier((x, *others))[0]
+
+    def with_siblings(column, facing):
+        return [z for pair in zip(column, facing) for b in pair for z in (b, sibling(b))]
+
+    def pack():
+        return pl.pallas_call(
+            functools.partial(pack_kernel, experts),
+            out_shape=shape((tokens, width + tokens), bf16),
+            grid=(1,),
+            in_specs=[pl.BlockSpec((chosen, tokens), lambda i: (0, 0))] * 2
+            + [pl.BlockSpec((tokens, width), lambda i: (0, 0))],
+            out_specs=pl.BlockSpec((tokens, width + tokens), lambda i: (0, 0)),
+            compiler_params=params(8),
+            name="pack",
+        )(routes_t, gates_t, grad_out)
+
+    def later_pack(c, after):
+        return pl.pallas_call(
+            later_pack_kernel,
+            out_shape=shape((tokens, width), bf16),
+            grid=(1,),
+            in_specs=[
+                pl.BlockSpec((tokens, width), lambda i: (0, c)),
+                pl.BlockSpec(memory_space=pl.ANY),
+            ],
+            out_specs=pl.BlockSpec((tokens, width), lambda i: (0, 0)),
+            compiler_params=params(8),
+            name="later_pack",
+        )(grad_out, after)
+
+    chunk_shapes = [
+        shape((slots, width), bf16),
+        shape((half, width), bf16),
+        shape((half, width), f32),
     ]
-    for c in range(CHUNKS):
-        cost = pl.CostEstimate(flops=flops, bytes_accessed=12 * 2**20, transcendentals=0)
-        if c == 0:
-            row, out, keep, pmat, gslot, hs = pl.pallas_call(
-                functools.partial(first_kernel, experts, capacity, half, width),
-                out_shape=shapes
-                + [
-                    jax.ShapeDtypeStruct((slots, 2 * tokens), bf16),
-                    jax.ShapeDtypeStruct((1, slots), f32),
-                    jax.ShapeDtypeStruct((units, slots), bf16),
-                ],
-                in_specs=[VMEM] * (experts + 1),
-                out_specs=[VMEM] * 6,
-                compiler_params=params(40),
-                cost_estimate=cost,
-                name="first_chunk",
-            )(*blocks[0], hidden_t)
-        else:
-            row, out, keep = pl.pallas_call(
-                functools.partial(later_kernel, experts, half, width),
-                out_shape=shapes,
-                in_specs=[VMEM] * (experts + 2),
-                out_specs=[VMEM] * 3,
-                compiler_params=params(40),
-                cost_estimate=cost,
-                name="later_chunk",
-            )(*blocks[c], pmat, hs)
-        rows.append(row)
-        send.append(lax.ppermute(out, "dp", swap_dp))
-        own.append(keep)
-
-    tile = 256
-    grad_hidden, back = pl.pallas_call(
-        functools.partial(raw_kernel, half, CHUNKS),
-        grid=(slots // tile,),
-        out_shape=[
-            jax.ShapeDtypeStruct((units, slots), bf16),
-            jax.ShapeDtypeStruct((experts, tokens), f32),
-        ],
-        in_specs=[pl.BlockSpec((tile, width), lambda i: (i, 0))] * CHUNKS
-        + [pl.BlockSpec((half, model), lambda i: (0, 0))] * 2
-        + [
-            pl.BlockSpec((units, tile), lambda i: (0, i)),
-            pl.BlockSpec((1, tile), lambda i: (0, i)),
-            pl.BlockSpec((tile, 2 * tokens), lambda i: (i, 0)),
-        ],
-        out_specs=[
-            pl.BlockSpec((units, tile), lambda i: (0, i)),
-            pl.BlockSpec((experts, tokens), lambda i: (0, 0)),
-        ],
-        compiler_params=params(40),
-        cost_estimate=pl.CostEstimate(
-            flops=2 * slots * model * units, bytes_accessed=12 * 2**20, transcendentals=0
-        ),
-        name="raw",
-    )(*rows, weight, got_weight, hidden_t, gslot, pmat)
-
+
+    def first_chunk(blocks):
+        return pl.pallas_call(
+            functools.partial(first_kernel, experts, capacity, half, width),
+            out_shape=chunk_shapes
+            + [
+                shape((slots, 2 * tokens), bf16),
+                shape((1, slots), f32),
+                shape((units, slots), bf16),
+            ],
+            in_specs=[VMEM] * (experts + 1),
+            out_specs=[VMEM] * 6,
+            compiler_params=params(40),
+            name="first_chunk",
+        )(*blocks, hidden_t)
+
+    def later_chunk(blocks, pmat, hs):
+        return pl.pallas_call(
+            functools.partial(later_kernel, experts, half, width),
+            out_shape=chunk_shapes,
+            in_specs=[VMEM] * (experts + 2),
+            out_specs=[VMEM] * 3,
+            compiler_params=params(40),
+            name="later_chunk",
+        )(*blocks, pmat, hs)
+
+    def raw_part(rows, got_weight):
+        return pl.pallas_call(
+            functools.partial(raw_part_kernel, half),
+            grid=(slots // tile,),
+            out_shape=shape((units, slots), f32),
+            in_specs=[pl.BlockSpec((tile, width), lambda i: (i, 0)), columns[0], columns[0]],
+            out_specs=pl.BlockSpec((units, tile), lambda i: (0, i)),
+            compiler_params=params(24),
+            name="raw_part",
+        )(rows, weight, got_weight)
+
+    def raw_rest(rows, got_weight, raw, gslot, pmat):
+        by_slot = pl.BlockSpec((units, tile), lambda i: (0, i))
+        return pl.pallas_call(
+            functools.partial(raw_kernel, half),
+            grid=(slots // tile,),
+            out_shape=[shape((units, slots), bf16), shape((experts, tokens), f32)],
+            in_specs=[
+                pl.BlockSpec((tile, width), lambda i: (i, 0)),
+                columns[1],
+                columns[1],
+                by_slot,
+                by_slot,
+                pl.BlockSpec((1, tile), lambda i: (0, i)),
+                pl.BlockSpec((tile, 2 * tokens), lambda i: (i, 0)),
+            ],
+            out_specs=[by_slot, pl.BlockSpec((experts, tokens), lambda i: (0, 0))],
+            compiler_params=params(24),
+            name="raw",
+        )(rows, weight, got_weight, raw, hidden_t, gslot, pmat)
+
+    def finish(c, own, got, *before):
+        part = 256
+        spec = pl.BlockSpec((half, part), lambda i: (0, i))
+        return pl.pallas_call(
+            finish_kernel,
+            grid=(width // part,),
+            out_shape=shape((half, model), bf16),
+            in_specs=[spec, spec] + [pl.BlockSpec(memory_space=pl.ANY)] * len(before),
+            out_specs=pl.BlockSpec((half, part), lambda i: (0, c * (width // part) + i)),
+            input_output_aliases={2: 0} if before else {},
+            compiler_params=params(8),
+            name="finish",
+        )(own, got, *before)
+
+    got_weight = swap(weight)
+
+    x = pack()
+    pred, succ, facing = forward(x), backward(x), across(x)
+    far = forward(pred)
+    blocks = with_siblings(
+        [behind(x, succ), pred, far, succ], [facing, across(pred), across(far), across(succ)]
+    )
+    rows0, send0, own0, pmat, gslot, hs = first_chunk(blocks)
+    got0 = swap(send0)
+    raw = raw_part(rows0, got_weight)
+
+    x = later_pack(1, far)
+    pred, succ, facing = forward(x), backward(x), across(x)
+    pred, facing = behind(pred, rows0), behind(facing, rows0)
+    far = forward(pred)
+    across_far = behind(across(far), raw, got0)
+    blocks = with_siblings(
+        [x, pred, far, succ], [facing, across(pred), across_far, backward(facing)]
+    )
+    rows1, send1, own1 = later_chunk(blocks, pmat, hs)
+    got1 = swap(send1)
+
+    grad_hidden, back = raw_rest(rows1, got_weight, raw, gslot, pmat)
     returned = lax.all_to_all(back, "expert", split_axis=0, concat_axis=0, tiled=True)
     grad_gates = pl.pallas_call(
         gates_kernel,
-        out_shape=jax.ShapeDtypeStruct((chosen, tokens), f32),
+        out_shape=shape((chosen, tokens), f32),
         in_specs=[VMEM] * 2,
         out_specs=VMEM,
         name="grad_gates",
     )(routes_t, returned)
 
-    grad_weight = jnp.concatenate(
-        [(mine + theirs.astype(f32)).astype(bf16) for mine, theirs in zip(own, send)], axis=1
-    )
+    grad_weight = finish(1, own1, got1, finish(0, own0, got0))
     return grad_weight[None], grad_hidden.T[None, None], grad_gates.T
 
 

time: 104 us -> 110 us (1.058)
  waiting for transfers between devices: 43.1 us -> 55.1 us
  blocking collectives: 11.3 us -> 0 us
  Pallas kernels: 16.6 us -> 22.4 us
  other arithmetic: 3.85 us -> 0 us
  local copies, waits for them, and re-layouts: 3.78 us -> 5.26 us
  starting transfers between devices: 24.5 us -> 25.9 us
    all_to_all x1 -> x0, blocking collectives: 11.3 us -> none  [ring_shards(): lax.all_to_all(back, 'expert', split_axis=0, concat_axis=0, tiled=True)]
    ppermute x33, waiting for transfers between devices: 43.1 us -> 51.4 us  [the longest x4 26.5 us: forward(): return lax.ppermute(x, 'expert', ring_pairs(1))]
    pallas_call x5 -> x9, Pallas kernels: 16.6 us -> 22.4 us  [the longest x2 4.96 us: finish(): pl.pallas_call(finish_kernel, grid=(width // part,), out_shape=shape((hal...]
    all_to_all x0 -> x1, starting transfers between devices: none -> 3.86 us  [ring_shards(): lax.all_to_all(back, 'expert', split_axis=0, concat_axis=0, tiled=True)]
    all_to_all x0 -> x1, waiting for transfers between devices: none -> 3.66 us  [ring_shards(): lax.all_to_all(back, 'expert', split_axis=0, concat_axis=0, tiled=True)]
    convert_element_type x2 -> x0, other arithmetic: 2.65 us -> none  [ring_shards(): (mine + theirs.astype(f32)).astype(bf16)]
    ppermute x33, starting transfers between devices: 24.5 us -> 22.1 us  [the longest x7 5.61 us: across(): return lax.ppermute(x, 'expert', swap_pairs(2))]
    unnamed x12 -> x18, local copies, waits for them, and re-layouts: 3.78 us -> 5.26 us
  transfers between devices with their start and end apart: 33 -> 34, of which waited for: 15 -> 13; matrix products, arithmetic and copies ran while one was open for 1% -> 0% of each run, Pallas kernels for 16% -> 13%
where the time goes in v3:
time: 110 us; the launch traced here: 109 us
  waiting for transfers between devices  55.1 us (50%)
  starting transfers between devices  25.9 us (24%)
  Pallas kernels  22.4 us (20%)
  local copies, waits for them, and re-layouts  5.26 us (5%)
    ppermute x4, waiting for transfers between devices, forward(): return lax.ppermute(x, 'expert', ring_pairs(1))  26.5 us
    ppermute x7, waiting for transfers between devices, across(): return lax.ppermute(x, 'expert', swap_pairs(2))  20.4 us
    ppermute x7, starting transfers between devices, across(): return lax.ppermute(x, 'expert', swap_pairs(2))  5.61 us
    unnamed x18, local copies, waits for them, and re-layouts  5.26 us
    ppermute x3, starting transfers between devices, backward(): return lax.ppermute(x, 'expert', ring_pairs(-1))  5.06 us
    pallas_call x2, Pallas kernels, finish(): pl.pallas_call(finish_kernel, grid=(width // part,), out_shape=shape((hal...  4.96 us
    pallas_call x1, Pallas kernels, raw_rest(): pl.pallas_call(functools.partial(raw_kernel, half), grid=(slots // tile,)...  4.55 us
    ppermute x4, starting transfers between devices, forward(): return lax.ppermute(x, 'expert', ring_pairs(1))  4.51 us
  transfers between devices with their start and end apart: 34, of which 13 were waited for; matrix products, arithmetic and copies ran while one was open for 0% of the time, Pallas kernels for 13%

profile of v3, /device:TPU:0, one launch (start us, length us, event | category | flops | bytes accessed | tf_op | source)
XLA Modules:
  0.0 109.4 jit_solution(12174811671754387271)
XLA Ops:
  3.3 3.0 %collective-permute-start.6 = (bf16[128,1152]{1,0:T(8,128)(2,1)S(1)}, bf16[128,1152]{1,0:T(8,128)(2,1)S(1)}, u32[]{:S(2)}, u32[]{:S(2)}) collective-permute-start(bf16[128,1152]{1,0:T(8,128)(2,1)S(1)} %pack.1.refs_0_), channel_id=1, source_target_pairs={{0,2},{1,3},{2,0},{3,1},{4,6},{5,7},{6,4},{7,5},{8,10},{9,11},{10,... | collective-permute-start | bytes 884744 | tf_op jit(solution)/shard_map/ppermute | solution.py:222
  6.3 2.6 %collective-permute-start.4 = (bf16[128,1152]{1,0:T(8,128)(2,1)S(1)}, bf16[128,1152]{1,0:T(8,128)(2,1)S(1)}, u32[]{:S(2)}, u32[]{:S(2)}) collective-permute-start(bf16[128,1152]{1,0:T(8,128)(2,1)S(1)} %pack.1.refs_0_), channel_id=1, source_target_pairs={{0,8},{1,9},{2,10},{3,11},{4,0},{5,1},{6,2},{7,3},{12,4},{13,5},{1... | collective-permute-start | bytes 884744 | tf_op jit(solution)/shard_map/ppermute | solution.py:219
  8.9 4.4 %collective-permute-done.6.refs_2_ = bf16[128,1152]{1,0:T(8,128)(2,1)S(1)} collective-permute-done((bf16[128,1152]{1,0:T(8,128)(2,1)S(1)}, bf16[128,1152]{1,0:T(8,128)(2,1)S(1)}, u32[]{:S(2)}, u32[]{:S(2)}) %collective-permute-start.6) | collective-permute-done | bytes 294944 | tf_op jit(solution)/shard_map/ppermute | solution.py:222
  13.3 3.1 %collective-permute-done.4.refs_12_ = bf16[128,1152]{1,0:T(8,128)(2,1)S(1)} collective-permute-done((bf16[128,1152]{1,0:T(8,128)(2,1)S(1)}, bf16[128,1152]{1,0:T(8,128)(2,1)S(1)}, u32[]{:S(2)}, u32[]{:S(2)}) %collective-permute-start.4) | collective-permute-done | bytes 294944 | tf_op jit(solution)/shard_map/ppermute | solution.py:219
  16.9 6.1 %collective-permute-done.refs_4_ = bf16[128,1152]{1,0:T(8,128)(2,1)S(1)} collective-permute-done((bf16[128,1152]{1,0:T(8,128)(2,1)S(1)}, bf16[128,1152]{1,0:T(8,128)(2,1)S(1)}, u32[]{:S(2)}, u32[]{:S(2)}) %collective-permute-start) | collective-permute-done | bytes 294944 | tf_op jit(solution)/shard_map/ppermute | solution.py:216
  23.7 1.5 %collective-permute-start.25 = (bf16[352,2048]{1,0:T(8,128)(2,1)}, bf16[352,2048]{1,0:T(8,128)(2,1)S(1)}, u32[]{:S(2)}, u32[]{:S(2)}) collective-permute-start(bf16[352,2048]{1,0:T(8,128)(2,1)} %bitcast.17), channel_id=1, source_target_pairs={{0,16},{16,0},{1,17},{17,1},{2,18},{18,2},{3,19},{19,3},{4,20},{20... | collective-permute-start | bytes 4325384 | tf_op jit(solution)/shard_map/ppermute | solution.py:228
  25.9 6.9 %collective-permute-done.1.after_ref.refs_8_ = bf16[128,1152]{1,0:T(8,128)(2,1)S(1)} collective-permute-done((bf16[128,1152]{1,0:T(8,128)(2,1)S(1)}, bf16[128,1152]{1,0:T(8,128)(2,1)S(1)}, u32[]{:S(2)}, u32[]{:S(2)}) %collective-permute-start.1) | collective-permute-done | bytes 294944 | tf_op jit(solution)/shard_map/ppermute | solution.py:216
  35.1 5.8 %collective-permute-done.12.refs_10_ = bf16[128,1152]{1,0:T(8,128)(2,1)S(1)} collective-permute-done((bf16[128,1152]{1,0:T(8,128)(2,1)S(1)}, bf16[128,1152]{1,0:T(8,128)(2,1)S(1)}, u32[]{:S(2)}, u32[]{:S(2)}) %collective-permute-start.12) | collective-permute-done | bytes 294944 | tf_op jit(solution)/shard_map/ppermute | solution.py:222
  42.0 2.4 %collective-permute-start.18 = (bf16[128,1024]{1,0:T(8,128)(2,1)S(1)}, bf16[128,1024]{1,0:T(8,128)(2,1)S(1)}, u32[]{:S(2)}, u32[]{:S(2)}) collective-permute-start(bf16[128,1024]{1,0:T(8,128)(2,1)S(1)} %later_pack.1.refs_0_), channel_id=1, source_target_pairs={{0,4},{1,5},{2,6},{3,7},{4,12},{5,13},{6,14},{7,15},{12,8},{13,9},... | collective-permute-start | bytes 786440 | tf_op jit(solution)/shard_map/ppermute | solution.py:216
  44.4 4.2 %first_chunk.1 = (bf16[1024,1024]{1,0:T(8,128)(2,1)S(1)}, bf16[352,1024]{1,0:T(8,128)(2,1)S(1)}, f32[352,1024]{1,0:T(8,128)S(1)}, bf16[1024,256]{1,0:T(8,128)(2,...) custom-call(bf16[128,1152]{1,0:T(8,128)(2,1)S(1)} %pack.1.refs_0_, ...), custom_call_target="tpu_custom_call" | custom-call | tf_op jit(solution)/shard_map/first_chunk/pallas_call | solution.py:269
  49.3 2.4 %collective-permute-done.18.refs_4_ = bf16[128,1024]{1,0:T(8,128)(2,1)S(1)} collective-permute-done((bf16[128,1024]{1,0:T(8,128)(2,1)S(1)}, bf16[128,1024]{1,0:T(8,128)(2,1)S(1)}, u32[]{:S(2)}, u32[]{:S(2)}) %collective-permute-start.18) | collective-permute-done | bytes 262176 | tf_op jit(solution)/shard_map/ppermute | solution.py:216
  51.7 1.4 %collective-permute-start.22 = (bf16[128,1024]{1,0:T(8,128)(2,1)S(1)}, bf16[128,1024]{1,0:T(8,128)(2,1)S(1)}, u32[]{:S(2)}, u32[]{:S(2)}) collective-permute-start(bf16[128,1024]{1,0:T(8,128)(2,1)S(1)} %collective-permute-done.18.refs_4_), channel_id=1, source_target_pairs={{0,4},{1,5},{2,6},{3,7},{4,12},{5,13},{6,14},{7,15},{12,8},{13,9},... | collective-permute-start | bytes 786440 | tf_op jit(solution)/shard_map/ppermute | solution.py:216
  53.1 1.5 %collective-permute-start.28 = (bf16[128,1024]{1,0:T(8,128)(2,1)S(1)}, bf16[128,1024]{1,0:T(8,128)(2,1)S(1)}, u32[]{:S(2)}, u32[]{:S(2)}) collective-permute-start(bf16[128,1024]{1,0:T(8,128)(2,1)S(1)} %later_pack.1.refs_0_), channel_id=1, source_target_pairs={{0,8},{1,9},{2,10},{3,11},{4,0},{5,1},{6,2},{7,3},{12,4},{13,5},{1... | collective-permute-start | bytes 786440 | tf_op jit(solution)/shard_map/ppermute | solution.py:219
  55.1 11.1 %collective-permute-done.22.refs_8_ = bf16[128,1024]{1,0:T(8,128)(2,1)S(1)} collective-permute-done((bf16[128,1024]{1,0:T(8,128)(2,1)S(1)}, bf16[128,1024]{1,0:T(8,128)(2,1)S(1)}, u32[]{:S(2)}, u32[]{:S(2)}) %collective-permute-start.22) | collective-permute-done | bytes 262176 | tf_op jit(solution)/shard_map/ppermute | solution.py:216
  68.2 6.4 %collective-permute-done.24.refs_10_ = bf16[128,1024]{1,0:T(8,128)(2,1)S(1)} collective-permute-done((bf16[128,1024]{1,0:T(8,128)(2,1)S(1)}, bf16[128,1024]{1,0:T(8,128)(2,1)S(1)}, u32[]{:S(2)}, u32[]{:S(2)}) %collective-permute-start.24) | collective-permute-done | bytes 262176 | tf_op jit(solution)/shard_map/ppermute | solution.py:222
  74.7 2.7 %raw_part.1.refs_3_ = f32[704,1024]{1,0:T(8,128)S(1)} custom-call(bf16[1024,1024]{1,0:T(8,128)(2,1)S(1)} %get-tuple-element.19.rows_ref, bf16[352,2048]{1,0:T(8,128)(2,1)S(1)} %bitcast.18, bf16[352,2048]{1,0:T(8,128)(2,1)S(1)} %collective-permute-done.25.got_ref.refs_2_), custom_call_target="tpu_custom_call" | custom-call | tf_op jit(solution)/shard_map/raw_part/pallas_call | solution.py:294
  78.5 2.5 %collective-permute-done.20.refs_6_ = bf16[128,1024]{1,0:T(8,128)(2,1)S(1)} collective-permute-done((bf16[128,1024]{1,0:T(8,128)(2,1)S(1)}, bf16[128,1024]{1,0:T(8,128)(2,1)S(1)}, u32[]{:S(2)}, u32[]{:S(2)}) %collective-permute-start.20) | collective-permute-done | bytes 262176 | tf_op jit(solution)/shard_map/ppermute | solution.py:222
  82.9 4.4 %later_chunk.1 = (bf16[1024,1024]{1,0:T(8,128)(2,1)S(1)}, bf16[352,1024]{1,0:T(8,128)(2,1)}, f32[352,1024]{1,0:T(8,128)S(1)}) custom-call(bf16[128,1024]{1,0:T(8,128)(2,1)S(1)} %later_pack.1.refs_0_, bf16[128,1024]{1,0:T(8,128)(2,1)S(1)} %collective-permute-done.2.refs_1_, bf16[128,1024]{1,0:T(8,128)(2,1)S(1)} %collective-permute-done.3.refs_2_, ...), custom_call_target="tpu_custom_call" | custom-call | tf_op jit(solution)/shard_map/later_chunk/pallas_call | solution.py:284
  87.3 2.0 %collective-permute-start.32 = (bf16[352,1024]{1,0:T(8,128)(2,1)}, bf16[352,1024]{1,0:T(8,128)(2,1)}, u32[]{:S(2)}, u32[]{:S(2)}) collective-permute-start(bf16[352,1024]{1,0:T(8,128)(2,1)} %get-tuple-element.27), channel_id=1, source_target_pairs={{0,16},{16,0},{1,17},{17,1},{2,18},{18,2},{3,19},{19,3},{4,20},{20... | collective-permute-start | bytes 2162696 | tf_op jit(solution)/shard_map/ppermute | solution.py:228
  89.3 4.5 %raw.1 = (bf16[704,1024]{1,0:T(8,128)(2,1)}, f32[16,128]{1,0:T(8,128)}) custom-call(bf16[1024,1024]{1,0:T(8,128)(2,1)S(1)} %get-tuple-element.29.refs_0_, bf16[352,2048]{1,0:T(8,128)(2,1)S(1)} %bitcast.19, bf16[352,2048]{1,0:T(8,128)(2,1)S(1)} %collective-permute-done.25.got_ref.refs_2_, f32[704,1024]{1,0:T(8,128)S(1)} %raw_part.1.refs_3_, ...), custom_call_target="tpu_custom_call" | custom-call | tf_op jit(solution)/shard_map/raw/pallas_call | solution.py:306
  93.9 3.9 %all-to-all-start = ((f32[16,1,128]{2,1,0:T(1,128)}), f32[16,1,128]{2,1,0:T(1,128)S(1)}, u32[]{:S(2)}, u32[]{:S(2)}) async-start(f32[16,1,128]{2,1,0:T(1,128)} %bitcast.10), calls=%async_computation | async-start | bytes 16384 | tf_op jit(solution)/shard_map/all_to_all | solution.py:362
  98.9 1.6 %finish.2.refs_0_ = bf16[352,2048]{1,0:T(8,128)(2,1)} custom-call(f32[352,1024]{1,0:T(8,128)S(1)} %get-tuple-element.28.own_ref, bf16[352,1024]{1,0:T(8,128)(2,1)S(1)} %copy-done.5), custom_call_target="tpu_custom_call" | custom-call | tf_op jit(solution)/shard_map/finish/pallas_call | solution.py:327
  100.5 3.7 %all-to-all-done = f32[16,1,128]{2,1,0:T(1,128)S(1)} async-done(((f32[16,1,128]{2,1,0:T(1,128)}), f32[16,1,128]{2,1,0:T(1,128)S(1)}, u32[]{:S(2)}, u32[]{:S(2)}) %all-to-all-start) | async-done | bytes 8224 | tf_op jit(solution)/shard_map/all_to_all | solution.py:362
  106.1 3.3 %finish.3 = bf16[352,2048]{1,0:T(8,128)(2,1)} custom-call(f32[352,1024]{1,0:T(8,128)S(1)} %get-tuple-element.26.own_ref, bf16[352,1024]{1,0:T(8,128)(2,1)} %collective-permute-done.32.got_ref, bf16[352,2048]{1,0:T(8,128)(2,1)} %finish.2.refs_0_), custom_call_target="tpu_custom_call", output_to_operand_aliasing={{}: (2, {})} | custom-call | tf_op jit(solution)/shard_map/finish/pallas_call | solution.py:327
  (71 shorter events, 17.2 us)
Async XLA Ops:
  3.3 10.0 %collective-permute-start.6 = (bf16[128,1152]{1,0:T(8,128)(2,1)S(1)}, bf16[128,1152]{1,0:T(8,128)(2,1)S(1)}, u32[]{:S(2)}, u32[]{:S(2)}) collective-permute-start(bf16[128,1152]{1,0:T(8,128)(2,1)S(1)} %pack.1.refs_0_), channel_id=1, source_target_pairs={{0,2},{1,3},{2,0},{3,1},{4,6},{5,7},{6,4},{7,5},{8,10},{9,11},{10,... | collective-permute-start | bytes 884744 | tf_op jit(solution)/shard_map/ppermute | solution.py:222
  6.3 10.1 %collective-permute-start.4 = (bf16[128,1152]{1,0:T(8,128)(2,1)S(1)}, bf16[128,1152]{1,0:T(8,128)(2,1)S(1)}, u32[]{:S(2)}, u32[]{:S(2)}) collective-permute-start(bf16[128,1152]{1,0:T(8,128)(2,1)S(1)} %pack.1.refs_0_), channel_id=1, source_target_pairs={{0,8},{1,9},{2,10},{3,11},{4,0},{5,1},{6,2},{7,3},{12,4},{13,5},{1... | collective-permute-start | bytes 884744 | tf_op jit(solution)/shard_map/ppermute | solution.py:219
  8.9 14.1 %collective-permute-start = (bf16[128,1152]{1,0:T(8,128)(2,1)S(1)}, bf16[128,1152]{1,0:T(8,128)(2,1)S(1)}, u32[]{:S(2)}, u32[]{:S(2)}) collective-permute-start(bf16[128,1152]{1,0:T(8,128)(2,1)S(1)} %pack.1.refs_0_), channel_id=1, source_target_pairs={{0,4},{1,5},{2,6},{3,7},{4,12},{5,13},{6,14},{7,15},{12,8},{13,9},... | collective-permute-start | bytes 884744 | tf_op jit(solution)/shard_map/ppermute | solution.py:216
  13.3 11.9 %collective-permute-start.7 = (bf16[128,1152]{1,0:T(8,128)(2,1)S(1)}, bf16[128,1152]{1,0:T(8,128)(2,1)S(1)}, u32[]{:S(2)}, u32[]{:S(2)}) collective-permute-start(bf16[128,1152]{1,0:T(8,128)(2,1)S(1)} %collective-permute-done.6.refs_2_), channel_id=1, source_target_pairs={{0,1},{1,0},{2,3},{3,2},{4,5},{5,4},{6,7},{7,6},{8,9},{9,8},{10,11... | collective-permute-start | bytes 884744 | tf_op jit(solution)/shard_map/ppermute | solution.py:225
  16.4 8.8 %collective-permute-start.5 = (bf16[128,1152]{1,0:T(8,128)(2,1)S(1)}, bf16[128,1152]{1,0:T(8,128)(2,1)S(1)}, u32[]{:S(2)}, u32[]{:S(2)}) collective-permute-start(bf16[128,1152]{1,0:T(8,128)(2,1)S(1)} %pack.1.refs_0_), channel_id=1, source_target_pairs={{0,1},{1,0},{2,3},{3,2},{4,5},{5,4},{6,7},{7,6},{8,9},{9,8},{10,11... | collective-permute-start | bytes 884744 | tf_op jit(solution)/shard_map/ppermute | solution.py:225
  16.4 9.4 %collective-permute-start.15 = (bf16[128,1152]{1,0:T(8,128)(2,1)S(1)}, bf16[128,1152]{1,0:T(8,128)(2,1)S(1)}, u32[]{:S(2)}, u32[]{:S(2)}) collective-permute-start(bf16[128,1152]{1,0:T(8,128)(2,1)S(1)} %collective-permute-done.4.refs_12_), channel_id=1, source_target_pairs={{0,2},{1,3},{2,0},{3,1},{4,6},{5,7},{6,4},{7,5},{8,10},{9,11},{10,... | collective-permute-start | bytes 884744 | tf_op jit(solution)/shard_map/ppermute | solution.py:222
  23.0 9.8 %collective-permute-start.1 = (bf16[128,1152]{1,0:T(8,128)(2,1)S(1)}, bf16[128,1152]{1,0:T(8,128)(2,1)S(1)}, u32[]{:S(2)}, u32[]{:S(2)}) collective-permute-start(bf16[128,1152]{1,0:T(8,128)(2,1)S(1)} %collective-permute-done.refs_4_), channel_id=1, source_target_pairs={{0,4},{1,5},{2,6},{3,7},{4,12},{5,13},{6,14},{7,15},{12,8},{13,9},... | collective-permute-start | bytes 884744 | tf_op jit(solution)/shard_map/ppermute | solution.py:216
  23.7 43.5 %collective-permute-start.25 = (bf16[352,2048]{1,0:T(8,128)(2,1)}, bf16[352,2048]{1,0:T(8,128)(2,1)S(1)}, u32[]{:S(2)}, u32[]{:S(2)}) collective-permute-start(bf16[352,2048]{1,0:T(8,128)(2,1)} %bitcast.17), channel_id=1, source_target_pairs={{0,16},{16,0},{1,17},{17,1},{2,18},{18,2},{3,19},{19,3},{4,20},{20... | collective-permute-start | bytes 4325384 | tf_op jit(solution)/shard_map/ppermute | solution.py:228
  25.2 9.4 %collective-permute-start.9 = (bf16[128,1152]{1,0:T(8,128)(2,1)S(1)}, bf16[128,1152]{1,0:T(8,128)(2,1)S(1)}, u32[]{:S(2)}, u32[]{:S(2)}) collective-permute-start(bf16[128,1152]{1,0:T(8,128)(2,1)S(1)} %collective-permute-done.refs_4_), channel_id=1, source_target_pairs={{0,2},{1,3},{2,0},{3,1},{4,6},{5,7},{6,4},{7,5},{8,10},{9,11},{10,... | collective-permute-start | bytes 884744 | tf_op jit(solution)/shard_map/ppermute | solution.py:222
  25.8 8.8 %collective-permute-start.8 = (bf16[128,1152]{1,0:T(8,128)(2,1)S(1)}, bf16[128,1152]{1,0:T(8,128)(2,1)S(1)}, u32[]{:S(2)}, u32[]{:S(2)}) collective-permute-start(bf16[128,1152]{1,0:T(8,128)(2,1)S(1)} %collective-permute-done.refs_4_), channel_id=1, source_target_pairs={{0,1},{1,0},{2,3},{3,2},{4,5},{5,4},{6,7},{7,6},{8,9},{9,8},{10,11... | collective-permute-start | bytes 884744 | tf_op jit(solution)/shard_map/ppermute | solution.py:225
  33.3 8.7 %collective-permute-start.16 = (bf16[128,1152]{1,0:T(8,128)(2,1)S(1)}, bf16[128,1152]{1,0:T(8,128)(2,1)S(1)}, u32[]{:S(2)}, u32[]{:S(2)}) collective-permute-start(bf16[128,1152]{1,0:T(8,128)(2,1)S(1)} %collective-permute-done.15.refs_14_), channel_id=1, source_target_pairs={{0,1},{1,0},{2,3},{3,2},{4,5},{5,4},{6,7},{7,6},{8,9},{9,8},{10,11... | collective-permute-start | bytes 884744 | tf_op jit(solution)/shard_map/ppermute | solution.py:225
  34.6 9.8 %collective-permute-start.11 = (bf16[128,1152]{1,0:T(8,128)(2,1)S(1)}, bf16[128,1152]{1,0:T(8,128)(2,1)S(1)}, u32[]{:S(2)}, u32[]{:S(2)}) collective-permute-start(bf16[128,1152]{1,0:T(8,128)(2,1)S(1)} %collective-permute-done.1.after_ref.refs_8_), channel_id=1, source_target_pairs={{0,1},{1,0},{2,3},{3,2},{4,5},{5,4},{6,7},{7,6},{8,9},{9,8},{10,11... | collective-permute-start | bytes 884744 | tf_op jit(solution)/shard_map/ppermute | solution.py:225
  34.6 9.8 %collective-permute-start.10 = (bf16[128,1152]{1,0:T(8,128)(2,1)S(1)}, bf16[128,1152]{1,0:T(8,128)(2,1)S(1)}, u32[]{:S(2)}, u32[]{:S(2)}) collective-permute-start(bf16[128,1152]{1,0:T(8,128)(2,1)S(1)} %collective-permute-done.9.refs_6_), channel_id=1, source_target_pairs={{0,1},{1,0},{2,3},{3,2},{4,5},{5,4},{6,7},{7,6},{8,9},{9,8},{10,11... | collective-permute-start | bytes 884744 | tf_op jit(solution)/shard_map/ppermute | solution.py:225
  42.0 9.7 %collective-permute-start.18 = (bf16[128,1024]{1,0:T(8,128)(2,1)S(1)}, bf16[128,1024]{1,0:T(8,128)(2,1)S(1)}, u32[]{:S(2)}, u32[]{:S(2)}) collective-permute-start(bf16[128,1024]{1,0:T(8,128)(2,1)S(1)} %later_pack.1.refs_0_), channel_id=1, source_target_pairs={{0,4},{1,5},{2,6},{3,7},{4,12},{5,13},{6,14},{7,15},{12,8},{13,9},... | collective-permute-start | bytes 786440 | tf_op jit(solution)/shard_map/ppermute | solution.py:216
  48.7 26.0 %collective-permute-start.26 = (bf16[352,1024]{1,0:T(8,128)(2,1)S(1)}, bf16[352,1024]{1,0:T(8,128)(2,1)S(1)}, u32[]{:S(2)}, u32[]{:S(2)}) collective-permute-start(bf16[352,1024]{1,0:T(8,128)(2,1)S(1)} %get-tuple-element.22), channel_id=1, source_target_pairs={{0,16},{16,0},{1,17},{17,1},{2,18},{18,2},{3,19},{19,3},{4,20},{20... | collective-permute-start | bytes 2162696 | tf_op jit(solution)/shard_map/ppermute | solution.py:228
  51.7 14.5 %collective-permute-start.22 = (bf16[128,1024]{1,0:T(8,128)(2,1)S(1)}, bf16[128,1024]{1,0:T(8,128)(2,1)S(1)}, u32[]{:S(2)}, u32[]{:S(2)}) collective-permute-start(bf16[128,1024]{1,0:T(8,128)(2,1)S(1)} %collective-permute-done.18.refs_4_), channel_id=1, source_target_pairs={{0,4},{1,5},{2,6},{3,7},{4,12},{5,13},{6,14},{7,15},{12,8},{13,9},... | collective-permute-start | bytes 786440 | tf_op jit(solution)/shard_map/ppermute | solution.py:216
  53.1 13.6 %collective-permute-start.28 = (bf16[128,1024]{1,0:T(8,128)(2,1)S(1)}, bf16[128,1024]{1,0:T(8,128)(2,1)S(1)}, u32[]{:S(2)}, u32[]{:S(2)}) collective-permute-start(bf16[128,1024]{1,0:T(8,128)(2,1)S(1)} %later_pack.1.refs_0_), channel_id=1, source_target_pairs={{0,8},{1,9},{2,10},{3,11},{4,0},{5,1},{6,2},{7,3},{12,4},{13,5},{1... | collective-permute-start | bytes 786440 | tf_op jit(solution)/shard_map/ppermute | solution.py:219
  54.6 12.1 %collective-permute-start.3 = (bf16[128,1024]{1,0:T(8,128)(2,1)S(1)}, bf16[128,1024]{1,0:T(8,128)(2,1)S(1)}, u32[]{:S(2)}, u32[]{:S(2)}) collective-permute-start(bf16[128,1024]{1,0:T(8,128)(2,1)S(1)} %later_pack.1.refs_0_), channel_id=1, source_target_pairs={{0,2},{1,3},{2,0},{3,1},{4,6},{5,7},{6,4},{7,5},{8,10},{9,11},{10,... | collective-permute-start | bytes 786440 | tf_op jit(solution)/shard_map/ppermute | solution.py:222
  66.2 8.4 %collective-permute-start.24 = (bf16[128,1024]{1,0:T(8,128)(2,1)S(1)}, bf16[128,1024]{1,0:T(8,128)(2,1)S(1)}, u32[]{:S(2)}, u32[]{:S(2)}) collective-permute-start(bf16[128,1024]{1,0:T(8,128)(2,1)S(1)} %collective-permute-done.22.refs_8_), channel_id=1, source_target_pairs={{0,2},{1,3},{2,0},{3,1},{4,6},{5,7},{6,4},{7,5},{8,10},{9,11},{10,... | collective-permute-start | bytes 786440 | tf_op jit(solution)/shard_map/ppermute | solution.py:222
  66.7 10.7 %collective-permute-start.2 = (bf16[128,1024]{1,0:T(8,128)(2,1)S(1)}, bf16[128,1024]{1,0:T(8,128)(2,1)S(1)}, u32[]{:S(2)}, u32[]{:S(2)}) collective-permute-start(bf16[128,1024]{1,0:T(8,128)(2,1)S(1)} %later_pack.1.refs_0_), channel_id=1, source_target_pairs={{0,1},{1,0},{2,3},{3,2},{4,5},{5,4},{6,7},{7,6},{8,9},{9,8},{10,11... | collective-permute-start | bytes 786440 | tf_op jit(solution)/shard_map/ppermute | solution.py:225
  66.7 11.3 %collective-permute-start.29 = (bf16[128,1024]{1,0:T(8,128)(2,1)S(1)}, bf16[128,1024]{1,0:T(8,128)(2,1)S(1)}, u32[]{:S(2)}, u32[]{:S(2)}) collective-permute-start(bf16[128,1024]{1,0:T(8,128)(2,1)S(1)} %collective-permute-done.28.refs_12_), channel_id=1, source_target_pairs={{0,1},{1,0},{2,3},{3,2},{4,5},{5,4},{6,7},{7,6},{8,9},{9,8},{10,11... | collective-permute-start | bytes 786440 | tf_op jit(solution)/shard_map/ppermute | solution.py:225
  67.2 10.8 %collective-permute-start.30 = (bf16[128,1024]{1,0:T(8,128)(2,1)S(1)}, bf16[128,1024]{1,0:T(8,128)(2,1)S(1)}, u32[]{:S(2)}, u32[]{:S(2)}) collective-permute-start(bf16[128,1024]{1,0:T(8,128)(2,1)S(1)} %collective-permute-done.3.refs_2_), channel_id=1, source_target_pairs={{0,8},{1,9},{2,10},{3,11},{4,0},{5,1},{6,2},{7,3},{12,4},{13,5},{1... | collective-permute-start | bytes 786440 | tf_op jit(solution)/shard_map/ppermute | solution.py:219
  87.3 18.8 %collective-permute-start.32 = (bf16[352,1024]{1,0:T(8,128)(2,1)}, bf16[352,1024]{1,0:T(8,128)(2,1)}, u32[]{:S(2)}, u32[]{:S(2)}) collective-permute-start(bf16[352,1024]{1,0:T(8,128)(2,1)} %get-tuple-element.27), channel_id=1, source_target_pairs={{0,16},{16,0},{1,17},{17,1},{2,18},{18,2},{3,19},{19,3},{4,20},{20... | collective-permute-start | bytes 2162696 | tf_op jit(solution)/shard_map/ppermute | solution.py:228
  93.9 10.3 %all-to-all-start = ((f32[16,1,128]{2,1,0:T(1,128)}), f32[16,1,128]{2,1,0:T(1,128)S(1)}, u32[]{:S(2)}, u32[]{:S(2)}) async-start(f32[16,1,128]{2,1,0:T(1,128)} %bitcast.10), calls=%async_computation | async-start | bytes 16384 | tf_op jit(solution)/shard_map/all_to_all | solution.py:362
  (19 other events, 128.9 us)

commit v4 on v0

--- a/solution.py
+++ b/solution.py
@@ -1,7 +1,470 @@
+import functools
+
 import jax
 import jax.numpy as jnp
 from jax import lax
+from jax.experimental import pallas as pl
+from jax.experimental.pallas import tpu as pltpu
 from jax.sharding import PartitionSpec as P
+
+NZ, NY, NC = 4, 2, 2
+CHUNKS = 2
+PIECES = 2
+PART = 256
+LANES = 128
+NT = (((1,), (1,)), ((), ()))
+VMEM = pl.BlockSpec(memory_space=pltpu.VMEM)
+ANY = pl.BlockSpec(memory_space=pl.ANY)
+
+
+def params(mib):
+    return pltpu.CompilerParams(vmem_limit_bytes=mib * 2**20)
+
+
+def cost(micros):
+    return pl.CostEstimate(
+        flops=micros * 10**9, bytes_accessed=micros * 3 * 2**20, transcendentals=0
+    )
+
+
+def ring(z):
+    return z ^ (z >> 1)
+
+
+def ring_pairs(step):
+    size = NY * NC
+    return [
+        (ring(p) * size + rest, ring((p + step) % NZ) * size + rest)
+        for p in range(NZ)
+        for rest in range(size)
+    ]
+
+
+def swap_pairs(bit):
+    return [(i, i ^ bit) for i in range(NZ * NY * NC)]
+
+
+def pack_kernel(experts, width, routes_hbm, gates_hbm, grad_hbm, out_ref, routes_ref, gates_ref, sems):
+    copies = [
+        pltpu.make_async_copy(src, dst, sems.at[i])
+        for i, (src, dst) in enumerate(
+            (
+                (routes_hbm, routes_ref),
+                (gates_hbm, gates_ref),
+                (grad_hbm.at[:, :width], out_ref.at[:, :width]),
+            )
+        )
+    ]
+    for copy in copies:
+        copy.start()
+    copies[0].wait()
+    copies[1].wait()
+    chosen, tokens = routes_ref.shape
+    routes = routes_ref[...]
+    gates = gates_ref[...].astype(jnp.float32)
+    expert = lax.broadcasted_iota(jnp.int32, (experts, tokens), 0)
+    dense = jnp.zeros((experts, tokens), jnp.float32)
+    named = jnp.zeros((experts, tokens), jnp.float32)
+    for k in range(chosen):
+        hit = routes[k : k + 1, :] == expert
+        dense = jnp.where(hit, gates[k : k + 1, :], dense)
+        named = jnp.where(hit, 1.0, named)
+    earlier = (
+        lax.broadcasted_iota(jnp.int32, (tokens, tokens), 0)
+        < lax.broadcasted_iota(jnp.int32, (tokens, tokens), 1)
+    )
+    slots = jnp.dot(
+        named.astype(jnp.bfloat16),
+        jnp.where(earlier, 1.0, 0.0).astype(jnp.bfloat16),
+        preferred_element_type=jnp.float32,
+    )
+    slots = jnp.where(named > 0, slots, -1.0)
+    out_ref[:, width:] = jnp.zeros((tokens, tokens), jnp.bfloat16)
+    out_ref[:experts, width:] = dense.astype(jnp.bfloat16)
+    out_ref[experts : 2 * experts, width:] = slots.astype(jnp.bfloat16)
+    copies[2].wait()
+
+
+def later_pack_kernel(low, grad_hbm, after_ref, out_ref, sem):
+    del after_ref
+    copy = pltpu.make_async_copy(grad_hbm.at[:, pl.ds(low, out_ref.shape[1])], out_ref, sem)
+    copy.start()
+    copy.wait()
+
+
+def pair_place(arrival):
+    index = lax.axis_index("expert")
+    z, y = index >> 2, (index >> 1) & 1
+    z = ring((ring(z) - arrival // NY) & (NZ - 1))
+    return z * NY + (y ^ (arrival % NY))
+
+
+def pick(xs, pmat_ref, mine_ref, theirs_ref):
+    capacity = mine_ref.shape[0] // len(xs)
+
+    @pl.loop(0, mine_ref.shape[1] // 256)
+    def _(n):
+        cols = pl.ds(pl.multiple_of(n * 256, 256), 256)
+        for a, x_ref in enumerate(xs):
+            rows = jnp.dot(
+                pmat_ref[a * 2 * capacity : (a + 1) * 2 * capacity, :],
+                x_ref[:, cols],
+                preferred_element_type=jnp.float32,
+            ).astype(jnp.bfloat16)
+            where = pl.ds(pl.multiple_of(pair_place(a) * capacity, capacity), capacity)
+            mine_ref[where, cols] = rows[:capacity]
+            theirs_ref[where, cols] = rows[capacity:]
+
+
+def first_pick_kernel(experts, capacity, *refs):
+    pairs = experts // 2
+    xs = refs[:pairs]
+    mine_ref, theirs_ref, pmat_ref, gslot_ref, other_ref = refs[pairs:]
+    width = mine_ref.shape[1]
+    me = lax.axis_index("expert")
+    core = me & 1
+    tokens = xs[0].shape[0]
+    expert = lax.broadcasted_iota(jnp.int32, (experts, tokens), 0)
+    slot = lax.broadcasted_iota(jnp.int32, (2 * capacity, tokens), 0).astype(jnp.float32)
+    offset = (core * capacity).astype(jnp.float32)
+    other_ref[...] = jnp.zeros(other_ref.shape, jnp.float32)
+    for a, x_ref in enumerate(xs):
+        place = pl.ds(pair_place(a), 1)
+        ext = x_ref[: 2 * experts, width:].astype(jnp.float32)
+        one_hot = jnp.zeros(slot.shape, jnp.float32)
+        for s, (who, to_ref) in enumerate(((me, gslot_ref), (me ^ 1, other_ref))):
+            gate = jnp.sum(jnp.where(expert == who, ext[:experts], 0.0), axis=0, keepdims=True)
+            number = jnp.sum(jnp.where(expert == who, ext[experts:], 0.0), axis=0, keepdims=True)
+            routed = number >= 0
+            spot = jnp.where(routed, number + s * capacity, -1.0)
+            one_hot = jnp.where(slot == spot, 1.0, one_hot)
+            spot = jnp.where(routed, number + offset, -1.0)
+            by_slot = lax.dot_general(
+                jnp.broadcast_to(gate.astype(jnp.bfloat16), (16, tokens)),
+                jnp.where(slot == spot, 1.0, 0.0).astype(jnp.bfloat16),
+                NT,
+                preferred_element_type=jnp.float32,
+            )
+            to_ref[place, :] = by_slot[:1]
+        pmat_ref[a * 2 * capacity : (a + 1) * 2 * capacity, :] = one_hot.astype(jnp.bfloat16)
+    theirs_ref[pairs * capacity :, :] = jnp.zeros((16, width), jnp.bfloat16)
+    theirs_ref[pairs * capacity :, : 2 * capacity] = other_ref[...].astype(jnp.bfloat16)
+    pick(xs, pmat_ref, mine_ref, theirs_ref)
+
+
+def pick_kernel(*refs):
+    pick(refs[:-3], *refs[-3:])
+
+
+def products(half, capacity, mine_ref, got_ref, hs_ref, rows_ref, *outs):
+    mine = lax.axis_index("dp")
+    core = lax.axis_index("expert") & 1
+    pairs = mine_ref.shape[0] // capacity
+    pieces = len(outs) // 2
+    piece = mine_ref.shape[1] // pieces
+    for q in range(pieces):
+
+        @pl.loop(0, piece // 256)
+        def _(n, q=q):
+            cols = pl.ds(pl.multiple_of(q * piece + n * 256, 256), 256)
+            out = pl.ds(pl.multiple_of(n * 256, 256), 256)
+            for p in range(pairs):
+                for c, ref in ((core, mine_ref), (1 - core, got_ref)):
+                    to = pl.ds(pl.multiple_of((2 * p + c) * capacity, capacity), capacity)
+                    rows_ref[to, cols] = ref[p * capacity : (p + 1) * capacity, cols]
+            block = rows_ref[:, cols]
+            for d, ref in ((1 - mine, outs[q]), (mine, outs[pieces + q])):
+                units = pl.ds(pl.multiple_of(d * half, 16), half)
+                ref[:, out] = jnp.dot(
+                    hs_ref[units, :], block, preferred_element_type=jnp.float32
+                ).astype(jnp.bfloat16)
+
+
+def first_products_kernel(half, capacity, mine_ref, got_ref, gslot_ref, hidden_ref, *outs):
+    gates_ref, hs_ref = outs[:2]
+    pairs = mine_ref.shape[0] // capacity
+    got = got_ref[pairs * capacity :, : 2 * capacity].astype(jnp.float32)
+    by_pair = gslot_ref[...] + got[:pairs]
+    for p in range(pairs):
+        gates_ref[:, p * 2 * capacity : (p + 1) * 2 * capacity] = by_pair[p : p + 1, :]
+    hs_ref[...] = (hidden_ref[...].astype(jnp.float32) * gates_ref[...]).astype(jnp.bfloat16)
+    products(half, capacity, mine_ref, got_ref, hs_ref, *outs[2:])
+
+
+def raw_halves(half, rows_ref, own_ref, got_refs):
+    mine = lax.axis_index("dp")
+
+    def times(w_ref, rows):
+        return lax.dot_general(w_ref[...], rows, NT, preferred_element_type=jnp.float32)
+
+    yield pl.ds(pl.multiple_of(mine * half, 16), half), times(own_ref, rows_ref[...])
+    part = got_refs[0].shape[1]
+    yield (
+        pl.ds(pl.multiple_of((1 - mine) * half, 16), half),
+        sum(times(ref, rows_ref[:, q * part : (q + 1) * part]) for q, ref in enumerate(got_refs)),
+    )
+
+
+def raw_part_kernel(half, rows_ref, own_ref, *refs):
+    for units, raw in raw_halves(half, rows_ref, own_ref, refs[:-1]):
+        refs[-1][units, :] = raw
+
+
+def raw_kernel(half, capacity, rows_ref, own_ref, *refs):
+    sum_ref, hidden_ref, gates_ref, grad_ref, back_ref = refs[-5:]
+    step = pl.program_id(0)
+    gates = gates_ref[...]
+    total = jnp.zeros(gates.shape, jnp.float32)
+    for units, raw in raw_halves(half, rows_ref, own_ref, refs[:-5]):
+        raw += sum_ref[units, :]
+        grad_ref[units, :] = (raw * gates).astype(jnp.bfloat16)
+        total += jnp.sum(
+            raw * hidden_ref[units, :].astype(jnp.float32), axis=0, keepdims=True
+        )
+    blocks = gates.shape[1] // capacity
+    for i in range(blocks):
+        back_ref[pl.ds(step * blocks + i, 1), :] = total[:, i * capacity : (i + 1) * capacity]
+
+
+def gates_kernel(routes_ref, slots_ref, back_ref, out_ref):
+    back = back_ref[...]
+    routes = routes_ref[...]
+    experts, capacity = back.shape
+    tokens = routes.shape[1]
+    slots = slots_ref[experts : 2 * experts, :].astype(jnp.float32)
+    expert = lax.broadcasted_iota(jnp.int32, (experts, tokens), 0)
+    slot = lax.broadcasted_iota(jnp.int32, (capacity, tokens), 0).astype(jnp.float32)
+    for k in range(out_ref.shape[0]):
+        hit = expert == routes[k : k + 1, :]
+        number = jnp.sum(jnp.where(hit, slots, 0.0), axis=0, keepdims=True)
+        by_expert = jnp.dot(
+            back,
+            jnp.where(slot == number, 1.0, 0.0),
+            preferred_element_type=jnp.float32,
+            precision=lax.Precision.HIGHEST,
+        )
+        out_ref[k : k + 1, :] = jnp.sum(jnp.where(hit, by_expert, 0.0), axis=0, keepdims=True)
+
+
+def finish_kernel(own_ref, got_ref, *refs):
+    refs[-1][...] = (
+        own_ref[...].astype(jnp.float32) + got_ref[...].astype(jnp.float32)
+    ).astype(jnp.bfloat16)
+
+
+def ring_shards(grad_out, gates, routes, hidden, down_weight):
+    experts = lax.axis_size("expert")
+    tokens, chosen = routes.shape
+    model = grad_out.shape[1]
+    slots, units = hidden.shape[2:]
+    half = down_weight.shape[1]
+    capacity = slots // experts
+    width = model // CHUNKS
+    tile = 256
+    bf16, f32 = jnp.bfloat16, jnp.float32
+    shape = jax.ShapeDtypeStruct
+    hidden_t = hidden[0, 0].T
+    routes_t, gates_t = routes.T, gates.T
+    weight = down_weight[0]
+    columns = [pl.BlockSpec((half, width), lambda i, c=c: (0, c)) for c in range(CHUNKS)]
+    parts = [pl.BlockSpec((half, PART), lambda i: (0, 0))] * (width // PART)
+    dma = pltpu.SemaphoreType.DMA
+
+    def forward(x):
+        return lax.ppermute(x, "expert", ring_pairs(1))
+
+    def backward(x):
+        return lax.ppermute(x, "expert", ring_pairs(-1))
+
+    def across(x):
+        return lax.ppermute(x, "expert", swap_pairs(2))
+
+    def sibling(x):
+        return lax.ppermute(x, "expert", swap_pairs(1))
+
+    def swap(x):
+        return lax.ppermute(x, "dp", [(0, 1), (1, 0)])
+
+    def behind(x, *others):
+        return lax.optimization_barrier((x, *others))[0]
+
+    def pack():
+        return pl.pallas_call(
+            functools.partial(pack_kernel, experts, width),
+            out_shape=shape((tokens, width + tokens), bf16),
+            in_specs=[ANY] * 3,
+            out_specs=VMEM,
+            scratch_shapes=[
+                pltpu.VMEM(routes_t.shape, routes_t.dtype),
+                pltpu.VMEM(gates_t.shape, gates_t.dtype),
+                dma((3,)),
+            ],
+            compiler_params=params(48),
+            name="pack",
+        )(routes_t, gates_t, grad_out)
+
+    def later_pack(c, after):
+        return pl.pallas_call(
+            functools.partial(later_pack_kernel, c * width),
+            out_shape=shape((tokens, width), bf16),
+            in_specs=[ANY] * 2,
+            out_specs=VMEM,
+            scratch_shapes=[dma],
+            compiler_params=params(48),
+            name="later_pack",
+        )(grad_out, after)
+
+    mine_shape = shape((slots // 2, width), bf16)
+
+    def first_pick(blocks):
+        return pl.pallas_call(
+            functools.partial(first_pick_kernel, experts, capacity),
+            out_shape=[
+                mine_shape,
+                shape((slots // 2 + 16, width), bf16),
+                shape((slots, tokens), bf16),
+                shape((experts // 2, 2 * capacity), f32),
+            ],
+            in_specs=[VMEM] * len(blocks),
+            out_specs=[VMEM] * 4,
+            scratch_shapes=[pltpu.VMEM((16, 2 * capacity), f32)],
+            compiler_params=params(24),
+            cost_estimate=cost(3),
+            name="first_pick",
+        )(*blocks)
+
+    def later_pick(blocks, pmat):
+        return pl.pallas_call(
+            pick_kernel,
+            out_shape=[mine_shape] * 2,
+            in_specs=[VMEM] * (len(blocks) + 1),
+            out_specs=[VMEM] * 2,
+            compiler_params=params(24),
+            name="pick",
+        )(*blocks, pmat)
+
+    piece = width // PIECES
+    product_shapes = [shape((slots, width), bf16)] + [shape((half, piece), bf16)] * 2 * PIECES
+
+    def first_products(mine, got, gslot):
+        slot_gates, hs, rows, *halves = pl.pallas_call(
+            functools.partial(first_products_kernel, half, capacity),
+            out_shape=[shape((1, slots), f32), shape((units, slots), bf16)] + product_shapes,
+            in_specs=[VMEM] * 4,
+            out_specs=[VMEM] * (3 + 2 * PIECES),
+            compiler_params=params(24),
+            cost_estimate=cost(3),
+            name="first_products",
+        )(mine, got, gslot, hidden_t)
+        return rows, halves[:PIECES], halves[PIECES:], slot_gates, hs
+
+    def later_products(mine, got, hs):
+        rows, *halves = pl.pallas_call(
+            functools.partial(products, half, capacity),
+            out_shape=product_shapes,
+            in_specs=[VMEM] * 3,
+            out_specs=[VMEM] * (1 + 2 * PIECES),
+            compiler_params=params(24),
+            name="products",
+        )(mine, got, hs)
+        return rows, halves[:PIECES], halves[PIECES:]
+
+    def raw_part(rows, got_weight):
+        return pl.pallas_call(
+            functools.partial(raw_part_kernel, half),
+            grid=(slots // tile,),
+            out_shape=shape((units, slots), f32),
+            in_specs=[pl.BlockSpec((tile, width), lambda i: (i, 0)), columns[0]] + parts,
+            out_specs=pl.BlockSpec((units, tile), lambda i: (0, i)),
+            compiler_params=params(24),
+            cost_estimate=cost(3),
+            name="raw_part",
+        )(rows, weight, *got_weight)
+
+    def raw_rest(rows, got_weight, raw, slot_gates):
+        by_slot = pl.BlockSpec((units, tile), lambda i: (0, i))
+        return pl.pallas_call(
+            functools.partial(raw_kernel, half, capacity),
+            grid=(slots // tile,),
+            out_shape=[shape((units, slots), bf16), shape((experts, capacity), f32)],
+            in_specs=[
+                pl.BlockSpec((tile, width), lambda i: (i, 0)),
+                columns[1],
+                *parts,
+                by_slot,
+                by_slot,
+                pl.BlockSpec((1, tile), lambda i: (0, i)),
+            ],
+            out_specs=[by_slot, pl.BlockSpec((experts, capacity), lambda i: (0, 0))],
+            compiler_params=params(24),
+            name="raw",
+        )(rows, weight, *got_weight, raw, hidden_t, slot_gates)
+
+    def finish(place, own, got, *before):
+        spec = pl.BlockSpec((half // 2, piece), lambda i: (i, 0))
+        return pl.pallas_call(
+            finish_kernel,
+            grid=(2,),
+            out_shape=shape((half, model), bf16),
+            in_specs=[spec, spec] + [ANY] * len(before),
+            out_specs=pl.BlockSpec((half // 2, piece), lambda i: (i, place)),
+            input_output_aliases={2: 0} if before else {},
+            compiler_params=params(8),
+            name="finish",
+        )(own, got, *before)
+
+    got_weight = [swap(weight[:, k : k + PART]) for k in range(0, model, PART)]
+    x0 = pack()
+    pred0, facing0 = forward(x0), across(x0)
+    done = (facing0, got_weight[0])
+    far0, pred_across0 = forward(behind(pred0, *done)), across(behind(pred0, *done))
+    done = (far0, pred_across0, got_weight[1])
+    succ0, far_across0 = backward(behind(x0, *done)), across(behind(far0, *done))
+    done = (succ0, far_across0, got_weight[2], got_weight[3])
+    x1 = later_pack(1, far_across0)
+    pred1, succ_across0 = forward(behind(x1, *done)), across(behind(succ0, *done))
+    done = (pred1, succ_across0)
+    far1, facing1 = forward(behind(pred1, *done)), across(behind(x1, *done))
+    mine0, theirs0, pmat, gslot = first_pick(
+        [x0, facing0, pred0, pred_across0, far0, far_across0, succ0, behind(succ_across0, pred1)]
+    )
+    done = (far1, facing1, mine0, got_weight[4])
+    succ1, pred_across1 = backward(behind(x1, *done)), across(behind(pred1, *done))
+    got = sibling(behind(theirs0, facing1))
+    done = (succ1, pred_across1, got, *got_weight[5:7])
+    facing_back1, far_across1 = backward(behind(facing1, *done)), across(behind(far1, *done))
+    rows0, send0, own0, slot_gates, hs = first_products(mine0, got, gslot)
+    got0 = [swap(part) for part in send0]
+    raw = raw_part(rows0, got_weight[: len(parts)])
+    mine1, theirs1 = later_pick(
+        [x1, facing1, pred1, pred_across1, far1, far_across1, succ1, facing_back1],
+        behind(pmat, raw, got_weight[7]),
+    )
+    rows1, send1, own1 = later_products(mine1, sibling(theirs1), behind(hs, got0[0]))
+    got1 = [swap(part) for part in send1]
+
+    grad_hidden, back = raw_rest(rows1, got_weight[len(parts) :], raw, slot_gates)
+    returned = lax.all_to_all(back, "expert", split_axis=0, concat_axis=0, tiled=True)
+    grad_gates = pl.pallas_call(
+        gates_kernel,
+        grid=(1,),
+        out_shape=shape((chosen, tokens), f32),
+        in_specs=[
+            pl.BlockSpec((chosen, tokens), lambda i: (0, 0)),
+            pl.BlockSpec((2 * experts, tokens), lambda i: (0, width // tokens)),
+            pl.BlockSpec((experts, capacity), lambda i: (0, 0)),
+        ],
+        out_specs=pl.BlockSpec((chosen, tokens), lambda i: (0, 0)),
+        name="grad_gates",
+    )(routes_t, x0, returned)
+
+    grad_weight = ()
+    for i, (own, got) in enumerate(zip((*own0, *own1), (*got0, *got1))):
+        if i == 0:
+            own = behind(own, back)
+        grad_weight = (finish(i, own, got, *grad_weight),)
+    grad_weight = grad_weight[0]
+    return grad_weight[None], grad_hidden.T[None, None], grad_gates.T
 
 
 def shards(grad_out, gates, routes, hidden, down_weight):
@@ -53,8 +516,9 @@
 
 
 def solution(mesh):
+    small = mesh.shape["dp"] == 2 and mesh.shape["expert"] == NZ * NY * NC
     return jax.shard_map(
-        shards,
+        ring_shards if small else shards,
         mesh=mesh,
         in_specs=(
             P(("dp", "expert"), None),

time: 201 us -> 118 us (0.59)
  waiting for transfers between devices: 99.8 us -> 56 us
  local copies, waits for them, and re-layouts: 35 us -> 4.59 us
  Pallas kernels: 0 us -> 20.5 us
  between operations: 14.2 us -> 0.78 us
  matrix products: 12 us -> 0 us
  other arithmetic: 6.3 us -> 0 us
  starting transfers between devices: 33.3 us -> 35.9 us
    all_to_all x3 -> x1, waiting for transfers between devices: 83.1 us -> 4.78 us  [ring_shards(): lax.all_to_all(back, 'expert', split_axis=0, concat_axis=0, tiled=True)]
    ppermute x0 -> x28, waiting for transfers between devices: none -> 51.2 us  [the longest x12 36.4 us: swap(): return lax.ppermute(x, 'dp', [(0, 1), (1, 0)])]
    ppermute x0 -> x28, starting transfers between devices: none -> 32.4 us  [the longest x12 14.6 us: swap(): return lax.ppermute(x, 'dp', [(0, 1), (1, 0)])]
    all_to_all x3 -> x1, starting transfers between devices: 33.1 us -> 3.48 us  [ring_shards(): lax.all_to_all(back, 'expert', split_axis=0, concat_axis=0, tiled=True)]
    pallas_call x0 -> x13, Pallas kernels: none -> 20.5 us  [the longest x1 3.9 us: raw_rest(): pl.pallas_call(functools.partial(raw_kernel, half, capacity), grid=(slots...]
    scatter x2 -> x0, local copies, waits for them, and re-layouts: 18 us -> none  [the longest x1 9.4 us: shards(): send_rows = jnp.zeros((owners * capacity, width), grad_out.dtype).at[targ...]
    reduce_scatter x1 -> x0, waiting for transfers between devices: 16 us -> none  [shards(): lax.psum_scatter(lax.dot_general(saved, scaled, (((0,), (0,)), ((), ())),...]
    dot_general x2 -> x0, matrix products: 12 us -> none  [the longest x1 7.43 us: shards(): lax.dot_general(rows, whole_weight, contract, preferred_element_type=jnp....]
  transfers between devices with their start and end apart: 5 -> 29, of which waited for: 3 -> 17; matrix products, arithmetic and copies ran while one was open for 19% -> 1% of each run, Pallas kernels for 0% -> 16%
where the time goes in v4:
time: 118 us
  waiting for transfers between devices  56 us (47%)
  starting transfers between devices  35.9 us (30%)
  Pallas kernels  20.5 us (17%)
  local copies, waits for them, and re-layouts  4.59 us (4%)
    ppermute x12, waiting for transfers between devices, swap(): return lax.ppermute(x, 'dp', [(0, 1), (1, 0)])  36.4 us
    ppermute x12, starting transfers between devices, swap(): return lax.ppermute(x, 'dp', [(0, 1), (1, 0)])  14.6 us
    ppermute x4, waiting for transfers between devices, forward(): return lax.ppermute(x, 'expert', ring_pairs(1))  10.6 us
    ppermute x7, starting transfers between devices, across(): return lax.ppermute(x, 'expert', swap_pairs(2))  8.85 us
    ppermute x4, starting transfers between devices, forward(): return lax.ppermute(x, 'expert', ring_pairs(1))  5.67 us
    all_to_all x1, waiting for transfers between devices, ring_shards(): lax.all_to_all(back, 'expert', split_axis=0, concat_axis=0, tiled=True)  4.78 us
    pallas_call x1, Pallas kernels, raw_rest(): pl.pallas_call(functools.partial(raw_kernel, half, capacity), grid=(slots...  3.9 us
    ppermute x7, waiting for transfers between devices, across(): return lax.ppermute(x, 'expert', swap_pairs(2))  3.64 us
  transfers between devices with their start and end apart: 29, of which 17 were waited for; matrix products, arithmetic and copies ran while one was open for 1% of the time, Pallas kernels for 16%

profile of v4, /device:TPU:0, one launch (start us, length us, event | category | flops | bytes accessed | tf_op | source)
XLA Modules:
  0.0 117.8 jit_solution(5143627084483561250)
XLA Ops:
  3.3 3.0 %collective-permute-start.1 = (bf16[128,1152]{1,0:T(8,128)(2,1)S(1)}, bf16[128,1152]{1,0:T(8,128)(2,1)S(1)}, u32[]{:S(2)}, u32[]{:S(2)}) collective-permute-start(bf16[128,1152]{1,0:T(8,128)(2,1)S(1)} %pack.1.refs_0_.slots_ref), channel_id=1, source_target_pairs={{0,2},{1,3},{2,0},{3,1},{4,6},{5,7},{6,4},{7,5},{8,10},{9,11},{10,... | collective-permute-start | bytes 884744 | tf_op jit(solution)/shard_map/ppermute | solution.py:280
  11.0 4.2 %collective-permute-done.2.refs_0_ = bf16[352,256]{1,0:T(8,128)(2,1)S(1)} collective-permute-done((bf16[352,256]{1,0:T(8,128)(2,1)S(1)}, bf16[352,256]{1,0:T(8,128)(2,1)S(1)}, u32[]{:S(2)}, u32[]{:S(2)}) %collective-permute-start.2) | collective-permute-done | bytes 180256 | tf_op jit(solution)/shard_map/ppermute | solution.py:286
  16.1 2.2 %collective-permute-start.3 = (bf16[128,1152]{1,0:T(8,128)(2,1)S(1)}, bf16[128,1152]{1,0:T(8,128)(2,1)S(1)}, u32[]{:S(2)}, u32[]{:S(2)}) collective-permute-start(bf16[128,1152]{1,0:T(8,128)(2,1)S(1)} %collective-permute-done.refs_2_), channel_id=1, source_target_pairs={{0,4},{1,5},{2,6},{3,7},{4,12},{5,13},{6,14},{7,15},{12,8},{13,9},... | collective-permute-start | bytes 884744 | tf_op jit(solution)/shard_map/ppermute | solution.py:274
  19.8 4.0 %collective-permute-done.5.refs_1_ = bf16[352,256]{1,0:T(8,128)(2,1)S(1)} collective-permute-done((bf16[352,256]{1,0:T(8,128)(2,1)S(1)}, bf16[352,256]{1,0:T(8,128)(2,1)S(1)}, u32[]{:S(2)}, u32[]{:S(2)}) %collective-permute-start.5) | collective-permute-done | bytes 180256 | tf_op jit(solution)/shard_map/ppermute | solution.py:286
  29.4 3.5 %collective-permute-done.9.refs_3_ = bf16[352,256]{1,0:T(8,128)(2,1)S(1)} collective-permute-done((bf16[352,256]{1,0:T(8,128)(2,1)S(1)}, bf16[352,256]{1,0:T(8,128)(2,1)S(1)}, u32[]{:S(2)}, u32[]{:S(2)}) %collective-permute-start.9) | collective-permute-done | bytes 180256 | tf_op jit(solution)/shard_map/ppermute | solution.py:286
  32.9 1.9 %collective-permute-done.8.refs_2_ = bf16[352,256]{1,0:T(8,128)(2,1)S(1)} collective-permute-done((bf16[352,256]{1,0:T(8,128)(2,1)S(1)}, bf16[352,256]{1,0:T(8,128)(2,1)S(1)}, u32[]{:S(2)}, u32[]{:S(2)}) %collective-permute-start.8) | collective-permute-done | bytes 180256 | tf_op jit(solution)/shard_map/ppermute | solution.py:286
  36.3 6.5 %collective-permute-done.10.refs_2_ = bf16[128,1024]{1,0:T(8,128)(2,1)S(1)} collective-permute-done((bf16[128,1024]{1,0:T(8,128)(2,1)S(1)}, bf16[128,1024]{1,0:T(8,128)(2,1)S(1)}, u32[]{:S(2)}, u32[]{:S(2)}) %collective-permute-start.10) | collective-permute-done | bytes 262176 | tf_op jit(solution)/shard_map/ppermute | solution.py:274
  44.3 1.6 %first_pick.1 = (bf16[512,1024]{1,0:T(8,128)(2,1)S(1)}, bf16[528,1024]{1,0:T(8,128)(2,1)S(1)}, bf16[1024,128]{1,0:T(8,128)(2,1)S(1)}, f32[8,128]{1,0:T(8,128)S(1)}) custom-call(bf16[128,1152]{1,0:T(8,128)(2,1)S(1)} %pack.1.refs_0_.slots_ref, bf16[128,1152]{1,0:T(8,128)(2,1)S(1)} %collective-permute-done.1.refs_1_, ...), custom_call_target="tpu_custom_call" | custom-call | flops 3000000000 | bytes 9437184 | tf_op jit(solution)/shard_map/first_pick/pallas_call | solution.py:320
  45.9 3.4 %collective-permute-done.12.refs_1_ = bf16[128,1024]{1,0:T(8,128)(2,1)S(1)} collective-permute-done((bf16[128,1024]{1,0:T(8,128)(2,1)S(1)}, bf16[128,1024]{1,0:T(8,128)(2,1)S(1)}, u32[]{:S(2)}, u32[]{:S(2)}) %collective-permute-start.12) | collective-permute-done | bytes 262176 | tf_op jit(solution)/shard_map/ppermute | solution.py:280
  50.3 1.9 %collective-permute-start.14 = (bf16[352,256]{1,0:T(8,128)(2,1)S(1)}, bf16[352,256]{1,0:T(8,128)(2,1)S(1)}, u32[]{:S(2)}, u32[]{:S(2)}) collective-permute-start(bf16[352,256]{1,0:T(8,128)(2,1)S(1)} %get-tuple-element.78), channel_id=1, source_target_pairs={{0,16},{16,0},{1,17},{17,1},{2,18},{18,2},{3,19},{19,3},{4,20},{20... | collective-permute-start | bytes 540680 | tf_op jit(solution)/shard_map/ppermute | solution.py:286
  52.2 4.9 %collective-permute-done.14.refs_0_ = bf16[352,256]{1,0:T(8,128)(2,1)S(1)} collective-permute-done((bf16[352,256]{1,0:T(8,128)(2,1)S(1)}, bf16[352,256]{1,0:T(8,128)(2,1)S(1)}, u32[]{:S(2)}, u32[]{:S(2)}) %collective-permute-start.14) | collective-permute-done | bytes 180256 | tf_op jit(solution)/shard_map/ppermute | solution.py:286
  57.2 2.9 %collective-permute-done.13.refs_4_ = bf16[128,1024]{1,0:T(8,128)(2,1)S(1)} collective-permute-done((bf16[128,1024]{1,0:T(8,128)(2,1)S(1)}, bf16[128,1024]{1,0:T(8,128)(2,1)S(1)}, u32[]{:S(2)}, u32[]{:S(2)}) %collective-permute-start.13) | collective-permute-done | bytes 262176 | tf_op jit(solution)/shard_map/ppermute | solution.py:274
  60.3 1.6 %collective-permute-start.16 = (bf16[128,1024]{1,0:T(8,128)(2,1)S(1)}, bf16[128,1024]{1,0:T(8,128)(2,1)S(1)}, u32[]{:S(2)}, u32[]{:S(2)}) collective-permute-start(bf16[128,1024]{1,0:T(8,128)(2,1)S(1)} %later_pack.1.refs_0_), channel_id=1, source_target_pairs={{0,8},{1,9},{2,10},{3,11},{4,0},{5,1},{6,2},{7,3},{12,4},{13,5},{1... | collective-permute-start | bytes 786440 | tf_op jit(solution)/shard_map/ppermute | solution.py:277
  63.9 5.5 %collective-permute-done.19.refs_2_ = bf16[352,256]{1,0:T(8,128)(2,1)S(1)} collective-permute-done((bf16[352,256]{1,0:T(8,128)(2,1)S(1)}, bf16[352,256]{1,0:T(8,128)(2,1)S(1)}, u32[]{:S(2)}, u32[]{:S(2)}) %collective-permute-start.19) | collective-permute-done | bytes 180256 | tf_op jit(solution)/shard_map/ppermute | solution.py:286
  70.8 2.4 %collective-permute-done.18.refs_1_ = bf16[352,256]{1,0:T(8,128)(2,1)S(1)} collective-permute-done((bf16[352,256]{1,0:T(8,128)(2,1)S(1)}, bf16[352,256]{1,0:T(8,128)(2,1)S(1)}, u32[]{:S(2)}, u32[]{:S(2)}) %collective-permute-start.18) | collective-permute-done | bytes 180256 | tf_op jit(solution)/shard_map/ppermute | solution.py:286
  73.2 2.1 %collective-permute-start.20 = (bf16[128,1024]{1,0:T(8,128)(2,1)S(1)}, bf16[128,1024]{1,0:T(8,128)(2,1)S(1)}, u32[]{:S(2)}, u32[]{:S(2)}) collective-permute-start(bf16[128,1024]{1,0:T(8,128)(2,1)S(1)} %collective-permute-done.13.refs_4_), channel_id=1, source_target_pairs={{0,2},{1,3},{2,0},{3,1},{4,6},{5,7},{6,4},{7,5},{8,10},{9,11},{10,... | collective-permute-start | bytes 786440 | tf_op jit(solution)/shard_map/ppermute | solution.py:280
  75.4 3.0 %first_products.1 = (f32[1,1024]{1,0:T(1,128)S(1)}, bf16[704,1024]{1,0:T(8,128)(2,1)S(1)}, bf16[1024,1024]{1,0:T(8,128)(2,1)S(1)}, bf16[352,512]{1,0:T(8,128)(2,...) custom-call(bf16[512,1024]{1,0:T(8,128)(2,1)S(1)} %get-tuple-element.47.mine_ref, ...), custom_call_target="tpu_custom_call" | custom-call | flops 3000000000 | bytes 9437184 | tf_op jit(solution)/shard_map/first_products/pallas_call | solution.py:350
  78.4 2.7 %raw_part.1.refs_4_ = f32[704,1024]{1,0:T(8,128)S(1)} custom-call(bf16[1024,1024]{1,0:T(8,128)(2,1)S(1)} %get-tuple-element.56.rows_ref, bf16[352,2048]{1,0:T(8,128)(2,1)S(1)} %bitcast.16, bf16[352,256]{1,0:T(8,128)(2,1)S(1)} %collective-permute-done.2.refs_0_, bf16[352,256]{1,0:T(8,128)(2,1)S(1)} %collective-permute-done.5.refs_1_, ...), custom_call_target="tpu_custom_call" | custom-call | flops 3000000000 | bytes 9437184 | tf_op jit(solution)/shard_map/raw_part/pallas_call | solution.py:373
  85.1 9.2 %collective-permute-done.24.got_ref = bf16[352,512]{1,0:T(8,128)(2,1)S(1)} collective-permute-done((bf16[352,512]{1,0:T(8,128)(2,1)S(1)}, bf16[352,512]{1,0:T(8,128)(2,1)S(1)}, u32[]{:S(2)}, u32[]{:S(2)}) %collective-permute-start.24) | collective-permute-done | bytes 360480 | tf_op jit(solution)/shard_map/ppermute | solution.py:286
  94.3 3.2 %products.1 = (bf16[1024,1024]{1,0:T(8,128)(2,1)S(1)}, bf16[352,512]{1,0:T(8,128)(2,1)}, bf16[352,512]{1,0:T(8,128)(2,1)}, bf16[352,512]{1,0:T(8,128)(2,1)S(1)}, bf16[352,512]{1,0:T(8,128)(2,1)S(1)}) custom-call(bf16[512,1024]{1,0:T(8,128)(2,1)S(1)} %get-tuple-element.58.mine_ref, bf16[512,1024]{1,0:T(8,128)(2,1)S(1)} %collective-permute-done.23.got_ref, ...), custom_call_target="tpu_custom_call" | custom-call | tf_op jit(solution)/shard_map/products/pallas_call | solution.py:362
  99.5 3.9 %raw.1 = (bf16[704,1024]{1,0:T(8,128)(2,1)}, f32[16,64]{1,0:T(8,128)}) custom-call(bf16[1024,1024]{1,0:T(8,128)(2,1)S(1)} %get-tuple-element.70.rows_ref, bf16[352,2048]{1,0:T(8,128)(2,1)S(1)} %bitcast.17, bf16[352,256]{1,0:T(8,128)(2,1)S(1)} %collective-permute-done.14.refs_0_, bf16[352,256]{1,0:T(8,128)(2,1)S(1)} %collective-permute-done.18.refs_1_, ...), custom_call_target="tpu_custom_call" | custom-call | tf_op jit(solution)/shard_map/raw/pallas_call | solution.py:386
  103.4 3.5 %all-to-all-start = ((f32[16,1,64]{2,1,0:T(1,128)}), f32[16,1,64]{2,1,0:T(1,128)S(1)}, u32[]{:S(2)}, u32[]{:S(2)}) async-start(f32[16,1,64]{2,1,0:T(1,128)} %bitcast.10), calls=%async_computation | async-start | bytes 16384 | tf_op jit(solution)/shard_map/all_to_all | solution.py:447
  108.5 4.8 %all-to-all-done = f32[16,1,64]{2,1,0:T(1,128)S(1)} async-done(((f32[16,1,64]{2,1,0:T(1,128)}), f32[16,1,64]{2,1,0:T(1,128)S(1)}, u32[]{:S(2)}, u32[]{:S(2)}) %all-to-all-start) | async-done | bytes 4128 | tf_op jit(solution)/shard_map/all_to_all | solution.py:447
  113.8 1.6 %grad_gates.1 = f32[6,128]{1,0:T(8,128)} custom-call(s32[6,128]{1,0:T(8,128)} %bitcast.20, bf16[128,1152]{1,0:T(8,128)(2,1)} %copy-done.4, f32[16,64]{1,0:T(8,128)} %bitcast.24), custom_call_target="tpu_custom_call" | custom-call | tf_op jit(solution)/shard_map/grad_gates/pallas_call | solution.py:448
  (64 shorter events, 33.4 us)
Async XLA Ops:
  3.3 12.0 %collective-permute-start.1 = (bf16[128,1152]{1,0:T(8,128)(2,1)S(1)}, bf16[128,1152]{1,0:T(8,128)(2,1)S(1)}, u32[]{:S(2)}, u32[]{:S(2)}) collective-permute-start(bf16[128,1152]{1,0:T(8,128)(2,1)S(1)} %pack.1.refs_0_.slots_ref), channel_id=1, source_target_pairs={{0,2},{1,3},{2,0},{3,1},{4,6},{5,7},{6,4},{7,5},{8,10},{9,11},{10,... | collective-permute-start | bytes 884744 | tf_op jit(solution)/shard_map/ppermute | solution.py:280
  6.3 9.4 %collective-permute-start = (bf16[128,1152]{1,0:T(8,128)(2,1)S(1)}, bf16[128,1152]{1,0:T(8,128)(2,1)S(1)}, u32[]{:S(2)}, u32[]{:S(2)}) collective-permute-start(bf16[128,1152]{1,0:T(8,128)(2,1)S(1)} %pack.1.refs_0_.slots_ref), channel_id=1, source_target_pairs={{0,4},{1,5},{2,6},{3,7},{4,12},{5,13},{6,14},{7,15},{12,8},{13,9},... | collective-permute-start | bytes 884744 | tf_op jit(solution)/shard_map/ppermute | solution.py:274
  15.7 8.2 %collective-permute-start.4 = (bf16[128,1152]{1,0:T(8,128)(2,1)S(1)}, bf16[128,1152]{1,0:T(8,128)(2,1)S(1)}, u32[]{:S(2)}, u32[]{:S(2)}) collective-permute-start(bf16[128,1152]{1,0:T(8,128)(2,1)S(1)} %collective-permute-done.refs_2_), channel_id=1, source_target_pairs={{0,2},{1,3},{2,0},{3,1},{4,6},{5,7},{6,4},{7,5},{8,10},{9,11},{10,... | collective-permute-start | bytes 884744 | tf_op jit(solution)/shard_map/ppermute | solution.py:280
  16.1 8.5 %collective-permute-start.3 = (bf16[128,1152]{1,0:T(8,128)(2,1)S(1)}, bf16[128,1152]{1,0:T(8,128)(2,1)S(1)}, u32[]{:S(2)}, u32[]{:S(2)}) collective-permute-start(bf16[128,1152]{1,0:T(8,128)(2,1)S(1)} %collective-permute-done.refs_2_), channel_id=1, source_target_pairs={{0,4},{1,5},{2,6},{3,7},{4,12},{5,13},{6,14},{7,15},{12,8},{13,9},... | collective-permute-start | bytes 884744 | tf_op jit(solution)/shard_map/ppermute | solution.py:274
  24.6 10.3 %collective-permute-start.6 = (bf16[128,1152]{1,0:T(8,128)(2,1)S(1)}, bf16[128,1152]{1,0:T(8,128)(2,1)S(1)}, u32[]{:S(2)}, u32[]{:S(2)}) collective-permute-start(bf16[128,1152]{1,0:T(8,128)(2,1)S(1)} %collective-permute-done.3.refs_4_), channel_id=1, source_target_pairs={{0,2},{1,3},{2,0},{3,1},{4,6},{5,7},{6,4},{7,5},{8,10},{9,11},{10,... | collective-permute-start | bytes 884744 | tf_op jit(solution)/shard_map/ppermute | solution.py:280
  25.9 9.0 %collective-permute-start.7 = (bf16[128,1152]{1,0:T(8,128)(2,1)S(1)}, bf16[128,1152]{1,0:T(8,128)(2,1)S(1)}, u32[]{:S(2)}, u32[]{:S(2)}) collective-permute-start(bf16[128,1152]{1,0:T(8,128)(2,1)S(1)} %pack.1.refs_0_.slots_ref), channel_id=1, source_target_pairs={{0,8},{1,9},{2,10},{3,11},{4,0},{5,1},{6,2},{7,3},{12,4},{13,5},{1... | collective-permute-start | bytes 884744 | tf_op jit(solution)/shard_map/ppermute | solution.py:277
  34.9 8.1 %collective-permute-start.11 = (bf16[128,1152]{1,0:T(8,128)(2,1)S(1)}, bf16[128,1152]{1,0:T(8,128)(2,1)S(1)}, u32[]{:S(2)}, u32[]{:S(2)}) collective-permute-start(bf16[128,1152]{1,0:T(8,128)(2,1)S(1)} %collective-permute-done.7.refs_6_), channel_id=1, source_target_pairs={{0,2},{1,3},{2,0},{3,1},{4,6},{5,7},{6,4},{7,5},{8,10},{9,11},{10,... | collective-permute-start | bytes 884744 | tf_op jit(solution)/shard_map/ppermute | solution.py:280
  35.4 7.3 %collective-permute-start.10 = (bf16[128,1024]{1,0:T(8,128)(2,1)S(1)}, bf16[128,1024]{1,0:T(8,128)(2,1)S(1)}, u32[]{:S(2)}, u32[]{:S(2)}) collective-permute-start(bf16[128,1024]{1,0:T(8,128)(2,1)S(1)} %later_pack.1.refs_0_), channel_id=1, source_target_pairs={{0,4},{1,5},{2,6},{3,7},{4,12},{5,13},{6,14},{7,15},{12,8},{13,9},... | collective-permute-start | bytes 786440 | tf_op jit(solution)/shard_map/ppermute | solution.py:274
  42.9 6.4 %collective-permute-start.12 = (bf16[128,1024]{1,0:T(8,128)(2,1)S(1)}, bf16[128,1024]{1,0:T(8,128)(2,1)S(1)}, u32[]{:S(2)}, u32[]{:S(2)}) collective-permute-start(bf16[128,1024]{1,0:T(8,128)(2,1)S(1)} %later_pack.1.refs_0_), channel_id=1, source_target_pairs={{0,2},{1,3},{2,0},{3,1},{4,6},{5,7},{6,4},{7,5},{8,10},{9,11},{10,... | collective-permute-start | bytes 786440 | tf_op jit(solution)/shard_map/ppermute | solution.py:280
  49.3 23.9 %collective-permute-start.17 = (bf16[528,1024]{1,0:T(8,128)(2,1)S(1)}, bf16[528,1024]{1,0:T(8,128)(2,1)S(1)}, u32[]{:S(2)}, u32[]{:S(2)}) collective-permute-start(bf16[528,1024]{1,0:T(8,128)(2,1)S(1)} %get-tuple-element.51), channel_id=1, source_target_pairs={{0,1},{1,0},{2,3},{3,2},{4,5},{5,4},{6,7},{7,6},{8,9},{9,8},{10,11... | collective-permute-start | bytes 3244040 | tf_op jit(solution)/shard_map/ppermute | solution.py:283
  49.3 10.8 %collective-permute-start.13 = (bf16[128,1024]{1,0:T(8,128)(2,1)S(1)}, bf16[128,1024]{1,0:T(8,128)(2,1)S(1)}, u32[]{:S(2)}, u32[]{:S(2)}) collective-permute-start(bf16[128,1024]{1,0:T(8,128)(2,1)S(1)} %collective-permute-done.10.refs_2_), channel_id=1, source_target_pairs={{0,4},{1,5},{2,6},{3,7},{4,12},{5,13},{6,14},{7,15},{12,8},{13,9},... | collective-permute-start | bytes 786440 | tf_op jit(solution)/shard_map/ppermute | solution.py:274
  50.3 6.9 %collective-permute-start.14 = (bf16[352,256]{1,0:T(8,128)(2,1)S(1)}, bf16[352,256]{1,0:T(8,128)(2,1)S(1)}, u32[]{:S(2)}, u32[]{:S(2)}) collective-permute-start(bf16[352,256]{1,0:T(8,128)(2,1)S(1)} %get-tuple-element.78), channel_id=1, source_target_pairs={{0,16},{16,0},{1,17},{17,1},{2,18},{18,2},{3,19},{19,3},{4,20},{20... | collective-permute-start | bytes 540680 | tf_op jit(solution)/shard_map/ppermute | solution.py:286
  60.1 13.1 %collective-permute-start.15 = (bf16[128,1024]{1,0:T(8,128)(2,1)S(1)}, bf16[128,1024]{1,0:T(8,128)(2,1)S(1)}, u32[]{:S(2)}, u32[]{:S(2)}) collective-permute-start(bf16[128,1024]{1,0:T(8,128)(2,1)S(1)} %collective-permute-done.10.refs_2_), channel_id=1, source_target_pairs={{0,2},{1,3},{2,0},{3,1},{4,6},{5,7},{6,4},{7,5},{8,10},{9,11},{10,... | collective-permute-start | bytes 786440 | tf_op jit(solution)/shard_map/ppermute | solution.py:280
  60.3 12.9 %collective-permute-start.16 = (bf16[128,1024]{1,0:T(8,128)(2,1)S(1)}, bf16[128,1024]{1,0:T(8,128)(2,1)S(1)}, u32[]{:S(2)}, u32[]{:S(2)}) collective-permute-start(bf16[128,1024]{1,0:T(8,128)(2,1)S(1)} %later_pack.1.refs_0_), channel_id=1, source_target_pairs={{0,8},{1,9},{2,10},{3,11},{4,0},{5,1},{6,2},{7,3},{12,4},{13,5},{1... | collective-permute-start | bytes 786440 | tf_op jit(solution)/shard_map/ppermute | solution.py:277
  61.9 7.5 %collective-permute-start.19 = (bf16[352,256]{1,0:T(8,128)(2,1)S(1)}, bf16[352,256]{1,0:T(8,128)(2,1)S(1)}, u32[]{:S(2)}, u32[]{:S(2)}) collective-permute-start(bf16[352,256]{1,0:T(8,128)(2,1)S(1)} %get-tuple-element.76), channel_id=1, source_target_pairs={{0,16},{16,0},{1,17},{17,1},{2,18},{18,2},{3,19},{19,3},{4,20},{20... | collective-permute-start | bytes 540680 | tf_op jit(solution)/shard_map/ppermute | solution.py:286
  63.4 9.9 %collective-permute-start.18 = (bf16[352,256]{1,0:T(8,128)(2,1)S(1)}, bf16[352,256]{1,0:T(8,128)(2,1)S(1)}, u32[]{:S(2)}, u32[]{:S(2)}) collective-permute-start(bf16[352,256]{1,0:T(8,128)(2,1)S(1)} %get-tuple-element.77), channel_id=1, source_target_pairs={{0,16},{16,0},{1,17},{17,1},{2,18},{18,2},{3,19},{19,3},{4,20},{20... | collective-permute-start | bytes 540680 | tf_op jit(solution)/shard_map/ppermute | solution.py:286
  69.3 11.7 %collective-permute-start.22 = (bf16[352,256]{1,0:T(8,128)(2,1)S(1)}, bf16[352,256]{1,0:T(8,128)(2,1)S(1)}, u32[]{:S(2)}, u32[]{:S(2)}) collective-permute-start(bf16[352,256]{1,0:T(8,128)(2,1)S(1)} %get-tuple-element.75), channel_id=1, source_target_pairs={{0,16},{16,0},{1,17},{17,1},{2,18},{18,2},{3,19},{19,3},{4,20},{20... | collective-permute-start | bytes 540680 | tf_op jit(solution)/shard_map/ppermute | solution.py:286
  73.2 7.9 %collective-permute-start.20 = (bf16[128,1024]{1,0:T(8,128)(2,1)S(1)}, bf16[128,1024]{1,0:T(8,128)(2,1)S(1)}, u32[]{:S(2)}, u32[]{:S(2)}) collective-permute-start(bf16[128,1024]{1,0:T(8,128)(2,1)S(1)} %collective-permute-done.13.refs_4_), channel_id=1, source_target_pairs={{0,2},{1,3},{2,0},{3,1},{4,6},{5,7},{6,4},{7,5},{8,10},{9,11},{10,... | collective-permute-start | bytes 786440 | tf_op jit(solution)/shard_map/ppermute | solution.py:280
  82.9 11.4 %collective-permute-start.23 = (bf16[512,1024]{1,0:T(8,128)(2,1)S(1)}, bf16[512,1024]{1,0:T(8,128)(2,1)S(1)}, u32[]{:S(2)}, u32[]{:S(2)}) collective-permute-start(bf16[512,1024]{1,0:T(8,128)(2,1)S(1)} %get-tuple-element.59), channel_id=1, source_target_pairs={{0,1},{1,0},{2,3},{3,2},{4,5},{5,4},{6,7},{7,6},{8,9},{9,8},{10,11... | collective-permute-start | bytes 3145736 | tf_op jit(solution)/shard_map/ppermute | solution.py:283
  83.0 11.3 %collective-permute-start.24 = (bf16[352,512]{1,0:T(8,128)(2,1)S(1)}, bf16[352,512]{1,0:T(8,128)(2,1)S(1)}, u32[]{:S(2)}, u32[]{:S(2)}) collective-permute-start(bf16[352,512]{1,0:T(8,128)(2,1)S(1)} %get-tuple-element.61), channel_id=1, source_target_pairs={{0,16},{16,0},{1,17},{17,1},{2,18},{18,2},{3,19},{19,3},{4,20},{20... | collective-permute-start | bytes 1081352 | tf_op jit(solution)/shard_map/ppermute | solution.py:286
  84.5 23.2 %collective-permute-start.27 = (bf16[352,512]{1,0:T(8,128)(2,1)S(1)}, bf16[352,512]{1,0:T(8,128)(2,1)S(1)}, u32[]{:S(2)}, u32[]{:S(2)}) collective-permute-start(bf16[352,512]{1,0:T(8,128)(2,1)S(1)} %get-tuple-element.68), channel_id=1, source_target_pairs={{0,16},{16,0},{1,17},{17,1},{2,18},{18,2},{3,19},{19,3},{4,20},{20... | collective-permute-start | bytes 1081352 | tf_op jit(solution)/shard_map/ppermute | solution.py:286
  97.5 18.0 %collective-permute-start.26 = (bf16[352,512]{1,0:T(8,128)(2,1)}, bf16[352,512]{1,0:T(8,128)(2,1)S(1)}, u32[]{:S(2)}, u32[]{:S(2)}) collective-permute-start(bf16[352,512]{1,0:T(8,128)(2,1)} %get-tuple-element.66), channel_id=1, source_target_pairs={{0,16},{16,0},{1,17},{17,1},{2,18},{18,2},{3,19},{19,3},{4,20},{20... | collective-permute-start | bytes 1081352 | tf_op jit(solution)/shard_map/ppermute | solution.py:286
  98.9 18.1 %collective-permute-start.25 = (bf16[352,512]{1,0:T(8,128)(2,1)}, bf16[352,512]{1,0:T(8,128)(2,1)S(1)}, u32[]{:S(2)}, u32[]{:S(2)}) collective-permute-start(bf16[352,512]{1,0:T(8,128)(2,1)} %get-tuple-element.64), channel_id=1, source_target_pairs={{0,16},{16,0},{1,17},{17,1},{2,18},{18,2},{3,19},{19,3},{4,20},{20... | collective-permute-start | bytes 1081352 | tf_op jit(solution)/shard_map/ppermute | solution.py:286
  103.4 9.9 %all-to-all-start = ((f32[16,1,64]{2,1,0:T(1,128)}), f32[16,1,64]{2,1,0:T(1,128)S(1)}, u32[]{:S(2)}, u32[]{:S(2)}) async-start(f32[16,1,64]{2,1,0:T(1,128)} %bitcast.10), calls=%async_computation | async-start | bytes 16384 | tf_op jit(solution)/shard_map/all_to_all | solution.py:447
  (13 other events, 143.8 us)

commit v5 on v4

--- a/solution.py
+++ b/solution.py
@@ -10,7 +10,7 @@
 NZ, NY, NC = 4, 2, 2
 CHUNKS = 2
 PIECES = 2
-PART = 256
+PART = 512
 LANES = 128
 NT = (((1,), (1,)), ((), ()))
 VMEM = pl.BlockSpec(memory_space=pltpu.VMEM)
@@ -413,37 +413,31 @@
             name="finish",
         )(own, got, *before)
 
-    got_weight = [swap(weight[:, k : k + PART]) for k in range(0, model, PART)]
+    w = [swap(weight[:, k : k + PART]) for k in range(0, model, PART)]
     x0 = pack()
-    pred0, facing0 = forward(x0), across(x0)
-    done = (facing0, got_weight[0])
-    far0, pred_across0 = forward(behind(pred0, *done)), across(behind(pred0, *done))
-    done = (far0, pred_across0, got_weight[1])
-    succ0, far_across0 = backward(behind(x0, *done)), across(behind(far0, *done))
-    done = (succ0, far_across0, got_weight[2], got_weight[3])
-    x1 = later_pack(1, far_across0)
-    pred1, succ_across0 = forward(behind(x1, *done)), across(behind(succ0, *done))
-    done = (pred1, succ_across0)
-    far1, facing1 = forward(behind(pred1, *done)), across(behind(x1, *done))
+    f0, r0, y0 = forward(x0), backward(x0), across(x0)
+    ff0, yf0 = forward(behind(f0, w[0])), across(behind(f0, w[0]))
+    x1 = later_pack(1, r0)
+    f1, yr0 = forward(x1), across(behind(r0, y0))
+    r1, yff0 = backward(behind(x1, ff0)), across(behind(ff0, yf0, w[1]))
     mine0, theirs0, pmat, gslot = first_pick(
-        [x0, facing0, pred0, pred_across0, far0, far_across0, succ0, behind(succ_across0, pred1)]
-    )
-    done = (far1, facing1, mine0, got_weight[4])
-    succ1, pred_across1 = backward(behind(x1, *done)), across(behind(pred1, *done))
-    got = sibling(behind(theirs0, facing1))
-    done = (succ1, pred_across1, got, *got_weight[5:7])
-    facing_back1, far_across1 = backward(behind(facing1, *done)), across(behind(far1, *done))
+        [x0, y0, f0, yf0, ff0, yff0, r0, behind(yr0, f1, w[2])]
+    )
+    ff1, y1 = forward(f1), across(behind(x1, yr0))
+    yf1 = across(behind(f1, yff0, w[3]))
+    ry1 = backward(behind(y1, r1, mine0, w[3]))
+    got = sibling(theirs0)
     rows0, send0, own0, slot_gates, hs = first_products(mine0, got, gslot)
     got0 = [swap(part) for part in send0]
-    raw = raw_part(rows0, got_weight[: len(parts)])
+    yff1 = across(behind(ff1, y1))
+    raw = raw_part(rows0, w[: len(parts)])
     mine1, theirs1 = later_pick(
-        [x1, facing1, pred1, pred_across1, far1, far_across1, succ1, facing_back1],
-        behind(pmat, raw, got_weight[7]),
-    )
-    rows1, send1, own1 = later_products(mine1, sibling(theirs1), behind(hs, got0[0]))
+        [x1, y1, f1, yf1, ff1, yff1, r1, ry1], behind(pmat, raw, got0[0])
+    )
+    rows1, send1, own1 = later_products(mine1, sibling(theirs1), hs)
     got1 = [swap(part) for part in send1]
 
-    grad_hidden, back = raw_rest(rows1, got_weight[len(parts) :], raw, slot_gates)
+    grad_hidden, back = raw_rest(rows1, w[len(parts) :], raw, slot_gates)
     returned = lax.all_to_all(back, "expert", split_axis=0, concat_axis=0, tiled=True)
     grad_gates = pl.pallas_call(
         gates_kernel,

time: 118 us -> 101 us (0.86)
  waiting for transfers between devices: 56 us -> 27.2 us
  starting transfers between devices: 35.9 us -> 50.6 us
  local copies, waits for them, and re-layouts: 4.59 us -> 2.12 us
    ppermute x12 -> x8, waiting for transfers between devices: 36.4 us -> 0.02 us  [swap(): return lax.ppermute(x, 'dp', [(0, 1), (1, 0)])]
    ppermute x4, starting transfers between devices: 5.67 us -> 16.5 us  [forward(): return lax.ppermute(x, 'expert', ring_pairs(1))]
    all_to_all x1, starting transfers between devices: 3.48 us -> 11.2 us  [ring_shards(): lax.all_to_all(back, 'expert', split_axis=0, concat_axis=0, tiled=True)]
    ppermute x12 -> x8, starting transfers between devices: 14.6 us -> 9.98 us  [swap(): return lax.ppermute(x, 'dp', [(0, 1), (1, 0)])]
    ppermute x3, waiting for transfers between devices: 0.6 us -> 3.33 us  [backward(): return lax.ppermute(x, 'expert', ring_pairs(-1))]
    unnamed x16 -> x14, local copies, waits for them, and re-layouts: 3.01 us -> 0.62 us
    ppermute x4, waiting for transfers between devices: 10.6 us -> 12.8 us  [forward(): return lax.ppermute(x, 'expert', ring_pairs(1))]
    ppermute x7, waiting for transfers between devices: 3.64 us -> 5.07 us  [across(): return lax.ppermute(x, 'expert', swap_pairs(2))]
  transfers between devices with their start and end apart: 29 -> 25, of which waited for: 17 -> 10; matrix products, arithmetic and copies ran while one was open for 1% -> 0% of each run, Pallas kernels for 16% -> 17%
where the time goes in v5:
time: 101 us
  starting transfers between devices  50.6 us (50%)
  waiting for transfers between devices  27.2 us (27%)
  Pallas kernels  20.5 us (20%)
  local copies, waits for them, and re-layouts  2.12 us (2%)
    ppermute x4, starting transfers between devices, forward(): return lax.ppermute(x, 'expert', ring_pairs(1))  16.5 us
    ppermute x4, waiting for transfers between devices, forward(): return lax.ppermute(x, 'expert', ring_pairs(1))  12.8 us
    all_to_all x1, starting transfers between devices, ring_shards(): lax.all_to_all(back, 'expert', split_axis=0, concat_axis=0, tiled=True)  11.2 us
    ppermute x8, starting transfers between devices, swap(): return lax.ppermute(x, 'dp', [(0, 1), (1, 0)])  9.98 us
    ppermute x7, starting transfers between devices, across(): return lax.ppermute(x, 'expert', swap_pairs(2))  8.61 us
    ppermute x7, waiting for transfers between devices, across(): return lax.ppermute(x, 'expert', swap_pairs(2))  5.07 us
    all_to_all x1, waiting for transfers between devices, ring_shards(): lax.all_to_all(back, 'expert', split_axis=0, concat_axis=0, tiled=True)  4.82 us
    ppermute x3, starting transfers between devices, backward(): return lax.ppermute(x, 'expert', ring_pairs(-1))  4.1 us
  transfers between devices with their start and end apart: 25, of which 10 were waited for; matrix products, arithmetic and copies ran while one was open for 0% of the time, Pallas kernels for 17%

profile of v5, /device:TPU:0, one launch (start us, length us, event | category | flops | bytes accessed | tf_op | source)
XLA Modules:
  0.0 101.2 jit_solution(15637070327123254473)
XLA Ops:
  2.2 3.0 %collective-permute-start.6 = (bf16[352,512]{1,0:T(8,128)(2,1)S(1)}, bf16[352,512]{1,0:T(8,128)(2,1)S(1)}, u32[]{:S(2)}, u32[]{:S(2)}) collective-permute-start(bf16[352,512]{1,0:T(8,128)(2,1)S(1)} %get-tuple-element.68), channel_id=1, source_target_pairs={{0,16},{16,0},{1,17},{17,1},{2,18},{18,2},{3,19},{19,3},{4,20},{20... | collective-permute-start | bytes 1081352 | tf_op jit(solution)/shard_map/ppermute | solution.py:286
  5.4 1.6 %collective-permute-start.5 = (bf16[128,1152]{1,0:T(8,128)(2,1)S(1)}, bf16[128,1152]{1,0:T(8,128)(2,1)S(1)}, u32[]{:S(2)}, u32[]{:S(2)}) collective-permute-start(bf16[128,1152]{1,0:T(8,128)(2,1)S(1)} %pack.1.refs_0_.slots_ref), channel_id=1, source_target_pairs={{0,4},{1,5},{2,6},{3,7},{4,12},{5,13},{6,14},{7,15},{12,8},{13,9},... | collective-permute-start | bytes 884744 | tf_op jit(solution)/shard_map/ppermute | solution.py:274
  10.4 4.8 %collective-permute-done.5.refs_2_ = bf16[128,1152]{1,0:T(8,128)(2,1)S(1)} collective-permute-done((bf16[128,1152]{1,0:T(8,128)(2,1)S(1)}, bf16[128,1152]{1,0:T(8,128)(2,1)S(1)}, u32[]{:S(2)}, u32[]{:S(2)}) %collective-permute-start.5) | collective-permute-done | bytes 294944 | tf_op jit(solution)/shard_map/ppermute | solution.py:274
  15.2 1.5 %collective-permute-start.8 = (bf16[128,1152]{1,0:T(8,128)(2,1)S(1)}, bf16[128,1152]{1,0:T(8,128)(2,1)S(1)}, u32[]{:S(2)}, u32[]{:S(2)}) collective-permute-start(bf16[128,1152]{1,0:T(8,128)(2,1)S(1)} %collective-permute-done.5.refs_2_), channel_id=1, source_target_pairs={{0,2},{1,3},{2,0},{3,1},{4,6},{5,7},{6,4},{7,5},{8,10},{9,11},{10,... | collective-permute-start | bytes 884744 | tf_op jit(solution)/shard_map/ppermute | solution.py:280
  16.8 7.6 %collective-permute-start.7 = (bf16[128,1152]{1,0:T(8,128)(2,1)S(1)}, bf16[128,1152]{1,0:T(8,128)(2,1)S(1)}, u32[]{:S(2)}, u32[]{:S(2)}) collective-permute-start(bf16[128,1152]{1,0:T(8,128)(2,1)S(1)} %collective-permute-done.5.refs_2_), channel_id=1, source_target_pairs={{0,4},{1,5},{2,6},{3,7},{4,12},{5,13},{6,14},{7,15},{12,8},{13,9},... | collective-permute-start | bytes 884744 | tf_op jit(solution)/shard_map/ppermute | solution.py:274
  25.0 3.6 %collective-permute-done.7.refs_4_ = bf16[128,1152]{1,0:T(8,128)(2,1)S(1)} collective-permute-done((bf16[128,1152]{1,0:T(8,128)(2,1)S(1)}, bf16[128,1152]{1,0:T(8,128)(2,1)S(1)}, u32[]{:S(2)}, u32[]{:S(2)}) %collective-permute-start.7) | collective-permute-done | bytes 294944 | tf_op jit(solution)/shard_map/ppermute | solution.py:274
  30.1 4.5 %collective-permute-start.4 = (bf16[128,1024]{1,0:T(8,128)(2,1)S(1)}, bf16[128,1024]{1,0:T(8,128)(2,1)S(1)}, u32[]{:S(2)}, u32[]{:S(2)}) collective-permute-start(bf16[128,1024]{1,0:T(8,128)(2,1)S(1)} %later_pack.1.refs_0_), channel_id=1, source_target_pairs={{0,4},{1,5},{2,6},{3,7},{4,12},{5,13},{6,14},{7,15},{12,8},{13,9},... | collective-permute-start | bytes 786440 | tf_op jit(solution)/shard_map/ppermute | solution.py:274
  34.6 4.3 %collective-permute-done.4.refs_2_ = bf16[128,1024]{1,0:T(8,128)(2,1)S(1)} collective-permute-done((bf16[128,1024]{1,0:T(8,128)(2,1)S(1)}, bf16[128,1024]{1,0:T(8,128)(2,1)S(1)}, u32[]{:S(2)}, u32[]{:S(2)}) %collective-permute-start.4) | collective-permute-done | bytes 262176 | tf_op jit(solution)/shard_map/ppermute | solution.py:274
  38.9 1.6 %first_pick.1 = (bf16[512,1024]{1,0:T(8,128)(2,1)S(1)}, bf16[528,1024]{1,0:T(8,128)(2,1)S(1)}, bf16[1024,128]{1,0:T(8,128)(2,1)S(1)}, f32[8,128]{1,0:T(8,128)S(1)}) custom-call(bf16[128,1152]{1,0:T(8,128)(2,1)S(1)} %pack.1.refs_0_.slots_ref, bf16[128,1152]{1,0:T(8,128)(2,1)S(1)} %collective-permute-done.1.refs_1_, ...), custom_call_target="tpu_custom_call" | custom-call | flops 3000000000 | bytes 9437184 | tf_op jit(solution)/shard_map/first_pick/pallas_call | solution.py:320
  41.4 2.8 %collective-permute-start.13 = (bf16[128,1024]{1,0:T(8,128)(2,1)S(1)}, bf16[128,1024]{1,0:T(8,128)(2,1)S(1)}, u32[]{:S(2)}, u32[]{:S(2)}) collective-permute-start(bf16[128,1024]{1,0:T(8,128)(2,1)S(1)} %collective-permute-done.4.refs_2_), channel_id=1, source_target_pairs={{0,4},{1,5},{2,6},{3,7},{4,12},{5,13},{6,14},{7,15},{12,8},{13,9},... | collective-permute-start | bytes 786440 | tf_op jit(solution)/shard_map/ppermute | solution.py:274
  44.2 2.0 %collective-permute-start.3 = (bf16[128,1024]{1,0:T(8,128)(2,1)S(1)}, bf16[128,1024]{1,0:T(8,128)(2,1)S(1)}, u32[]{:S(2)}, u32[]{:S(2)}) collective-permute-start(bf16[128,1024]{1,0:T(8,128)(2,1)S(1)} %later_pack.1.refs_0_), channel_id=1, source_target_pairs={{0,2},{1,3},{2,0},{3,1},{4,6},{5,7},{6,4},{7,5},{8,10},{9,11},{10,... | collective-permute-start | bytes 786440 | tf_op jit(solution)/shard_map/ppermute | solution.py:280
  46.6 3.0 %first_products.1 = (f32[1,1024]{1,0:T(1,128)S(1)}, bf16[704,1024]{1,0:T(8,128)(2,1)S(1)}, bf16[1024,1024]{1,0:T(8,128)(2,1)S(1)}, bf16[352,512]{1,0:T(8,128)(2,...) custom-call(bf16[512,1024]{1,0:T(8,128)(2,1)S(1)} %get-tuple-element.42.mine_ref, ...), custom_call_target="tpu_custom_call" | custom-call | flops 3000000000 | bytes 9437184 | tf_op jit(solution)/shard_map/first_products/pallas_call | solution.py:350
  49.6 1.6 %collective-permute-start.19 = (bf16[352,512]{1,0:T(8,128)(2,1)S(1)}, bf16[352,512]{1,0:T(8,128)(2,1)S(1)}, u32[]{:S(2)}, u32[]{:S(2)}) collective-permute-start(bf16[352,512]{1,0:T(8,128)(2,1)S(1)} %get-tuple-element.48), channel_id=1, source_target_pairs={{0,16},{16,0},{1,17},{17,1},{2,18},{18,2},{3,19},{19,3},{4,20},{20... | collective-permute-start | bytes 1081352 | tf_op jit(solution)/shard_map/ppermute | solution.py:286
  52.5 1.7 %collective-permute-start.14 = (bf16[128,1024]{1,0:T(8,128)(2,1)S(1)}, bf16[128,1024]{1,0:T(8,128)(2,1)S(1)}, u32[]{:S(2)}, u32[]{:S(2)}) collective-permute-start(bf16[128,1024]{1,0:T(8,128)(2,1)S(1)} %collective-permute-done.13.refs_4_), channel_id=1, source_target_pairs={{0,2},{1,3},{2,0},{3,1},{4,6},{5,7},{6,4},{7,5},{8,10},{9,11},{10,... | collective-permute-start | bytes 786440 | tf_op jit(solution)/shard_map/ppermute | solution.py:280
  54.6 2.3 %collective-permute-done.15.refs_6_ = bf16[128,1024]{1,0:T(8,128)(2,1)S(1)} collective-permute-done((bf16[128,1024]{1,0:T(8,128)(2,1)S(1)}, bf16[128,1024]{1,0:T(8,128)(2,1)S(1)}, u32[]{:S(2)}, u32[]{:S(2)}) %collective-permute-start.15) | collective-permute-done | bytes 262176 | tf_op jit(solution)/shard_map/ppermute | solution.py:277
  56.9 2.3 %collective-permute-start.17 = (bf16[128,1024]{1,0:T(8,128)(2,1)S(1)}, bf16[128,1024]{1,0:T(8,128)(2,1)S(1)}, u32[]{:S(2)}, u32[]{:S(2)}) collective-permute-start(bf16[128,1024]{1,0:T(8,128)(2,1)S(1)} %collective-permute-done.3.refs_1_), channel_id=1, source_target_pairs={{0,8},{1,9},{2,10},{3,11},{4,0},{5,1},{6,2},{7,3},{12,4},{13,5},{1... | collective-permute-start | bytes 786440 | tf_op jit(solution)/shard_map/ppermute | solution.py:277
  59.1 2.6 %raw_part.1.refs_2_ = f32[704,1024]{1,0:T(8,128)S(1)} custom-call(bf16[1024,1024]{1,0:T(8,128)(2,1)S(1)} %get-tuple-element.47.rows_ref, bf16[352,2048]{1,0:T(8,128)(2,1)S(1)} %bitcast.16, bf16[352,512]{1,0:T(8,128)(2,1)S(1)} %collective-permute-done.6.refs_0_, bf16[352,512]{1,0:T(8,128)(2,1)S(1)} %collective-permute-done.9.refs_1_), custom_call_target="tpu_custom_call" | custom-call | flops 3000000000 | bytes 9437184 | tf_op jit(solution)/shard_map/raw_part/pallas_call | solution.py:373
  61.8 3.9 %collective-permute-done.12.refs_3_ = bf16[128,1024]{1,0:T(8,128)(2,1)S(1)} collective-permute-done((bf16[128,1024]{1,0:T(8,128)(2,1)S(1)}, bf16[128,1024]{1,0:T(8,128)(2,1)S(1)}, u32[]{:S(2)}, u32[]{:S(2)}) %collective-permute-start.12) | collective-permute-done | bytes 262176 | tf_op jit(solution)/shard_map/ppermute | solution.py:280
  68.0 1.6 %collective-permute-start.23 = (bf16[352,512]{1,0:T(8,128)(2,1)S(1)}, bf16[352,512]{1,0:T(8,128)(2,1)S(1)}, u32[]{:S(2)}, u32[]{:S(2)}) collective-permute-start(bf16[352,512]{1,0:T(8,128)(2,1)S(1)} %get-tuple-element.58), channel_id=1, source_target_pairs={{0,16},{16,0},{1,17},{17,1},{2,18},{18,2},{3,19},{19,3},{4,20},{20... | collective-permute-start | bytes 1081352 | tf_op jit(solution)/shard_map/ppermute | solution.py:286
  70.7 3.2 %products.1 = (bf16[1024,1024]{1,0:T(8,128)(2,1)S(1)}, bf16[352,512]{1,0:T(8,128)(2,1)}, bf16[352,512]{1,0:T(8,128)(2,1)}, bf16[352,512]{1,0:T(8,128)(2,1)S(1)}, bf16[352,512]{1,0:T(8,128)(2,1)S(1)}) custom-call(bf16[512,1024]{1,0:T(8,128)(2,1)S(1)} %get-tuple-element.50.mine_ref, bf16[512,1024]{1,0:T(8,128)(2,1)S(1)} %collective-permute-done.20.got_ref, ...), custom_call_target="tpu_custom_call" | custom-call | tf_op jit(solution)/shard_map/products/pallas_call | solution.py:362
  75.9 3.9 %raw.1 = (bf16[704,1024]{1,0:T(8,128)(2,1)}, f32[16,64]{1,0:T(8,128)}) custom-call(bf16[1024,1024]{1,0:T(8,128)(2,1)S(1)} %get-tuple-element.60.rows_ref, bf16[352,2048]{1,0:T(8,128)(2,1)S(1)} %bitcast.17, bf16[352,512]{1,0:T(8,128)(2,1)S(1)} %collective-permute-done.16.refs_0_, bf16[352,512]{1,0:T(8,128)(2,1)S(1)} %collective-permute-done.11.refs_1_, ...), custom_call_target="tpu_custom_call" | custom-call | tf_op jit(solution)/shard_map/raw/pallas_call | solution.py:386
  79.8 11.2 %all-to-all-start = ((f32[16,1,64]{2,1,0:T(1,128)}), f32[16,1,64]{2,1,0:T(1,128)S(1)}, u32[]{:S(2)}, u32[]{:S(2)}) async-start(f32[16,1,64]{2,1,0:T(1,128)} %bitcast.10), calls=%async_computation | async-start | bytes 16384 | tf_op jit(solution)/shard_map/all_to_all | solution.py:441
  92.6 4.8 %all-to-all-done = f32[16,1,64]{2,1,0:T(1,128)S(1)} async-done(((f32[16,1,64]{2,1,0:T(1,128)}), f32[16,1,64]{2,1,0:T(1,128)S(1)}, u32[]{:S(2)}, u32[]{:S(2)}) %all-to-all-start) | async-done | bytes 4128 | tf_op jit(solution)/shard_map/all_to_all | solution.py:441
  98.0 1.6 %grad_gates.1 = f32[6,128]{1,0:T(8,128)} custom-call(s32[6,128]{1,0:T(8,128)} %bitcast.20, bf16[128,1152]{1,0:T(8,128)(2,1)} %copy-done.3, f32[16,64]{1,0:T(8,128)} %bitcast.24), custom_call_target="tpu_custom_call" | custom-call | tf_op jit(solution)/shard_map/grad_gates/pallas_call | solution.py:442
  (54 shorter events, 19.3 us)
Async XLA Ops:
  2.2 13.1 %collective-permute-start.6 = (bf16[352,512]{1,0:T(8,128)(2,1)S(1)}, bf16[352,512]{1,0:T(8,128)(2,1)S(1)}, u32[]{:S(2)}, u32[]{:S(2)}) collective-permute-start(bf16[352,512]{1,0:T(8,128)(2,1)S(1)} %get-tuple-element.68), channel_id=1, source_target_pairs={{0,16},{16,0},{1,17},{17,1},{2,18},{18,2},{3,19},{19,3},{4,20},{20... | collective-permute-start | bytes 1081352 | tf_op jit(solution)/shard_map/ppermute | solution.py:286
  5.4 9.8 %collective-permute-start.5 = (bf16[128,1152]{1,0:T(8,128)(2,1)S(1)}, bf16[128,1152]{1,0:T(8,128)(2,1)S(1)}, u32[]{:S(2)}, u32[]{:S(2)}) collective-permute-start(bf16[128,1152]{1,0:T(8,128)(2,1)S(1)} %pack.1.refs_0_.slots_ref), channel_id=1, source_target_pairs={{0,4},{1,5},{2,6},{3,7},{4,12},{5,13},{6,14},{7,15},{12,8},{13,9},... | collective-permute-start | bytes 884744 | tf_op jit(solution)/shard_map/ppermute | solution.py:274
  7.0 17.3 %collective-permute-start.1 = (bf16[128,1152]{1,0:T(8,128)(2,1)S(1)}, bf16[128,1152]{1,0:T(8,128)(2,1)S(1)}, u32[]{:S(2)}, u32[]{:S(2)}) collective-permute-start(bf16[128,1152]{1,0:T(8,128)(2,1)S(1)} %pack.1.refs_0_.slots_ref), channel_id=1, source_target_pairs={{0,2},{1,3},{2,0},{3,1},{4,6},{5,7},{6,4},{7,5},{8,10},{9,11},{10,... | collective-permute-start | bytes 884744 | tf_op jit(solution)/shard_map/ppermute | solution.py:280
  8.5 16.5 %collective-permute-start.9 = (bf16[352,512]{1,0:T(8,128)(2,1)S(1)}, bf16[352,512]{1,0:T(8,128)(2,1)S(1)}, u32[]{:S(2)}, u32[]{:S(2)}) collective-permute-start(bf16[352,512]{1,0:T(8,128)(2,1)S(1)} %get-tuple-element.67), channel_id=1, source_target_pairs={{0,16},{16,0},{1,17},{17,1},{2,18},{18,2},{3,19},{19,3},{4,20},{20... | collective-permute-start | bytes 1081352 | tf_op jit(solution)/shard_map/ppermute | solution.py:286
  9.1 15.8 %collective-permute-start = (bf16[128,1152]{1,0:T(8,128)(2,1)S(1)}, bf16[128,1152]{1,0:T(8,128)(2,1)S(1)}, u32[]{:S(2)}, u32[]{:S(2)}) collective-permute-start(bf16[128,1152]{1,0:T(8,128)(2,1)S(1)} %pack.1.refs_0_.slots_ref), channel_id=1, source_target_pairs={{0,8},{1,9},{2,10},{3,11},{4,0},{5,1},{6,2},{7,3},{12,4},{13,5},{1... | collective-permute-start | bytes 884744 | tf_op jit(solution)/shard_map/ppermute | solution.py:277
  15.2 9.8 %collective-permute-start.8 = (bf16[128,1152]{1,0:T(8,128)(2,1)S(1)}, bf16[128,1152]{1,0:T(8,128)(2,1)S(1)}, u32[]{:S(2)}, u32[]{:S(2)}) collective-permute-start(bf16[128,1152]{1,0:T(8,128)(2,1)S(1)} %collective-permute-done.5.refs_2_), channel_id=1, source_target_pairs={{0,2},{1,3},{2,0},{3,1},{4,6},{5,7},{6,4},{7,5},{8,10},{9,11},{10,... | collective-permute-start | bytes 884744 | tf_op jit(solution)/shard_map/ppermute | solution.py:280
  16.8 11.8 %collective-permute-start.7 = (bf16[128,1152]{1,0:T(8,128)(2,1)S(1)}, bf16[128,1152]{1,0:T(8,128)(2,1)S(1)}, u32[]{:S(2)}, u32[]{:S(2)}) collective-permute-start(bf16[128,1152]{1,0:T(8,128)(2,1)S(1)} %collective-permute-done.5.refs_2_), channel_id=1, source_target_pairs={{0,4},{1,5},{2,6},{3,7},{4,12},{5,13},{6,14},{7,15},{12,8},{13,9},... | collective-permute-start | bytes 884744 | tf_op jit(solution)/shard_map/ppermute | solution.py:274
  24.4 10.2 %collective-permute-start.16 = (bf16[352,512]{1,0:T(8,128)(2,1)S(1)}, bf16[352,512]{1,0:T(8,128)(2,1)S(1)}, u32[]{:S(2)}, u32[]{:S(2)}) collective-permute-start(bf16[352,512]{1,0:T(8,128)(2,1)S(1)} %get-tuple-element.65), channel_id=1, source_target_pairs={{0,16},{16,0},{1,17},{17,1},{2,18},{18,2},{3,19},{19,3},{4,20},{20... | collective-permute-start | bytes 1081352 | tf_op jit(solution)/shard_map/ppermute | solution.py:286
  24.9 14.0 %collective-permute-start.2 = (bf16[128,1152]{1,0:T(8,128)(2,1)S(1)}, bf16[128,1152]{1,0:T(8,128)(2,1)S(1)}, u32[]{:S(2)}, u32[]{:S(2)}) collective-permute-start(bf16[128,1152]{1,0:T(8,128)(2,1)S(1)} %collective-permute-done.after_ref.refs_6_), channel_id=1, source_target_pairs={{0,2},{1,3},{2,0},{3,1},{4,6},{5,7},{6,4},{7,5},{8,10},{9,11},{10,... | collective-permute-start | bytes 884744 | tf_op jit(solution)/shard_map/ppermute | solution.py:280
  28.6 10.3 %collective-permute-start.10 = (bf16[128,1152]{1,0:T(8,128)(2,1)S(1)}, bf16[128,1152]{1,0:T(8,128)(2,1)S(1)}, u32[]{:S(2)}, u32[]{:S(2)}) collective-permute-start(bf16[128,1152]{1,0:T(8,128)(2,1)S(1)} %collective-permute-done.7.refs_4_), channel_id=1, source_target_pairs={{0,2},{1,3},{2,0},{3,1},{4,6},{5,7},{6,4},{7,5},{8,10},{9,11},{10,... | collective-permute-start | bytes 884744 | tf_op jit(solution)/shard_map/ppermute | solution.py:280
  30.1 8.8 %collective-permute-start.4 = (bf16[128,1024]{1,0:T(8,128)(2,1)S(1)}, bf16[128,1024]{1,0:T(8,128)(2,1)S(1)}, u32[]{:S(2)}, u32[]{:S(2)}) collective-permute-start(bf16[128,1024]{1,0:T(8,128)(2,1)S(1)} %later_pack.1.refs_0_), channel_id=1, source_target_pairs={{0,4},{1,5},{2,6},{3,7},{4,12},{5,13},{6,14},{7,15},{12,8},{13,9},... | collective-permute-start | bytes 786440 | tf_op jit(solution)/shard_map/ppermute | solution.py:274
  40.5 6.2 %collective-permute-start.18 = (bf16[528,1024]{1,0:T(8,128)(2,1)S(1)}, bf16[528,1024]{1,0:T(8,128)(2,1)S(1)}, u32[]{:S(2)}, u32[]{:S(2)}) collective-permute-start(bf16[528,1024]{1,0:T(8,128)(2,1)S(1)} %get-tuple-element.45), channel_id=1, source_target_pairs={{0,1},{1,0},{2,3},{3,2},{4,5},{5,4},{6,7},{7,6},{8,9},{9,8},{10,11... | collective-permute-start | bytes 3244040 | tf_op jit(solution)/shard_map/ppermute | solution.py:283
  40.6 13.7 %collective-permute-start.11 = (bf16[352,512]{1,0:T(8,128)(2,1)S(1)}, bf16[352,512]{1,0:T(8,128)(2,1)S(1)}, u32[]{:S(2)}, u32[]{:S(2)}) collective-permute-start(bf16[352,512]{1,0:T(8,128)(2,1)S(1)} %get-tuple-element.66), channel_id=1, source_target_pairs={{0,16},{16,0},{1,17},{17,1},{2,18},{18,2},{3,19},{19,3},{4,20},{20... | collective-permute-start | bytes 1081352 | tf_op jit(solution)/shard_map/ppermute | solution.py:286
  41.4 10.0 %collective-permute-start.13 = (bf16[128,1024]{1,0:T(8,128)(2,1)S(1)}, bf16[128,1024]{1,0:T(8,128)(2,1)S(1)}, u32[]{:S(2)}, u32[]{:S(2)}) collective-permute-start(bf16[128,1024]{1,0:T(8,128)(2,1)S(1)} %collective-permute-done.4.refs_2_), channel_id=1, source_target_pairs={{0,4},{1,5},{2,6},{3,7},{4,12},{5,13},{6,14},{7,15},{12,8},{13,9},... | collective-permute-start | bytes 786440 | tf_op jit(solution)/shard_map/ppermute | solution.py:274
  44.2 8.4 %collective-permute-start.3 = (bf16[128,1024]{1,0:T(8,128)(2,1)S(1)}, bf16[128,1024]{1,0:T(8,128)(2,1)S(1)}, u32[]{:S(2)}, u32[]{:S(2)}) collective-permute-start(bf16[128,1024]{1,0:T(8,128)(2,1)S(1)} %later_pack.1.refs_0_), channel_id=1, source_target_pairs={{0,2},{1,3},{2,0},{3,1},{4,6},{5,7},{6,4},{7,5},{8,10},{9,11},{10,... | collective-permute-start | bytes 786440 | tf_op jit(solution)/shard_map/ppermute | solution.py:280
  46.2 10.7 %collective-permute-start.15 = (bf16[128,1024]{1,0:T(8,128)(2,1)S(1)}, bf16[128,1024]{1,0:T(8,128)(2,1)S(1)}, u32[]{:S(2)}, u32[]{:S(2)}) collective-permute-start(bf16[128,1024]{1,0:T(8,128)(2,1)S(1)} %later_pack.1.refs_0_), channel_id=1, source_target_pairs={{0,8},{1,9},{2,10},{3,11},{4,0},{5,1},{6,2},{7,3},{12,4},{13,5},{1... | collective-permute-start | bytes 786440 | tf_op jit(solution)/shard_map/ppermute | solution.py:277
  49.6 12.2 %collective-permute-start.19 = (bf16[352,512]{1,0:T(8,128)(2,1)S(1)}, bf16[352,512]{1,0:T(8,128)(2,1)S(1)}, u32[]{:S(2)}, u32[]{:S(2)}) collective-permute-start(bf16[352,512]{1,0:T(8,128)(2,1)S(1)} %get-tuple-element.48), channel_id=1, source_target_pairs={{0,16},{16,0},{1,17},{17,1},{2,18},{18,2},{3,19},{19,3},{4,20},{20... | collective-permute-start | bytes 1081352 | tf_op jit(solution)/shard_map/ppermute | solution.py:286
  52.5 9.3 %collective-permute-start.14 = (bf16[128,1024]{1,0:T(8,128)(2,1)S(1)}, bf16[128,1024]{1,0:T(8,128)(2,1)S(1)}, u32[]{:S(2)}, u32[]{:S(2)}) collective-permute-start(bf16[128,1024]{1,0:T(8,128)(2,1)S(1)} %collective-permute-done.13.refs_4_), channel_id=1, source_target_pairs={{0,2},{1,3},{2,0},{3,1},{4,6},{5,7},{6,4},{7,5},{8,10},{9,11},{10,... | collective-permute-start | bytes 786440 | tf_op jit(solution)/shard_map/ppermute | solution.py:280
  54.3 11.4 %collective-permute-start.12 = (bf16[128,1024]{1,0:T(8,128)(2,1)S(1)}, bf16[128,1024]{1,0:T(8,128)(2,1)S(1)}, u32[]{:S(2)}, u32[]{:S(2)}) collective-permute-start(bf16[128,1024]{1,0:T(8,128)(2,1)S(1)} %collective-permute-done.4.refs_2_), channel_id=1, source_target_pairs={{0,2},{1,3},{2,0},{3,1},{4,6},{5,7},{6,4},{7,5},{8,10},{9,11},{10,... | collective-permute-start | bytes 786440 | tf_op jit(solution)/shard_map/ppermute | solution.py:280
  56.9 9.9 %collective-permute-start.17 = (bf16[128,1024]{1,0:T(8,128)(2,1)S(1)}, bf16[128,1024]{1,0:T(8,128)(2,1)S(1)}, u32[]{:S(2)}, u32[]{:S(2)}) collective-permute-start(bf16[128,1024]{1,0:T(8,128)(2,1)S(1)} %collective-permute-done.3.refs_1_), channel_id=1, source_target_pairs={{0,8},{1,9},{2,10},{3,11},{4,0},{5,1},{6,2},{7,3},{12,4},{13,5},{1... | collective-permute-start | bytes 786440 | tf_op jit(solution)/shard_map/ppermute | solution.py:277
  68.0 23.8 %collective-permute-start.23 = (bf16[352,512]{1,0:T(8,128)(2,1)S(1)}, bf16[352,512]{1,0:T(8,128)(2,1)S(1)}, u32[]{:S(2)}, u32[]{:S(2)}) collective-permute-start(bf16[352,512]{1,0:T(8,128)(2,1)S(1)} %get-tuple-element.58), channel_id=1, source_target_pairs={{0,16},{16,0},{1,17},{17,1},{2,18},{18,2},{3,19},{19,3},{4,20},{20... | collective-permute-start | bytes 1081352 | tf_op jit(solution)/shard_map/ppermute | solution.py:286
  73.9 25.8 %collective-permute-start.22 = (bf16[352,512]{1,0:T(8,128)(2,1)}, bf16[352,512]{1,0:T(8,128)(2,1)S(1)}, u32[]{:S(2)}, u32[]{:S(2)}) collective-permute-start(bf16[352,512]{1,0:T(8,128)(2,1)} %get-tuple-element.56), channel_id=1, source_target_pairs={{0,16},{16,0},{1,17},{17,1},{2,18},{18,2},{3,19},{19,3},{4,20},{20... | collective-permute-start | bytes 1081352 | tf_op jit(solution)/shard_map/ppermute | solution.py:286
  75.4 25.0 %collective-permute-start.21 = (bf16[352,512]{1,0:T(8,128)(2,1)}, bf16[352,512]{1,0:T(8,128)(2,1)S(1)}, u32[]{:S(2)}, u32[]{:S(2)}) collective-permute-start(bf16[352,512]{1,0:T(8,128)(2,1)} %get-tuple-element.54), channel_id=1, source_target_pairs={{0,16},{16,0},{1,17},{17,1},{2,18},{18,2},{3,19},{19,3},{4,20},{20... | collective-permute-start | bytes 1081352 | tf_op jit(solution)/shard_map/ppermute | solution.py:286
  79.8 17.6 %all-to-all-start = ((f32[16,1,64]{2,1,0:T(1,128)}), f32[16,1,64]{2,1,0:T(1,128)S(1)}, u32[]{:S(2)}, u32[]{:S(2)}) async-start(f32[16,1,64]{2,1,0:T(1,128)} %bitcast.10), calls=%async_computation | async-start | bytes 16384 | tf_op jit(solution)/shard_map/all_to_all | solution.py:441
  (8 other events, 81.1 us)

commit v6 on v5

--- a/solution.py
+++ b/solution.py
@@ -10,7 +10,6 @@
 NZ, NY, NC = 4, 2, 2
 CHUNKS = 2
 PIECES = 2
-PART = 512
 LANES = 128
 NT = (((1,), (1,)), ((), ()))
 VMEM = pl.BlockSpec(memory_space=pltpu.VMEM)
@@ -191,22 +190,19 @@
     products(half, capacity, mine_ref, got_ref, hs_ref, *outs[2:])
 
 
-def raw_halves(half, rows_ref, own_ref, got_refs):
+def raw_parts(half, rows_ref, own_ref, got_refs):
     mine = lax.axis_index("dp")
-
-    def times(w_ref, rows):
-        return lax.dot_general(w_ref[...], rows, NT, preferred_element_type=jnp.float32)
-
-    yield pl.ds(pl.multiple_of(mine * half, 16), half), times(own_ref, rows_ref[...])
-    part = got_refs[0].shape[1]
-    yield (
-        pl.ds(pl.multiple_of((1 - mine) * half, 16), half),
-        sum(times(ref, rows_ref[:, q * part : (q + 1) * part]) for q, ref in enumerate(got_refs)),
-    )
+    at = mine * half
+    for w_ref in (own_ref, *got_refs):
+        units = pl.ds(pl.multiple_of(at, 16), w_ref.shape[0])
+        yield units, lax.dot_general(
+            w_ref[...], rows_ref[...], NT, preferred_element_type=jnp.float32
+        )
+        at = at + w_ref.shape[0] if w_ref is not own_ref else (1 - mine) * half
 
 
 def raw_part_kernel(half, rows_ref, own_ref, *refs):
-    for units, raw in raw_halves(half, rows_ref, own_ref, refs[:-1]):
+    for units, raw in raw_parts(half, rows_ref, own_ref, refs[:-1]):
         refs[-1][units, :] = raw
 
 
@@ -215,7 +211,7 @@
     step = pl.program_id(0)
     gates = gates_ref[...]
     total = jnp.zeros(gates.shape, jnp.float32)
-    for units, raw in raw_halves(half, rows_ref, own_ref, refs[:-5]):
+    for units, raw in raw_parts(half, rows_ref, own_ref, refs[:-5]):
         raw += sum_ref[units, :]
         grad_ref[units, :] = (raw * gates).astype(jnp.bfloat16)
         total += jnp.sum(
@@ -267,7 +263,11 @@
     routes_t, gates_t = routes.T, gates.T
     weight = down_weight[0]
     columns = [pl.BlockSpec((half, width), lambda i, c=c: (0, c)) for c in range(CHUNKS)]
-    parts = [pl.BlockSpec((half, PART), lambda i: (0, 0))] * (width // PART)
+    split = half * 6 // 11 // 32 * 32
+    parts = [
+        [pl.BlockSpec((n, width), lambda i, c=c: (0, c)) for n in (split, half - split)]
+        for c in range(CHUNKS)
+    ]
     dma = pltpu.SemaphoreType.DMA
 
     def forward(x):
@@ -374,7 +374,7 @@
             functools.partial(raw_part_kernel, half),
             grid=(slots // tile,),
             out_shape=shape((units, slots), f32),
-            in_specs=[pl.BlockSpec((tile, width), lambda i: (i, 0)), columns[0]] + parts,
+            in_specs=[pl.BlockSpec((tile, width), lambda i: (i, 0)), columns[0]] + parts[0],
             out_specs=pl.BlockSpec((units, tile), lambda i: (0, i)),
             compiler_params=params(24),
             cost_estimate=cost(3),
@@ -390,7 +390,7 @@
             in_specs=[
                 pl.BlockSpec((tile, width), lambda i: (i, 0)),
                 columns[1],
-                *parts,
+                *parts[1],
                 by_slot,
                 by_slot,
                 pl.BlockSpec((1, tile), lambda i: (0, i)),
@@ -413,31 +413,30 @@
             name="finish",
         )(own, got, *before)
 
-    w = [swap(weight[:, k : k + PART]) for k in range(0, model, PART)]
     x0 = pack()
+    w = [swap(weight[:split]), swap(weight[split:])]
+    x1 = later_pack(1, x0)
     f0, r0, y0 = forward(x0), backward(x0), across(x0)
-    ff0, yf0 = forward(behind(f0, w[0])), across(behind(f0, w[0]))
-    x1 = later_pack(1, r0)
-    f1, yr0 = forward(x1), across(behind(r0, y0))
-    r1, yff0 = backward(behind(x1, ff0)), across(behind(ff0, yf0, w[1]))
-    mine0, theirs0, pmat, gslot = first_pick(
-        [x0, y0, f0, yf0, ff0, yff0, r0, behind(yr0, f1, w[2])]
-    )
-    ff1, y1 = forward(f1), across(behind(x1, yr0))
-    yf1 = across(behind(f1, yff0, w[3]))
-    ry1 = backward(behind(y1, r1, mine0, w[3]))
-    got = sibling(theirs0)
+    ff0, yf0 = forward(f0), across(f0)
+    y1 = across(behind(x1, y0))
+    f1, yr0 = forward(behind(x1, r0)), across(behind(r0, y1))
+    yff0 = across(behind(ff0, yf0, w[0]))
+    ry1 = backward(behind(y1, ff0))
+    mine0, theirs0, pmat, gslot = first_pick([x0, y0, f0, yf0, ff0, yff0, r0, behind(yr0, w[1])])
+    got = sibling(behind(theirs0, f1))
+    ff1, yf1 = forward(f1), across(behind(f1, yff0))
+    r1 = backward(behind(x1, ry1))
     rows0, send0, own0, slot_gates, hs = first_products(mine0, got, gslot)
     got0 = [swap(part) for part in send0]
-    yff1 = across(behind(ff1, y1))
-    raw = raw_part(rows0, w[: len(parts)])
+    yff1 = across(behind(ff1, yf1))
+    raw = raw_part(rows0, w)
     mine1, theirs1 = later_pick(
         [x1, y1, f1, yf1, ff1, yff1, r1, ry1], behind(pmat, raw, got0[0])
     )
     rows1, send1, own1 = later_products(mine1, sibling(theirs1), hs)
     got1 = [swap(part) for part in send1]
 
-    grad_hidden, back = raw_rest(rows1, w[len(parts) :], raw, slot_gates)
+    grad_hidden, back = raw_rest(rows1, w, raw, slot_gates)
     returned = lax.all_to_all(back, "expert", split_axis=0, concat_axis=0, tiled=True)
     grad_gates = pl.pallas_call(
         gates_kernel,

time: 101 us -> 105 us (1.040)
  waiting for transfers between devices: 27.2 us -> 31.2 us
  starting transfers between devices: 50.6 us -> 47.2 us
  local copies, waits for them, and re-layouts: 2.12 us -> 4.37 us
    ppermute x4, waiting for transfers between devices: 12.8 us -> 1.84 us  [forward(): return lax.ppermute(x, 'expert', ring_pairs(1))]
    ppermute x3, waiting for transfers between devices: 3.33 us -> 10.4 us  [backward(): return lax.ppermute(x, 'expert', ring_pairs(-1))]
    ppermute x8 -> x6, waiting for transfers between devices: 0.02 us -> 4.19 us  [swap(): return lax.ppermute(x, 'dp', [(0, 1), (1, 0)])]
    ppermute x7, waiting for transfers between devices: 5.07 us -> 8.9 us  [across(): return lax.ppermute(x, 'expert', swap_pairs(2))]
    ppermute x8 -> x6, starting transfers between devices: 9.98 us -> 7.3 us  [swap(): return lax.ppermute(x, 'dp', [(0, 1), (1, 0)])]
    unnamed x14, local copies, waits for them, and re-layouts: 0.62 us -> 3.12 us
    ppermute x4, starting transfers between devices: 16.5 us -> 19 us  [forward(): return lax.ppermute(x, 'expert', ring_pairs(1))]
    ppermute x7, starting transfers between devices: 8.61 us -> 6.28 us  [across(): return lax.ppermute(x, 'expert', swap_pairs(2))]
  transfers between devices with their start and end apart: 25 -> 23, of which waited for: 10 -> 9; matrix products, arithmetic and copies ran while one was open for 0% -> 1% of each run, Pallas kernels for 17% -> 18%
where the time goes in v6:
time: 105 us
  starting transfers between devices  47.2 us (45%)
  waiting for transfers between devices  31.2 us (30%)
  Pallas kernels  21.2 us (20%)
  local copies, waits for them, and re-layouts  4.37 us (4%)
    ppermute x4, starting transfers between devices, forward(): return lax.ppermute(x, 'expert', ring_pairs(1))  19 us
    ppermute x3, waiting for transfers between devices, backward(): return lax.ppermute(x, 'expert', ring_pairs(-1))  10.4 us
    all_to_all x1, starting transfers between devices, ring_shards(): lax.all_to_all(back, 'expert', split_axis=0, concat_axis=0, tiled=True)  9.99 us
    ppermute x7, waiting for transfers between devices, across(): return lax.ppermute(x, 'expert', swap_pairs(2))  8.9 us
    ppermute x6, starting transfers between devices, swap(): return lax.ppermute(x, 'dp', [(0, 1), (1, 0)])  7.3 us
    ppermute x7, starting transfers between devices, across(): return lax.ppermute(x, 'expert', swap_pairs(2))  6.28 us
    all_to_all x1, waiting for transfers between devices, ring_shards(): lax.all_to_all(back, 'expert', split_axis=0, concat_axis=0, tiled=True)  4.81 us
    ppermute x3, starting transfers between devices, backward(): return lax.ppermute(x, 'expert', ring_pairs(-1))  4.52 us
  transfers between devices with their start and end apart: 23, of which 9 were waited for; matrix products, arithmetic and copies ran while one was open for 1% of the time, Pallas kernels for 18%

profile of v6, /device:TPU:0, one launch (start us, length us, event | category | flops | bytes accessed | tf_op | source)
XLA Modules:
  0.0 104.8 jit_solution(6688368373390658184)
XLA Ops:
  3.4 3.1 %collective-permute-start.4 = (bf16[128,1152]{1,0:T(8,128)(2,1)S(1)}, bf16[128,1152]{1,0:T(8,128)(2,1)S(1)}, u32[]{:S(2)}, u32[]{:S(2)}) collective-permute-start(bf16[128,1152]{1,0:T(8,128)(2,1)S(1)} %pack.1.after_ref.refs_0_.slots_ref), channel_id=1, source_target_pairs={{0,4},{1,5},{2,6},{3,7},{4,12},{5,13},{6,14},{7,15},{12,8},{13,9},... | collective-permute-start | bytes 884744 | tf_op jit(solution)/shard_map/ppermute | solution.py:274
  7.5 1.8 %collective-permute-start = (bf16[128,1152]{1,0:T(8,128)(2,1)S(1)}, bf16[128,1152]{1,0:T(8,128)(2,1)S(1)}, u32[]{:S(2)}, u32[]{:S(2)}) collective-permute-start(bf16[128,1152]{1,0:T(8,128)(2,1)S(1)} %pack.1.after_ref.refs_0_.slots_ref), channel_id=1, source_target_pairs={{0,2},{1,3},{2,0},{3,1},{4,6},{5,7},{6,4},{7,5},{8,10},{9,11},{10,... | collective-permute-start | bytes 884744 | tf_op jit(solution)/shard_map/ppermute | solution.py:280
  10.5 1.6 %collective-permute-start.7 = (bf16[192,2048]{1,0:T(8,128)(2,1)S(1)}, bf16[192,2048]{1,0:T(8,128)(2,1)S(1)}, u32[]{:S(2)}, u32[]{:S(2)}) collective-permute-start(bf16[192,2048]{1,0:T(8,128)(2,1)S(1)} %slice_bitcast_fusion), channel_id=1, source_target_pairs={{0,16},{16,0},{1,17},{17,1},{2,18},{18,2},{3,19},{19,3},{4,20},{20... | collective-permute-start | bytes 2359304 | tf_op jit(solution)/shard_map/ppermute | solution.py:286
  12.7 1.8 %collective-permute-done.4.refs_2_ = bf16[128,1152]{1,0:T(8,128)(2,1)S(1)} collective-permute-done((bf16[128,1152]{1,0:T(8,128)(2,1)S(1)}, bf16[128,1152]{1,0:T(8,128)(2,1)S(1)}, u32[]{:S(2)}, u32[]{:S(2)}) %collective-permute-start.4) | collective-permute-done | bytes 294944 | tf_op jit(solution)/shard_map/ppermute | solution.py:274
  14.6 1.6 %collective-permute-start.6 = (bf16[128,1152]{1,0:T(8,128)(2,1)S(1)}, bf16[128,1152]{1,0:T(8,128)(2,1)S(1)}, u32[]{:S(2)}, u32[]{:S(2)}) collective-permute-start(bf16[128,1152]{1,0:T(8,128)(2,1)S(1)} %collective-permute-done.4.refs_2_), channel_id=1, source_target_pairs={{0,2},{1,3},{2,0},{3,1},{4,6},{5,7},{6,4},{7,5},{8,10},{9,11},{10,... | collective-permute-start | bytes 884744 | tf_op jit(solution)/shard_map/ppermute | solution.py:280
  16.2 8.0 %collective-permute-start.5 = (bf16[128,1152]{1,0:T(8,128)(2,1)S(1)}, bf16[128,1152]{1,0:T(8,128)(2,1)S(1)}, u32[]{:S(2)}, u32[]{:S(2)}) collective-permute-start(bf16[128,1152]{1,0:T(8,128)(2,1)S(1)} %collective-permute-done.4.refs_2_), channel_id=1, source_target_pairs={{0,4},{1,5},{2,6},{3,7},{4,12},{5,13},{6,14},{7,15},{12,8},{13,9},... | collective-permute-start | bytes 884744 | tf_op jit(solution)/shard_map/ppermute | solution.py:274
  24.3 8.0 %collective-permute-done.1.refs_1_ = bf16[128,1024]{1,0:T(8,128)(2,1)S(1)} collective-permute-done((bf16[128,1024]{1,0:T(8,128)(2,1)S(1)}, bf16[128,1024]{1,0:T(8,128)(2,1)S(1)}, u32[]{:S(2)}, u32[]{:S(2)}) %collective-permute-start.1) | collective-permute-done | bytes 262176 | tf_op jit(solution)/shard_map/ppermute | solution.py:280
  32.4 2.1 %collective-permute-start.8 = (bf16[128,1152]{1,0:T(8,128)(2,1)S(1)}, bf16[128,1152]{1,0:T(8,128)(2,1)S(1)}, u32[]{:S(2)}, u32[]{:S(2)}) collective-permute-start(bf16[128,1152]{1,0:T(8,128)(2,1)S(1)} %collective-permute-done.5.refs_4_), channel_id=1, source_target_pairs={{0,2},{1,3},{2,0},{3,1},{4,6},{5,7},{6,4},{7,5},{8,10},{9,11},{10,... | collective-permute-start | bytes 884744 | tf_op jit(solution)/shard_map/ppermute | solution.py:280
  34.5 4.5 %collective-permute-start.3 = (bf16[128,1024]{1,0:T(8,128)(2,1)S(1)}, bf16[128,1024]{1,0:T(8,128)(2,1)S(1)}, u32[]{:S(2)}, u32[]{:S(2)}) collective-permute-start(bf16[128,1024]{1,0:T(8,128)(2,1)S(1)} %later_pack.1.refs_0_), channel_id=1, source_target_pairs={{0,4},{1,5},{2,6},{3,7},{4,12},{5,13},{6,14},{7,15},{12,8},{13,9},... | collective-permute-start | bytes 786440 | tf_op jit(solution)/shard_map/ppermute | solution.py:274
  38.9 4.2 %collective-permute-done.15.refs_1_ = bf16[160,2048]{1,0:T(8,128)(2,1)S(1)} collective-permute-done((bf16[160,2048]{1,0:T(8,128)(2,1)S(1)}, bf16[160,2048]{1,0:T(8,128)(2,1)S(1)}, u32[]{:S(2)}, u32[]{:S(2)}) %collective-permute-start.15) | collective-permute-done | bytes 655392 | tf_op jit(solution)/shard_map/ppermute | solution.py:286
  43.3 1.6 %first_pick.1 = (bf16[512,1024]{1,0:T(8,128)(2,1)S(1)}, bf16[528,1024]{1,0:T(8,128)(2,1)S(1)}, bf16[1024,128]{1,0:T(8,128)(2,1)S(1)}, f32[8,128]{1,0:T(8,128)S(1)}) custom-call(bf16[128,1152]{1,0:T(8,128)(2,1)S(1)} %pack.1.after_ref.refs_0_.slots_ref, bf16[128,1152]{1,0:T(8,128)(2,1)S(1)} %collective-permute-done.refs_1_, ...), custom_call_target="tpu_custom_call" | custom-call | flops 3000000000 | bytes 9437184 | tf_op jit(solution)/shard_map/first_pick/pallas_call | solution.py:320
  45.0 3.4 %collective-permute-start.10 = (bf16[128,1024]{1,0:T(8,128)(2,1)S(1)}, bf16[128,1024]{1,0:T(8,128)(2,1)S(1)}, u32[]{:S(2)}, u32[]{:S(2)}) collective-permute-start(bf16[128,1024]{1,0:T(8,128)(2,1)S(1)} %collective-permute-done.3.refs_2_), channel_id=1, source_target_pairs={{0,4},{1,5},{2,6},{3,7},{4,12},{5,13},{6,14},{7,15},{12,8},{13,9},... | collective-permute-start | bytes 786440 | tf_op jit(solution)/shard_map/ppermute | solution.py:274
  48.8 3.0 %first_products.1 = (f32[1,1024]{1,0:T(1,128)S(1)}, bf16[704,1024]{1,0:T(8,128)(2,1)S(1)}, bf16[1024,1024]{1,0:T(8,128)(2,1)S(1)}, bf16[352,512]{1,0:T(8,128)(2,...) custom-call(bf16[512,1024]{1,0:T(8,128)(2,1)S(1)} %get-tuple-element.45.mine_ref, ...), custom_call_target="tpu_custom_call" | custom-call | flops 3000000000 | bytes 9437184 | tf_op jit(solution)/shard_map/first_products/pallas_call | solution.py:350
  51.8 1.6 %collective-permute-start.17 = (bf16[352,512]{1,0:T(8,128)(2,1)S(1)}, bf16[352,512]{1,0:T(8,128)(2,1)S(1)}, u32[]{:S(2)}, u32[]{:S(2)}) collective-permute-start(bf16[352,512]{1,0:T(8,128)(2,1)S(1)} %get-tuple-element.50), channel_id=1, source_target_pairs={{0,16},{16,0},{1,17},{17,1},{2,18},{18,2},{3,19},{19,3},{4,20},{20... | collective-permute-start | bytes 1081352 | tf_op jit(solution)/shard_map/ppermute | solution.py:286
  53.4 6.9 %collective-permute-done.12.refs_7_ = bf16[128,1024]{1,0:T(8,128)(2,1)S(1)} collective-permute-done((bf16[128,1024]{1,0:T(8,128)(2,1)S(1)}, bf16[128,1024]{1,0:T(8,128)(2,1)S(1)}, u32[]{:S(2)}, u32[]{:S(2)}) %collective-permute-start.12) | collective-permute-done | bytes 262176 | tf_op jit(solution)/shard_map/ppermute | solution.py:277
  60.3 3.4 %collective-permute-start.13 = (bf16[128,1024]{1,0:T(8,128)(2,1)S(1)}, bf16[128,1024]{1,0:T(8,128)(2,1)S(1)}, u32[]{:S(2)}, u32[]{:S(2)}) collective-permute-start(bf16[128,1024]{1,0:T(8,128)(2,1)S(1)} %later_pack.1.refs_0_), channel_id=1, source_target_pairs={{0,8},{1,9},{2,10},{3,11},{4,0},{5,1},{6,2},{7,3},{12,4},{13,5},{1... | collective-permute-start | bytes 786440 | tf_op jit(solution)/shard_map/ppermute | solution.py:277
  64.1 3.1 %raw_part.1.refs_2_ = f32[704,1024]{1,0:T(8,128)S(1)} custom-call(bf16[1024,1024]{1,0:T(8,128)(2,1)S(1)} %get-tuple-element.49.rows_ref, bf16[352,2048]{1,0:T(8,128)(2,1)S(1)} %bitcast.19, bf16[192,2048]{1,0:T(8,128)(2,1)S(1)} %collective-permute-done.7.refs_0_, bf16[160,2048]{1,0:T(8,128)(2,1)S(1)} %collective-permute-done.15.refs_1_), custom_call_target="tpu_custom_call" | custom-call | flops 3000000000 | bytes 9437184 | tf_op jit(solution)/shard_map/raw_part/pallas_call | solution.py:373
  67.2 3.4 %collective-permute-done.13.refs_6_ = bf16[128,1024]{1,0:T(8,128)(2,1)S(1)} collective-permute-done((bf16[128,1024]{1,0:T(8,128)(2,1)S(1)}, bf16[128,1024]{1,0:T(8,128)(2,1)S(1)}, u32[]{:S(2)}, u32[]{:S(2)}) %collective-permute-start.13) | collective-permute-done | bytes 262176 | tf_op jit(solution)/shard_map/ppermute | solution.py:277
  72.5 1.6 %collective-permute-start.21 = (bf16[352,512]{1,0:T(8,128)(2,1)S(1)}, bf16[352,512]{1,0:T(8,128)(2,1)S(1)}, u32[]{:S(2)}, u32[]{:S(2)}) collective-permute-start(bf16[352,512]{1,0:T(8,128)(2,1)S(1)} %get-tuple-element.60), channel_id=1, source_target_pairs={{0,16},{16,0},{1,17},{17,1},{2,18},{18,2},{3,19},{19,3},{4,20},{20... | collective-permute-start | bytes 1081352 | tf_op jit(solution)/shard_map/ppermute | solution.py:286
  75.2 3.2 %products.1 = (bf16[1024,1024]{1,0:T(8,128)(2,1)S(1)}, bf16[352,512]{1,0:T(8,128)(2,1)}, bf16[352,512]{1,0:T(8,128)(2,1)}, bf16[352,512]{1,0:T(8,128)(2,1)S(1)}, bf16[352,512]{1,0:T(8,128)(2,1)S(1)}) custom-call(bf16[512,1024]{1,0:T(8,128)(2,1)S(1)} %get-tuple-element.52.mine_ref, bf16[512,1024]{1,0:T(8,128)(2,1)S(1)} %collective-permute-done.18.got_ref, ...), custom_call_target="tpu_custom_call" | custom-call | tf_op jit(solution)/shard_map/products/pallas_call | solution.py:362
  80.4 4.2 %raw.1 = (bf16[704,1024]{1,0:T(8,128)(2,1)}, f32[16,64]{1,0:T(8,128)}) custom-call(bf16[1024,1024]{1,0:T(8,128)(2,1)S(1)} %get-tuple-element.62.rows_ref, bf16[352,2048]{1,0:T(8,128)(2,1)S(1)} %bitcast.20, bf16[192,2048]{1,0:T(8,128)(2,1)S(1)} %collective-permute-done.7.refs_0_, bf16[160,2048]{1,0:T(8,128)(2,1)S(1)} %collective-permute-done.15.refs_1_, ...), custom_call_target="tpu_custom_call" | custom-call | tf_op jit(solution)/shard_map/raw/pallas_call | solution.py:386
  84.6 10.0 %all-to-all-start = ((f32[16,1,64]{2,1,0:T(1,128)}), f32[16,1,64]{2,1,0:T(1,128)S(1)}, u32[]{:S(2)}, u32[]{:S(2)}) async-start(f32[16,1,64]{2,1,0:T(1,128)} %bitcast.12), calls=%async_computation | async-start | bytes 16384 | tf_op jit(solution)/shard_map/all_to_all | solution.py:440
  96.2 4.8 %all-to-all-done = f32[16,1,64]{2,1,0:T(1,128)S(1)} async-done(((f32[16,1,64]{2,1,0:T(1,128)}), f32[16,1,64]{2,1,0:T(1,128)S(1)}, u32[]{:S(2)}, u32[]{:S(2)}) %all-to-all-start) | async-done | bytes 4128 | tf_op jit(solution)/shard_map/all_to_all | solution.py:440
  101.6 1.6 %grad_gates.1 = f32[6,128]{1,0:T(8,128)} custom-call(s32[6,128]{1,0:T(8,128)} %bitcast.23, bf16[128,1152]{1,0:T(8,128)(2,1)} %copy-done.1, f32[16,64]{1,0:T(8,128)} %bitcast.27), custom_call_target="tpu_custom_call" | custom-call | tf_op jit(solution)/shard_map/grad_gates/pallas_call | solution.py:441
  (51 shorter events, 15.6 us)
Async XLA Ops:
  3.4 40.0 %copy-start.1 = (bf16[128,1152]{1,0:T(8,128)(2,1)}, bf16[128,1152]{1,0:T(8,128)(2,1)S(1)}, u32[]{:S(2)}) copy-start(bf16[128,1152]{1,0:T(8,128)(2,1)S(1)} %pack.1.after_ref.refs_0_.slots_ref) | copy-start | bytes 884740
  3.4 11.2 %collective-permute-start.4 = (bf16[128,1152]{1,0:T(8,128)(2,1)S(1)}, bf16[128,1152]{1,0:T(8,128)(2,1)S(1)}, u32[]{:S(2)}, u32[]{:S(2)}) collective-permute-start(bf16[128,1152]{1,0:T(8,128)(2,1)S(1)} %pack.1.after_ref.refs_0_.slots_ref), channel_id=1, source_target_pairs={{0,4},{1,5},{2,6},{3,7},{4,12},{5,13},{6,14},{7,15},{12,8},{13,9},... | collective-permute-start | bytes 884744 | tf_op jit(solution)/shard_map/ppermute | solution.py:274
  6.4 17.8 %collective-permute-start.2 = (bf16[128,1152]{1,0:T(8,128)(2,1)S(1)}, bf16[128,1152]{1,0:T(8,128)(2,1)S(1)}, u32[]{:S(2)}, u32[]{:S(2)}) collective-permute-start(bf16[128,1152]{1,0:T(8,128)(2,1)S(1)} %pack.1.after_ref.refs_0_.slots_ref), channel_id=1, source_target_pairs={{0,8},{1,9},{2,10},{3,11},{4,0},{5,1},{6,2},{7,3},{12,4},{13,5},{1... | collective-permute-start | bytes 884744 | tf_op jit(solution)/shard_map/ppermute | solution.py:277
  7.5 8.6 %collective-permute-start = (bf16[128,1152]{1,0:T(8,128)(2,1)S(1)}, bf16[128,1152]{1,0:T(8,128)(2,1)S(1)}, u32[]{:S(2)}, u32[]{:S(2)}) collective-permute-start(bf16[128,1152]{1,0:T(8,128)(2,1)S(1)} %pack.1.after_ref.refs_0_.slots_ref), channel_id=1, source_target_pairs={{0,2},{1,3},{2,0},{3,1},{4,6},{5,7},{6,4},{7,5},{8,10},{9,11},{10,... | collective-permute-start | bytes 884744 | tf_op jit(solution)/shard_map/ppermute | solution.py:280
  10.5 21.8 %collective-permute-start.7 = (bf16[192,2048]{1,0:T(8,128)(2,1)S(1)}, bf16[192,2048]{1,0:T(8,128)(2,1)S(1)}, u32[]{:S(2)}, u32[]{:S(2)}) collective-permute-start(bf16[192,2048]{1,0:T(8,128)(2,1)S(1)} %slice_bitcast_fusion), channel_id=1, source_target_pairs={{0,16},{16,0},{1,17},{17,1},{2,18},{18,2},{3,19},{19,3},{4,20},{20... | collective-permute-start | bytes 2359304 | tf_op jit(solution)/shard_map/ppermute | solution.py:286
  12.1 30.9 %collective-permute-start.15 = (bf16[160,2048]{1,0:T(8,128)(2,1)S(1)}, bf16[160,2048]{1,0:T(8,128)(2,1)S(1)}, u32[]{:S(2)}, u32[]{:S(2)}) collective-permute-start(bf16[160,2048]{1,0:T(8,128)(2,1)S(1)} %slice_bitcast_fusion.1), channel_id=1, source_target_pairs={{0,16},{16,0},{1,17},{17,1},{2,18},{18,2},{3,19},{19,3},{4,20},{20... | collective-permute-start | bytes 1966088 | tf_op jit(solution)/shard_map/ppermute | solution.py:286
  14.6 17.8 %collective-permute-start.6 = (bf16[128,1152]{1,0:T(8,128)(2,1)S(1)}, bf16[128,1152]{1,0:T(8,128)(2,1)S(1)}, u32[]{:S(2)}, u32[]{:S(2)}) collective-permute-start(bf16[128,1152]{1,0:T(8,128)(2,1)S(1)} %collective-permute-done.4.refs_2_), channel_id=1, source_target_pairs={{0,2},{1,3},{2,0},{3,1},{4,6},{5,7},{6,4},{7,5},{8,10},{9,11},{10,... | collective-permute-start | bytes 884744 | tf_op jit(solution)/shard_map/ppermute | solution.py:280
  16.2 16.2 %collective-permute-start.5 = (bf16[128,1152]{1,0:T(8,128)(2,1)S(1)}, bf16[128,1152]{1,0:T(8,128)(2,1)S(1)}, u32[]{:S(2)}, u32[]{:S(2)}) collective-permute-start(bf16[128,1152]{1,0:T(8,128)(2,1)S(1)} %collective-permute-done.4.refs_2_), channel_id=1, source_target_pairs={{0,4},{1,5},{2,6},{3,7},{4,12},{5,13},{6,14},{7,15},{12,8},{13,9},... | collective-permute-start | bytes 884744 | tf_op jit(solution)/shard_map/ppermute | solution.py:274
  24.3 8.1 %collective-permute-start.1 = (bf16[128,1024]{1,0:T(8,128)(2,1)S(1)}, bf16[128,1024]{1,0:T(8,128)(2,1)S(1)}, u32[]{:S(2)}, u32[]{:S(2)}) collective-permute-start(bf16[128,1024]{1,0:T(8,128)(2,1)S(1)} %later_pack.1.refs_0_), channel_id=1, source_target_pairs={{0,2},{1,3},{2,0},{3,1},{4,6},{5,7},{6,4},{7,5},{8,10},{9,11},{10,... | collective-permute-start | bytes 786440 | tf_op jit(solution)/shard_map/ppermute | solution.py:280
  32.4 10.7 %collective-permute-start.14 = (bf16[128,1152]{1,0:T(8,128)(2,1)S(1)}, bf16[128,1152]{1,0:T(8,128)(2,1)S(1)}, u32[]{:S(2)}, u32[]{:S(2)}) collective-permute-start(bf16[128,1152]{1,0:T(8,128)(2,1)S(1)} %collective-permute-done.2.refs_6_), channel_id=1, source_target_pairs={{0,2},{1,3},{2,0},{3,1},{4,6},{5,7},{6,4},{7,5},{8,10},{9,11},{10,... | collective-permute-start | bytes 884744 | tf_op jit(solution)/shard_map/ppermute | solution.py:280
  32.4 11.0 %collective-permute-start.8 = (bf16[128,1152]{1,0:T(8,128)(2,1)S(1)}, bf16[128,1152]{1,0:T(8,128)(2,1)S(1)}, u32[]{:S(2)}, u32[]{:S(2)}) collective-permute-start(bf16[128,1152]{1,0:T(8,128)(2,1)S(1)} %collective-permute-done.5.refs_4_), channel_id=1, source_target_pairs={{0,2},{1,3},{2,0},{3,1},{4,6},{5,7},{6,4},{7,5},{8,10},{9,11},{10,... | collective-permute-start | bytes 884744 | tf_op jit(solution)/shard_map/ppermute | solution.py:280
  34.5 10.5 %collective-permute-start.3 = (bf16[128,1024]{1,0:T(8,128)(2,1)S(1)}, bf16[128,1024]{1,0:T(8,128)(2,1)S(1)}, u32[]{:S(2)}, u32[]{:S(2)}) collective-permute-start(bf16[128,1024]{1,0:T(8,128)(2,1)S(1)} %later_pack.1.refs_0_), channel_id=1, source_target_pairs={{0,4},{1,5},{2,6},{3,7},{4,12},{5,13},{6,14},{7,15},{12,8},{13,9},... | collective-permute-start | bytes 786440 | tf_op jit(solution)/shard_map/ppermute | solution.py:274
  45.0 3.9 %collective-permute-start.16 = (bf16[528,1024]{1,0:T(8,128)(2,1)S(1)}, bf16[528,1024]{1,0:T(8,128)(2,1)S(1)}, u32[]{:S(2)}, u32[]{:S(2)}) collective-permute-start(bf16[528,1024]{1,0:T(8,128)(2,1)S(1)} %get-tuple-element.47), channel_id=1, source_target_pairs={{0,1},{1,0},{2,3},{3,2},{4,5},{5,4},{6,7},{7,6},{8,9},{9,8},{10,11... | collective-permute-start | bytes 3244040 | tf_op jit(solution)/shard_map/ppermute | solution.py:283
  45.0 18.7 %collective-permute-start.10 = (bf16[128,1024]{1,0:T(8,128)(2,1)S(1)}, bf16[128,1024]{1,0:T(8,128)(2,1)S(1)}, u32[]{:S(2)}, u32[]{:S(2)}) collective-permute-start(bf16[128,1024]{1,0:T(8,128)(2,1)S(1)} %collective-permute-done.3.refs_2_), channel_id=1, source_target_pairs={{0,4},{1,5},{2,6},{3,7},{4,12},{5,13},{6,14},{7,15},{12,8},{13,9},... | collective-permute-start | bytes 786440 | tf_op jit(solution)/shard_map/ppermute | solution.py:274
  48.4 11.8 %collective-permute-start.12 = (bf16[128,1024]{1,0:T(8,128)(2,1)S(1)}, bf16[128,1024]{1,0:T(8,128)(2,1)S(1)}, u32[]{:S(2)}, u32[]{:S(2)}) collective-permute-start(bf16[128,1024]{1,0:T(8,128)(2,1)S(1)} %collective-permute-done.1.refs_1_), channel_id=1, source_target_pairs={{0,8},{1,9},{2,10},{3,11},{4,0},{5,1},{6,2},{7,3},{12,4},{13,5},{1... | collective-permute-start | bytes 786440 | tf_op jit(solution)/shard_map/ppermute | solution.py:277
  48.4 15.3 %collective-permute-start.9 = (bf16[128,1024]{1,0:T(8,128)(2,1)S(1)}, bf16[128,1024]{1,0:T(8,128)(2,1)S(1)}, u32[]{:S(2)}, u32[]{:S(2)}) collective-permute-start(bf16[128,1024]{1,0:T(8,128)(2,1)S(1)} %collective-permute-done.3.refs_2_), channel_id=1, source_target_pairs={{0,2},{1,3},{2,0},{3,1},{4,6},{5,7},{6,4},{7,5},{8,10},{9,11},{10,... | collective-permute-start | bytes 786440 | tf_op jit(solution)/shard_map/ppermute | solution.py:280
  51.8 15.4 %collective-permute-start.17 = (bf16[352,512]{1,0:T(8,128)(2,1)S(1)}, bf16[352,512]{1,0:T(8,128)(2,1)S(1)}, u32[]{:S(2)}, u32[]{:S(2)}) collective-permute-start(bf16[352,512]{1,0:T(8,128)(2,1)S(1)} %get-tuple-element.50), channel_id=1, source_target_pairs={{0,16},{16,0},{1,17},{17,1},{2,18},{18,2},{3,19},{19,3},{4,20},{20... | collective-permute-start | bytes 1081352 | tf_op jit(solution)/shard_map/ppermute | solution.py:286
  60.3 10.3 %collective-permute-start.13 = (bf16[128,1024]{1,0:T(8,128)(2,1)S(1)}, bf16[128,1024]{1,0:T(8,128)(2,1)S(1)}, u32[]{:S(2)}, u32[]{:S(2)}) collective-permute-start(bf16[128,1024]{1,0:T(8,128)(2,1)S(1)} %later_pack.1.refs_0_), channel_id=1, source_target_pairs={{0,8},{1,9},{2,10},{3,11},{4,0},{5,1},{6,2},{7,3},{12,4},{13,5},{1... | collective-permute-start | bytes 786440 | tf_op jit(solution)/shard_map/ppermute | solution.py:277
  63.7 7.5 %collective-permute-start.11 = (bf16[128,1024]{1,0:T(8,128)(2,1)S(1)}, bf16[128,1024]{1,0:T(8,128)(2,1)S(1)}, u32[]{:S(2)}, u32[]{:S(2)}) collective-permute-start(bf16[128,1024]{1,0:T(8,128)(2,1)S(1)} %collective-permute-done.10.refs_4_), channel_id=1, source_target_pairs={{0,2},{1,3},{2,0},{3,1},{4,6},{5,7},{6,4},{7,5},{8,10},{9,11},{10,... | collective-permute-start | bytes 786440 | tf_op jit(solution)/shard_map/ppermute | solution.py:280
  72.5 2.7 %collective-permute-start.18 = (bf16[512,1024]{1,0:T(8,128)(2,1)S(1)}, bf16[512,1024]{1,0:T(8,128)(2,1)S(1)}, u32[]{:S(2)}, u32[]{:S(2)}) collective-permute-start(bf16[512,1024]{1,0:T(8,128)(2,1)S(1)} %get-tuple-element.53), channel_id=1, source_target_pairs={{0,1},{1,0},{2,3},{3,2},{4,5},{5,4},{6,7},{7,6},{8,9},{9,8},{10,11... | collective-permute-start | bytes 3145736 | tf_op jit(solution)/shard_map/ppermute | solution.py:283
  72.5 22.9 %collective-permute-start.21 = (bf16[352,512]{1,0:T(8,128)(2,1)S(1)}, bf16[352,512]{1,0:T(8,128)(2,1)S(1)}, u32[]{:S(2)}, u32[]{:S(2)}) collective-permute-start(bf16[352,512]{1,0:T(8,128)(2,1)S(1)} %get-tuple-element.60), channel_id=1, source_target_pairs={{0,16},{16,0},{1,17},{17,1},{2,18},{18,2},{3,19},{19,3},{4,20},{20... | collective-permute-start | bytes 1081352 | tf_op jit(solution)/shard_map/ppermute | solution.py:286
  78.4 24.9 %collective-permute-start.20 = (bf16[352,512]{1,0:T(8,128)(2,1)}, bf16[352,512]{1,0:T(8,128)(2,1)S(1)}, u32[]{:S(2)}, u32[]{:S(2)}) collective-permute-start(bf16[352,512]{1,0:T(8,128)(2,1)} %get-tuple-element.58), channel_id=1, source_target_pairs={{0,16},{16,0},{1,17},{17,1},{2,18},{18,2},{3,19},{19,3},{4,20},{20... | collective-permute-start | bytes 1081352 | tf_op jit(solution)/shard_map/ppermute | solution.py:286
  79.9 24.1 %collective-permute-start.19 = (bf16[352,512]{1,0:T(8,128)(2,1)}, bf16[352,512]{1,0:T(8,128)(2,1)S(1)}, u32[]{:S(2)}, u32[]{:S(2)}) collective-permute-start(bf16[352,512]{1,0:T(8,128)(2,1)} %get-tuple-element.56), channel_id=1, source_target_pairs={{0,16},{16,0},{1,17},{17,1},{2,18},{18,2},{3,19},{19,3},{4,20},{20... | collective-permute-start | bytes 1081352 | tf_op jit(solution)/shard_map/ppermute | solution.py:286
  84.6 16.4 %all-to-all-start = ((f32[16,1,64]{2,1,0:T(1,128)}), f32[16,1,64]{2,1,0:T(1,128)S(1)}, u32[]{:S(2)}, u32[]{:S(2)}) async-start(f32[16,1,64]{2,1,0:T(1,128)} %bitcast.12), calls=%async_computation | async-start | bytes 16384 | tf_op jit(solution)/shard_map/all_to_all | solution.py:440
  (6 other events, 39.2 us)

commit v7 on v5

--- a/solution.py
+++ b/solution.py
@@ -9,7 +9,7 @@
 
 NZ, NY, NC = 4, 2, 2
 CHUNKS = 2
-PIECES = 2
+PIECES = (2, 2)
 PART = 512
 LANES = 128
 NT = (((1,), (1,)), ((), ()))
@@ -191,39 +191,77 @@
     products(half, capacity, mine_ref, got_ref, hs_ref, *outs[2:])
 
 
+def weight_parts(half, own_ref, got_refs):
+    mine = lax.axis_index("dp")
+    yield pl.ds(pl.multiple_of(mine * half, 16), half), 0, own_ref
+    part = got_refs[0].shape[1]
+    for q, ref in enumerate(got_refs):
+        yield pl.ds(pl.multiple_of((1 - mine) * half, 16), half), q * part, ref
+
+
 def raw_halves(half, rows_ref, own_ref, got_refs):
-    mine = lax.axis_index("dp")
-
-    def times(w_ref, rows):
-        return lax.dot_general(w_ref[...], rows, NT, preferred_element_type=jnp.float32)
-
-    yield pl.ds(pl.multiple_of(mine * half, 16), half), times(own_ref, rows_ref[...])
-    part = got_refs[0].shape[1]
-    yield (
-        pl.ds(pl.multiple_of((1 - mine) * half, 16), half),
-        sum(times(ref, rows_ref[:, q * part : (q + 1) * part]) for q, ref in enumerate(got_refs)),
-    )
-
-
-def raw_part_kernel(half, rows_ref, own_ref, *refs):
-    for units, raw in raw_halves(half, rows_ref, own_ref, refs[:-1]):
-        refs[-1][units, :] = raw
-
-
-def raw_kernel(half, capacity, rows_ref, own_ref, *refs):
-    sum_ref, hidden_ref, gates_ref, grad_ref, back_ref = refs[-5:]
-    step = pl.program_id(0)
-    gates = gates_ref[...]
-    total = jnp.zeros(gates.shape, jnp.float32)
-    for units, raw in raw_halves(half, rows_ref, own_ref, refs[:-5]):
-        raw += sum_ref[units, :]
-        grad_ref[units, :] = (raw * gates).astype(jnp.bfloat16)
+    raws = {}
+    for units, low, w_ref in weight_parts(half, own_ref, got_refs):
+        term = lax.dot_general(
+            w_ref[...],
+            rows_ref[:, low : low + w_ref.shape[1]],
+            NT,
+            preferred_element_type=jnp.float32,
+        )
+        key = w_ref is own_ref
+        raws[key] = (units, raws[key][1] + term if key in raws else term)
+    return raws.values()
+
+
+def raw_part_kernel(half, capacity, rows_ref, own_ref, *refs):
+    *got_refs, hidden_ref, raw_ref, back_ref = refs
+    total = jnp.zeros((1, rows_ref.shape[0]), jnp.float32)
+    for units, raw in raw_halves(half, rows_ref, own_ref, got_refs):
+        raw_ref[units, :] = raw
         total += jnp.sum(
             raw * hidden_ref[units, :].astype(jnp.float32), axis=0, keepdims=True
         )
-    blocks = gates.shape[1] // capacity
+    blocks = total.shape[1] // capacity
     for i in range(blocks):
-        back_ref[pl.ds(step * blocks + i, 1), :] = total[:, i * capacity : (i + 1) * capacity]
+        to = pl.ds(pl.program_id(0) * blocks + i, 1)
+        back_ref[to, :] = total[:, i * capacity : (i + 1) * capacity]
+
+
+def raw_kernel(half, rows_ref, own_ref, *refs):
+    *got_refs, sum_ref, gates_ref, grad_ref = refs
+    for units, raw in raw_halves(half, rows_ref, own_ref, got_refs):
+        grad_ref[units, :] = ((raw + sum_ref[units, :]) * gates_ref[...]).astype(jnp.bfloat16)
+
+
+def forward_kernel(half, own_ref, *refs):
+    *got_refs, hidden_ref, out_ref = refs
+    mine = lax.axis_index("dp")
+    own_units = pl.ds(pl.multiple_of(mine * half, 16), half)
+    got_units = pl.ds(pl.multiple_of((1 - mine) * half, 16), half)
+    part = got_refs[0].shape[1]
+    turned = (((0,), (0,)), ((), ()))
+    for q, ref in enumerate(got_refs):
+        cols = slice(q * part, (q + 1) * part)
+        out_ref[:, cols] = lax.dot_general(
+            hidden_ref[own_units, :], own_ref[:, cols], turned, preferred_element_type=jnp.float32
+        ) + lax.dot_general(
+            hidden_ref[got_units, :], ref[...], turned, preferred_element_type=jnp.float32
+        )
+
+
+def slot_grads_kernel(rows_ref, forward_ref, part_ref, back_ref):
+    capacity = back_ref.shape[1]
+    pair = 2 * capacity
+    for p in range(rows_ref.shape[0] // pair):
+        at = slice(p * pair, (p + 1) * pair)
+        some = jnp.zeros((pair, LANES), jnp.float32)
+        for n in range(0, rows_ref.shape[1], LANES):
+            cols = slice(n, n + LANES)
+            some += rows_ref[at, cols].astype(jnp.float32) * forward_ref[at, cols]
+        total = jnp.sum(some.T, axis=0, keepdims=True)
+        for i in range(2):
+            to = slice(2 * p + i, 2 * p + i + 1)
+            back_ref[to, :] = part_ref[to, :] + total[:, i * capacity : (i + 1) * capacity]
 
 
 def gates_kernel(routes_ref, slots_ref, back_ref, out_ref):
@@ -343,71 +381,97 @@
             name="pick",
         )(*blocks, pmat)
 
-    piece = width // PIECES
-    product_shapes = [shape((slots, width), bf16)] + [shape((half, piece), bf16)] * 2 * PIECES
+    def product_shapes(c):
+        piece = shape((half, width // PIECES[c]), bf16)
+        return [shape((slots, width), bf16)] + [piece] * (2 * PIECES[c])
 
     def first_products(mine, got, gslot):
         slot_gates, hs, rows, *halves = pl.pallas_call(
             functools.partial(first_products_kernel, half, capacity),
-            out_shape=[shape((1, slots), f32), shape((units, slots), bf16)] + product_shapes,
+            out_shape=[shape((1, slots), f32), shape((units, slots), bf16)] + product_shapes(0),
             in_specs=[VMEM] * 4,
-            out_specs=[VMEM] * (3 + 2 * PIECES),
+            out_specs=[VMEM] * (3 + 2 * PIECES[0]),
             compiler_params=params(24),
             cost_estimate=cost(3),
             name="first_products",
         )(mine, got, gslot, hidden_t)
-        return rows, halves[:PIECES], halves[PIECES:], slot_gates, hs
+        return rows, halves[: PIECES[0]], halves[PIECES[0] :], slot_gates, hs
 
     def later_products(mine, got, hs):
         rows, *halves = pl.pallas_call(
             functools.partial(products, half, capacity),
-            out_shape=product_shapes,
+            out_shape=product_shapes(1),
             in_specs=[VMEM] * 3,
-            out_specs=[VMEM] * (1 + 2 * PIECES),
+            out_specs=[VMEM] * (1 + 2 * PIECES[1]),
             compiler_params=params(24),
             name="products",
         )(mine, got, hs)
-        return rows, halves[:PIECES], halves[PIECES:]
+        return rows, halves[: PIECES[1]], halves[PIECES[1] :]
+
+    by_slot = pl.BlockSpec((units, tile), lambda i: (0, i))
+    some_rows = pl.BlockSpec((tile, width), lambda i: (i, 0))
+    back_shape = shape((experts, capacity), f32)
 
     def raw_part(rows, got_weight):
         return pl.pallas_call(
-            functools.partial(raw_part_kernel, half),
+            functools.partial(raw_part_kernel, half, capacity),
             grid=(slots // tile,),
-            out_shape=shape((units, slots), f32),
-            in_specs=[pl.BlockSpec((tile, width), lambda i: (i, 0)), columns[0]] + parts,
-            out_specs=pl.BlockSpec((units, tile), lambda i: (0, i)),
+            out_shape=[shape((units, slots), f32), back_shape],
+            in_specs=[some_rows, columns[0], *parts, by_slot],
+            out_specs=[by_slot, pl.BlockSpec((experts, capacity), lambda i: (0, 0))],
             compiler_params=params(24),
             cost_estimate=cost(3),
             name="raw_part",
-        )(rows, weight, *got_weight)
+        )(rows, weight, *got_weight, hidden_t)
 
     def raw_rest(rows, got_weight, raw, slot_gates):
-        by_slot = pl.BlockSpec((units, tile), lambda i: (0, i))
-        return pl.pallas_call(
-            functools.partial(raw_kernel, half, capacity),
+        return pl.pallas_call(
+            functools.partial(raw_kernel, half),
             grid=(slots // tile,),
-            out_shape=[shape((units, slots), bf16), shape((experts, capacity), f32)],
+            out_shape=shape((units, slots), bf16),
             in_specs=[
-                pl.BlockSpec((tile, width), lambda i: (i, 0)),
+                some_rows,
                 columns[1],
                 *parts,
                 by_slot,
-                by_slot,
                 pl.BlockSpec((1, tile), lambda i: (0, i)),
             ],
-            out_specs=[by_slot, pl.BlockSpec((experts, capacity), lambda i: (0, 0))],
+            out_specs=by_slot,
             compiler_params=params(24),
             name="raw",
-        )(rows, weight, *got_weight, raw, hidden_t, slot_gates)
-
-    def finish(place, own, got, *before):
+        )(rows, weight, *got_weight, raw, slot_gates)
+
+    def forward_columns(got_weight):
+        return pl.pallas_call(
+            functools.partial(forward_kernel, half),
+            grid=(slots // tile,),
+            out_shape=shape((slots, width), f32),
+            in_specs=[columns[1], *parts, by_slot],
+            out_specs=some_rows,
+            compiler_params=params(24),
+            cost_estimate=cost(4),
+            name="hidden_weight",
+        )(weight, *got_weight, hidden_t)
+
+    def slot_grads(rows, forwarded, part):
+        return pl.pallas_call(
+            slot_grads_kernel,
+            out_shape=back_shape,
+            in_specs=[VMEM] * 3,
+            out_specs=VMEM,
+            compiler_params=params(24),
+            name="slot_grads",
+        )(rows, forwarded, part)
+
+    def finish(low, own, got, *before):
+        piece = own.shape[1]
         spec = pl.BlockSpec((half // 2, piece), lambda i: (i, 0))
         return pl.pallas_call(
             finish_kernel,
             grid=(2,),
             out_shape=shape((half, model), bf16),
             in_specs=[spec, spec] + [ANY] * len(before),
-            out_specs=pl.BlockSpec((half // 2, piece), lambda i: (i, place)),
+            out_specs=pl.BlockSpec((half // 2, piece), lambda i: (i, low // piece)),
             input_output_aliases={2: 0} if before else {},
             compiler_params=params(8),
             name="finish",
@@ -419,25 +483,26 @@
     ff0, yf0 = forward(behind(f0, w[0])), across(behind(f0, w[0]))
     x1 = later_pack(1, r0)
     f1, yr0 = forward(x1), across(behind(r0, y0))
-    r1, yff0 = backward(behind(x1, ff0)), across(behind(ff0, yf0, w[1]))
+    yff0 = across(behind(ff0, yf0, w[1]))
     mine0, theirs0, pmat, gslot = first_pick(
         [x0, y0, f0, yf0, ff0, yff0, r0, behind(yr0, f1, w[2])]
     )
-    ff1, y1 = forward(f1), across(behind(x1, yr0))
-    yf1 = across(behind(f1, yff0, w[3]))
-    ry1 = backward(behind(y1, r1, mine0, w[3]))
+    ff1, yf1 = forward(f1), across(behind(f1, yr0))
+    r1, y1 = backward(behind(x1, ff0)), across(behind(x1, yff0))
     got = sibling(theirs0)
     rows0, send0, own0, slot_gates, hs = first_products(mine0, got, gslot)
     got0 = [swap(part) for part in send0]
-    yff1 = across(behind(ff1, y1))
-    raw = raw_part(rows0, w[: len(parts)])
+    done = (ff1, yf1, r1, y1)
+    yff1, ry1 = across(behind(ff1, *done)), backward(behind(y1, *done))
+    raw, part = raw_part(rows0, w[: len(parts)])
+    forwarded = forward_columns(w[len(parts) :])
     mine1, theirs1 = later_pick(
-        [x1, y1, f1, yf1, ff1, yff1, r1, ry1], behind(pmat, raw, got0[0])
-    )
-    rows1, send1, own1 = later_products(mine1, sibling(theirs1), hs)
-    got1 = [swap(part) for part in send1]
-
-    grad_hidden, back = raw_rest(rows1, w[len(parts) :], raw, slot_gates)
+        [x1, y1, f1, yf1, ff1, yff1, r1, ry1], behind(pmat, raw, forwarded)
+    )
+    rows1, send1, own1 = later_products(mine1, sibling(behind(theirs1, *got0)), hs)
+    got1 = [swap(half) for half in send1]
+
+    back = slot_grads(rows1, forwarded, part)
     returned = lax.all_to_all(back, "expert", split_axis=0, concat_axis=0, tiled=True)
     grad_gates = pl.pallas_call(
         gates_kernel,
@@ -452,11 +517,13 @@
         name="grad_gates",
     )(routes_t, x0, returned)
 
-    grad_weight = ()
-    for i, (own, got) in enumerate(zip((*own0, *own1), (*got0, *got1))):
-        if i == 0:
+    grad_hidden = raw_rest(rows1, w[len(parts) :], raw, slot_gates)
+    grad_weight, low = (), 0
+    for own, got in zip((*own0, *own1), (*got0, *got1)):
+        if low == 0:
             own = behind(own, back)
-        grad_weight = (finish(i, own, got, *grad_weight),)
+        grad_weight = (finish(low, own, got, *grad_weight),)
+        low += own.shape[1]
     grad_weight = grad_weight[0]
     return grad_weight[None], grad_hidden.T[None, None], grad_gates.T
 

time: 101 us -> 103 us (1.020)
  local copies, waits for them, and re-layouts: 2.12 us -> 8.62 us
  starting transfers between devices: 50.6 us -> 44.2 us
  Pallas kernels: 20.5 us -> 26.7 us
  waiting for transfers between devices: 27.2 us -> 22.3 us
    unnamed x14 -> x50, local copies, waits for them, and re-layouts: 0.62 us -> 7.13 us
    all_to_all x1, starting transfers between devices: 11.2 us -> 5.94 us  [ring_shards(): lax.all_to_all(back, 'expert', split_axis=0, concat_axis=0, tiled=True)]
    all_to_all x1, waiting for transfers between devices: 4.82 us -> 0.01 us  [ring_shards(): lax.all_to_all(back, 'expert', split_axis=0, concat_axis=0, tiled=True)]
    pallas_call x2 -> x4, Pallas kernels: 6.56 us -> 10.8 us  [the longest x1 3.45 us: raw_rest(): pl.pallas_call(functools.partial(raw_kernel, half), grid=(slots // tile,)...]
    ppermute x7, waiting for transfers between devices: 5.07 us -> 1.29 us  [across(): return lax.ppermute(x, 'expert', swap_pairs(2))]
    pallas_call x4, Pallas kernels: 3.13 us -> 5.1 us  [finish(): pl.pallas_call(finish_kernel, grid=(2,), out_shape=shape((half, model), b...]
    ppermute x2, waiting for transfers between devices: 1.09 us -> 2.65 us  [sibling(): return lax.ppermute(x, 'expert', swap_pairs(1))]
    ppermute x3, waiting for transfers between devices: 3.33 us -> 4.62 us  [backward(): return lax.ppermute(x, 'expert', ring_pairs(-1))]
  transfers between devices with their start and end apart: 25 -> 25, of which waited for: 10 -> 8; matrix products, arithmetic and copies ran while one was open for 0% -> 0% of each run, Pallas kernels for 17% -> 20%
where the time goes in v7:
time: 103 us
  starting transfers between devices  44.2 us (43%)
  Pallas kernels  26.7 us (26%)
  waiting for transfers between devices  22.3 us (22%)
  local copies, waits for them, and re-layouts  8.62 us (8%)
    ppermute x4, starting transfers between devices, forward(): return lax.ppermute(x, 'expert', ring_pairs(1))  16.5 us
    ppermute x4, waiting for transfers between devices, forward(): return lax.ppermute(x, 'expert', ring_pairs(1))  12.7 us
    ppermute x8, starting transfers between devices, swap(): return lax.ppermute(x, 'dp', [(0, 1), (1, 0)])  8.99 us
    ppermute x7, starting transfers between devices, across(): return lax.ppermute(x, 'expert', swap_pairs(2))  8.34 us
    unnamed x50, local copies, waits for them, and re-layouts  7.13 us
    all_to_all x1, starting transfers between devices, ring_shards(): lax.all_to_all(back, 'expert', split_axis=0, concat_axis=0, tiled=True)  5.94 us
    pallas_call x4, Pallas kernels, finish(): pl.pallas_call(finish_kernel, grid=(2,), out_shape=shape((half, model), b...  5.1 us
    ppermute x3, waiting for transfers between devices, backward(): return lax.ppermute(x, 'expert', ring_pairs(-1))  4.62 us
  transfers between devices with their start and end apart: 25, of which 8 were waited for; matrix products, arithmetic and copies ran while one was open for 0% of the time, Pallas kernels for 20%

profile of v7, /device:TPU:0, one launch (start us, length us, event | category | flops | bytes accessed | tf_op | source)
XLA Modules:
  0.0 102.7 jit_solution(4359917469744911049)
XLA Ops:
  2.2 3.0 %collective-permute-start.2 = (bf16[352,512]{1,0:T(8,128)(2,1)S(1)}, bf16[352,512]{1,0:T(8,128)(2,1)S(1)}, u32[]{:S(2)}, u32[]{:S(2)}) collective-permute-start(bf16[352,512]{1,0:T(8,128)(2,1)S(1)} %get-tuple-element.70), channel_id=1, source_target_pairs={{0,16},{16,0},{1,17},{17,1},{2,18},{18,2},{3,19},{19,3},{4,20},{20... | collective-permute-start | bytes 1081352 | tf_op jit(solution)/shard_map/ppermute | solution.py:324
  5.4 1.6 %collective-permute-start.1 = (bf16[128,1152]{1,0:T(8,128)(2,1)S(1)}, bf16[128,1152]{1,0:T(8,128)(2,1)S(1)}, u32[]{:S(2)}, u32[]{:S(2)}) collective-permute-start(bf16[128,1152]{1,0:T(8,128)(2,1)S(1)} %pack.1.refs_0_.slots_ref), channel_id=1, source_target_pairs={{0,4},{1,5},{2,6},{3,7},{4,12},{5,13},{6,14},{7,15},{12,8},{13,9},... | collective-permute-start | bytes 884744 | tf_op jit(solution)/shard_map/ppermute | solution.py:312
  10.4 4.8 %collective-permute-done.1.refs_2_ = bf16[128,1152]{1,0:T(8,128)(2,1)S(1)} collective-permute-done((bf16[128,1152]{1,0:T(8,128)(2,1)S(1)}, bf16[128,1152]{1,0:T(8,128)(2,1)S(1)}, u32[]{:S(2)}, u32[]{:S(2)}) %collective-permute-start.1) | collective-permute-done | bytes 294944 | tf_op jit(solution)/shard_map/ppermute | solution.py:312
  16.8 7.6 %collective-permute-start.3 = (bf16[128,1152]{1,0:T(8,128)(2,1)S(1)}, bf16[128,1152]{1,0:T(8,128)(2,1)S(1)}, u32[]{:S(2)}, u32[]{:S(2)}) collective-permute-start(bf16[128,1152]{1,0:T(8,128)(2,1)S(1)} %collective-permute-done.1.refs_2_), channel_id=1, source_target_pairs={{0,4},{1,5},{2,6},{3,7},{4,12},{5,13},{6,14},{7,15},{12,8},{13,9},... | collective-permute-start | bytes 884744 | tf_op jit(solution)/shard_map/ppermute | solution.py:312
  25.0 3.6 %collective-permute-done.3.refs_4_ = bf16[128,1152]{1,0:T(8,128)(2,1)S(1)} collective-permute-done((bf16[128,1152]{1,0:T(8,128)(2,1)S(1)}, bf16[128,1152]{1,0:T(8,128)(2,1)S(1)}, u32[]{:S(2)}, u32[]{:S(2)}) %collective-permute-start.3) | collective-permute-done | bytes 294944 | tf_op jit(solution)/shard_map/ppermute | solution.py:312
  30.0 4.5 %collective-permute-start.8 = (bf16[128,1024]{1,0:T(8,128)(2,1)S(1)}, bf16[128,1024]{1,0:T(8,128)(2,1)S(1)}, u32[]{:S(2)}, u32[]{:S(2)}) collective-permute-start(bf16[128,1024]{1,0:T(8,128)(2,1)S(1)} %later_pack.1.refs_0_), channel_id=1, source_target_pairs={{0,4},{1,5},{2,6},{3,7},{4,12},{5,13},{6,14},{7,15},{12,8},{13,9},... | collective-permute-start | bytes 786440 | tf_op jit(solution)/shard_map/ppermute | solution.py:312
  34.6 4.3 %collective-permute-done.8.refs_2_ = bf16[128,1024]{1,0:T(8,128)(2,1)S(1)} collective-permute-done((bf16[128,1024]{1,0:T(8,128)(2,1)S(1)}, bf16[128,1024]{1,0:T(8,128)(2,1)S(1)}, u32[]{:S(2)}, u32[]{:S(2)}) %collective-permute-start.8) | collective-permute-done | bytes 262176 | tf_op jit(solution)/shard_map/ppermute | solution.py:312
  38.9 1.6 %first_pick.1 = (bf16[512,1024]{1,0:T(8,128)(2,1)S(1)}, bf16[528,1024]{1,0:T(8,128)(2,1)S(1)}, bf16[1024,128]{1,0:T(8,128)(2,1)S(1)}, f32[8,128]{1,0:T(8,128)S(1)}) custom-call(bf16[128,1152]{1,0:T(8,128)(2,1)S(1)} %pack.1.refs_0_.slots_ref, bf16[128,1152]{1,0:T(8,128)(2,1)S(1)} %collective-permute-done.9.refs_1_, ...), custom_call_target="tpu_custom_call" | custom-call | flops 3000000000 | bytes 9437184 | tf_op jit(solution)/shard_map/first_pick/pallas_call | solution.py:358
  41.3 2.8 %collective-permute-start.12 = (bf16[128,1024]{1,0:T(8,128)(2,1)S(1)}, bf16[128,1024]{1,0:T(8,128)(2,1)S(1)}, u32[]{:S(2)}, u32[]{:S(2)}) collective-permute-start(bf16[128,1024]{1,0:T(8,128)(2,1)S(1)} %collective-permute-done.8.refs_2_), channel_id=1, source_target_pairs={{0,4},{1,5},{2,6},{3,7},{4,12},{5,13},{6,14},{7,15},{12,8},{13,9},... | collective-permute-start | bytes 786440 | tf_op jit(solution)/shard_map/ppermute | solution.py:312
  44.2 2.0 %collective-permute-start.11 = (bf16[128,1024]{1,0:T(8,128)(2,1)S(1)}, bf16[128,1024]{1,0:T(8,128)(2,1)S(1)}, u32[]{:S(2)}, u32[]{:S(2)}) collective-permute-start(bf16[128,1024]{1,0:T(8,128)(2,1)S(1)} %collective-permute-done.8.refs_2_), channel_id=1, source_target_pairs={{0,2},{1,3},{2,0},{3,1},{4,6},{5,7},{6,4},{7,5},{8,10},{9,11},{10,... | collective-permute-start | bytes 786440 | tf_op jit(solution)/shard_map/ppermute | solution.py:318
  46.7 3.0 %first_products.1 = (f32[1,1024]{1,0:T(1,128)S(1)}, bf16[704,1024]{1,0:T(8,128)(2,1)S(1)}, bf16[1024,1024]{1,0:T(8,128)(2,1)S(1)}, bf16[352,512]{1,0:T(8,128)(2,...) custom-call(bf16[512,1024]{1,0:T(8,128)(2,1)S(1)} %get-tuple-element.45.mine_ref, ...), custom_call_target="tpu_custom_call" | custom-call | flops 3000000000 | bytes 9437184 | tf_op jit(solution)/shard_map/first_products/pallas_call | solution.py:389
  53.4 3.3 %hidden_weight.1.forward_ref = f32[1024,1024]{1,0:T(8,128)S(1)} custom-call(bf16[352,2048]{1,0:T(8,128)(2,1)S(1)} %bitcast.16, bf16[352,512]{1,0:T(8,128)(2,1)S(1)} %collective-permute-done.16.refs_0_, bf16[352,512]{1,0:T(8,128)(2,1)S(1)} %collective-permute-done.18.refs_1_, bf16[704,1024]{1,0:T(8,128)(2,1)S(1)} %bitcast.23), custom_call_target="tpu_custom_call" | custom-call | flops 4000000000 | bytes 12582912 | tf_op jit(solution)/shard_map/hidden_weight/pallas_call | solution.py:445
  58.1 1.7 %collective-permute-start.14 = (bf16[128,1024]{1,0:T(8,128)(2,1)S(1)}, bf16[128,1024]{1,0:T(8,128)(2,1)S(1)}, u32[]{:S(2)}, u32[]{:S(2)}) collective-permute-start(bf16[128,1024]{1,0:T(8,128)(2,1)S(1)} %collective-permute-done.12.refs_4_), channel_id=1, source_target_pairs={{0,2},{1,3},{2,0},{3,1},{4,6},{5,7},{6,4},{7,5},{8,10},{9,11},{10,... | collective-permute-start | bytes 786440 | tf_op jit(solution)/shard_map/ppermute | solution.py:318
  59.9 2.4 %collective-permute-start.15 = (bf16[128,1024]{1,0:T(8,128)(2,1)S(1)}, bf16[128,1024]{1,0:T(8,128)(2,1)S(1)}, u32[]{:S(2)}, u32[]{:S(2)}) collective-permute-start(bf16[128,1024]{1,0:T(8,128)(2,1)S(1)} %collective-permute-done.7.refs_1_), channel_id=1, source_target_pairs={{0,8},{1,9},{2,10},{3,11},{4,0},{5,1},{6,2},{7,3},{12,4},{13,5},{1... | collective-permute-start | bytes 786440 | tf_op jit(solution)/shard_map/ppermute | solution.py:315
  62.3 2.9 %raw_part.1 = (f32[704,1024]{1,0:T(8,128)S(1)}, f32[16,64]{1,0:T(8,128)S(1)}) custom-call(bf16[1024,1024]{1,0:T(8,128)(2,1)S(1)} %get-tuple-element.48.rows_ref, bf16[352,2048]{1,0:T(8,128)(2,1)S(1)} %bitcast.17, bf16[352,512]{1,0:T(8,128)(2,1)S(1)} %collective-permute-done.2.refs_0_, bf16[352,512]{1,0:T(8,128)(2,1)S(1)} %collective-permute-done.5.refs_1_, ...), custom_call_target="tpu_custom_call" | custom-call | flops 3000000000 | bytes 9437184 | tf_op jit(solution)/shard_map/raw_part/pallas_call | solution.py:416
  66.8 4.5 %collective-permute-done.15.refs_7_ = bf16[128,1024]{1,0:T(8,128)(2,1)S(1)} collective-permute-done((bf16[128,1024]{1,0:T(8,128)(2,1)S(1)}, bf16[128,1024]{1,0:T(8,128)(2,1)S(1)}, u32[]{:S(2)}, u32[]{:S(2)}) %collective-permute-start.15) | collective-permute-done | bytes 262176 | tf_op jit(solution)/shard_map/ppermute | solution.py:315
  72.6 2.6 %collective-permute-done.21.got_ref = bf16[512,1024]{1,0:T(8,128)(2,1)S(1)} collective-permute-done((bf16[512,1024]{1,0:T(8,128)(2,1)S(1)}, bf16[512,1024]{1,0:T(8,128)(2,1)S(1)}, u32[]{:S(2)}, u32[]{:S(2)}) %collective-permute-start.21) | collective-permute-done | bytes 1048608 | tf_op jit(solution)/shard_map/ppermute | solution.py:321
  75.2 3.2 %products.1 = (bf16[1024,1024]{1,0:T(8,128)(2,1)S(1)}, bf16[352,512]{1,0:T(8,128)(2,1)}, bf16[352,512]{1,0:T(8,128)(2,1)}, bf16[352,512]{1,0:T(8,128)(2,1)S(1)}, bf16[352,512]{1,0:T(8,128)(2,1)S(1)}) custom-call(bf16[512,1024]{1,0:T(8,128)(2,1)S(1)} %get-tuple-element.51.mine_ref, bf16[512,1024]{1,0:T(8,128)(2,1)S(1)} %collective-permute-done.21.got_ref, ...), custom_call_target="tpu_custom_call" | custom-call | tf_op jit(solution)/shard_map/products/pallas_call | solution.py:401
  81.8 5.9 %all-to-all-start = ((f32[16,1,64]{2,1,0:T(1,128)}), f32[16,1,64]{2,1,0:T(1,128)S(1)}, u32[]{:S(2)}, u32[]{:S(2)}) async-start(f32[16,1,64]{2,1,0:T(1,128)} %bitcast.10), calls=%async_computation | async-start | bytes 16384 | tf_op jit(solution)/shard_map/all_to_all | solution.py:506
  87.7 1.8 %copy-done.2 = f32[704,1024]{1,0:T(8,128)S(1)} copy-done((f32[704,1024]{1,0:T(8,128)S(1)}, f32[704,1024]{1,0:T(8,128)}, u32[]{:S(2)}) %copy-start.2) | copy-done | bytes 2883608
  91.5 3.4 %raw.1 = bf16[704,1024]{1,0:T(8,128)(2,1)} custom-call(bf16[1024,1024]{1,0:T(8,128)(2,1)S(1)} %get-tuple-element.63.rows_ref, bf16[352,2048]{1,0:T(8,128)(2,1)S(1)} %bitcast.18, bf16[352,512]{1,0:T(8,128)(2,1)S(1)} %copy-done.18, bf16[352,512]{1,0:T(8,128)(2,1)S(1)} %copy-done.20, f32[704,1024]{1,0:T(8,128)S(1)} %copy-done.2, ...), custom_call_target="tpu_custom_call" | custom-call | tf_op jit(solution)/shard_map/raw/pallas_call | solution.py:428
  97.6 1.6 %grad_gates.1 = f32[6,128]{1,0:T(8,128)} custom-call(s32[6,128]{1,0:T(8,128)} %bitcast.19, bf16[128,1152]{1,0:T(8,128)(2,1)} %copy-done.4, f32[16,64]{1,0:T(8,128)} %bitcast.27), custom_call_target="tpu_custom_call" | custom-call | tf_op jit(solution)/shard_map/grad_gates/pallas_call | solution.py:507
  99.2 1.8 %finish.6.refs_0_ = bf16[352,2048]{1,0:T(8,128)(2,1)} custom-call(bf16[352,512]{1,0:T(8,128)(2,1)S(1)} %copy-done.12, bf16[352,512]{1,0:T(8,128)(2,1)} %collective-permute-done.23.got_ref, bf16[352,2048]{1,0:T(8,128)(2,1)} %finish.5.refs_0_), custom_call_target="tpu_custom_call", output_to_operand_aliasing={{}: (2, {})} | custom-call | tf_op jit(solution)/shard_map/finish/pallas_call | solution.py:469
  101.0 1.7 %finish.7 = bf16[352,2048]{1,0:T(8,128)(2,1)} custom-call(bf16[352,512]{1,0:T(8,128)(2,1)S(1)} %copy-done.10, bf16[352,512]{1,0:T(8,128)(2,1)} %collective-permute-done.22.got_ref, bf16[352,2048]{1,0:T(8,128)(2,1)} %finish.6.refs_0_), custom_call_target="tpu_custom_call", output_to_operand_aliasing={{}: (2, {})} | custom-call | tf_op jit(solution)/shard_map/finish/pallas_call | solution.py:469
  (92 shorter events, 26.0 us)
Async XLA Ops:
  2.2 13.1 %collective-permute-start.2 = (bf16[352,512]{1,0:T(8,128)(2,1)S(1)}, bf16[352,512]{1,0:T(8,128)(2,1)S(1)}, u32[]{:S(2)}, u32[]{:S(2)}) collective-permute-start(bf16[352,512]{1,0:T(8,128)(2,1)S(1)} %get-tuple-element.70), channel_id=1, source_target_pairs={{0,16},{16,0},{1,17},{17,1},{2,18},{18,2},{3,19},{19,3},{4,20},{20... | collective-permute-start | bytes 1081352 | tf_op jit(solution)/shard_map/ppermute | solution.py:324
  5.4 9.8 %collective-permute-start.1 = (bf16[128,1152]{1,0:T(8,128)(2,1)S(1)}, bf16[128,1152]{1,0:T(8,128)(2,1)S(1)}, u32[]{:S(2)}, u32[]{:S(2)}) collective-permute-start(bf16[128,1152]{1,0:T(8,128)(2,1)S(1)} %pack.1.refs_0_.slots_ref), channel_id=1, source_target_pairs={{0,4},{1,5},{2,6},{3,7},{4,12},{5,13},{6,14},{7,15},{12,8},{13,9},... | collective-permute-start | bytes 884744 | tf_op jit(solution)/shard_map/ppermute | solution.py:312
  7.0 17.3 %collective-permute-start.9 = (bf16[128,1152]{1,0:T(8,128)(2,1)S(1)}, bf16[128,1152]{1,0:T(8,128)(2,1)S(1)}, u32[]{:S(2)}, u32[]{:S(2)}) collective-permute-start(bf16[128,1152]{1,0:T(8,128)(2,1)S(1)} %pack.1.refs_0_.slots_ref), channel_id=1, source_target_pairs={{0,2},{1,3},{2,0},{3,1},{4,6},{5,7},{6,4},{7,5},{8,10},{9,11},{10,... | collective-permute-start | bytes 884744 | tf_op jit(solution)/shard_map/ppermute | solution.py:318
  8.5 16.5 %collective-permute-start.5 = (bf16[352,512]{1,0:T(8,128)(2,1)S(1)}, bf16[352,512]{1,0:T(8,128)(2,1)S(1)}, u32[]{:S(2)}, u32[]{:S(2)}) collective-permute-start(bf16[352,512]{1,0:T(8,128)(2,1)S(1)} %get-tuple-element.69), channel_id=1, source_target_pairs={{0,16},{16,0},{1,17},{17,1},{2,18},{18,2},{3,19},{19,3},{4,20},{20... | collective-permute-start | bytes 1081352 | tf_op jit(solution)/shard_map/ppermute | solution.py:324
  9.1 15.8 %collective-permute-start = (bf16[128,1152]{1,0:T(8,128)(2,1)S(1)}, bf16[128,1152]{1,0:T(8,128)(2,1)S(1)}, u32[]{:S(2)}, u32[]{:S(2)}) collective-permute-start(bf16[128,1152]{1,0:T(8,128)(2,1)S(1)} %pack.1.refs_0_.slots_ref), channel_id=1, source_target_pairs={{0,8},{1,9},{2,10},{3,11},{4,0},{5,1},{6,2},{7,3},{12,4},{13,5},{1... | collective-permute-start | bytes 884744 | tf_op jit(solution)/shard_map/ppermute | solution.py:315
  15.2 9.8 %collective-permute-start.4 = (bf16[128,1152]{1,0:T(8,128)(2,1)S(1)}, bf16[128,1152]{1,0:T(8,128)(2,1)S(1)}, u32[]{:S(2)}, u32[]{:S(2)}) collective-permute-start(bf16[128,1152]{1,0:T(8,128)(2,1)S(1)} %collective-permute-done.1.refs_2_), channel_id=1, source_target_pairs={{0,2},{1,3},{2,0},{3,1},{4,6},{5,7},{6,4},{7,5},{8,10},{9,11},{10,... | collective-permute-start | bytes 884744 | tf_op jit(solution)/shard_map/ppermute | solution.py:318
  16.8 11.8 %collective-permute-start.3 = (bf16[128,1152]{1,0:T(8,128)(2,1)S(1)}, bf16[128,1152]{1,0:T(8,128)(2,1)S(1)}, u32[]{:S(2)}, u32[]{:S(2)}) collective-permute-start(bf16[128,1152]{1,0:T(8,128)(2,1)S(1)} %collective-permute-done.1.refs_2_), channel_id=1, source_target_pairs={{0,4},{1,5},{2,6},{3,7},{4,12},{5,13},{6,14},{7,15},{12,8},{13,9},... | collective-permute-start | bytes 884744 | tf_op jit(solution)/shard_map/ppermute | solution.py:312
  24.3 10.2 %collective-permute-start.16 = (bf16[352,512]{1,0:T(8,128)(2,1)S(1)}, bf16[352,512]{1,0:T(8,128)(2,1)S(1)}, u32[]{:S(2)}, u32[]{:S(2)}) collective-permute-start(bf16[352,512]{1,0:T(8,128)(2,1)S(1)} %get-tuple-element.68), channel_id=1, source_target_pairs={{0,16},{16,0},{1,17},{17,1},{2,18},{18,2},{3,19},{19,3},{4,20},{20... | collective-permute-start | bytes 1081352 | tf_op jit(solution)/shard_map/ppermute | solution.py:324
  24.9 14.0 %collective-permute-start.10 = (bf16[128,1152]{1,0:T(8,128)(2,1)S(1)}, bf16[128,1152]{1,0:T(8,128)(2,1)S(1)}, u32[]{:S(2)}, u32[]{:S(2)}) collective-permute-start(bf16[128,1152]{1,0:T(8,128)(2,1)S(1)} %collective-permute-done.after_ref.refs_6_), channel_id=1, source_target_pairs={{0,2},{1,3},{2,0},{3,1},{4,6},{5,7},{6,4},{7,5},{8,10},{9,11},{10,... | collective-permute-start | bytes 884744 | tf_op jit(solution)/shard_map/ppermute | solution.py:318
  28.6 10.3 %collective-permute-start.6 = (bf16[128,1152]{1,0:T(8,128)(2,1)S(1)}, bf16[128,1152]{1,0:T(8,128)(2,1)S(1)}, u32[]{:S(2)}, u32[]{:S(2)}) collective-permute-start(bf16[128,1152]{1,0:T(8,128)(2,1)S(1)} %collective-permute-done.3.refs_4_), channel_id=1, source_target_pairs={{0,2},{1,3},{2,0},{3,1},{4,6},{5,7},{6,4},{7,5},{8,10},{9,11},{10,... | collective-permute-start | bytes 884744 | tf_op jit(solution)/shard_map/ppermute | solution.py:318
  30.0 8.8 %collective-permute-start.8 = (bf16[128,1024]{1,0:T(8,128)(2,1)S(1)}, bf16[128,1024]{1,0:T(8,128)(2,1)S(1)}, u32[]{:S(2)}, u32[]{:S(2)}) collective-permute-start(bf16[128,1024]{1,0:T(8,128)(2,1)S(1)} %later_pack.1.refs_0_), channel_id=1, source_target_pairs={{0,4},{1,5},{2,6},{3,7},{4,12},{5,13},{6,14},{7,15},{12,8},{13,9},... | collective-permute-start | bytes 786440 | tf_op jit(solution)/shard_map/ppermute | solution.py:312
  40.5 6.2 %collective-permute-start.17 = (bf16[528,1024]{1,0:T(8,128)(2,1)S(1)}, bf16[528,1024]{1,0:T(8,128)(2,1)S(1)}, u32[]{:S(2)}, u32[]{:S(2)}) collective-permute-start(bf16[528,1024]{1,0:T(8,128)(2,1)S(1)} %get-tuple-element.46), channel_id=1, source_target_pairs={{0,1},{1,0},{2,3},{3,2},{4,5},{5,4},{6,7},{7,6},{8,9},{9,8},{10,11... | collective-permute-start | bytes 3244040 | tf_op jit(solution)/shard_map/ppermute | solution.py:321
  40.6 10.8 %collective-permute-start.18 = (bf16[352,512]{1,0:T(8,128)(2,1)S(1)}, bf16[352,512]{1,0:T(8,128)(2,1)S(1)}, u32[]{:S(2)}, u32[]{:S(2)}) collective-permute-start(bf16[352,512]{1,0:T(8,128)(2,1)S(1)} %get-tuple-element.67), channel_id=1, source_target_pairs={{0,16},{16,0},{1,17},{17,1},{2,18},{18,2},{3,19},{19,3},{4,20},{20... | collective-permute-start | bytes 1081352 | tf_op jit(solution)/shard_map/ppermute | solution.py:324
  41.3 10.8 %collective-permute-start.12 = (bf16[128,1024]{1,0:T(8,128)(2,1)S(1)}, bf16[128,1024]{1,0:T(8,128)(2,1)S(1)}, u32[]{:S(2)}, u32[]{:S(2)}) collective-permute-start(bf16[128,1024]{1,0:T(8,128)(2,1)S(1)} %collective-permute-done.8.refs_2_), channel_id=1, source_target_pairs={{0,4},{1,5},{2,6},{3,7},{4,12},{5,13},{6,14},{7,15},{12,8},{13,9},... | collective-permute-start | bytes 786440 | tf_op jit(solution)/shard_map/ppermute | solution.py:312
  44.2 12.6 %collective-permute-start.11 = (bf16[128,1024]{1,0:T(8,128)(2,1)S(1)}, bf16[128,1024]{1,0:T(8,128)(2,1)S(1)}, u32[]{:S(2)}, u32[]{:S(2)}) collective-permute-start(bf16[128,1024]{1,0:T(8,128)(2,1)S(1)} %collective-permute-done.8.refs_2_), channel_id=1, source_target_pairs={{0,2},{1,3},{2,0},{3,1},{4,6},{5,7},{6,4},{7,5},{8,10},{9,11},{10,... | collective-permute-start | bytes 786440 | tf_op jit(solution)/shard_map/ppermute | solution.py:318
  46.2 10.7 %collective-permute-start.13 = (bf16[128,1024]{1,0:T(8,128)(2,1)S(1)}, bf16[128,1024]{1,0:T(8,128)(2,1)S(1)}, u32[]{:S(2)}, u32[]{:S(2)}) collective-permute-start(bf16[128,1024]{1,0:T(8,128)(2,1)S(1)} %later_pack.1.refs_0_), channel_id=1, source_target_pairs={{0,8},{1,9},{2,10},{3,11},{4,0},{5,1},{6,2},{7,3},{12,4},{13,5},{1... | collective-permute-start | bytes 786440 | tf_op jit(solution)/shard_map/ppermute | solution.py:315
  46.6 11.5 %collective-permute-start.7 = (bf16[128,1024]{1,0:T(8,128)(2,1)S(1)}, bf16[128,1024]{1,0:T(8,128)(2,1)S(1)}, u32[]{:S(2)}, u32[]{:S(2)}) collective-permute-start(bf16[128,1024]{1,0:T(8,128)(2,1)S(1)} %later_pack.1.refs_0_), channel_id=1, source_target_pairs={{0,2},{1,3},{2,0},{3,1},{4,6},{5,7},{6,4},{7,5},{8,10},{9,11},{10,... | collective-permute-start | bytes 786440 | tf_op jit(solution)/shard_map/ppermute | solution.py:318
  51.4 21.1 %collective-permute-start.19 = (bf16[352,512]{1,0:T(8,128)(2,1)S(1)}, bf16[352,512]{1,0:T(8,128)(2,1)S(1)}, u32[]{:S(2)}, u32[]{:S(2)}) collective-permute-start(bf16[352,512]{1,0:T(8,128)(2,1)S(1)} %get-tuple-element.53), channel_id=1, source_target_pairs={{0,16},{16,0},{1,17},{17,1},{2,18},{18,2},{3,19},{19,3},{4,20},{20... | collective-permute-start | bytes 1081352 | tf_op jit(solution)/shard_map/ppermute | solution.py:324
  52.1 20.4 %collective-permute-start.20 = (bf16[352,512]{1,0:T(8,128)(2,1)S(1)}, bf16[352,512]{1,0:T(8,128)(2,1)S(1)}, u32[]{:S(2)}, u32[]{:S(2)}) collective-permute-start(bf16[352,512]{1,0:T(8,128)(2,1)S(1)} %get-tuple-element.54), channel_id=1, source_target_pairs={{0,16},{16,0},{1,17},{17,1},{2,18},{18,2},{3,19},{19,3},{4,20},{20... | collective-permute-start | bytes 1081352 | tf_op jit(solution)/shard_map/ppermute | solution.py:324
  58.1 8.6 %collective-permute-start.14 = (bf16[128,1024]{1,0:T(8,128)(2,1)S(1)}, bf16[128,1024]{1,0:T(8,128)(2,1)S(1)}, u32[]{:S(2)}, u32[]{:S(2)}) collective-permute-start(bf16[128,1024]{1,0:T(8,128)(2,1)S(1)} %collective-permute-done.12.refs_4_), channel_id=1, source_target_pairs={{0,2},{1,3},{2,0},{3,1},{4,6},{5,7},{6,4},{7,5},{8,10},{9,11},{10,... | collective-permute-start | bytes 786440 | tf_op jit(solution)/shard_map/ppermute | solution.py:318
  59.9 11.4 %collective-permute-start.15 = (bf16[128,1024]{1,0:T(8,128)(2,1)S(1)}, bf16[128,1024]{1,0:T(8,128)(2,1)S(1)}, u32[]{:S(2)}, u32[]{:S(2)}) collective-permute-start(bf16[128,1024]{1,0:T(8,128)(2,1)S(1)} %collective-permute-done.7.refs_1_), channel_id=1, source_target_pairs={{0,8},{1,9},{2,10},{3,11},{4,0},{5,1},{6,2},{7,3},{12,4},{13,5},{1... | collective-permute-start | bytes 786440 | tf_op jit(solution)/shard_map/ppermute | solution.py:315
  78.5 20.7 %collective-permute-start.23 = (bf16[352,512]{1,0:T(8,128)(2,1)}, bf16[352,512]{1,0:T(8,128)(2,1)}, u32[]{:S(2)}, u32[]{:S(2)}) collective-permute-start(bf16[352,512]{1,0:T(8,128)(2,1)} %get-tuple-element.60), channel_id=1, source_target_pairs={{0,16},{16,0},{1,17},{17,1},{2,18},{18,2},{3,19},{19,3},{4,20},{20... | collective-permute-start | bytes 1081352 | tf_op jit(solution)/shard_map/ppermute | solution.py:324
  79.1 21.9 %collective-permute-start.22 = (bf16[352,512]{1,0:T(8,128)(2,1)}, bf16[352,512]{1,0:T(8,128)(2,1)}, u32[]{:S(2)}, u32[]{:S(2)}) collective-permute-start(bf16[352,512]{1,0:T(8,128)(2,1)} %get-tuple-element.58), channel_id=1, source_target_pairs={{0,16},{16,0},{1,17},{17,1},{2,18},{18,2},{3,19},{19,3},{4,20},{20... | collective-permute-start | bytes 1081352 | tf_op jit(solution)/shard_map/ppermute | solution.py:324
  81.8 15.2 %all-to-all-start = ((f32[16,1,64]{2,1,0:T(1,128)}), f32[16,1,64]{2,1,0:T(1,128)S(1)}, u32[]{:S(2)}, u32[]{:S(2)}) async-start(f32[16,1,64]{2,1,0:T(1,128)} %bitcast.10), calls=%async_computation | async-start | bytes 16384 | tf_op jit(solution)/shard_map/all_to_all | solution.py:506
  (26 other events, 144.5 us)

commit v8 on v7

--- a/solution.py
+++ b/solution.py
@@ -10,7 +10,6 @@
 NZ, NY, NC = 4, 2, 2
 CHUNKS = 2
 PIECES = (2, 2)
-PART = 512
 LANES = 128
 NT = (((1,), (1,)), ((), ()))
 VMEM = pl.BlockSpec(memory_space=pltpu.VMEM)
@@ -193,30 +192,24 @@
 
 def weight_parts(half, own_ref, got_refs):
     mine = lax.axis_index("dp")
-    yield pl.ds(pl.multiple_of(mine * half, 16), half), 0, own_ref
-    part = got_refs[0].shape[1]
-    for q, ref in enumerate(got_refs):
-        yield pl.ds(pl.multiple_of((1 - mine) * half, 16), half), q * part, ref
-
-
-def raw_halves(half, rows_ref, own_ref, got_refs):
-    raws = {}
-    for units, low, w_ref in weight_parts(half, own_ref, got_refs):
-        term = lax.dot_general(
-            w_ref[...],
-            rows_ref[:, low : low + w_ref.shape[1]],
-            NT,
-            preferred_element_type=jnp.float32,
+    yield pl.ds(pl.multiple_of(mine * half, 16), half), own_ref
+    low = (1 - mine) * half
+    for ref in got_refs:
+        yield pl.ds(pl.multiple_of(low, 16), ref.shape[0]), ref
+        low = low + ref.shape[0]
+
+
+def raw_parts(half, rows_ref, own_ref, got_refs):
+    for units, w_ref in weight_parts(half, own_ref, got_refs):
+        yield units, lax.dot_general(
+            w_ref[...], rows_ref[...], NT, preferred_element_type=jnp.float32
         )
-        key = w_ref is own_ref
-        raws[key] = (units, raws[key][1] + term if key in raws else term)
-    return raws.values()
 
 
 def raw_part_kernel(half, capacity, rows_ref, own_ref, *refs):
     *got_refs, hidden_ref, raw_ref, back_ref = refs
     total = jnp.zeros((1, rows_ref.shape[0]), jnp.float32)
-    for units, raw in raw_halves(half, rows_ref, own_ref, got_refs):
+    for units, raw in raw_parts(half, rows_ref, own_ref, got_refs):
         raw_ref[units, :] = raw
         total += jnp.sum(
             raw * hidden_ref[units, :].astype(jnp.float32), axis=0, keepdims=True
@@ -229,24 +222,21 @@
 
 def raw_kernel(half, rows_ref, own_ref, *refs):
     *got_refs, sum_ref, gates_ref, grad_ref = refs
-    for units, raw in raw_halves(half, rows_ref, own_ref, got_refs):
+    for units, raw in raw_parts(half, rows_ref, own_ref, got_refs):
         grad_ref[units, :] = ((raw + sum_ref[units, :]) * gates_ref[...]).astype(jnp.bfloat16)
 
 
 def forward_kernel(half, own_ref, *refs):
     *got_refs, hidden_ref, out_ref = refs
-    mine = lax.axis_index("dp")
-    own_units = pl.ds(pl.multiple_of(mine * half, 16), half)
-    got_units = pl.ds(pl.multiple_of((1 - mine) * half, 16), half)
-    part = got_refs[0].shape[1]
-    turned = (((0,), (0,)), ((), ()))
-    for q, ref in enumerate(got_refs):
-        cols = slice(q * part, (q + 1) * part)
-        out_ref[:, cols] = lax.dot_general(
-            hidden_ref[own_units, :], own_ref[:, cols], turned, preferred_element_type=jnp.float32
-        ) + lax.dot_general(
-            hidden_ref[got_units, :], ref[...], turned, preferred_element_type=jnp.float32
+    out_ref[...] = sum(
+        lax.dot_general(
+            hidden_ref[units, :],
+            w_ref[...],
+            (((0,), (0,)), ((), ())),
+            preferred_element_type=jnp.float32,
         )
+        for units, w_ref in weight_parts(half, own_ref, got_refs)
+    ).astype(out_ref.dtype)
 
 
 def slot_grads_kernel(rows_ref, forward_ref, part_ref, back_ref):
@@ -257,7 +247,9 @@
         some = jnp.zeros((pair, LANES), jnp.float32)
         for n in range(0, rows_ref.shape[1], LANES):
             cols = slice(n, n + LANES)
-            some += rows_ref[at, cols].astype(jnp.float32) * forward_ref[at, cols]
+            some += rows_ref[at, cols].astype(jnp.float32) * forward_ref[at, cols].astype(
+                jnp.float32
+            )
         total = jnp.sum(some.T, axis=0, keepdims=True)
         for i in range(2):
             to = slice(2 * p + i, 2 * p + i + 1)
@@ -305,7 +297,11 @@
     routes_t, gates_t = routes.T, gates.T
     weight = down_weight[0]
     columns = [pl.BlockSpec((half, width), lambda i, c=c: (0, c)) for c in range(CHUNKS)]
-    parts = [pl.BlockSpec((half, PART), lambda i: (0, 0))] * (width // PART)
+    split = half // 32 * 16
+    parts = [
+        [pl.BlockSpec((n, width), lambda i, c=c: (0, c)) for n in (split, half - split)]
+        for c in range(CHUNKS)
+    ]
     dma = pltpu.SemaphoreType.DMA
 
     def forward(x):
@@ -417,7 +413,7 @@
             functools.partial(raw_part_kernel, half, capacity),
             grid=(slots // tile,),
             out_shape=[shape((units, slots), f32), back_shape],
-            in_specs=[some_rows, columns[0], *parts, by_slot],
+            in_specs=[some_rows, columns[0], *parts[0], by_slot],
             out_specs=[by_slot, pl.BlockSpec((experts, capacity), lambda i: (0, 0))],
             compiler_params=params(24),
             cost_estimate=cost(3),
@@ -432,7 +428,7 @@
             in_specs=[
                 some_rows,
                 columns[1],
-                *parts,
+                *parts[1],
                 by_slot,
                 pl.BlockSpec((1, tile), lambda i: (0, i)),
             ],
@@ -445,8 +441,8 @@
         return pl.pallas_call(
             functools.partial(forward_kernel, half),
             grid=(slots // tile,),
-            out_shape=shape((slots, width), f32),
-            in_specs=[columns[1], *parts, by_slot],
+            out_shape=shape((slots, width), bf16),
+            in_specs=[columns[1], *parts[1], by_slot],
             out_specs=some_rows,
             compiler_params=params(24),
             cost_estimate=cost(4),
@@ -477,25 +473,28 @@
             name="finish",
         )(own, got, *before)
 
-    w = [swap(weight[:, k : k + PART]) for k in range(0, model, PART)]
     x0 = pack()
-    f0, r0, y0 = forward(x0), backward(x0), across(x0)
-    ff0, yf0 = forward(behind(f0, w[0])), across(behind(f0, w[0]))
-    x1 = later_pack(1, r0)
-    f1, yr0 = forward(x1), across(behind(r0, y0))
-    yff0 = across(behind(ff0, yf0, w[1]))
-    mine0, theirs0, pmat, gslot = first_pick(
-        [x0, y0, f0, yf0, ff0, yff0, r0, behind(yr0, f1, w[2])]
-    )
-    ff1, yf1 = forward(f1), across(behind(f1, yr0))
-    r1, y1 = backward(behind(x1, ff0)), across(behind(x1, yff0))
+    w = [swap(weight[:split]), swap(weight[split:])]
+    f0, y0 = forward(x0), across(x0)
+    done = (f0, y0)
+    ff0, yf0 = forward(behind(f0, *done)), across(behind(f0, *done))
+    done = (ff0, yf0)
+    r0, yff0 = backward(behind(x0, *done)), across(behind(ff0, *done))
+    x1 = later_pack(1, ff0)
+    done = (r0, yff0, w[0])
+    f1, yr0 = forward(behind(x1, *done)), across(behind(r0, *done))
+    done = (f1, yr0)
+    ff1, y1 = forward(behind(f1, *done)), across(behind(x1, *done))
+    mine0, theirs0, pmat, gslot = first_pick([x0, y0, f0, yf0, ff0, yff0, r0, behind(yr0, f1, w[1])])
     got = sibling(theirs0)
+    done = (ff1, y1, mine0)
+    r1, yf1 = backward(behind(x1, *done)), across(behind(f1, *done))
     rows0, send0, own0, slot_gates, hs = first_products(mine0, got, gslot)
     got0 = [swap(part) for part in send0]
-    done = (ff1, yf1, r1, y1)
-    yff1, ry1 = across(behind(ff1, *done)), backward(behind(y1, *done))
-    raw, part = raw_part(rows0, w[: len(parts)])
-    forwarded = forward_columns(w[len(parts) :])
+    done = (r1, yf1, rows0)
+    ry1, yff1 = backward(behind(y1, *done)), across(behind(ff1, *done))
+    raw, part = raw_part(rows0, w)
+    forwarded = forward_columns(w)
     mine1, theirs1 = later_pick(
         [x1, y1, f1, yf1, ff1, yff1, r1, ry1], behind(pmat, raw, forwarded)
     )
@@ -517,7 +516,7 @@
         name="grad_gates",
     )(routes_t, x0, returned)
 
-    grad_hidden = raw_rest(rows1, w[len(parts) :], raw, slot_gates)
+    grad_hidden = raw_rest(rows1, w, raw, slot_gates)
     grad_weight, low = (), 0
     for own, got in zip((*own0, *own1), (*got0, *got1)):
         if low == 0:

time: 103 us -> 107 us (1.039)
  starting transfers between devices: 44.2 us -> 30.4 us
  waiting for transfers between devices: 22.3 us -> 35.2 us
  local copies, waits for them, and re-layouts: 8.62 us -> 12 us
    ppermute x7, waiting for transfers between devices: 1.29 us -> 14.8 us  [across(): return lax.ppermute(x, 'expert', swap_pairs(2))]
    ppermute x4, starting transfers between devices: 16.5 us -> 5.41 us  [forward(): return lax.ppermute(x, 'expert', ring_pairs(1))]
    ppermute x8 -> x6, waiting for transfers between devices: 1.03 us -> 9.98 us  [swap(): return lax.ppermute(x, 'dp', [(0, 1), (1, 0)])]
    ppermute x4, waiting for transfers between devices: 12.7 us -> 4.93 us  [forward(): return lax.ppermute(x, 'expert', ring_pairs(1))]
    unnamed x50 -> x52, local copies, waits for them, and re-layouts: 7.13 us -> 10.6 us
    ppermute x8 -> x6, starting transfers between devices: 8.99 us -> 7.16 us  [swap(): return lax.ppermute(x, 'dp', [(0, 1), (1, 0)])]
    ppermute x3, waiting for transfers between devices: 4.62 us -> 2.84 us  [backward(): return lax.ppermute(x, 'expert', ring_pairs(-1))]
    all_to_all x1, starting transfers between devices: 5.94 us -> 4.31 us  [ring_shards(): lax.all_to_all(back, 'expert', split_axis=0, concat_axis=0, tiled=True)]
  transfers between devices with their start and end apart: 25 -> 23, of which waited for: 8 -> 13; matrix products, arithmetic and copies ran while one was open for 0% -> 1% of each run, Pallas kernels for 20% -> 20%
where the time goes in v8:
time: 107 us; the launch traced here: 106 us
  waiting for transfers between devices  35.2 us (33%)
  starting transfers between devices  30.4 us (28%)
  Pallas kernels  27.7 us (26%)
  local copies, waits for them, and re-layouts  12 us (11%)
    ppermute x7, waiting for transfers between devices, across(): return lax.ppermute(x, 'expert', swap_pairs(2))  14.8 us
    unnamed x52, local copies, waits for them, and re-layouts  10.6 us
    ppermute x6, waiting for transfers between devices, swap(): return lax.ppermute(x, 'dp', [(0, 1), (1, 0)])  9.98 us
    ppermute x7, starting transfers between devices, across(): return lax.ppermute(x, 'expert', swap_pairs(2))  9.19 us
    ppermute x6, starting transfers between devices, swap(): return lax.ppermute(x, 'dp', [(0, 1), (1, 0)])  7.16 us
    ppermute x4, starting transfers between devices, forward(): return lax.ppermute(x, 'expert', ring_pairs(1))  5.41 us
    pallas_call x4, Pallas kernels, finish(): pl.pallas_call(finish_kernel, grid=(2,), out_shape=shape((half, model), b...  5.1 us
    ppermute x4, waiting for transfers between devices, forward(): return lax.ppermute(x, 'expert', ring_pairs(1))  4.93 us
  transfers between devices with their start and end apart: 23, of which 13 were waited for; matrix products, arithmetic and copies ran while one was open for 1% of the time, Pallas kernels for 20%

profile of v8, /device:TPU:0, one launch (start us, length us, event | category | flops | bytes accessed | tf_op | source)
XLA Modules:
  0.0 106.2 jit_solution(10932416840122366189)
XLA Ops:
  3.3 3.0 %collective-permute-start.1 = (bf16[128,1152]{1,0:T(8,128)(2,1)S(1)}, bf16[128,1152]{1,0:T(8,128)(2,1)S(1)}, u32[]{:S(2)}, u32[]{:S(2)}) collective-permute-start(bf16[128,1152]{1,0:T(8,128)(2,1)S(1)} %pack.1.refs_0_.slots_ref), channel_id=1, source_target_pairs={{0,2},{1,3},{2,0},{3,1},{4,6},{5,7},{6,4},{7,5},{8,10},{9,11},{10,... | collective-permute-start | bytes 884744 | tf_op jit(solution)/shard_map/ppermute | solution.py:314
  6.3 1.6 %collective-permute-start = (bf16[128,1152]{1,0:T(8,128)(2,1)S(1)}, bf16[128,1152]{1,0:T(8,128)(2,1)S(1)}, u32[]{:S(2)}, u32[]{:S(2)}) collective-permute-start(bf16[128,1152]{1,0:T(8,128)(2,1)S(1)} %pack.1.refs_0_.slots_ref), channel_id=1, source_target_pairs={{0,4},{1,5},{2,6},{3,7},{4,12},{5,13},{6,14},{7,15},{12,8},{13,9},... | collective-permute-start | bytes 884744 | tf_op jit(solution)/shard_map/ppermute | solution.py:308
  10.9 2.4 %collective-permute-done.1.refs_1_ = bf16[128,1152]{1,0:T(8,128)(2,1)S(1)} collective-permute-done((bf16[128,1152]{1,0:T(8,128)(2,1)S(1)}, bf16[128,1152]{1,0:T(8,128)(2,1)S(1)}, u32[]{:S(2)}, u32[]{:S(2)}) %collective-permute-start.1) | collective-permute-done | bytes 294944 | tf_op jit(solution)/shard_map/ppermute | solution.py:314
  13.3 2.4 %collective-permute-done.refs_2_ = bf16[128,1152]{1,0:T(8,128)(2,1)S(1)} collective-permute-done((bf16[128,1152]{1,0:T(8,128)(2,1)S(1)}, bf16[128,1152]{1,0:T(8,128)(2,1)S(1)}, u32[]{:S(2)}, u32[]{:S(2)}) %collective-permute-start) | collective-permute-done | bytes 294944 | tf_op jit(solution)/shard_map/ppermute | solution.py:308
  18.4 4.8 %collective-permute-done.3.refs_3_ = bf16[128,1152]{1,0:T(8,128)(2,1)S(1)} collective-permute-done((bf16[128,1152]{1,0:T(8,128)(2,1)S(1)}, bf16[128,1152]{1,0:T(8,128)(2,1)S(1)}, u32[]{:S(2)}, u32[]{:S(2)}) %collective-permute-start.3) | collective-permute-done | bytes 294944 | tf_op jit(solution)/shard_map/ppermute | solution.py:314
  28.5 2.8 %collective-permute-done.4.refs_6_ = bf16[128,1152]{1,0:T(8,128)(2,1)S(1)} collective-permute-done((bf16[128,1152]{1,0:T(8,128)(2,1)S(1)}, bf16[128,1152]{1,0:T(8,128)(2,1)S(1)}, u32[]{:S(2)}, u32[]{:S(2)}) %collective-permute-start.4) | collective-permute-done | bytes 294944 | tf_op jit(solution)/shard_map/ppermute | solution.py:311
  31.3 2.0 %collective-permute-done.5.refs_5_ = bf16[128,1152]{1,0:T(8,128)(2,1)S(1)} collective-permute-done((bf16[128,1152]{1,0:T(8,128)(2,1)S(1)}, bf16[128,1152]{1,0:T(8,128)(2,1)S(1)}, u32[]{:S(2)}, u32[]{:S(2)}) %collective-permute-start.5) | collective-permute-done | bytes 294944 | tf_op jit(solution)/shard_map/ppermute | solution.py:314
  35.4 6.8 %collective-permute-done.11.refs_1_ = bf16[176,2048]{1,0:T(8,128)(2,1)S(1)} collective-permute-done((bf16[176,2048]{1,0:T(8,128)(2,1)S(1)}, bf16[176,2048]{1,0:T(8,128)(2,1)S(1)}, u32[]{:S(2)}, u32[]{:S(2)}) %collective-permute-start.11) | collective-permute-done | bytes 720928 | tf_op jit(solution)/shard_map/ppermute | solution.py:320
  42.3 1.6 %first_pick.1 = (bf16[512,1024]{1,0:T(8,128)(2,1)S(1)}, bf16[528,1024]{1,0:T(8,128)(2,1)S(1)}, bf16[1024,128]{1,0:T(8,128)(2,1)S(1)}, f32[8,128]{1,0:T(8,128)S(1)}) custom-call(bf16[128,1152]{1,0:T(8,128)(2,1)S(1)} %pack.1.refs_0_.slots_ref, bf16[128,1152]{1,0:T(8,128)(2,1)S(1)} %collective-permute-done.1.refs_1_, ...), custom_call_target="tpu_custom_call" | custom-call | flops 3000000000 | bytes 9437184 | tf_op jit(solution)/shard_map/first_pick/pallas_call | solution.py:354
  44.5 2.5 %collective-permute-start.10 = (bf16[128,1024]{1,0:T(8,128)(2,1)S(1)}, bf16[128,1024]{1,0:T(8,128)(2,1)S(1)}, u32[]{:S(2)}, u32[]{:S(2)}) collective-permute-start(bf16[128,1024]{1,0:T(8,128)(2,1)S(1)} %collective-permute-done.7.refs_2_), channel_id=1, source_target_pairs={{0,4},{1,5},{2,6},{3,7},{4,12},{5,13},{6,14},{7,15},{12,8},{13,9},... | collective-permute-start | bytes 786440 | tf_op jit(solution)/shard_map/ppermute | solution.py:308
  47.1 5.6 %collective-permute-done.9.refs_1_ = bf16[128,1024]{1,0:T(8,128)(2,1)S(1)} collective-permute-done((bf16[128,1024]{1,0:T(8,128)(2,1)S(1)}, bf16[128,1024]{1,0:T(8,128)(2,1)S(1)}, u32[]{:S(2)}, u32[]{:S(2)}) %collective-permute-start.9) | collective-permute-done | bytes 262176 | tf_op jit(solution)/shard_map/ppermute | solution.py:314
  56.4 3.0 %first_products.1 = (f32[1,1024]{1,0:T(1,128)S(1)}, bf16[704,1024]{1,0:T(8,128)(2,1)S(1)}, bf16[1024,1024]{1,0:T(8,128)(2,1)S(1)}, bf16[352,512]{1,0:T(8,128)(2,...) custom-call(bf16[512,1024]{1,0:T(8,128)(2,1)S(1)} %get-tuple-element.46.mine_ref, ...), custom_call_target="tpu_custom_call" | custom-call | flops 3000000000 | bytes 9437184 | tf_op jit(solution)/shard_map/first_products/pallas_call | solution.py:385
  61.5 3.3 %hidden_weight.1.forward_ref = bf16[1024,1024]{1,0:T(8,128)(2,1)S(1)} custom-call(bf16[352,2048]{1,0:T(8,128)(2,1)S(1)} %bitcast.19, bf16[176,2048]{1,0:T(8,128)(2,1)S(1)} %collective-permute-done.6.refs_0_, bf16[176,2048]{1,0:T(8,128)(2,1)S(1)} %collective-permute-done.11.refs_1_, bf16[704,1024]{1,0:T(8,128)(2,1)S(1)} %bitcast.26), custom_call_target="tpu_custom_call" | custom-call | flops 4000000000 | bytes 12582912 | tf_op jit(solution)/shard_map/hidden_weight/pallas_call | solution.py:441
  65.5 1.9 %collective-permute-start.16 = (bf16[128,1024]{1,0:T(8,128)(2,1)S(1)}, bf16[128,1024]{1,0:T(8,128)(2,1)S(1)}, u32[]{:S(2)}, u32[]{:S(2)}) collective-permute-start(bf16[128,1024]{1,0:T(8,128)(2,1)S(1)} %collective-permute-done.9.refs_1_), channel_id=1, source_target_pairs={{0,8},{1,9},{2,10},{3,11},{4,0},{5,1},{6,2},{7,3},{12,4},{13,5},{1... | collective-permute-start | bytes 786440 | tf_op jit(solution)/shard_map/ppermute | solution.py:311
  67.4 3.4 %raw_part.1 = (f32[704,1024]{1,0:T(8,128)S(1)}, f32[16,64]{1,0:T(8,128)S(1)}) custom-call(bf16[1024,1024]{1,0:T(8,128)(2,1)S(1)} %get-tuple-element.51.rows_ref, bf16[352,2048]{1,0:T(8,128)(2,1)S(1)} %bitcast.20, bf16[176,2048]{1,0:T(8,128)(2,1)S(1)} %collective-permute-done.6.refs_0_, bf16[176,2048]{1,0:T(8,128)(2,1)S(1)} %collective-permute-done.11.refs_1_, ...), custom_call_target="tpu_custom_call" | custom-call | flops 3000000000 | bytes 9437184 | tf_op jit(solution)/shard_map/raw_part/pallas_call | solution.py:412
  74.3 2.0 %collective-permute-done.18.got_ref = bf16[352,512]{1,0:T(8,128)(2,1)S(1)} collective-permute-done((bf16[352,512]{1,0:T(8,128)(2,1)S(1)}, bf16[352,512]{1,0:T(8,128)(2,1)S(1)}, u32[]{:S(2)}, u32[]{:S(2)}) %collective-permute-start.18) | collective-permute-done | bytes 360480 | tf_op jit(solution)/shard_map/ppermute | solution.py:320
  77.1 2.7 %collective-permute-done.19.got_ref = bf16[512,1024]{1,0:T(8,128)(2,1)S(1)} collective-permute-done((bf16[512,1024]{1,0:T(8,128)(2,1)S(1)}, bf16[512,1024]{1,0:T(8,128)(2,1)S(1)}, u32[]{:S(2)}, u32[]{:S(2)}) %collective-permute-start.19) | collective-permute-done | bytes 1048608 | tf_op jit(solution)/shard_map/ppermute | solution.py:317
  79.7 3.2 %products.1 = (bf16[1024,1024]{1,0:T(8,128)(2,1)S(1)}, bf16[352,512]{1,0:T(8,128)(2,1)}, bf16[352,512]{1,0:T(8,128)(2,1)}, bf16[352,512]{1,0:T(8,128)(2,1)S(1)}, bf16[352,512]{1,0:T(8,128)(2,1)S(1)}) custom-call(bf16[512,1024]{1,0:T(8,128)(2,1)S(1)} %get-tuple-element.57.mine_ref, bf16[512,1024]{1,0:T(8,128)(2,1)S(1)} %collective-permute-done.19.got_ref, ...), custom_call_target="tpu_custom_call" | custom-call | tf_op jit(solution)/shard_map/products/pallas_call | solution.py:397
  86.3 4.3 %all-to-all-start = ((f32[16,1,64]{2,1,0:T(1,128)}), f32[16,1,64]{2,1,0:T(1,128)S(1)}, u32[]{:S(2)}, u32[]{:S(2)}) async-start(f32[16,1,64]{2,1,0:T(1,128)} %bitcast.12), calls=%async_computation | async-start | bytes 16384 | tf_op jit(solution)/shard_map/all_to_all | solution.py:505
  90.6 1.8 %copy-done.2 = f32[704,1024]{1,0:T(8,128)S(1)} copy-done((f32[704,1024]{1,0:T(8,128)S(1)}, f32[704,1024]{1,0:T(8,128)}, u32[]{:S(2)}) %copy-start.2) | copy-done | bytes 2883608
  94.6 3.8 %raw.1 = bf16[704,1024]{1,0:T(8,128)(2,1)} custom-call(bf16[1024,1024]{1,0:T(8,128)(2,1)S(1)} %get-tuple-element.69.rows_ref, bf16[352,2048]{1,0:T(8,128)(2,1)S(1)} %bitcast.21, bf16[176,2048]{1,0:T(8,128)(2,1)S(1)} %copy-done.7, bf16[176,2048]{1,0:T(8,128)(2,1)S(1)} %copy-done.9, f32[704,1024]{1,0:T(8,128)S(1)} %copy-done.2, ...), custom_call_target="tpu_custom_call" | custom-call | tf_op jit(solution)/shard_map/raw/pallas_call | solution.py:424
  101.1 1.6 %grad_gates.1 = f32[6,128]{1,0:T(8,128)} custom-call(s32[6,128]{1,0:T(8,128)} %bitcast.22, bf16[128,1152]{1,0:T(8,128)(2,1)} %copy-done.5, f32[16,64]{1,0:T(8,128)} %bitcast.30), custom_call_target="tpu_custom_call" | custom-call | tf_op jit(solution)/shard_map/grad_gates/pallas_call | solution.py:506
  102.7 1.8 %finish.6.refs_0_ = bf16[352,2048]{1,0:T(8,128)(2,1)} custom-call(bf16[352,512]{1,0:T(8,128)(2,1)S(1)} %copy-done.17, bf16[352,512]{1,0:T(8,128)(2,1)} %collective-permute-done.21.got_ref, bf16[352,2048]{1,0:T(8,128)(2,1)} %finish.5.refs_0_), custom_call_target="tpu_custom_call", output_to_operand_aliasing={{}: (2, {})} | custom-call | tf_op jit(solution)/shard_map/finish/pallas_call | solution.py:465
  104.5 1.7 %finish.7 = bf16[352,2048]{1,0:T(8,128)(2,1)} custom-call(bf16[352,512]{1,0:T(8,128)(2,1)S(1)} %copy-done.15, bf16[352,512]{1,0:T(8,128)(2,1)} %collective-permute-done.20.got_ref, bf16[352,2048]{1,0:T(8,128)(2,1)} %finish.6.refs_0_), custom_call_target="tpu_custom_call", output_to_operand_aliasing={{}: (2, {})} | custom-call | tf_op jit(solution)/shard_map/finish/pallas_call | solution.py:465
  (90 shorter events, 35.3 us)
Async XLA Ops:
  3.2 39.0 %copy-start.5 = (bf16[128,1152]{1,0:T(8,128)(2,1)}, bf16[128,1152]{1,0:T(8,128)(2,1)S(1)}, u32[]{:S(2)}) copy-start(bf16[128,1152]{1,0:T(8,128)(2,1)S(1)} %pack.1.refs_0_.slots_ref) | copy-start | bytes 884740
  3.3 10.0 %collective-permute-start.1 = (bf16[128,1152]{1,0:T(8,128)(2,1)S(1)}, bf16[128,1152]{1,0:T(8,128)(2,1)S(1)}, u32[]{:S(2)}, u32[]{:S(2)}) collective-permute-start(bf16[128,1152]{1,0:T(8,128)(2,1)S(1)} %pack.1.refs_0_.slots_ref), channel_id=1, source_target_pairs={{0,2},{1,3},{2,0},{3,1},{4,6},{5,7},{6,4},{7,5},{8,10},{9,11},{10,... | collective-permute-start | bytes 884744 | tf_op jit(solution)/shard_map/ppermute | solution.py:314
  6.3 9.4 %collective-permute-start = (bf16[128,1152]{1,0:T(8,128)(2,1)S(1)}, bf16[128,1152]{1,0:T(8,128)(2,1)S(1)}, u32[]{:S(2)}, u32[]{:S(2)}) collective-permute-start(bf16[128,1152]{1,0:T(8,128)(2,1)S(1)} %pack.1.refs_0_.slots_ref), channel_id=1, source_target_pairs={{0,4},{1,5},{2,6},{3,7},{4,12},{5,13},{6,14},{7,15},{12,8},{13,9},... | collective-permute-start | bytes 884744 | tf_op jit(solution)/shard_map/ppermute | solution.py:308
  9.4 19.1 %collective-permute-start.6 = (bf16[176,2048]{1,0:T(8,128)(2,1)S(1)}, bf16[176,2048]{1,0:T(8,128)(2,1)S(1)}, u32[]{:S(2)}, u32[]{:S(2)}) collective-permute-start(bf16[176,2048]{1,0:T(8,128)(2,1)S(1)} %get-tuple-element.74), channel_id=1, source_target_pairs={{0,16},{16,0},{1,17},{17,1},{2,18},{18,2},{3,19},{19,3},{4,20},{20... | collective-permute-start | bytes 2162696 | tf_op jit(solution)/shard_map/ppermute | solution.py:320
  15.7 7.6 %collective-permute-start.3 = (bf16[128,1152]{1,0:T(8,128)(2,1)S(1)}, bf16[128,1152]{1,0:T(8,128)(2,1)S(1)}, u32[]{:S(2)}, u32[]{:S(2)}) collective-permute-start(bf16[128,1152]{1,0:T(8,128)(2,1)S(1)} %collective-permute-done.refs_2_), channel_id=1, source_target_pairs={{0,2},{1,3},{2,0},{3,1},{4,6},{5,7},{6,4},{7,5},{8,10},{9,11},{10,... | collective-permute-start | bytes 884744 | tf_op jit(solution)/shard_map/ppermute | solution.py:314
  16.1 8.5 %collective-permute-start.2 = (bf16[128,1152]{1,0:T(8,128)(2,1)S(1)}, bf16[128,1152]{1,0:T(8,128)(2,1)S(1)}, u32[]{:S(2)}, u32[]{:S(2)}) collective-permute-start(bf16[128,1152]{1,0:T(8,128)(2,1)S(1)} %collective-permute-done.refs_2_), channel_id=1, source_target_pairs={{0,4},{1,5},{2,6},{3,7},{4,12},{5,13},{6,14},{7,15},{12,8},{13,9},... | collective-permute-start | bytes 884744 | tf_op jit(solution)/shard_map/ppermute | solution.py:308
  17.0 25.2 %collective-permute-start.11 = (bf16[176,2048]{1,0:T(8,128)(2,1)S(1)}, bf16[176,2048]{1,0:T(8,128)(2,1)S(1)}, u32[]{:S(2)}, u32[]{:S(2)}) collective-permute-start(bf16[176,2048]{1,0:T(8,128)(2,1)S(1)} %get-tuple-element.73), channel_id=1, source_target_pairs={{0,16},{16,0},{1,17},{17,1},{2,18},{18,2},{3,19},{19,3},{4,20},{20... | collective-permute-start | bytes 2162696 | tf_op jit(solution)/shard_map/ppermute | solution.py:320
  24.6 6.7 %collective-permute-start.4 = (bf16[128,1152]{1,0:T(8,128)(2,1)S(1)}, bf16[128,1152]{1,0:T(8,128)(2,1)S(1)}, u32[]{:S(2)}, u32[]{:S(2)}) collective-permute-start(bf16[128,1152]{1,0:T(8,128)(2,1)S(1)} %pack.1.refs_0_.slots_ref), channel_id=1, source_target_pairs={{0,8},{1,9},{2,10},{3,11},{4,0},{5,1},{6,2},{7,3},{12,4},{13,5},{1... | collective-permute-start | bytes 884744 | tf_op jit(solution)/shard_map/ppermute | solution.py:311
  25.9 7.5 %collective-permute-start.5 = (bf16[128,1152]{1,0:T(8,128)(2,1)S(1)}, bf16[128,1152]{1,0:T(8,128)(2,1)S(1)}, u32[]{:S(2)}, u32[]{:S(2)}) collective-permute-start(bf16[128,1152]{1,0:T(8,128)(2,1)S(1)} %collective-permute-done.2.after_ref.refs_4_), channel_id=1, source_target_pairs={{0,2},{1,3},{2,0},{3,1},{4,6},{5,7},{6,4},{7,5},{8,10},{9,11},{10,... | collective-permute-start | bytes 884744 | tf_op jit(solution)/shard_map/ppermute | solution.py:314
  33.3 8.9 %collective-permute-start.8 = (bf16[128,1152]{1,0:T(8,128)(2,1)S(1)}, bf16[128,1152]{1,0:T(8,128)(2,1)S(1)}, u32[]{:S(2)}, u32[]{:S(2)}) collective-permute-start(bf16[128,1152]{1,0:T(8,128)(2,1)S(1)} %collective-permute-done.4.refs_6_), channel_id=1, source_target_pairs={{0,2},{1,3},{2,0},{3,1},{4,6},{5,7},{6,4},{7,5},{8,10},{9,11},{10,... | collective-permute-start | bytes 884744 | tf_op jit(solution)/shard_map/ppermute | solution.py:314
  34.9 7.3 %collective-permute-start.7 = (bf16[128,1024]{1,0:T(8,128)(2,1)S(1)}, bf16[128,1024]{1,0:T(8,128)(2,1)S(1)}, u32[]{:S(2)}, u32[]{:S(2)}) collective-permute-start(bf16[128,1024]{1,0:T(8,128)(2,1)S(1)} %later_pack.1.refs_0_), channel_id=1, source_target_pairs={{0,4},{1,5},{2,6},{3,7},{4,12},{5,13},{6,14},{7,15},{12,8},{13,9},... | collective-permute-start | bytes 786440 | tf_op jit(solution)/shard_map/ppermute | solution.py:308
  43.9 12.6 %collective-permute-start.14 = (bf16[528,1024]{1,0:T(8,128)(2,1)S(1)}, bf16[528,1024]{1,0:T(8,128)(2,1)S(1)}, u32[]{:S(2)}, u32[]{:S(2)}) collective-permute-start(bf16[528,1024]{1,0:T(8,128)(2,1)S(1)} %get-tuple-element.49), channel_id=1, source_target_pairs={{0,1},{1,0},{2,3},{3,2},{4,5},{5,4},{6,7},{7,6},{8,9},{9,8},{10,11... | collective-permute-start | bytes 3244040 | tf_op jit(solution)/shard_map/ppermute | solution.py:317
  43.9 8.7 %collective-permute-start.9 = (bf16[128,1024]{1,0:T(8,128)(2,1)S(1)}, bf16[128,1024]{1,0:T(8,128)(2,1)S(1)}, u32[]{:S(2)}, u32[]{:S(2)}) collective-permute-start(bf16[128,1024]{1,0:T(8,128)(2,1)S(1)} %later_pack.1.refs_0_), channel_id=1, source_target_pairs={{0,2},{1,3},{2,0},{3,1},{4,6},{5,7},{6,4},{7,5},{8,10},{9,11},{10,... | collective-permute-start | bytes 786440 | tf_op jit(solution)/shard_map/ppermute | solution.py:314
  44.5 9.3 %collective-permute-start.10 = (bf16[128,1024]{1,0:T(8,128)(2,1)S(1)}, bf16[128,1024]{1,0:T(8,128)(2,1)S(1)}, u32[]{:S(2)}, u32[]{:S(2)}) collective-permute-start(bf16[128,1024]{1,0:T(8,128)(2,1)S(1)} %collective-permute-done.7.refs_2_), channel_id=1, source_target_pairs={{0,4},{1,5},{2,6},{3,7},{4,12},{5,13},{6,14},{7,15},{12,8},{13,9},... | collective-permute-start | bytes 786440 | tf_op jit(solution)/shard_map/ppermute | solution.py:308
  53.8 11.1 %collective-permute-start.12 = (bf16[128,1024]{1,0:T(8,128)(2,1)S(1)}, bf16[128,1024]{1,0:T(8,128)(2,1)S(1)}, u32[]{:S(2)}, u32[]{:S(2)}) collective-permute-start(bf16[128,1024]{1,0:T(8,128)(2,1)S(1)} %collective-permute-done.7.refs_2_), channel_id=1, source_target_pairs={{0,2},{1,3},{2,0},{3,1},{4,6},{5,7},{6,4},{7,5},{8,10},{9,11},{10,... | collective-permute-start | bytes 786440 | tf_op jit(solution)/shard_map/ppermute | solution.py:314
  55.3 9.6 %collective-permute-start.13 = (bf16[128,1024]{1,0:T(8,128)(2,1)S(1)}, bf16[128,1024]{1,0:T(8,128)(2,1)S(1)}, u32[]{:S(2)}, u32[]{:S(2)}) collective-permute-start(bf16[128,1024]{1,0:T(8,128)(2,1)S(1)} %later_pack.1.refs_0_), channel_id=1, source_target_pairs={{0,8},{1,9},{2,10},{3,11},{4,0},{5,1},{6,2},{7,3},{12,4},{13,5},{1... | collective-permute-start | bytes 786440 | tf_op jit(solution)/shard_map/ppermute | solution.py:311
  59.4 14.1 %collective-permute-start.17 = (bf16[352,512]{1,0:T(8,128)(2,1)S(1)}, bf16[352,512]{1,0:T(8,128)(2,1)S(1)}, u32[]{:S(2)}, u32[]{:S(2)}) collective-permute-start(bf16[352,512]{1,0:T(8,128)(2,1)S(1)} %get-tuple-element.59), channel_id=1, source_target_pairs={{0,16},{16,0},{1,17},{17,1},{2,18},{18,2},{3,19},{19,3},{4,20},{20... | collective-permute-start | bytes 1081352 | tf_op jit(solution)/shard_map/ppermute | solution.py:320
  61.0 15.3 %collective-permute-start.18 = (bf16[352,512]{1,0:T(8,128)(2,1)S(1)}, bf16[352,512]{1,0:T(8,128)(2,1)S(1)}, u32[]{:S(2)}, u32[]{:S(2)}) collective-permute-start(bf16[352,512]{1,0:T(8,128)(2,1)S(1)} %get-tuple-element.60), channel_id=1, source_target_pairs={{0,16},{16,0},{1,17},{17,1},{2,18},{18,2},{3,19},{19,3},{4,20},{20... | collective-permute-start | bytes 1081352 | tf_op jit(solution)/shard_map/ppermute | solution.py:320
  64.9 7.4 %collective-permute-start.15 = (bf16[128,1024]{1,0:T(8,128)(2,1)S(1)}, bf16[128,1024]{1,0:T(8,128)(2,1)S(1)}, u32[]{:S(2)}, u32[]{:S(2)}) collective-permute-start(bf16[128,1024]{1,0:T(8,128)(2,1)S(1)} %collective-permute-done.10.refs_4_), channel_id=1, source_target_pairs={{0,2},{1,3},{2,0},{3,1},{4,6},{5,7},{6,4},{7,5},{8,10},{9,11},{10,... | collective-permute-start | bytes 786440 | tf_op jit(solution)/shard_map/ppermute | solution.py:314
  65.5 6.8 %collective-permute-start.16 = (bf16[128,1024]{1,0:T(8,128)(2,1)S(1)}, bf16[128,1024]{1,0:T(8,128)(2,1)S(1)}, u32[]{:S(2)}, u32[]{:S(2)}) collective-permute-start(bf16[128,1024]{1,0:T(8,128)(2,1)S(1)} %collective-permute-done.9.refs_1_), channel_id=1, source_target_pairs={{0,8},{1,9},{2,10},{3,11},{4,0},{5,1},{6,2},{7,3},{12,4},{13,5},{1... | collective-permute-start | bytes 786440 | tf_op jit(solution)/shard_map/ppermute | solution.py:311
  77.1 2.7 %collective-permute-start.19 = (bf16[512,1024]{1,0:T(8,128)(2,1)S(1)}, bf16[512,1024]{1,0:T(8,128)(2,1)S(1)}, u32[]{:S(2)}, u32[]{:S(2)}) collective-permute-start(bf16[512,1024]{1,0:T(8,128)(2,1)S(1)} %get-tuple-element.61), channel_id=1, source_target_pairs={{0,1},{1,0},{2,3},{3,2},{4,5},{5,4},{6,7},{7,6},{8,9},{9,8},{10,11... | collective-permute-start | bytes 3145736 | tf_op jit(solution)/shard_map/ppermute | solution.py:317
  82.9 19.7 %collective-permute-start.21 = (bf16[352,512]{1,0:T(8,128)(2,1)}, bf16[352,512]{1,0:T(8,128)(2,1)}, u32[]{:S(2)}, u32[]{:S(2)}) collective-permute-start(bf16[352,512]{1,0:T(8,128)(2,1)} %get-tuple-element.66), channel_id=1, source_target_pairs={{0,16},{16,0},{1,17},{17,1},{2,18},{18,2},{3,19},{19,3},{4,20},{20... | collective-permute-start | bytes 1081352 | tf_op jit(solution)/shard_map/ppermute | solution.py:320
  84.5 20.0 %collective-permute-start.20 = (bf16[352,512]{1,0:T(8,128)(2,1)}, bf16[352,512]{1,0:T(8,128)(2,1)}, u32[]{:S(2)}, u32[]{:S(2)}) collective-permute-start(bf16[352,512]{1,0:T(8,128)(2,1)} %get-tuple-element.64), channel_id=1, source_target_pairs={{0,16},{16,0},{1,17},{17,1},{2,18},{18,2},{3,19},{19,3},{4,20},{20... | collective-permute-start | bytes 1081352 | tf_op jit(solution)/shard_map/ppermute | solution.py:320
  86.3 14.2 %all-to-all-start = ((f32[16,1,64]{2,1,0:T(1,128)}), f32[16,1,64]{2,1,0:T(1,128)S(1)}, u32[]{:S(2)}, u32[]{:S(2)}) async-start(f32[16,1,64]{2,1,0:T(1,128)} %bitcast.12), calls=%async_computation | async-start | bytes 16384 | tf_op jit(solution)/shard_map/all_to_all | solution.py:505
  (25 other events, 164.7 us)

commit v9 on v8

--- a/solution.py
+++ b/solution.py
@@ -8,7 +8,7 @@
 from jax.sharding import PartitionSpec as P
 
 NZ, NY, NC = 4, 2, 2
-CHUNKS = 2
+CHUNKS = (4, 4)
 PIECES = (2, 2)
 LANES = 128
 NT = (((1,), (1,)), ((), ()))
@@ -199,17 +199,17 @@
         low = low + ref.shape[0]
 
 
-def raw_parts(half, rows_ref, own_ref, got_refs):
+def raw_parts(half, cols, rows_ref, own_ref, got_refs):
     for units, w_ref in weight_parts(half, own_ref, got_refs):
         yield units, lax.dot_general(
-            w_ref[...], rows_ref[...], NT, preferred_element_type=jnp.float32
+            w_ref[:, cols], rows_ref[...], NT, preferred_element_type=jnp.float32
         )
 
 
-def raw_part_kernel(half, capacity, rows_ref, own_ref, *refs):
+def raw_part_kernel(half, capacity, cols, rows_ref, own_ref, *refs):
     *got_refs, hidden_ref, raw_ref, back_ref = refs
     total = jnp.zeros((1, rows_ref.shape[0]), jnp.float32)
-    for units, raw in raw_parts(half, rows_ref, own_ref, got_refs):
+    for units, raw in raw_parts(half, cols, rows_ref, own_ref, got_refs):
         raw_ref[units, :] = raw
         total += jnp.sum(
             raw * hidden_ref[units, :].astype(jnp.float32), axis=0, keepdims=True
@@ -220,18 +220,18 @@
         back_ref[to, :] = total[:, i * capacity : (i + 1) * capacity]
 
 
-def raw_kernel(half, rows_ref, own_ref, *refs):
+def raw_kernel(half, cols, rows_ref, own_ref, *refs):
     *got_refs, sum_ref, gates_ref, grad_ref = refs
-    for units, raw in raw_parts(half, rows_ref, own_ref, got_refs):
+    for units, raw in raw_parts(half, cols, rows_ref, own_ref, got_refs):
         grad_ref[units, :] = ((raw + sum_ref[units, :]) * gates_ref[...]).astype(jnp.bfloat16)
 
 
-def forward_kernel(half, own_ref, *refs):
+def forward_kernel(half, cols, own_ref, *refs):
     *got_refs, hidden_ref, out_ref = refs
     out_ref[...] = sum(
         lax.dot_general(
             hidden_ref[units, :],
-            w_ref[...],
+            w_ref[:, cols],
             (((0,), (0,)), ((), ())),
             preferred_element_type=jnp.float32,
         )
@@ -276,10 +276,14 @@
         out_ref[k : k + 1, :] = jnp.sum(jnp.where(hit, by_expert, 0.0), axis=0, keepdims=True)
 
 
-def finish_kernel(own_ref, got_ref, *refs):
-    refs[-1][...] = (
+def finish_kernel(low, own_ref, got_ref, *refs):
+    out_hbm, sum_ref, sem = refs[-3:]
+    sum_ref[...] = (
         own_ref[...].astype(jnp.float32) + got_ref[...].astype(jnp.float32)
     ).astype(jnp.bfloat16)
+    copy = pltpu.make_async_copy(sum_ref, out_hbm.at[:, pl.ds(low, sum_ref.shape[1])], sem)
+    copy.start()
+    copy.wait()
 
 
 def ring_shards(grad_out, gates, routes, hidden, down_weight):
@@ -289,18 +293,17 @@
     slots, units = hidden.shape[2:]
     half = down_weight.shape[1]
     capacity = slots // experts
-    width = model // CHUNKS
+    widths = [model // 8 * n for n in CHUNKS]
+    columns = [slice(0, widths[0]), slice(widths[0], model)]
     tile = 256
     bf16, f32 = jnp.bfloat16, jnp.float32
     shape = jax.ShapeDtypeStruct
     hidden_t = hidden[0, 0].T
     routes_t, gates_t = routes.T, gates.T
     weight = down_weight[0]
-    columns = [pl.BlockSpec((half, width), lambda i, c=c: (0, c)) for c in range(CHUNKS)]
     split = half // 32 * 16
-    parts = [
-        [pl.BlockSpec((n, width), lambda i, c=c: (0, c)) for n in (split, half - split)]
-        for c in range(CHUNKS)
+    weight_specs = [
+        pl.BlockSpec((n, model), lambda i: (0, 0)) for n in (half, split, half - split)
     ]
     dma = pltpu.SemaphoreType.DMA
 
@@ -324,8 +327,8 @@
 
     def pack():
         return pl.pallas_call(
-            functools.partial(pack_kernel, experts, width),
-            out_shape=shape((tokens, width + tokens), bf16),
+            functools.partial(pack_kernel, experts, widths[0]),
+            out_shape=shape((tokens, widths[0] + tokens), bf16),
             in_specs=[ANY] * 3,
             out_specs=VMEM,
             scratch_shapes=[
@@ -337,10 +340,10 @@
             name="pack",
         )(routes_t, gates_t, grad_out)
 
-    def later_pack(c, after):
-        return pl.pallas_call(
-            functools.partial(later_pack_kernel, c * width),
-            out_shape=shape((tokens, width), bf16),
+    def later_pack(after):
+        return pl.pallas_call(
+            functools.partial(later_pack_kernel, widths[0]),
+            out_shape=shape((tokens, widths[1]), bf16),
             in_specs=[ANY] * 2,
             out_specs=VMEM,
             scratch_shapes=[dma],
@@ -348,14 +351,12 @@
             name="later_pack",
         )(grad_out, after)
 
-    mine_shape = shape((slots // 2, width), bf16)
-
     def first_pick(blocks):
         return pl.pallas_call(
             functools.partial(first_pick_kernel, experts, capacity),
             out_shape=[
-                mine_shape,
-                shape((slots // 2 + 16, width), bf16),
+                shape((slots // 2, widths[0]), bf16),
+                shape((slots // 2 + 16, widths[0]), bf16),
                 shape((slots, tokens), bf16),
                 shape((experts // 2, 2 * capacity), f32),
             ],
@@ -370,7 +371,7 @@
     def later_pick(blocks, pmat):
         return pl.pallas_call(
             pick_kernel,
-            out_shape=[mine_shape] * 2,
+            out_shape=[shape((slots // 2, widths[1]), bf16)] * 2,
             in_specs=[VMEM] * (len(blocks) + 1),
             out_specs=[VMEM] * 2,
             compiler_params=params(24),
@@ -378,8 +379,8 @@
         )(*blocks, pmat)
 
     def product_shapes(c):
-        piece = shape((half, width // PIECES[c]), bf16)
-        return [shape((slots, width), bf16)] + [piece] * (2 * PIECES[c])
+        piece = shape((half, widths[c] // PIECES[c]), bf16)
+        return [shape((slots, widths[c]), bf16)] + [piece] * (2 * PIECES[c])
 
     def first_products(mine, got, gslot):
         slot_gates, hs, rows, *halves = pl.pallas_call(
@@ -405,15 +406,15 @@
         return rows, halves[: PIECES[1]], halves[PIECES[1] :]
 
     by_slot = pl.BlockSpec((units, tile), lambda i: (0, i))
-    some_rows = pl.BlockSpec((tile, width), lambda i: (i, 0))
+    by_row = [pl.BlockSpec((tile, n), lambda i: (i, 0)) for n in widths]
     back_shape = shape((experts, capacity), f32)
 
     def raw_part(rows, got_weight):
         return pl.pallas_call(
-            functools.partial(raw_part_kernel, half, capacity),
+            functools.partial(raw_part_kernel, half, capacity, columns[0]),
             grid=(slots // tile,),
             out_shape=[shape((units, slots), f32), back_shape],
-            in_specs=[some_rows, columns[0], *parts[0], by_slot],
+            in_specs=[by_row[0], *weight_specs, by_slot],
             out_specs=[by_slot, pl.BlockSpec((experts, capacity), lambda i: (0, 0))],
             compiler_params=params(24),
             cost_estimate=cost(3),
@@ -422,30 +423,29 @@
 
     def raw_rest(rows, got_weight, raw, slot_gates):
         return pl.pallas_call(
-            functools.partial(raw_kernel, half),
+            functools.partial(raw_kernel, half, columns[1]),
             grid=(slots // tile,),
             out_shape=shape((units, slots), bf16),
             in_specs=[
-                some_rows,
-                columns[1],
-                *parts[1],
+                by_row[1],
+                *weight_specs,
                 by_slot,
                 pl.BlockSpec((1, tile), lambda i: (0, i)),
             ],
             out_specs=by_slot,
-            compiler_params=params(24),
+            compiler_params=params(48),
             name="raw",
         )(rows, weight, *got_weight, raw, slot_gates)
 
     def forward_columns(got_weight):
         return pl.pallas_call(
-            functools.partial(forward_kernel, half),
+            functools.partial(forward_kernel, half, columns[1]),
             grid=(slots // tile,),
-            out_shape=shape((slots, width), bf16),
-            in_specs=[columns[1], *parts[1], by_slot],
-            out_specs=some_rows,
-            compiler_params=params(24),
-            cost_estimate=cost(4),
+            out_shape=shape((slots, widths[1]), bf16),
+            in_specs=[*weight_specs, by_slot],
+            out_specs=by_row[1],
+            compiler_params=params(24),
+            cost_estimate=cost(3),
             name="hidden_weight",
         )(weight, *got_weight, hidden_t)
 
@@ -460,46 +460,44 @@
         )(rows, forwarded, part)
 
     def finish(low, own, got, *before):
-        piece = own.shape[1]
-        spec = pl.BlockSpec((half // 2, piece), lambda i: (i, 0))
-        return pl.pallas_call(
-            finish_kernel,
-            grid=(2,),
+        return pl.pallas_call(
+            functools.partial(finish_kernel, low),
             out_shape=shape((half, model), bf16),
-            in_specs=[spec, spec] + [ANY] * len(before),
-            out_specs=pl.BlockSpec((half // 2, piece), lambda i: (i, low // piece)),
+            in_specs=[VMEM] * 2 + [ANY] * len(before),
+            out_specs=ANY,
+            scratch_shapes=[pltpu.VMEM(own.shape, bf16), dma],
             input_output_aliases={2: 0} if before else {},
             compiler_params=params(8),
             name="finish",
         )(own, got, *before)
 
     x0 = pack()
-    w = [swap(weight[:split]), swap(weight[split:])]
-    f0, y0 = forward(x0), across(x0)
-    done = (f0, y0)
-    ff0, yf0 = forward(behind(f0, *done)), across(behind(f0, *done))
-    done = (ff0, yf0)
-    r0, yff0 = backward(behind(x0, *done)), across(behind(ff0, *done))
-    x1 = later_pack(1, ff0)
-    done = (r0, yff0, w[0])
-    f1, yr0 = forward(behind(x1, *done)), across(behind(r0, *done))
-    done = (f1, yr0)
-    ff1, y1 = forward(behind(f1, *done)), across(behind(x1, *done))
-    mine0, theirs0, pmat, gslot = first_pick([x0, y0, f0, yf0, ff0, yff0, r0, behind(yr0, f1, w[1])])
+    later = behind(weight, x0)
+    w = [swap(later[:split]), swap(later[split:])]
+    f0, r0, y0 = forward(x0), backward(x0), across(x0)
+    ff0, yf0 = forward(f0), across(f0)
+    x1 = later_pack(r0)
+    f1, yr0 = forward(x1), across(behind(r0, y0))
+    yff0 = across(behind(ff0, yf0, w[0]))
+    mine0, theirs0, pmat, gslot = first_pick(
+        [x0, y0, f0, yf0, ff0, yff0, r0, behind(yr0, f1, w[1])]
+    )
+    ff1, y1 = forward(f1), across(behind(x1, yr0))
+    r1, yf1 = backward(behind(x1, ff0)), across(behind(f1, yr0))
     got = sibling(theirs0)
-    done = (ff1, y1, mine0)
-    r1, yf1 = backward(behind(x1, *done)), across(behind(f1, *done))
     rows0, send0, own0, slot_gates, hs = first_products(mine0, got, gslot)
     got0 = [swap(part) for part in send0]
-    done = (r1, yf1, rows0)
-    ry1, yff1 = backward(behind(y1, *done)), across(behind(ff1, *done))
+    yff1, ry1 = across(behind(ff1, y1, yf1, r1)), backward(behind(y1, yf1, r1))
     raw, part = raw_part(rows0, w)
     forwarded = forward_columns(w)
     mine1, theirs1 = later_pick(
         [x1, y1, f1, yf1, ff1, yff1, r1, ry1], behind(pmat, raw, forwarded)
     )
-    rows1, send1, own1 = later_products(mine1, sibling(behind(theirs1, *got0)), hs)
-    got1 = [swap(half) for half in send1]
+    grad_weight = finish(0, own0[0], got0[0])
+    grad_weight = finish(widths[0] // 2, own0[1], got0[1], grad_weight)
+    got = sibling(behind(theirs1, *got0))
+    rows1, send1, own1 = later_products(mine1, got, behind(hs, grad_weight))
+    got1 = [swap(part) for part in send1]
 
     back = slot_grads(rows1, forwarded, part)
     returned = lax.all_to_all(back, "expert", split_axis=0, concat_axis=0, tiled=True)
@@ -509,7 +507,7 @@
         out_shape=shape((chosen, tokens), f32),
         in_specs=[
             pl.BlockSpec((chosen, tokens), lambda i: (0, 0)),
-            pl.BlockSpec((2 * experts, tokens), lambda i: (0, width // tokens)),
+            pl.BlockSpec((2 * experts, tokens), lambda i: (0, widths[0] // tokens)),
             pl.BlockSpec((experts, capacity), lambda i: (0, 0)),
         ],
         out_specs=pl.BlockSpec((chosen, tokens), lambda i: (0, 0)),
@@ -517,13 +515,8 @@
     )(routes_t, x0, returned)
 
     grad_hidden = raw_rest(rows1, w, raw, slot_gates)
-    grad_weight, low = (), 0
-    for own, got in zip((*own0, *own1), (*got0, *got1)):
-        if low == 0:
-            own = behind(own, back)
-        grad_weight = (finish(low, own, got, *grad_weight),)
-        low += own.shape[1]
-    grad_weight = grad_weight[0]
+    grad_weight = finish(widths[0], own1[0], got1[0], grad_weight)
+    grad_weight = finish(widths[0] + widths[1] // 2, own1[1], got1[1], grad_weight)
     return grad_weight[None], grad_hidden.T[None, None], grad_gates.T
 
 

time: 107 us -> 103 us (0.963)
  waiting for transfers between devices: 35.2 us -> 24.2 us
  starting transfers between devices: 30.4 us -> 40.4 us
  local copies, waits for them, and re-layouts: 12 us -> 7.84 us
  Pallas kernels: 27.7 us -> 29.1 us
    ppermute x7, waiting for transfers between devices: 14.8 us -> 0.73 us  [across(): return lax.ppermute(x, 'expert', swap_pairs(2))]
    ppermute x4, starting transfers between devices: 5.41 us -> 16.7 us  [forward(): return lax.ppermute(x, 'expert', ring_pairs(1))]
    ppermute x6, waiting for transfers between devices: 9.98 us -> 0.02 us  [swap(): return lax.ppermute(x, 'dp', [(0, 1), (1, 0)])]
    ppermute x4, waiting for transfers between devices: 4.93 us -> 13.3 us  [forward(): return lax.ppermute(x, 'expert', ring_pairs(1))]
    ppermute x3, waiting for transfers between devices: 2.84 us -> 9.22 us  [backward(): return lax.ppermute(x, 'expert', ring_pairs(-1))]
    unnamed x52 -> x34, local copies, waits for them, and re-layouts: 10.6 us -> 6.24 us
    ppermute x2, waiting for transfers between devices: 2.66 us -> 0.96 us  [sibling(): return lax.ppermute(x, 'expert', swap_pairs(1))]
    pallas_call x10, Pallas kernels: 17 us -> 18.4 us  [the longest x4 5.33 us: finish(): pl.pallas_call(functools.partial(finish_kernel, low), out_shape=shape((ha...]
  transfers between devices with their start and end apart: 23 -> 23, of which waited for: 13 -> 7; matrix products, arithmetic and copies ran while one was open for 1% -> 0% of each run, Pallas kernels for 20% -> 22%
where the time goes in v9:
time: 103 us; the launch traced here: 102 us
  starting transfers between devices  40.4 us (39%)
  Pallas kernels  29.1 us (28%)
  waiting for transfers between devices  24.2 us (23%)
  local copies, waits for them, and re-layouts  7.84 us (8%)
    ppermute x4, starting transfers between devices, forward(): return lax.ppermute(x, 'expert', ring_pairs(1))  16.7 us
    ppermute x4, waiting for transfers between devices, forward(): return lax.ppermute(x, 'expert', ring_pairs(1))  13.3 us
    ppermute x3, waiting for transfers between devices, backward(): return lax.ppermute(x, 'expert', ring_pairs(-1))  9.22 us
    ppermute x7, starting transfers between devices, across(): return lax.ppermute(x, 'expert', swap_pairs(2))  8.59 us
    ppermute x6, starting transfers between devices, swap(): return lax.ppermute(x, 'dp', [(0, 1), (1, 0)])  6.75 us
    unnamed x34, local copies, waits for them, and re-layouts  6.24 us
    pallas_call x4, Pallas kernels, finish(): pl.pallas_call(functools.partial(finish_kernel, low), out_shape=shape((ha...  5.33 us
    pallas_call x1, Pallas kernels, raw_rest(): pl.pallas_call(functools.partial(raw_kernel, half, columns[1]), grid=(slo...  5.2 us
  transfers between devices with their start and end apart: 23, of which 7 were waited for; matrix products, arithmetic and copies ran while one was open for 0% of the time, Pallas kernels for 22%

profile of v9, /device:TPU:0, one launch (start us, length us, event | category | flops | bytes accessed | tf_op | source)
XLA Modules:
  0.0 102.5 jit_solution(15518345809907616567)
XLA Ops:
  3.3 1.6 %fusion = (bf16[176,2048]{1,0:T(8,128)(2,1)S(1)}, bf16[176,2048]{1,0:T(8,128)(2,1)S(1)}) fusion(bf16[352,2048]{1,0:T(8,128)(2,1)} %bitcast.15), kind=kLoop, calls=%fused_computation | loop fusion | bytes 2883584 | tf_op jit(solution)/shard_map/slice | solution.py:476
  4.9 3.0 %collective-permute-start.13 = (bf16[176,2048]{1,0:T(8,128)(2,1)S(1)}, bf16[176,2048]{1,0:T(8,128)(2,1)S(1)}, u32[]{:S(2)}, u32[]{:S(2)}) collective-permute-start(bf16[176,2048]{1,0:T(8,128)(2,1)S(1)} %get-tuple-element.68), channel_id=1, source_target_pairs={{0,16},{16,0},{1,17},{17,1},{2,18},{18,2},{3,19},{19,3},{4,20},{20... | collective-permute-start | bytes 2162696 | tf_op jit(solution)/shard_map/ppermute | solution.py:323
  7.9 1.6 %collective-permute-start.7 = (bf16[128,1152]{1,0:T(8,128)(2,1)S(1)}, bf16[128,1152]{1,0:T(8,128)(2,1)S(1)}, u32[]{:S(2)}, u32[]{:S(2)}) collective-permute-start(bf16[128,1152]{1,0:T(8,128)(2,1)S(1)} %pack.1.refs_0_.slots_ref), channel_id=1, source_target_pairs={{0,4},{1,5},{2,6},{3,7},{4,12},{5,13},{6,14},{7,15},{12,8},{13,9},... | collective-permute-start | bytes 884744 | tf_op jit(solution)/shard_map/ppermute | solution.py:311
  12.9 4.8 %collective-permute-done.7.refs_2_ = bf16[128,1152]{1,0:T(8,128)(2,1)S(1)} collective-permute-done((bf16[128,1152]{1,0:T(8,128)(2,1)S(1)}, bf16[128,1152]{1,0:T(8,128)(2,1)S(1)}, u32[]{:S(2)}, u32[]{:S(2)}) %collective-permute-start.7) | collective-permute-done | bytes 294944 | tf_op jit(solution)/shard_map/ppermute | solution.py:311
  19.2 7.6 %collective-permute-start.8 = (bf16[128,1152]{1,0:T(8,128)(2,1)S(1)}, bf16[128,1152]{1,0:T(8,128)(2,1)S(1)}, u32[]{:S(2)}, u32[]{:S(2)}) collective-permute-start(bf16[128,1152]{1,0:T(8,128)(2,1)S(1)} %collective-permute-done.7.refs_2_), channel_id=1, source_target_pairs={{0,4},{1,5},{2,6},{3,7},{4,12},{5,13},{6,14},{7,15},{12,8},{13,9},... | collective-permute-start | bytes 884744 | tf_op jit(solution)/shard_map/ppermute | solution.py:311
  26.8 4.2 %collective-permute-done.8.refs_4_ = bf16[128,1152]{1,0:T(8,128)(2,1)S(1)} collective-permute-done((bf16[128,1152]{1,0:T(8,128)(2,1)S(1)}, bf16[128,1152]{1,0:T(8,128)(2,1)S(1)}, u32[]{:S(2)}, u32[]{:S(2)}) %collective-permute-start.8) | collective-permute-done | bytes 294944 | tf_op jit(solution)/shard_map/ppermute | solution.py:311
  32.5 4.5 %collective-permute-start.4 = (bf16[128,1024]{1,0:T(8,128)(2,1)S(1)}, bf16[128,1024]{1,0:T(8,128)(2,1)S(1)}, u32[]{:S(2)}, u32[]{:S(2)}) collective-permute-start(bf16[128,1024]{1,0:T(8,128)(2,1)S(1)} %later_pack.1.refs_0_), channel_id=1, source_target_pairs={{0,4},{1,5},{2,6},{3,7},{4,12},{5,13},{6,14},{7,15},{12,8},{13,9},... | collective-permute-start | bytes 786440 | tf_op jit(solution)/shard_map/ppermute | solution.py:311
  37.0 4.3 %collective-permute-done.4.refs_2_ = bf16[128,1024]{1,0:T(8,128)(2,1)S(1)} collective-permute-done((bf16[128,1024]{1,0:T(8,128)(2,1)S(1)}, bf16[128,1024]{1,0:T(8,128)(2,1)S(1)}, u32[]{:S(2)}, u32[]{:S(2)}) %collective-permute-start.4) | collective-permute-done | bytes 262176 | tf_op jit(solution)/shard_map/ppermute | solution.py:311
  41.3 1.6 %first_pick.1 = (bf16[512,1024]{1,0:T(8,128)(2,1)S(1)}, bf16[528,1024]{1,0:T(8,128)(2,1)S(1)}, bf16[1024,128]{1,0:T(8,128)(2,1)S(1)}, f32[8,128]{1,0:T(8,128)S(1)}) custom-call(bf16[128,1152]{1,0:T(8,128)(2,1)S(1)} %pack.1.refs_0_.slots_ref, bf16[128,1152]{1,0:T(8,128)(2,1)S(1)} %collective-permute-done.1.refs_1_, ...), custom_call_target="tpu_custom_call" | custom-call | flops 3000000000 | bytes 9437184 | tf_op jit(solution)/shard_map/first_pick/pallas_call | solution.py:355
  43.0 3.0 %collective-permute-start.6 = (bf16[128,1024]{1,0:T(8,128)(2,1)S(1)}, bf16[128,1024]{1,0:T(8,128)(2,1)S(1)}, u32[]{:S(2)}, u32[]{:S(2)}) collective-permute-start(bf16[128,1024]{1,0:T(8,128)(2,1)S(1)} %collective-permute-done.4.refs_2_), channel_id=1, source_target_pairs={{0,4},{1,5},{2,6},{3,7},{4,12},{5,13},{6,14},{7,15},{12,8},{13,9},... | collective-permute-start | bytes 786440 | tf_op jit(solution)/shard_map/ppermute | solution.py:311
  46.6 2.0 %collective-permute-start.3 = (bf16[128,1024]{1,0:T(8,128)(2,1)S(1)}, bf16[128,1024]{1,0:T(8,128)(2,1)S(1)}, u32[]{:S(2)}, u32[]{:S(2)}) collective-permute-start(bf16[128,1024]{1,0:T(8,128)(2,1)S(1)} %later_pack.1.refs_0_), channel_id=1, source_target_pairs={{0,2},{1,3},{2,0},{3,1},{4,6},{5,7},{6,4},{7,5},{8,10},{9,11},{10,... | collective-permute-start | bytes 786440 | tf_op jit(solution)/shard_map/ppermute | solution.py:317
  48.7 3.0 %first_products.1 = (f32[1,1024]{1,0:T(1,128)S(1)}, bf16[704,1024]{1,0:T(8,128)(2,1)S(1)}, bf16[1024,1024]{1,0:T(8,128)(2,1)S(1)}, bf16[352,512]{1,0:T(8,128)(2,...) custom-call(bf16[512,1024]{1,0:T(8,128)(2,1)S(1)} %get-tuple-element.45.mine_ref, ...), custom_call_target="tpu_custom_call" | custom-call | flops 3000000000 | bytes 9437184 | tf_op jit(solution)/shard_map/first_products/pallas_call | solution.py:386
  52.3 6.8 %collective-permute-done.9.refs_6_ = bf16[128,1024]{1,0:T(8,128)(2,1)S(1)} collective-permute-done((bf16[128,1024]{1,0:T(8,128)(2,1)S(1)}, bf16[128,1024]{1,0:T(8,128)(2,1)S(1)}, u32[]{:S(2)}, u32[]{:S(2)}) %collective-permute-start.9) | collective-permute-done | bytes 262176 | tf_op jit(solution)/shard_map/ppermute | solution.py:314
  59.6 3.2 %hidden_weight.1.forward_ref = bf16[1024,1024]{1,0:T(8,128)(2,1)S(1)} custom-call(bf16[352,2048]{1,0:T(8,128)(2,1)S(1)} %bitcast.16, bf16[176,2048]{1,0:T(8,128)(2,1)S(1)} %collective-permute-done.13.refs_0_, bf16[176,2048]{1,0:T(8,128)(2,1)S(1)} %collective-permute-done.15.refs_1_, bf16[704,1024]{1,0:T(8,128)(2,1)S(1)} %bitcast.23), custom_call_target="tpu_custom_call" | custom-call | flops 3000000000 | bytes 9437184 | tf_op jit(solution)/shard_map/hidden_weight/pallas_call | solution.py:441
  62.9 2.1 %collective-permute-start.10 = (bf16[128,1024]{1,0:T(8,128)(2,1)S(1)}, bf16[128,1024]{1,0:T(8,128)(2,1)S(1)}, u32[]{:S(2)}, u32[]{:S(2)}) collective-permute-start(bf16[128,1024]{1,0:T(8,128)(2,1)S(1)} %collective-permute-done.6.refs_4_), channel_id=1, source_target_pairs={{0,2},{1,3},{2,0},{3,1},{4,6},{5,7},{6,4},{7,5},{8,10},{9,11},{10,... | collective-permute-start | bytes 786440 | tf_op jit(solution)/shard_map/ppermute | solution.py:317
  64.9 2.3 %collective-permute-start.11 = (bf16[128,1024]{1,0:T(8,128)(2,1)S(1)}, bf16[128,1024]{1,0:T(8,128)(2,1)S(1)}, u32[]{:S(2)}, u32[]{:S(2)}) collective-permute-start(bf16[128,1024]{1,0:T(8,128)(2,1)S(1)} %collective-permute-done.3.refs_1_), channel_id=1, source_target_pairs={{0,8},{1,9},{2,10},{3,11},{4,0},{5,1},{6,2},{7,3},{12,4},{13,5},{1... | collective-permute-start | bytes 786440 | tf_op jit(solution)/shard_map/ppermute | solution.py:314
  67.2 3.3 %raw_part.1 = (f32[704,1024]{1,0:T(8,128)S(1)}, f32[16,64]{1,0:T(8,128)S(1)}) custom-call(bf16[1024,1024]{1,0:T(8,128)(2,1)S(1)} %get-tuple-element.48.rows_ref, bf16[352,2048]{1,0:T(8,128)(2,1)S(1)} %bitcast.17, bf16[176,2048]{1,0:T(8,128)(2,1)S(1)} %collective-permute-done.13.refs_0_, bf16[176,2048]{1,0:T(8,128)(2,1)S(1)} %collective-permute-done.15.refs_1_, ...), custom_call_target="tpu_custom_call" | custom-call | flops 3000000000 | bytes 9437184 | tf_op jit(solution)/shard_map/raw_part/pallas_call | solution.py:413
  71.2 2.4 %collective-permute-done.11.refs_7_ = bf16[128,1024]{1,0:T(8,128)(2,1)S(1)} collective-permute-done((bf16[128,1024]{1,0:T(8,128)(2,1)S(1)}, bf16[128,1024]{1,0:T(8,128)(2,1)S(1)}, u32[]{:S(2)}, u32[]{:S(2)}) %collective-permute-start.11) | collective-permute-done | bytes 262176 | tf_op jit(solution)/shard_map/ppermute | solution.py:314
  77.6 3.2 %products.1 = (bf16[1024,1024]{1,0:T(8,128)(2,1)S(1)}, bf16[352,512]{1,0:T(8,128)(2,1)}, bf16[352,512]{1,0:T(8,128)(2,1)}, bf16[352,512]{1,0:T(8,128)(2,1)S(1)}, bf16[352,512]{1,0:T(8,128)(2,1)S(1)}) custom-call(bf16[512,1024]{1,0:T(8,128)(2,1)S(1)} %get-tuple-element.51.mine_ref, bf16[512,1024]{1,0:T(8,128)(2,1)S(1)} %collective-permute-done.19.got_ref, ...), custom_call_target="tpu_custom_call" | custom-call | tf_op jit(solution)/shard_map/products/pallas_call | solution.py:398
  84.1 4.0 %all-to-all-start = ((f32[16,1,64]{2,1,0:T(1,128)}), f32[16,1,64]{2,1,0:T(1,128)S(1)}, u32[]{:S(2)}, u32[]{:S(2)}) async-start(f32[16,1,64]{2,1,0:T(1,128)} %bitcast.10), calls=%async_computation | async-start | bytes 16384 | tf_op jit(solution)/shard_map/all_to_all | solution.py:503
  90.4 5.2 %raw.1 = bf16[704,1024]{1,0:T(8,128)(2,1)} custom-call(bf16[1024,1024]{1,0:T(8,128)(2,1)S(1)} %get-tuple-element.64.rows_ref, bf16[352,2048]{1,0:T(8,128)(2,1)S(1)} %bitcast.18, bf16[176,2048]{1,0:T(8,128)(2,1)S(1)} %copy-done.6, bf16[176,2048]{1,0:T(8,128)(2,1)S(1)} %copy-done.8, f32[704,1024]{1,0:T(8,128)} %copy-done.1, ...), custom_call_target="tpu_custom_call" | custom-call | tf_op jit(solution)/shard_map/raw/pallas_call | solution.py:425
  96.2 1.6 %grad_gates.1 = f32[6,128]{1,0:T(8,128)} custom-call(s32[6,128]{1,0:T(8,128)} %bitcast.19, bf16[128,1152]{1,0:T(8,128)(2,1)} %copy-done.4, f32[16,64]{1,0:T(8,128)} %bitcast.27), custom_call_target="tpu_custom_call" | custom-call | tf_op jit(solution)/shard_map/grad_gates/pallas_call | solution.py:504
  98.8 1.9 %finish.6.refs_0_ = bf16[352,2048]{1,0:T(8,128)(2,1)} custom-call(bf16[352,512]{1,0:T(8,128)(2,1)S(1)} %copy-done.12, bf16[352,512]{1,0:T(8,128)(2,1)} %collective-permute-done.21.got_ref, bf16[352,2048]{1,0:T(8,128)(2,1)} %finish.5.refs_0_), custom_call_target="tpu_custom_call", output_to_operand_aliasing={{}: (2, {})} | custom-call | tf_op jit(solution)/shard_map/finish/pallas_call | solution.py:463
  100.6 1.8 %finish.7 = bf16[352,2048]{1,0:T(8,128)(2,1)} custom-call(bf16[352,512]{1,0:T(8,128)(2,1)S(1)} %copy-done.10, bf16[352,512]{1,0:T(8,128)(2,1)} %collective-permute-done.20.got_ref, bf16[352,2048]{1,0:T(8,128)(2,1)} %finish.6.refs_0_), custom_call_target="tpu_custom_call", output_to_operand_aliasing={{}: (2, {})} | custom-call | tf_op jit(solution)/shard_map/finish/pallas_call | solution.py:463
  (72 shorter events, 22.6 us)
Async XLA Ops:
  3.2 38.1 %copy-start.4 = (bf16[128,1152]{1,0:T(8,128)(2,1)}, bf16[128,1152]{1,0:T(8,128)(2,1)S(1)}, u32[]{:S(2)}) copy-start(bf16[128,1152]{1,0:T(8,128)(2,1)S(1)} %pack.1.refs_0_.slots_ref) | copy-start | bytes 884740
  4.9 26.2 %collective-permute-start.13 = (bf16[176,2048]{1,0:T(8,128)(2,1)S(1)}, bf16[176,2048]{1,0:T(8,128)(2,1)S(1)}, u32[]{:S(2)}, u32[]{:S(2)}) collective-permute-start(bf16[176,2048]{1,0:T(8,128)(2,1)S(1)} %get-tuple-element.68), channel_id=1, source_target_pairs={{0,16},{16,0},{1,17},{17,1},{2,18},{18,2},{3,19},{19,3},{4,20},{20... | collective-permute-start | bytes 2162696 | tf_op jit(solution)/shard_map/ppermute | solution.py:323
  7.9 9.8 %collective-permute-start.7 = (bf16[128,1152]{1,0:T(8,128)(2,1)S(1)}, bf16[128,1152]{1,0:T(8,128)(2,1)S(1)}, u32[]{:S(2)}, u32[]{:S(2)}) collective-permute-start(bf16[128,1152]{1,0:T(8,128)(2,1)S(1)} %pack.1.refs_0_.slots_ref), channel_id=1, source_target_pairs={{0,4},{1,5},{2,6},{3,7},{4,12},{5,13},{6,14},{7,15},{12,8},{13,9},... | collective-permute-start | bytes 884744 | tf_op jit(solution)/shard_map/ppermute | solution.py:311
  9.5 9.7 %collective-permute-start.1 = (bf16[128,1152]{1,0:T(8,128)(2,1)S(1)}, bf16[128,1152]{1,0:T(8,128)(2,1)S(1)}, u32[]{:S(2)}, u32[]{:S(2)}) collective-permute-start(bf16[128,1152]{1,0:T(8,128)(2,1)S(1)} %pack.1.refs_0_.slots_ref), channel_id=1, source_target_pairs={{0,2},{1,3},{2,0},{3,1},{4,6},{5,7},{6,4},{7,5},{8,10},{9,11},{10,... | collective-permute-start | bytes 884744 | tf_op jit(solution)/shard_map/ppermute | solution.py:317
  11.0 30.3 %collective-permute-start.15 = (bf16[176,2048]{1,0:T(8,128)(2,1)S(1)}, bf16[176,2048]{1,0:T(8,128)(2,1)S(1)}, u32[]{:S(2)}, u32[]{:S(2)}) collective-permute-start(bf16[176,2048]{1,0:T(8,128)(2,1)S(1)} %get-tuple-element.67), channel_id=1, source_target_pairs={{0,16},{16,0},{1,17},{17,1},{2,18},{18,2},{3,19},{19,3},{4,20},{20... | collective-permute-start | bytes 2162696 | tf_op jit(solution)/shard_map/ppermute | solution.py:323
  11.5 15.3 %collective-permute-start = (bf16[128,1152]{1,0:T(8,128)(2,1)S(1)}, bf16[128,1152]{1,0:T(8,128)(2,1)S(1)}, u32[]{:S(2)}, u32[]{:S(2)}) collective-permute-start(bf16[128,1152]{1,0:T(8,128)(2,1)S(1)} %pack.1.refs_0_.slots_ref), channel_id=1, source_target_pairs={{0,8},{1,9},{2,10},{3,11},{4,0},{5,1},{6,2},{7,3},{12,4},{13,5},{1... | collective-permute-start | bytes 884744 | tf_op jit(solution)/shard_map/ppermute | solution.py:314
  17.7 9.1 %collective-permute-start.12 = (bf16[128,1152]{1,0:T(8,128)(2,1)S(1)}, bf16[128,1152]{1,0:T(8,128)(2,1)S(1)}, u32[]{:S(2)}, u32[]{:S(2)}) collective-permute-start(bf16[128,1152]{1,0:T(8,128)(2,1)S(1)} %collective-permute-done.7.refs_2_), channel_id=1, source_target_pairs={{0,2},{1,3},{2,0},{3,1},{4,6},{5,7},{6,4},{7,5},{8,10},{9,11},{10,... | collective-permute-start | bytes 884744 | tf_op jit(solution)/shard_map/ppermute | solution.py:317
  19.2 11.8 %collective-permute-start.8 = (bf16[128,1152]{1,0:T(8,128)(2,1)S(1)}, bf16[128,1152]{1,0:T(8,128)(2,1)S(1)}, u32[]{:S(2)}, u32[]{:S(2)}) collective-permute-start(bf16[128,1152]{1,0:T(8,128)(2,1)S(1)} %collective-permute-done.7.refs_2_), channel_id=1, source_target_pairs={{0,4},{1,5},{2,6},{3,7},{4,12},{5,13},{6,14},{7,15},{12,8},{13,9},... | collective-permute-start | bytes 884744 | tf_op jit(solution)/shard_map/ppermute | solution.py:311
  26.8 14.5 %collective-permute-start.2 = (bf16[128,1152]{1,0:T(8,128)(2,1)S(1)}, bf16[128,1152]{1,0:T(8,128)(2,1)S(1)}, u32[]{:S(2)}, u32[]{:S(2)}) collective-permute-start(bf16[128,1152]{1,0:T(8,128)(2,1)S(1)} %collective-permute-done.after_ref.refs_6_), channel_id=1, source_target_pairs={{0,2},{1,3},{2,0},{3,1},{4,6},{5,7},{6,4},{7,5},{8,10},{9,11},{10,... | collective-permute-start | bytes 884744 | tf_op jit(solution)/shard_map/ppermute | solution.py:317
  31.0 10.3 %collective-permute-start.14 = (bf16[128,1152]{1,0:T(8,128)(2,1)S(1)}, bf16[128,1152]{1,0:T(8,128)(2,1)S(1)}, u32[]{:S(2)}, u32[]{:S(2)}) collective-permute-start(bf16[128,1152]{1,0:T(8,128)(2,1)S(1)} %collective-permute-done.8.refs_4_), channel_id=1, source_target_pairs={{0,2},{1,3},{2,0},{3,1},{4,6},{5,7},{6,4},{7,5},{8,10},{9,11},{10,... | collective-permute-start | bytes 884744 | tf_op jit(solution)/shard_map/ppermute | solution.py:317
  32.5 8.8 %collective-permute-start.4 = (bf16[128,1024]{1,0:T(8,128)(2,1)S(1)}, bf16[128,1024]{1,0:T(8,128)(2,1)S(1)}, u32[]{:S(2)}, u32[]{:S(2)}) collective-permute-start(bf16[128,1024]{1,0:T(8,128)(2,1)S(1)} %later_pack.1.refs_0_), channel_id=1, source_target_pairs={{0,4},{1,5},{2,6},{3,7},{4,12},{5,13},{6,14},{7,15},{12,8},{13,9},... | collective-permute-start | bytes 786440 | tf_op jit(solution)/shard_map/ppermute | solution.py:311
  42.9 5.7 %collective-permute-start.16 = (bf16[528,1024]{1,0:T(8,128)(2,1)S(1)}, bf16[528,1024]{1,0:T(8,128)(2,1)S(1)}, u32[]{:S(2)}, u32[]{:S(2)}) collective-permute-start(bf16[528,1024]{1,0:T(8,128)(2,1)S(1)} %get-tuple-element.46), channel_id=1, source_target_pairs={{0,1},{1,0},{2,3},{3,2},{4,5},{5,4},{6,7},{7,6},{8,9},{9,8},{10,11... | collective-permute-start | bytes 3244040 | tf_op jit(solution)/shard_map/ppermute | solution.py:320
  43.0 19.8 %collective-permute-start.6 = (bf16[128,1024]{1,0:T(8,128)(2,1)S(1)}, bf16[128,1024]{1,0:T(8,128)(2,1)S(1)}, u32[]{:S(2)}, u32[]{:S(2)}) collective-permute-start(bf16[128,1024]{1,0:T(8,128)(2,1)S(1)} %collective-permute-done.4.refs_2_), channel_id=1, source_target_pairs={{0,4},{1,5},{2,6},{3,7},{4,12},{5,13},{6,14},{7,15},{12,8},{13,9},... | collective-permute-start | bytes 786440 | tf_op jit(solution)/shard_map/ppermute | solution.py:311
  46.1 13.0 %collective-permute-start.9 = (bf16[128,1024]{1,0:T(8,128)(2,1)S(1)}, bf16[128,1024]{1,0:T(8,128)(2,1)S(1)}, u32[]{:S(2)}, u32[]{:S(2)}) collective-permute-start(bf16[128,1024]{1,0:T(8,128)(2,1)S(1)} %later_pack.1.refs_0_), channel_id=1, source_target_pairs={{0,8},{1,9},{2,10},{3,11},{4,0},{5,1},{6,2},{7,3},{12,4},{13,5},{1... | collective-permute-start | bytes 786440 | tf_op jit(solution)/shard_map/ppermute | solution.py:314
  46.6 16.2 %collective-permute-start.3 = (bf16[128,1024]{1,0:T(8,128)(2,1)S(1)}, bf16[128,1024]{1,0:T(8,128)(2,1)S(1)}, u32[]{:S(2)}, u32[]{:S(2)}) collective-permute-start(bf16[128,1024]{1,0:T(8,128)(2,1)S(1)} %later_pack.1.refs_0_), channel_id=1, source_target_pairs={{0,2},{1,3},{2,0},{3,1},{4,6},{5,7},{6,4},{7,5},{8,10},{9,11},{10,... | collective-permute-start | bytes 786440 | tf_op jit(solution)/shard_map/ppermute | solution.py:317
  48.6 14.2 %collective-permute-start.5 = (bf16[128,1024]{1,0:T(8,128)(2,1)S(1)}, bf16[128,1024]{1,0:T(8,128)(2,1)S(1)}, u32[]{:S(2)}, u32[]{:S(2)}) collective-permute-start(bf16[128,1024]{1,0:T(8,128)(2,1)S(1)} %collective-permute-done.4.refs_2_), channel_id=1, source_target_pairs={{0,2},{1,3},{2,0},{3,1},{4,6},{5,7},{6,4},{7,5},{8,10},{9,11},{10,... | collective-permute-start | bytes 786440 | tf_op jit(solution)/shard_map/ppermute | solution.py:317
  51.6 23.2 %collective-permute-start.17 = (bf16[352,512]{1,0:T(8,128)(2,1)S(1)}, bf16[352,512]{1,0:T(8,128)(2,1)S(1)}, u32[]{:S(2)}, u32[]{:S(2)}) collective-permute-start(bf16[352,512]{1,0:T(8,128)(2,1)S(1)} %get-tuple-element.53), channel_id=1, source_target_pairs={{0,16},{16,0},{1,17},{17,1},{2,18},{18,2},{3,19},{19,3},{4,20},{20... | collective-permute-start | bytes 1081352 | tf_op jit(solution)/shard_map/ppermute | solution.py:323
  59.1 15.8 %collective-permute-start.18 = (bf16[352,512]{1,0:T(8,128)(2,1)S(1)}, bf16[352,512]{1,0:T(8,128)(2,1)S(1)}, u32[]{:S(2)}, u32[]{:S(2)}) collective-permute-start(bf16[352,512]{1,0:T(8,128)(2,1)S(1)} %get-tuple-element.54), channel_id=1, source_target_pairs={{0,16},{16,0},{1,17},{17,1},{2,18},{18,2},{3,19},{19,3},{4,20},{20... | collective-permute-start | bytes 1081352 | tf_op jit(solution)/shard_map/ppermute | solution.py:323
  62.9 8.3 %collective-permute-start.10 = (bf16[128,1024]{1,0:T(8,128)(2,1)S(1)}, bf16[128,1024]{1,0:T(8,128)(2,1)S(1)}, u32[]{:S(2)}, u32[]{:S(2)}) collective-permute-start(bf16[128,1024]{1,0:T(8,128)(2,1)S(1)} %collective-permute-done.6.refs_4_), channel_id=1, source_target_pairs={{0,2},{1,3},{2,0},{3,1},{4,6},{5,7},{6,4},{7,5},{8,10},{9,11},{10,... | collective-permute-start | bytes 786440 | tf_op jit(solution)/shard_map/ppermute | solution.py:317
  64.9 8.7 %collective-permute-start.11 = (bf16[128,1024]{1,0:T(8,128)(2,1)S(1)}, bf16[128,1024]{1,0:T(8,128)(2,1)S(1)}, u32[]{:S(2)}, u32[]{:S(2)}) collective-permute-start(bf16[128,1024]{1,0:T(8,128)(2,1)S(1)} %collective-permute-done.3.refs_1_), channel_id=1, source_target_pairs={{0,8},{1,9},{2,10},{3,11},{4,0},{5,1},{6,2},{7,3},{12,4},{13,5},{1... | collective-permute-start | bytes 786440 | tf_op jit(solution)/shard_map/ppermute | solution.py:314
  74.8 2.7 %collective-permute-start.19 = (bf16[512,1024]{1,0:T(8,128)(2,1)S(1)}, bf16[512,1024]{1,0:T(8,128)(2,1)S(1)}, u32[]{:S(2)}, u32[]{:S(2)}) collective-permute-start(bf16[512,1024]{1,0:T(8,128)(2,1)S(1)} %get-tuple-element.55), channel_id=1, source_target_pairs={{0,1},{1,0},{2,3},{3,2},{4,5},{5,4},{6,7},{7,6},{8,9},{9,8},{10,11... | collective-permute-start | bytes 3145736 | tf_op jit(solution)/shard_map/ppermute | solution.py:320
  80.7 17.0 %collective-permute-start.21 = (bf16[352,512]{1,0:T(8,128)(2,1)}, bf16[352,512]{1,0:T(8,128)(2,1)}, u32[]{:S(2)}, u32[]{:S(2)}) collective-permute-start(bf16[352,512]{1,0:T(8,128)(2,1)} %get-tuple-element.63), channel_id=1, source_target_pairs={{0,16},{16,0},{1,17},{17,1},{2,18},{18,2},{3,19},{19,3},{4,20},{20... | collective-permute-start | bytes 1081352 | tf_op jit(solution)/shard_map/ppermute | solution.py:323
  82.3 18.4 %collective-permute-start.20 = (bf16[352,512]{1,0:T(8,128)(2,1)}, bf16[352,512]{1,0:T(8,128)(2,1)}, u32[]{:S(2)}, u32[]{:S(2)}) collective-permute-start(bf16[352,512]{1,0:T(8,128)(2,1)} %get-tuple-element.61), channel_id=1, source_target_pairs={{0,16},{16,0},{1,17},{17,1},{2,18},{18,2},{3,19},{19,3},{4,20},{20... | collective-permute-start | bytes 1081352 | tf_op jit(solution)/shard_map/ppermute | solution.py:323
  84.1 11.5 %all-to-all-start = ((f32[16,1,64]{2,1,0:T(1,128)}), f32[16,1,64]{2,1,0:T(1,128)S(1)}, u32[]{:S(2)}, u32[]{:S(2)}) async-start(f32[16,1,64]{2,1,0:T(1,128)} %bitcast.10), calls=%async_computation | async-start | bytes 16384 | tf_op jit(solution)/shard_map/all_to_all | solution.py:503
  (16 other events, 138.5 us)

commit v10 on v9

--- a/solution.py
+++ b/solution.py
@@ -43,7 +43,10 @@
     return [(i, i ^ bit) for i in range(NZ * NY * NC)]
 
 
-def pack_kernel(experts, width, routes_hbm, gates_hbm, grad_hbm, out_ref, routes_ref, gates_ref, sems):
+def pack_kernel(experts, width, *refs):
+    routes_hbm, gates_hbm, grad_hbm, weight_hbm, out_ref, low_ref, high_ref, *scratch = refs
+    routes_ref, gates_ref, sems = scratch
+    low = low_ref.shape[0]
     copies = [
         pltpu.make_async_copy(src, dst, sems.at[i])
         for i, (src, dst) in enumerate(
@@ -51,6 +54,8 @@
                 (routes_hbm, routes_ref),
                 (gates_hbm, gates_ref),
                 (grad_hbm.at[:, :width], out_ref.at[:, :width]),
+                (weight_hbm.at[:low], low_ref),
+                (weight_hbm.at[low:], high_ref),
             )
         )
     ]
@@ -81,7 +86,8 @@
     out_ref[:, width:] = jnp.zeros((tokens, tokens), jnp.bfloat16)
     out_ref[:experts, width:] = dense.astype(jnp.bfloat16)
     out_ref[experts : 2 * experts, width:] = slots.astype(jnp.bfloat16)
-    copies[2].wait()
+    for copy in copies[2:]:
+        copy.wait()
 
 
 def later_pack_kernel(low, grad_hbm, after_ref, out_ref, sem):
@@ -276,14 +282,10 @@
         out_ref[k : k + 1, :] = jnp.sum(jnp.where(hit, by_expert, 0.0), axis=0, keepdims=True)
 
 
-def finish_kernel(low, own_ref, got_ref, *refs):
-    out_hbm, sum_ref, sem = refs[-3:]
-    sum_ref[...] = (
+def finish_kernel(own_ref, got_ref, *refs):
+    refs[-1][...] = (
         own_ref[...].astype(jnp.float32) + got_ref[...].astype(jnp.float32)
     ).astype(jnp.bfloat16)
-    copy = pltpu.make_async_copy(sum_ref, out_hbm.at[:, pl.ds(low, sum_ref.shape[1])], sem)
-    copy.start()
-    copy.wait()
 
 
 def ring_shards(grad_out, gates, routes, hidden, down_weight):
@@ -328,17 +330,21 @@
     def pack():
         return pl.pallas_call(
             functools.partial(pack_kernel, experts, widths[0]),
-            out_shape=shape((tokens, widths[0] + tokens), bf16),
-            in_specs=[ANY] * 3,
-            out_specs=VMEM,
+            out_shape=[
+                shape((tokens, widths[0] + tokens), bf16),
+                shape((split, model), bf16),
+                shape((half - split, model), bf16),
+            ],
+            in_specs=[ANY] * 4,
+            out_specs=[VMEM] * 3,
             scratch_shapes=[
                 pltpu.VMEM(routes_t.shape, routes_t.dtype),
                 pltpu.VMEM(gates_t.shape, gates_t.dtype),
-                dma((3,)),
+                dma((5,)),
             ],
             compiler_params=params(48),
             name="pack",
-        )(routes_t, gates_t, grad_out)
+        )(routes_t, gates_t, grad_out, weight)
 
     def later_pack(after):
         return pl.pallas_call(
@@ -433,7 +439,7 @@
                 pl.BlockSpec((1, tile), lambda i: (0, i)),
             ],
             out_specs=by_slot,
-            compiler_params=params(48),
+            compiler_params=params(20),
             name="raw",
         )(rows, weight, *got_weight, raw, slot_gates)
 
@@ -460,20 +466,21 @@
         )(rows, forwarded, part)
 
     def finish(low, own, got, *before):
-        return pl.pallas_call(
-            functools.partial(finish_kernel, low),
+        piece = own.shape[1]
+        spec = pl.BlockSpec((half // 2, piece), lambda i: (i, 0))
+        return pl.pallas_call(
+            finish_kernel,
+            grid=(2,),
             out_shape=shape((half, model), bf16),
-            in_specs=[VMEM] * 2 + [ANY] * len(before),
-            out_specs=ANY,
-            scratch_shapes=[pltpu.VMEM(own.shape, bf16), dma],
+            in_specs=[spec, spec] + [ANY] * len(before),
+            out_specs=pl.BlockSpec((half // 2, piece), lambda i: (i, low // piece)),
             input_output_aliases={2: 0} if before else {},
             compiler_params=params(8),
             name="finish",
         )(own, got, *before)
 
-    x0 = pack()
-    later = behind(weight, x0)
-    w = [swap(later[:split]), swap(later[split:])]
+    x0, *w = pack()
+    w = [swap(part) for part in w]
     f0, r0, y0 = forward(x0), backward(x0), across(x0)
     ff0, yf0 = forward(f0), across(f0)
     x1 = later_pack(r0)
@@ -487,16 +494,15 @@
     got = sibling(theirs0)
     rows0, send0, own0, slot_gates, hs = first_products(mine0, got, gslot)
     got0 = [swap(part) for part in send0]
-    yff1, ry1 = across(behind(ff1, y1, yf1, r1)), backward(behind(y1, yf1, r1))
+    done = (yf1, r1, rows0)
+    yff1, ry1 = across(behind(ff1, y1, *done)), backward(behind(y1, *done))
     raw, part = raw_part(rows0, w)
-    forwarded = forward_columns(w)
     mine1, theirs1 = later_pick(
-        [x1, y1, f1, yf1, ff1, yff1, r1, ry1], behind(pmat, raw, forwarded)
-    )
-    grad_weight = finish(0, own0[0], got0[0])
-    grad_weight = finish(widths[0] // 2, own0[1], got0[1], grad_weight)
+        [x1, y1, f1, yf1, ff1, yff1, r1, ry1], behind(pmat, raw)
+    )
     got = sibling(behind(theirs1, *got0))
-    rows1, send1, own1 = later_products(mine1, got, behind(hs, grad_weight))
+    forwarded = forward_columns([behind(w[0], theirs1), w[1]])
+    rows1, send1, own1 = later_products(mine1, got, behind(hs, forwarded))
     got1 = [swap(part) for part in send1]
 
     back = slot_grads(rows1, forwarded, part)
@@ -515,6 +521,8 @@
     )(routes_t, x0, returned)
 
     grad_hidden = raw_rest(rows1, w, raw, slot_gates)
+    grad_weight = finish(0, behind(own0[0], back), got0[0])
+    grad_weight = finish(widths[0] // 2, own0[1], got0[1], grad_weight)
     grad_weight = finish(widths[0], own1[0], got1[0], grad_weight)
     grad_weight = finish(widths[0] + widths[1] // 2, own1[1], got1[1], grad_weight)
     return grad_weight[None], grad_hidden.T[None, None], grad_gates.T

time: 103 us -> 104 us (level)
  local copies, waits for them, and re-layouts: 7.84 us -> 9.58 us
  starting transfers between devices: 40.4 us -> 42.1 us
  waiting for transfers between devices: 24.2 us -> 22.9 us
  Pallas kernels: 29.1 us -> 28 us
    unnamed x34 -> x54, local copies, waits for them, and re-layouts: 6.24 us -> 9.58 us
    slice x1 -> x0, local copies, waits for them, and re-layouts: 1.6 us -> none  [ring_shards(): w = [swap(later[:split]), swap(later[split:])]]
    pallas_call x1, Pallas kernels: 5.2 us -> 3.67 us  [raw_rest(): pl.pallas_call(functools.partial(raw_kernel, half, columns[1]), grid=(slo...]
    all_to_all x1, starting transfers between devices: 4.03 us -> 5.45 us  [ring_shards(): lax.all_to_all(back, 'expert', split_axis=0, concat_axis=0, tiled=True)]
  transfers between devices with their start and end apart: 23 -> 23, of which waited for: 7 -> 6; matrix products, arithmetic and copies ran while one was open for 0% -> 0% of each run, Pallas kernels for 22% -> 20%
where the time goes in v10:
time: 104 us; the launch traced here: 103 us
  starting transfers between devices  42.1 us (40%)
  Pallas kernels  28 us (27%)
  waiting for transfers between devices  22.9 us (22%)
  local copies, waits for them, and re-layouts  9.58 us (9%)
    ppermute x4, starting transfers between devices, forward(): return lax.ppermute(x, 'expert', ring_pairs(1))  16.7 us
    ppermute x4, waiting for transfers between devices, forward(): return lax.ppermute(x, 'expert', ring_pairs(1))  13.3 us
    unnamed x54, local copies, waits for them, and re-layouts  9.58 us
    ppermute x3, waiting for transfers between devices, backward(): return lax.ppermute(x, 'expert', ring_pairs(-1))  8.34 us
    ppermute x7, starting transfers between devices, across(): return lax.ppermute(x, 'expert', swap_pairs(2))  8.27 us
    ppermute x6, starting transfers between devices, swap(): return lax.ppermute(x, 'dp', [(0, 1), (1, 0)])  6.67 us
    all_to_all x1, starting transfers between devices, ring_shards(): lax.all_to_all(back, 'expert', split_axis=0, concat_axis=0, tiled=True)  5.45 us
    pallas_call x4, Pallas kernels, finish(): pl.pallas_call(finish_kernel, grid=(2,), out_shape=shape((half, model), b...  5.1 us
  transfers between devices with their start and end apart: 23, of which 6 were waited for; matrix products, arithmetic and copies ran while one was open for 0% of the time, Pallas kernels for 20%

profile of v10, /device:TPU:0, one launch (start us, length us, event | category | flops | bytes accessed | tf_op | source)
XLA Modules:
  0.0 103.4 jit_solution(1714946318682294087)
XLA Ops:
  5.2 3.0 %collective-permute-start.11 = (bf16[176,2048]{1,0:T(8,128)(2,1)S(1)}, bf16[176,2048]{1,0:T(8,128)(2,1)S(1)}, u32[]{:S(2)}, u32[]{:S(2)}) collective-permute-start(bf16[176,2048]{1,0:T(8,128)(2,1)S(1)} %get-tuple-element.44), channel_id=1, source_target_pairs={{0,16},{16,0},{1,17},{17,1},{2,18},{18,2},{3,19},{19,3},{4,20},{20... | collective-permute-start | bytes 2162696 | tf_op jit(solution)/shard_map/ppermute | solution.py:325
  8.2 1.6 %collective-permute-start.7 = (bf16[128,1152]{1,0:T(8,128)(2,1)S(1)}, bf16[128,1152]{1,0:T(8,128)(2,1)S(1)}, u32[]{:S(2)}, u32[]{:S(2)}) collective-permute-start(bf16[128,1152]{1,0:T(8,128)(2,1)S(1)} %get-tuple-element.39.refs_0_.slots_ref), channel_id=1, source_target_pairs={{0,4},{1,5},{2,6},{3,7},{4,12},{5,13},{6,14},{7,15},{12,8},{13,9},... | collective-permute-start | bytes 884744 | tf_op jit(solution)/shard_map/ppermute | solution.py:313
  13.2 4.8 %collective-permute-done.7.refs_2_ = bf16[128,1152]{1,0:T(8,128)(2,1)S(1)} collective-permute-done((bf16[128,1152]{1,0:T(8,128)(2,1)S(1)}, bf16[128,1152]{1,0:T(8,128)(2,1)S(1)}, u32[]{:S(2)}, u32[]{:S(2)}) %collective-permute-start.7) | collective-permute-done | bytes 294944 | tf_op jit(solution)/shard_map/ppermute | solution.py:313
  19.5 7.6 %collective-permute-start.8 = (bf16[128,1152]{1,0:T(8,128)(2,1)S(1)}, bf16[128,1152]{1,0:T(8,128)(2,1)S(1)}, u32[]{:S(2)}, u32[]{:S(2)}) collective-permute-start(bf16[128,1152]{1,0:T(8,128)(2,1)S(1)} %collective-permute-done.7.refs_2_), channel_id=1, source_target_pairs={{0,4},{1,5},{2,6},{3,7},{4,12},{5,13},{6,14},{7,15},{12,8},{13,9},... | collective-permute-start | bytes 884744 | tf_op jit(solution)/shard_map/ppermute | solution.py:313
  27.1 4.2 %collective-permute-done.8.refs_4_ = bf16[128,1152]{1,0:T(8,128)(2,1)S(1)} collective-permute-done((bf16[128,1152]{1,0:T(8,128)(2,1)S(1)}, bf16[128,1152]{1,0:T(8,128)(2,1)S(1)}, u32[]{:S(2)}, u32[]{:S(2)}) %collective-permute-start.8) | collective-permute-done | bytes 294944 | tf_op jit(solution)/shard_map/ppermute | solution.py:313
  32.8 4.5 %collective-permute-start.4 = (bf16[128,1024]{1,0:T(8,128)(2,1)S(1)}, bf16[128,1024]{1,0:T(8,128)(2,1)S(1)}, u32[]{:S(2)}, u32[]{:S(2)}) collective-permute-start(bf16[128,1024]{1,0:T(8,128)(2,1)S(1)} %later_pack.1.refs_0_), channel_id=1, source_target_pairs={{0,4},{1,5},{2,6},{3,7},{4,12},{5,13},{6,14},{7,15},{12,8},{13,9},... | collective-permute-start | bytes 786440 | tf_op jit(solution)/shard_map/ppermute | solution.py:313
  37.4 4.3 %collective-permute-done.4.refs_2_ = bf16[128,1024]{1,0:T(8,128)(2,1)S(1)} collective-permute-done((bf16[128,1024]{1,0:T(8,128)(2,1)S(1)}, bf16[128,1024]{1,0:T(8,128)(2,1)S(1)}, u32[]{:S(2)}, u32[]{:S(2)}) %collective-permute-start.4) | collective-permute-done | bytes 262176 | tf_op jit(solution)/shard_map/ppermute | solution.py:313
  41.7 1.6 %first_pick.1 = (bf16[512,1024]{1,0:T(8,128)(2,1)S(1)}, bf16[528,1024]{1,0:T(8,128)(2,1)S(1)}, bf16[1024,128]{1,0:T(8,128)(2,1)S(1)}, f32[8,128]{1,0:T(8,128)S(1)}) custom-call(bf16[128,1152]{1,0:T(8,128)(2,1)S(1)} %get-tuple-element.39.refs_0_.slots_ref, bf16[128,1152]{1,0:T(8,128)(2,1)S(1)} %collective-permute-done.1.refs_1_, ...), custom_call_target="tpu_custom_call" | custom-call | flops 3000000000 | bytes 9437184 | tf_op jit(solution)/shard_map/first_pick/pallas_call | solution.py:361
  43.4 3.0 %collective-permute-start.6 = (bf16[128,1024]{1,0:T(8,128)(2,1)S(1)}, bf16[128,1024]{1,0:T(8,128)(2,1)S(1)}, u32[]{:S(2)}, u32[]{:S(2)}) collective-permute-start(bf16[128,1024]{1,0:T(8,128)(2,1)S(1)} %collective-permute-done.4.refs_2_), channel_id=1, source_target_pairs={{0,4},{1,5},{2,6},{3,7},{4,12},{5,13},{6,14},{7,15},{12,8},{13,9},... | collective-permute-start | bytes 786440 | tf_op jit(solution)/shard_map/ppermute | solution.py:313
  47.0 2.0 %collective-permute-start.3 = (bf16[128,1024]{1,0:T(8,128)(2,1)S(1)}, bf16[128,1024]{1,0:T(8,128)(2,1)S(1)}, u32[]{:S(2)}, u32[]{:S(2)}) collective-permute-start(bf16[128,1024]{1,0:T(8,128)(2,1)S(1)} %later_pack.1.refs_0_), channel_id=1, source_target_pairs={{0,2},{1,3},{2,0},{3,1},{4,6},{5,7},{6,4},{7,5},{8,10},{9,11},{10,... | collective-permute-start | bytes 786440 | tf_op jit(solution)/shard_map/ppermute | solution.py:319
  49.0 3.0 %first_products.1 = (f32[1,1024]{1,0:T(1,128)S(1)}, bf16[704,1024]{1,0:T(8,128)(2,1)S(1)}, bf16[1024,1024]{1,0:T(8,128)(2,1)S(1)}, bf16[352,512]{1,0:T(8,128)(2,...) custom-call(bf16[512,1024]{1,0:T(8,128)(2,1)S(1)} %get-tuple-element.48.mine_ref, ...), custom_call_target="tpu_custom_call" | custom-call | flops 3000000000 | bytes 9437184 | tf_op jit(solution)/shard_map/first_products/pallas_call | solution.py:392
  53.3 6.1 %collective-permute-done.9.refs_6_ = bf16[128,1024]{1,0:T(8,128)(2,1)S(1)} collective-permute-done((bf16[128,1024]{1,0:T(8,128)(2,1)S(1)}, bf16[128,1024]{1,0:T(8,128)(2,1)S(1)}, u32[]{:S(2)}, u32[]{:S(2)}) %collective-permute-start.9) | collective-permute-done | bytes 262176 | tf_op jit(solution)/shard_map/ppermute | solution.py:316
  61.1 1.7 %collective-permute-start.15 = (bf16[128,1024]{1,0:T(8,128)(2,1)S(1)}, bf16[128,1024]{1,0:T(8,128)(2,1)S(1)}, u32[]{:S(2)}, u32[]{:S(2)}) collective-permute-start(bf16[128,1024]{1,0:T(8,128)(2,1)S(1)} %collective-permute-done.6.refs_4_), channel_id=1, source_target_pairs={{0,2},{1,3},{2,0},{3,1},{4,6},{5,7},{6,4},{7,5},{8,10},{9,11},{10,... | collective-permute-start | bytes 786440 | tf_op jit(solution)/shard_map/ppermute | solution.py:319
  62.9 2.9 %collective-permute-start.16 = (bf16[128,1024]{1,0:T(8,128)(2,1)S(1)}, bf16[128,1024]{1,0:T(8,128)(2,1)S(1)}, u32[]{:S(2)}, u32[]{:S(2)}) collective-permute-start(bf16[128,1024]{1,0:T(8,128)(2,1)S(1)} %collective-permute-done.3.refs_1_), channel_id=1, source_target_pairs={{0,8},{1,9},{2,10},{3,11},{4,0},{5,1},{6,2},{7,3},{12,4},{13,5},{1... | collective-permute-start | bytes 786440 | tf_op jit(solution)/shard_map/ppermute | solution.py:316
  65.8 3.3 %raw_part.1 = (f32[704,1024]{1,0:T(8,128)S(1)}, f32[16,64]{1,0:T(8,128)S(1)}) custom-call(bf16[1024,1024]{1,0:T(8,128)(2,1)S(1)} %get-tuple-element.51.rows_ref, bf16[352,2048]{1,0:T(8,128)(2,1)S(1)} %bitcast.16, bf16[176,2048]{1,0:T(8,128)(2,1)S(1)} %collective-permute-done.11.refs_0_, bf16[176,2048]{1,0:T(8,128)(2,1)S(1)} %collective-permute-done.13.refs_1_, ...), custom_call_target="tpu_custom_call" | custom-call | flops 3000000000 | bytes 9437184 | tf_op jit(solution)/shard_map/raw_part/pallas_call | solution.py:419
  69.1 2.2 %collective-permute-done.16.refs_7_ = bf16[128,1024]{1,0:T(8,128)(2,1)S(1)} collective-permute-done((bf16[128,1024]{1,0:T(8,128)(2,1)S(1)}, bf16[128,1024]{1,0:T(8,128)(2,1)S(1)}, u32[]{:S(2)}, u32[]{:S(2)}) %collective-permute-start.16) | collective-permute-done | bytes 262176 | tf_op jit(solution)/shard_map/ppermute | solution.py:316
  72.7 3.2 %hidden_weight.1.forward_ref = bf16[1024,1024]{1,0:T(8,128)(2,1)S(1)} custom-call(bf16[352,2048]{1,0:T(8,128)(2,1)S(1)} %bitcast.17, bf16[176,2048]{1,0:T(8,128)(2,1)S(1)} %collective-permute-done.11.refs_0_, bf16[176,2048]{1,0:T(8,128)(2,1)S(1)} %collective-permute-done.13.refs_1_, bf16[704,1024]{1,0:T(8,128)(2,1)S(1)} %bitcast.24), custom_call_target="tpu_custom_call" | custom-call | flops 3000000000 | bytes 9437184 | tf_op jit(solution)/shard_map/hidden_weight/pallas_call | solution.py:447
  76.0 3.2 %products.1 = (bf16[1024,1024]{1,0:T(8,128)(2,1)S(1)}, bf16[352,512]{1,0:T(8,128)(2,1)}, bf16[352,512]{1,0:T(8,128)(2,1)}, bf16[352,512]{1,0:T(8,128)(2,1)S(1)}, bf16[352,512]{1,0:T(8,128)(2,1)S(1)}) custom-call(bf16[512,1024]{1,0:T(8,128)(2,1)S(1)} %get-tuple-element.57.mine_ref, bf16[512,1024]{1,0:T(8,128)(2,1)S(1)} %collective-permute-done.19.got_ref, ...), custom_call_target="tpu_custom_call" | custom-call | tf_op jit(solution)/shard_map/products/pallas_call | solution.py:404
  82.5 5.5 %all-to-all-start = ((f32[16,1,64]{2,1,0:T(1,128)}), f32[16,1,64]{2,1,0:T(1,128)S(1)}, u32[]{:S(2)}, u32[]{:S(2)}) async-start(f32[16,1,64]{2,1,0:T(1,128)} %bitcast.10), calls=%async_computation | async-start | bytes 16384 | tf_op jit(solution)/shard_map/all_to_all | solution.py:509
  88.0 1.8 %copy-done.3 = f32[704,1024]{1,0:T(8,128)S(1)} copy-done((f32[704,1024]{1,0:T(8,128)S(1)}, f32[704,1024]{1,0:T(8,128)}, u32[]{:S(2)}) %copy-start.3) | copy-done | bytes 2883608
  92.0 3.7 %raw.1 = bf16[704,1024]{1,0:T(8,128)(2,1)} custom-call(bf16[1024,1024]{1,0:T(8,128)(2,1)S(1)} %get-tuple-element.71.rows_ref, bf16[352,2048]{1,0:T(8,128)(2,1)S(1)} %bitcast.18, bf16[176,2048]{1,0:T(8,128)(2,1)S(1)} %copy-done.7, bf16[176,2048]{1,0:T(8,128)(2,1)S(1)} %copy-done.9, f32[704,1024]{1,0:T(8,128)S(1)} %copy-done.3, ...), custom_call_target="tpu_custom_call" | custom-call | tf_op jit(solution)/shard_map/raw/pallas_call | solution.py:431
  98.3 1.6 %grad_gates.1 = f32[6,128]{1,0:T(8,128)} custom-call(s32[6,128]{1,0:T(8,128)} %bitcast.19, bf16[128,1152]{1,0:T(8,128)(2,1)} %copy-done.22, f32[16,64]{1,0:T(8,128)} %bitcast.27), custom_call_target="tpu_custom_call" | custom-call | tf_op jit(solution)/shard_map/grad_gates/pallas_call | solution.py:510
  99.9 1.8 %finish.6.refs_0_ = bf16[352,2048]{1,0:T(8,128)(2,1)} custom-call(bf16[352,512]{1,0:T(8,128)(2,1)S(1)} %copy-done.17, bf16[352,512]{1,0:T(8,128)(2,1)} %collective-permute-done.21.got_ref, bf16[352,2048]{1,0:T(8,128)(2,1)} %finish.5.refs_0_), custom_call_target="tpu_custom_call", output_to_operand_aliasing={{}: (2, {})} | custom-call | tf_op jit(solution)/shard_map/finish/pallas_call | solution.py:471
  101.7 1.7 %finish.7 = bf16[352,2048]{1,0:T(8,128)(2,1)} custom-call(bf16[352,512]{1,0:T(8,128)(2,1)S(1)} %copy-done.15, bf16[352,512]{1,0:T(8,128)(2,1)} %collective-permute-done.20.got_ref, bf16[352,2048]{1,0:T(8,128)(2,1)} %finish.6.refs_0_), custom_call_target="tpu_custom_call", output_to_operand_aliasing={{}: (2, {})} | custom-call | tf_op jit(solution)/shard_map/finish/pallas_call | solution.py:471
  (91 shorter events, 24.1 us)
Async XLA Ops:
  5.2 26.2 %collective-permute-start.11 = (bf16[176,2048]{1,0:T(8,128)(2,1)S(1)}, bf16[176,2048]{1,0:T(8,128)(2,1)S(1)}, u32[]{:S(2)}, u32[]{:S(2)}) collective-permute-start(bf16[176,2048]{1,0:T(8,128)(2,1)S(1)} %get-tuple-element.44), channel_id=1, source_target_pairs={{0,16},{16,0},{1,17},{17,1},{2,18},{18,2},{3,19},{19,3},{4,20},{20... | collective-permute-start | bytes 2162696 | tf_op jit(solution)/shard_map/ppermute | solution.py:325
  8.2 9.8 %collective-permute-start.7 = (bf16[128,1152]{1,0:T(8,128)(2,1)S(1)}, bf16[128,1152]{1,0:T(8,128)(2,1)S(1)}, u32[]{:S(2)}, u32[]{:S(2)}) collective-permute-start(bf16[128,1152]{1,0:T(8,128)(2,1)S(1)} %get-tuple-element.39.refs_0_.slots_ref), channel_id=1, source_target_pairs={{0,4},{1,5},{2,6},{3,7},{4,12},{5,13},{6,14},{7,15},{12,8},{13,9},... | collective-permute-start | bytes 884744 | tf_op jit(solution)/shard_map/ppermute | solution.py:313
  9.8 9.7 %collective-permute-start.1 = (bf16[128,1152]{1,0:T(8,128)(2,1)S(1)}, bf16[128,1152]{1,0:T(8,128)(2,1)S(1)}, u32[]{:S(2)}, u32[]{:S(2)}) collective-permute-start(bf16[128,1152]{1,0:T(8,128)(2,1)S(1)} %get-tuple-element.39.refs_0_.slots_ref), channel_id=1, source_target_pairs={{0,2},{1,3},{2,0},{3,1},{4,6},{5,7},{6,4},{7,5},{8,10},{9,11},{10,... | collective-permute-start | bytes 884744 | tf_op jit(solution)/shard_map/ppermute | solution.py:319
  11.3 30.3 %collective-permute-start.13 = (bf16[176,2048]{1,0:T(8,128)(2,1)S(1)}, bf16[176,2048]{1,0:T(8,128)(2,1)S(1)}, u32[]{:S(2)}, u32[]{:S(2)}) collective-permute-start(bf16[176,2048]{1,0:T(8,128)(2,1)S(1)} %get-tuple-element.46), channel_id=1, source_target_pairs={{0,16},{16,0},{1,17},{17,1},{2,18},{18,2},{3,19},{19,3},{4,20},{20... | collective-permute-start | bytes 2162696 | tf_op jit(solution)/shard_map/ppermute | solution.py:325
  11.8 15.3 %collective-permute-start = (bf16[128,1152]{1,0:T(8,128)(2,1)S(1)}, bf16[128,1152]{1,0:T(8,128)(2,1)S(1)}, u32[]{:S(2)}, u32[]{:S(2)}) collective-permute-start(bf16[128,1152]{1,0:T(8,128)(2,1)S(1)} %get-tuple-element.39.refs_0_.slots_ref), channel_id=1, source_target_pairs={{0,8},{1,9},{2,10},{3,11},{4,0},{5,1},{6,2},{7,3},{12,4},{13,5},{1... | collective-permute-start | bytes 884744 | tf_op jit(solution)/shard_map/ppermute | solution.py:316
  18.0 9.1 %collective-permute-start.10 = (bf16[128,1152]{1,0:T(8,128)(2,1)S(1)}, bf16[128,1152]{1,0:T(8,128)(2,1)S(1)}, u32[]{:S(2)}, u32[]{:S(2)}) collective-permute-start(bf16[128,1152]{1,0:T(8,128)(2,1)S(1)} %collective-permute-done.7.refs_2_), channel_id=1, source_target_pairs={{0,2},{1,3},{2,0},{3,1},{4,6},{5,7},{6,4},{7,5},{8,10},{9,11},{10,... | collective-permute-start | bytes 884744 | tf_op jit(solution)/shard_map/ppermute | solution.py:319
  19.5 11.8 %collective-permute-start.8 = (bf16[128,1152]{1,0:T(8,128)(2,1)S(1)}, bf16[128,1152]{1,0:T(8,128)(2,1)S(1)}, u32[]{:S(2)}, u32[]{:S(2)}) collective-permute-start(bf16[128,1152]{1,0:T(8,128)(2,1)S(1)} %collective-permute-done.7.refs_2_), channel_id=1, source_target_pairs={{0,4},{1,5},{2,6},{3,7},{4,12},{5,13},{6,14},{7,15},{12,8},{13,9},... | collective-permute-start | bytes 884744 | tf_op jit(solution)/shard_map/ppermute | solution.py:313
  27.1 14.5 %collective-permute-start.2 = (bf16[128,1152]{1,0:T(8,128)(2,1)S(1)}, bf16[128,1152]{1,0:T(8,128)(2,1)S(1)}, u32[]{:S(2)}, u32[]{:S(2)}) collective-permute-start(bf16[128,1152]{1,0:T(8,128)(2,1)S(1)} %collective-permute-done.after_ref.refs_6_), channel_id=1, source_target_pairs={{0,2},{1,3},{2,0},{3,1},{4,6},{5,7},{6,4},{7,5},{8,10},{9,11},{10,... | collective-permute-start | bytes 884744 | tf_op jit(solution)/shard_map/ppermute | solution.py:319
  31.4 41.3 %copy-start.6 = (bf16[176,2048]{1,0:T(8,128)(2,1)}, bf16[176,2048]{1,0:T(8,128)(2,1)S(1)}, u32[]{:S(2)}) copy-start(bf16[176,2048]{1,0:T(8,128)(2,1)S(1)} %collective-permute-done.11.refs_0_) | copy-start | bytes 2162692
  31.4 10.3 %collective-permute-start.12 = (bf16[128,1152]{1,0:T(8,128)(2,1)S(1)}, bf16[128,1152]{1,0:T(8,128)(2,1)S(1)}, u32[]{:S(2)}, u32[]{:S(2)}) collective-permute-start(bf16[128,1152]{1,0:T(8,128)(2,1)S(1)} %collective-permute-done.8.refs_4_), channel_id=1, source_target_pairs={{0,2},{1,3},{2,0},{3,1},{4,6},{5,7},{6,4},{7,5},{8,10},{9,11},{10,... | collective-permute-start | bytes 884744 | tf_op jit(solution)/shard_map/ppermute | solution.py:319
  32.8 8.8 %collective-permute-start.4 = (bf16[128,1024]{1,0:T(8,128)(2,1)S(1)}, bf16[128,1024]{1,0:T(8,128)(2,1)S(1)}, u32[]{:S(2)}, u32[]{:S(2)}) collective-permute-start(bf16[128,1024]{1,0:T(8,128)(2,1)S(1)} %later_pack.1.refs_0_), channel_id=1, source_target_pairs={{0,4},{1,5},{2,6},{3,7},{4,12},{5,13},{6,14},{7,15},{12,8},{13,9},... | collective-permute-start | bytes 786440 | tf_op jit(solution)/shard_map/ppermute | solution.py:313
  43.3 5.7 %collective-permute-start.14 = (bf16[528,1024]{1,0:T(8,128)(2,1)S(1)}, bf16[528,1024]{1,0:T(8,128)(2,1)S(1)}, u32[]{:S(2)}, u32[]{:S(2)}) collective-permute-start(bf16[528,1024]{1,0:T(8,128)(2,1)S(1)} %get-tuple-element.49), channel_id=1, source_target_pairs={{0,1},{1,0},{2,3},{3,2},{4,5},{5,4},{6,7},{7,6},{8,9},{9,8},{10,11... | collective-permute-start | bytes 3244040 | tf_op jit(solution)/shard_map/ppermute | solution.py:322
  43.4 17.8 %collective-permute-start.6 = (bf16[128,1024]{1,0:T(8,128)(2,1)S(1)}, bf16[128,1024]{1,0:T(8,128)(2,1)S(1)}, u32[]{:S(2)}, u32[]{:S(2)}) collective-permute-start(bf16[128,1024]{1,0:T(8,128)(2,1)S(1)} %collective-permute-done.4.refs_2_), channel_id=1, source_target_pairs={{0,4},{1,5},{2,6},{3,7},{4,12},{5,13},{6,14},{7,15},{12,8},{13,9},... | collective-permute-start | bytes 786440 | tf_op jit(solution)/shard_map/ppermute | solution.py:313
  46.4 13.0 %collective-permute-start.9 = (bf16[128,1024]{1,0:T(8,128)(2,1)S(1)}, bf16[128,1024]{1,0:T(8,128)(2,1)S(1)}, u32[]{:S(2)}, u32[]{:S(2)}) collective-permute-start(bf16[128,1024]{1,0:T(8,128)(2,1)S(1)} %later_pack.1.refs_0_), channel_id=1, source_target_pairs={{0,8},{1,9},{2,10},{3,11},{4,0},{5,1},{6,2},{7,3},{12,4},{13,5},{1... | collective-permute-start | bytes 786440 | tf_op jit(solution)/shard_map/ppermute | solution.py:316
  47.0 13.0 %collective-permute-start.3 = (bf16[128,1024]{1,0:T(8,128)(2,1)S(1)}, bf16[128,1024]{1,0:T(8,128)(2,1)S(1)}, u32[]{:S(2)}, u32[]{:S(2)}) collective-permute-start(bf16[128,1024]{1,0:T(8,128)(2,1)S(1)} %later_pack.1.refs_0_), channel_id=1, source_target_pairs={{0,2},{1,3},{2,0},{3,1},{4,6},{5,7},{6,4},{7,5},{8,10},{9,11},{10,... | collective-permute-start | bytes 786440 | tf_op jit(solution)/shard_map/ppermute | solution.py:319
  49.0 12.2 %collective-permute-start.5 = (bf16[128,1024]{1,0:T(8,128)(2,1)S(1)}, bf16[128,1024]{1,0:T(8,128)(2,1)S(1)}, u32[]{:S(2)}, u32[]{:S(2)}) collective-permute-start(bf16[128,1024]{1,0:T(8,128)(2,1)S(1)} %collective-permute-done.4.refs_2_), channel_id=1, source_target_pairs={{0,2},{1,3},{2,0},{3,1},{4,6},{5,7},{6,4},{7,5},{8,10},{9,11},{10,... | collective-permute-start | bytes 786440 | tf_op jit(solution)/shard_map/ppermute | solution.py:319
  52.7 19.8 %collective-permute-start.17 = (bf16[352,512]{1,0:T(8,128)(2,1)S(1)}, bf16[352,512]{1,0:T(8,128)(2,1)S(1)}, u32[]{:S(2)}, u32[]{:S(2)}) collective-permute-start(bf16[352,512]{1,0:T(8,128)(2,1)S(1)} %get-tuple-element.59), channel_id=1, source_target_pairs={{0,16},{16,0},{1,17},{17,1},{2,18},{18,2},{3,19},{19,3},{4,20},{20... | collective-permute-start | bytes 1081352 | tf_op jit(solution)/shard_map/ppermute | solution.py:325
  59.4 13.1 %collective-permute-start.18 = (bf16[352,512]{1,0:T(8,128)(2,1)S(1)}, bf16[352,512]{1,0:T(8,128)(2,1)S(1)}, u32[]{:S(2)}, u32[]{:S(2)}) collective-permute-start(bf16[352,512]{1,0:T(8,128)(2,1)S(1)} %get-tuple-element.60), channel_id=1, source_target_pairs={{0,16},{16,0},{1,17},{17,1},{2,18},{18,2},{3,19},{19,3},{4,20},{20... | collective-permute-start | bytes 1081352 | tf_op jit(solution)/shard_map/ppermute | solution.py:325
  61.1 8.0 %collective-permute-start.15 = (bf16[128,1024]{1,0:T(8,128)(2,1)S(1)}, bf16[128,1024]{1,0:T(8,128)(2,1)S(1)}, u32[]{:S(2)}, u32[]{:S(2)}) collective-permute-start(bf16[128,1024]{1,0:T(8,128)(2,1)S(1)} %collective-permute-done.6.refs_4_), channel_id=1, source_target_pairs={{0,2},{1,3},{2,0},{3,1},{4,6},{5,7},{6,4},{7,5},{8,10},{9,11},{10,... | collective-permute-start | bytes 786440 | tf_op jit(solution)/shard_map/ppermute | solution.py:319
  62.9 8.4 %collective-permute-start.16 = (bf16[128,1024]{1,0:T(8,128)(2,1)S(1)}, bf16[128,1024]{1,0:T(8,128)(2,1)S(1)}, u32[]{:S(2)}, u32[]{:S(2)}) collective-permute-start(bf16[128,1024]{1,0:T(8,128)(2,1)S(1)} %collective-permute-done.3.refs_1_), channel_id=1, source_target_pairs={{0,8},{1,9},{2,10},{3,11},{4,0},{5,1},{6,2},{7,3},{12,4},{13,5},{1... | collective-permute-start | bytes 786440 | tf_op jit(solution)/shard_map/ppermute | solution.py:316
  72.6 3.4 %collective-permute-start.19 = (bf16[512,1024]{1,0:T(8,128)(2,1)S(1)}, bf16[512,1024]{1,0:T(8,128)(2,1)S(1)}, u32[]{:S(2)}, u32[]{:S(2)}) collective-permute-start(bf16[512,1024]{1,0:T(8,128)(2,1)S(1)} %get-tuple-element.61), channel_id=1, source_target_pairs={{0,1},{1,0},{2,3},{3,2},{4,5},{5,4},{6,7},{7,6},{8,9},{9,8},{10,11... | collective-permute-start | bytes 3145736 | tf_op jit(solution)/shard_map/ppermute | solution.py:322
  79.2 20.7 %collective-permute-start.21 = (bf16[352,512]{1,0:T(8,128)(2,1)}, bf16[352,512]{1,0:T(8,128)(2,1)}, u32[]{:S(2)}, u32[]{:S(2)}) collective-permute-start(bf16[352,512]{1,0:T(8,128)(2,1)} %get-tuple-element.68), channel_id=1, source_target_pairs={{0,16},{16,0},{1,17},{17,1},{2,18},{18,2},{3,19},{19,3},{4,20},{20... | collective-permute-start | bytes 1081352 | tf_op jit(solution)/shard_map/ppermute | solution.py:325
  80.1 21.6 %collective-permute-start.20 = (bf16[352,512]{1,0:T(8,128)(2,1)}, bf16[352,512]{1,0:T(8,128)(2,1)}, u32[]{:S(2)}, u32[]{:S(2)}) collective-permute-start(bf16[352,512]{1,0:T(8,128)(2,1)} %get-tuple-element.66), channel_id=1, source_target_pairs={{0,16},{16,0},{1,17},{17,1},{2,18},{18,2},{3,19},{19,3},{4,20},{20... | collective-permute-start | bytes 1081352 | tf_op jit(solution)/shard_map/ppermute | solution.py:325
  82.5 15.2 %all-to-all-start = ((f32[16,1,64]{2,1,0:T(1,128)}), f32[16,1,64]{2,1,0:T(1,128)S(1)}, u32[]{:S(2)}, u32[]{:S(2)}) async-start(f32[16,1,64]{2,1,0:T(1,128)} %bitcast.10), calls=%async_computation | async-start | bytes 16384 | tf_op jit(solution)/shard_map/all_to_all | solution.py:509
  (26 other events, 190.5 us)

commit v11 on v9

--- a/solution.py
+++ b/solution.py
@@ -9,7 +9,7 @@
 
 NZ, NY, NC = 4, 2, 2
 CHUNKS = (4, 4)
-PIECES = (2, 2)
+PIECES = (2, 1)
 LANES = 128
 NT = (((1,), (1,)), ((), ()))
 VMEM = pl.BlockSpec(memory_space=pltpu.VMEM)
@@ -43,7 +43,8 @@
     return [(i, i ^ bit) for i in range(NZ * NY * NC)]
 
 
-def pack_kernel(experts, width, routes_hbm, gates_hbm, grad_hbm, out_ref, routes_ref, gates_ref, sems):
+def pack_kernel(experts, width, routes_hbm, gates_hbm, grad_hbm, out_ref, *scratch):
+    routes_ref, gates_ref, sems = scratch
     copies = [
         pltpu.make_async_copy(src, dst, sems.at[i])
         for i, (src, dst) in enumerate(
@@ -276,14 +277,10 @@
         out_ref[k : k + 1, :] = jnp.sum(jnp.where(hit, by_expert, 0.0), axis=0, keepdims=True)
 
 
-def finish_kernel(low, own_ref, got_ref, *refs):
-    out_hbm, sum_ref, sem = refs[-3:]
-    sum_ref[...] = (
+def finish_kernel(own_ref, got_ref, *refs):
+    refs[-1][...] = (
         own_ref[...].astype(jnp.float32) + got_ref[...].astype(jnp.float32)
     ).astype(jnp.bfloat16)
-    copy = pltpu.make_async_copy(sum_ref, out_hbm.at[:, pl.ds(low, sum_ref.shape[1])], sem)
-    copy.start()
-    copy.wait()
 
 
 def ring_shards(grad_out, gates, routes, hidden, down_weight):
@@ -433,7 +430,7 @@
                 pl.BlockSpec((1, tile), lambda i: (0, i)),
             ],
             out_specs=by_slot,
-            compiler_params=params(48),
+            compiler_params=params(60),
             name="raw",
         )(rows, weight, *got_weight, raw, slot_gates)
 
@@ -460,20 +457,21 @@
         )(rows, forwarded, part)
 
     def finish(low, own, got, *before):
-        return pl.pallas_call(
-            functools.partial(finish_kernel, low),
+        piece = own.shape[1]
+        spec = pl.BlockSpec((half // 2, piece), lambda i: (i, 0))
+        return pl.pallas_call(
+            finish_kernel,
+            grid=(2,),
             out_shape=shape((half, model), bf16),
-            in_specs=[VMEM] * 2 + [ANY] * len(before),
-            out_specs=ANY,
-            scratch_shapes=[pltpu.VMEM(own.shape, bf16), dma],
+            in_specs=[spec, spec] + [ANY] * len(before),
+            out_specs=pl.BlockSpec((half // 2, piece), lambda i: (i, low // piece)),
             input_output_aliases={2: 0} if before else {},
             compiler_params=params(8),
             name="finish",
         )(own, got, *before)
 
     x0 = pack()
-    later = behind(weight, x0)
-    w = [swap(later[:split]), swap(later[split:])]
+    w = [swap(weight[:split]), swap(weight[split:])]
     f0, r0, y0 = forward(x0), backward(x0), across(x0)
     ff0, yf0 = forward(f0), across(f0)
     x1 = later_pack(r0)
@@ -487,9 +485,10 @@
     got = sibling(theirs0)
     rows0, send0, own0, slot_gates, hs = first_products(mine0, got, gslot)
     got0 = [swap(part) for part in send0]
-    yff1, ry1 = across(behind(ff1, y1, yf1, r1)), backward(behind(y1, yf1, r1))
+    done = (yf1, r1, rows0)
+    yff1, ry1 = across(behind(ff1, y1, *done)), backward(behind(y1, *done))
+    forwarded = forward_columns(w)
     raw, part = raw_part(rows0, w)
-    forwarded = forward_columns(w)
     mine1, theirs1 = later_pick(
         [x1, y1, f1, yf1, ff1, yff1, r1, ry1], behind(pmat, raw, forwarded)
     )
@@ -516,7 +515,6 @@
 
     grad_hidden = raw_rest(rows1, w, raw, slot_gates)
     grad_weight = finish(widths[0], own1[0], got1[0], grad_weight)
-    grad_weight = finish(widths[0] + widths[1] // 2, own1[1], got1[1], grad_weight)
     return grad_weight[None], grad_hidden.T[None, None], grad_gates.T
 
 

time: 103 us -> 98.1 us (0.952)
  local copies, waits for them, and re-layouts: 7.84 us -> 2.14 us
  waiting for transfers between devices: 24.2 us -> 27 us
  Pallas kernels: 29.1 us -> 27.9 us
    unnamed x34 -> x24, local copies, waits for them, and re-layouts: 6.24 us -> 0.64 us
    pallas_call x4 -> x3, Pallas kernels: 5.33 us -> 2.52 us  [finish(): pl.pallas_call(finish_kernel, grid=(2,), out_shape=shape((half, model), b...]
    ppermute x6 -> x5, waiting for transfers between devices: 0.02 us -> 2.67 us  [swap(): return lax.ppermute(x, 'dp', [(0, 1), (1, 0)])]
    pallas_call x1, Pallas kernels: 5.2 us -> 6.68 us  [raw_rest(): pl.pallas_call(functools.partial(raw_kernel, half, columns[1]), grid=(slo...]
    ppermute x6 -> x5, starting transfers between devices: 6.75 us -> 6.21 us  [swap(): return lax.ppermute(x, 'dp', [(0, 1), (1, 0)])]
  transfers between devices with their start and end apart: 23 -> 22, of which waited for: 7 -> 8; matrix products, arithmetic and copies ran while one was open for 0% -> 0% of each run, Pallas kernels for 22% -> 23%
where the time goes in v11:
time: 98.1 us; the launch traced here: 97.8 us
  starting transfers between devices  39.9 us (41%)
  Pallas kernels  27.9 us (28%)
  waiting for transfers between devices  27 us (28%)
  local copies, waits for them, and re-layouts  2.14 us (2%)
    ppermute x4, starting transfers between devices, forward(): return lax.ppermute(x, 'expert', ring_pairs(1))  16.8 us
    ppermute x4, waiting for transfers between devices, forward(): return lax.ppermute(x, 'expert', ring_pairs(1))  13.3 us
    ppermute x3, waiting for transfers between devices, backward(): return lax.ppermute(x, 'expert', ring_pairs(-1))  9.21 us
    ppermute x7, starting transfers between devices, across(): return lax.ppermute(x, 'expert', swap_pairs(2))  8.6 us
    pallas_call x1, Pallas kernels, raw_rest(): pl.pallas_call(functools.partial(raw_kernel, half, columns[1]), grid=(slo...  6.68 us
    ppermute x5, starting transfers between devices, swap(): return lax.ppermute(x, 'dp', [(0, 1), (1, 0)])  6.21 us
    ppermute x3, starting transfers between devices, backward(): return lax.ppermute(x, 'expert', ring_pairs(-1))  4.17 us
    all_to_all x1, starting transfers between devices, ring_shards(): lax.all_to_all(back, 'expert', split_axis=0, concat_axis=0, tiled=True)  4.02 us
  transfers between devices with their start and end apart: 22, of which 8 were waited for; matrix products, arithmetic and copies ran while one was open for 0% of the time, Pallas kernels for 23%

profile of v11, /device:TPU:0, one launch (start us, length us, event | category | flops | bytes accessed | tf_op | source)
XLA Modules:
  0.0 97.8 jit_solution(10605248019672731571)
XLA Ops:
  2.2 3.0 %collective-permute-start.11 = (bf16[176,2048]{1,0:T(8,128)(2,1)S(1)}, bf16[176,2048]{1,0:T(8,128)(2,1)S(1)}, u32[]{:S(2)}, u32[]{:S(2)}) collective-permute-start(bf16[176,2048]{1,0:T(8,128)(2,1)S(1)} %get-tuple-element.62), channel_id=1, source_target_pairs={{0,16},{16,0},{1,17},{17,1},{2,18},{18,2},{3,19},{19,3},{4,20},{20... | collective-permute-start | bytes 2162696 | tf_op jit(solution)/shard_map/ppermute | solution.py:320
  5.4 1.6 %collective-permute-start.7 = (bf16[128,1152]{1,0:T(8,128)(2,1)S(1)}, bf16[128,1152]{1,0:T(8,128)(2,1)S(1)}, u32[]{:S(2)}, u32[]{:S(2)}) collective-permute-start(bf16[128,1152]{1,0:T(8,128)(2,1)S(1)} %pack.1.refs_0_.slots_ref), channel_id=1, source_target_pairs={{0,4},{1,5},{2,6},{3,7},{4,12},{5,13},{6,14},{7,15},{12,8},{13,9},... | collective-permute-start | bytes 884744 | tf_op jit(solution)/shard_map/ppermute | solution.py:308
  7.0 1.5 %collective-permute-start.1 = (bf16[128,1152]{1,0:T(8,128)(2,1)S(1)}, bf16[128,1152]{1,0:T(8,128)(2,1)S(1)}, u32[]{:S(2)}, u32[]{:S(2)}) collective-permute-start(bf16[128,1152]{1,0:T(8,128)(2,1)S(1)} %pack.1.refs_0_.slots_ref), channel_id=1, source_target_pairs={{0,2},{1,3},{2,0},{3,1},{4,6},{5,7},{6,4},{7,5},{8,10},{9,11},{10,... | collective-permute-start | bytes 884744 | tf_op jit(solution)/shard_map/ppermute | solution.py:314
  10.4 4.8 %collective-permute-done.7.refs_2_ = bf16[128,1152]{1,0:T(8,128)(2,1)S(1)} collective-permute-done((bf16[128,1152]{1,0:T(8,128)(2,1)S(1)}, bf16[128,1152]{1,0:T(8,128)(2,1)S(1)}, u32[]{:S(2)}, u32[]{:S(2)}) %collective-permute-start.7) | collective-permute-done | bytes 294944 | tf_op jit(solution)/shard_map/ppermute | solution.py:308
  15.2 1.5 %collective-permute-start.10 = (bf16[128,1152]{1,0:T(8,128)(2,1)S(1)}, bf16[128,1152]{1,0:T(8,128)(2,1)S(1)}, u32[]{:S(2)}, u32[]{:S(2)}) collective-permute-start(bf16[128,1152]{1,0:T(8,128)(2,1)S(1)} %collective-permute-done.7.refs_2_), channel_id=1, source_target_pairs={{0,2},{1,3},{2,0},{3,1},{4,6},{5,7},{6,4},{7,5},{8,10},{9,11},{10,... | collective-permute-start | bytes 884744 | tf_op jit(solution)/shard_map/ppermute | solution.py:314
  16.8 7.6 %collective-permute-start.8 = (bf16[128,1152]{1,0:T(8,128)(2,1)S(1)}, bf16[128,1152]{1,0:T(8,128)(2,1)S(1)}, u32[]{:S(2)}, u32[]{:S(2)}) collective-permute-start(bf16[128,1152]{1,0:T(8,128)(2,1)S(1)} %collective-permute-done.7.refs_2_), channel_id=1, source_target_pairs={{0,4},{1,5},{2,6},{3,7},{4,12},{5,13},{6,14},{7,15},{12,8},{13,9},... | collective-permute-start | bytes 884744 | tf_op jit(solution)/shard_map/ppermute | solution.py:308
  24.4 4.2 %collective-permute-done.8.refs_4_ = bf16[128,1152]{1,0:T(8,128)(2,1)S(1)} collective-permute-done((bf16[128,1152]{1,0:T(8,128)(2,1)S(1)}, bf16[128,1152]{1,0:T(8,128)(2,1)S(1)}, u32[]{:S(2)}, u32[]{:S(2)}) %collective-permute-start.8) | collective-permute-done | bytes 294944 | tf_op jit(solution)/shard_map/ppermute | solution.py:308
  30.1 4.5 %collective-permute-start.4 = (bf16[128,1024]{1,0:T(8,128)(2,1)S(1)}, bf16[128,1024]{1,0:T(8,128)(2,1)S(1)}, u32[]{:S(2)}, u32[]{:S(2)}) collective-permute-start(bf16[128,1024]{1,0:T(8,128)(2,1)S(1)} %later_pack.1.refs_0_), channel_id=1, source_target_pairs={{0,4},{1,5},{2,6},{3,7},{4,12},{5,13},{6,14},{7,15},{12,8},{13,9},... | collective-permute-start | bytes 786440 | tf_op jit(solution)/shard_map/ppermute | solution.py:308
  34.6 4.3 %collective-permute-done.4.refs_2_ = bf16[128,1024]{1,0:T(8,128)(2,1)S(1)} collective-permute-done((bf16[128,1024]{1,0:T(8,128)(2,1)S(1)}, bf16[128,1024]{1,0:T(8,128)(2,1)S(1)}, u32[]{:S(2)}, u32[]{:S(2)}) %collective-permute-start.4) | collective-permute-done | bytes 262176 | tf_op jit(solution)/shard_map/ppermute | solution.py:308
  38.9 1.6 %first_pick.1 = (bf16[512,1024]{1,0:T(8,128)(2,1)S(1)}, bf16[528,1024]{1,0:T(8,128)(2,1)S(1)}, bf16[1024,128]{1,0:T(8,128)(2,1)S(1)}, f32[8,128]{1,0:T(8,128)S(1)}) custom-call(bf16[128,1152]{1,0:T(8,128)(2,1)S(1)} %pack.1.refs_0_.slots_ref, bf16[128,1152]{1,0:T(8,128)(2,1)S(1)} %collective-permute-done.1.refs_1_, ...), custom_call_target="tpu_custom_call" | custom-call | flops 3000000000 | bytes 9437184 | tf_op jit(solution)/shard_map/first_pick/pallas_call | solution.py:352
  40.6 3.0 %collective-permute-start.6 = (bf16[128,1024]{1,0:T(8,128)(2,1)S(1)}, bf16[128,1024]{1,0:T(8,128)(2,1)S(1)}, u32[]{:S(2)}, u32[]{:S(2)}) collective-permute-start(bf16[128,1024]{1,0:T(8,128)(2,1)S(1)} %collective-permute-done.4.refs_2_), channel_id=1, source_target_pairs={{0,4},{1,5},{2,6},{3,7},{4,12},{5,13},{6,14},{7,15},{12,8},{13,9},... | collective-permute-start | bytes 786440 | tf_op jit(solution)/shard_map/ppermute | solution.py:308
  44.2 2.0 %collective-permute-start.3 = (bf16[128,1024]{1,0:T(8,128)(2,1)S(1)}, bf16[128,1024]{1,0:T(8,128)(2,1)S(1)}, u32[]{:S(2)}, u32[]{:S(2)}) collective-permute-start(bf16[128,1024]{1,0:T(8,128)(2,1)S(1)} %later_pack.1.refs_0_), channel_id=1, source_target_pairs={{0,2},{1,3},{2,0},{3,1},{4,6},{5,7},{6,4},{7,5},{8,10},{9,11},{10,... | collective-permute-start | bytes 786440 | tf_op jit(solution)/shard_map/ppermute | solution.py:314
  46.2 3.0 %first_products.1 = (f32[1,1024]{1,0:T(1,128)S(1)}, bf16[704,1024]{1,0:T(8,128)(2,1)S(1)}, bf16[1024,1024]{1,0:T(8,128)(2,1)S(1)}, bf16[352,512]{1,0:T(8,128)(2,...) custom-call(bf16[512,1024]{1,0:T(8,128)(2,1)S(1)} %get-tuple-element.38.mine_ref, ...), custom_call_target="tpu_custom_call" | custom-call | flops 3000000000 | bytes 9437184 | tf_op jit(solution)/shard_map/first_products/pallas_call | solution.py:383
  49.8 6.8 %collective-permute-done.9.refs_6_ = bf16[128,1024]{1,0:T(8,128)(2,1)S(1)} collective-permute-done((bf16[128,1024]{1,0:T(8,128)(2,1)S(1)}, bf16[128,1024]{1,0:T(8,128)(2,1)S(1)}, u32[]{:S(2)}, u32[]{:S(2)}) %collective-permute-start.9) | collective-permute-done | bytes 262176 | tf_op jit(solution)/shard_map/ppermute | solution.py:311
  57.2 3.2 %hidden_weight.1.forward_ref = bf16[1024,1024]{1,0:T(8,128)(2,1)S(1)} custom-call(bf16[352,2048]{1,0:T(8,128)(2,1)S(1)} %bitcast.20, bf16[176,2048]{1,0:T(8,128)(2,1)S(1)} %collective-permute-done.11.refs_0_, bf16[176,2048]{1,0:T(8,128)(2,1)S(1)} %collective-permute-done.13.refs_1_, bf16[704,1024]{1,0:T(8,128)(2,1)S(1)} %bitcast.26), custom_call_target="tpu_custom_call" | custom-call | flops 3000000000 | bytes 9437184 | tf_op jit(solution)/shard_map/hidden_weight/pallas_call | solution.py:438
  60.4 2.1 %collective-permute-start.15 = (bf16[128,1024]{1,0:T(8,128)(2,1)S(1)}, bf16[128,1024]{1,0:T(8,128)(2,1)S(1)}, u32[]{:S(2)}, u32[]{:S(2)}) collective-permute-start(bf16[128,1024]{1,0:T(8,128)(2,1)S(1)} %collective-permute-done.6.refs_4_), channel_id=1, source_target_pairs={{0,2},{1,3},{2,0},{3,1},{4,6},{5,7},{6,4},{7,5},{8,10},{9,11},{10,... | collective-permute-start | bytes 786440 | tf_op jit(solution)/shard_map/ppermute | solution.py:314
  62.5 2.3 %collective-permute-start.16 = (bf16[128,1024]{1,0:T(8,128)(2,1)S(1)}, bf16[128,1024]{1,0:T(8,128)(2,1)S(1)}, u32[]{:S(2)}, u32[]{:S(2)}) collective-permute-start(bf16[128,1024]{1,0:T(8,128)(2,1)S(1)} %collective-permute-done.3.refs_1_), channel_id=1, source_target_pairs={{0,8},{1,9},{2,10},{3,11},{4,0},{5,1},{6,2},{7,3},{12,4},{13,5},{1... | collective-permute-start | bytes 786440 | tf_op jit(solution)/shard_map/ppermute | solution.py:311
  64.8 3.3 %raw_part.1 = (f32[704,1024]{1,0:T(8,128)S(1)}, f32[16,64]{1,0:T(8,128)S(1)}) custom-call(bf16[1024,1024]{1,0:T(8,128)(2,1)S(1)} %get-tuple-element.41.rows_ref, bf16[352,2048]{1,0:T(8,128)(2,1)S(1)} %bitcast.21, bf16[176,2048]{1,0:T(8,128)(2,1)S(1)} %collective-permute-done.11.refs_0_, bf16[176,2048]{1,0:T(8,128)(2,1)S(1)} %collective-permute-done.13.refs_1_, ...), custom_call_target="tpu_custom_call" | custom-call | flops 3000000000 | bytes 9437184 | tf_op jit(solution)/shard_map/raw_part/pallas_call | solution.py:410
  68.8 2.4 %collective-permute-done.16.refs_7_ = bf16[128,1024]{1,0:T(8,128)(2,1)S(1)} collective-permute-done((bf16[128,1024]{1,0:T(8,128)(2,1)S(1)}, bf16[128,1024]{1,0:T(8,128)(2,1)S(1)}, u32[]{:S(2)}, u32[]{:S(2)}) %collective-permute-start.16) | collective-permute-done | bytes 262176 | tf_op jit(solution)/shard_map/ppermute | solution.py:311
  75.1 3.3 %products.1 = (bf16[1024,1024]{1,0:T(8,128)(2,1)S(1)}, bf16[352,1024]{1,0:T(8,128)(2,1)}, bf16[352,1024]{1,0:T(8,128)(2,1)S(1)}) custom-call(bf16[512,1024]{1,0:T(8,128)(2,1)S(1)} %get-tuple-element.47.mine_ref, bf16[512,1024]{1,0:T(8,128)(2,1)S(1)} %collective-permute-done.19.got_ref, bf16[704,1024]{1,0:T(8,128)(2,1)S(1)} %get-tuple-element.55.hs_ref), custom_call_target="tpu_custom_call" | custom-call | tf_op jit(solution)/shard_map/products/pallas_call | solution.py:395
  81.3 4.0 %all-to-all-start = ((f32[16,1,64]{2,1,0:T(1,128)}), f32[16,1,64]{2,1,0:T(1,128)S(1)}, u32[]{:S(2)}, u32[]{:S(2)}) async-start(f32[16,1,64]{2,1,0:T(1,128)} %bitcast.12), calls=%async_computation | async-start | bytes 16384 | tf_op jit(solution)/shard_map/all_to_all | solution.py:502
  85.3 6.7 %raw.1 = bf16[704,1024]{1,0:T(8,128)(2,1)} custom-call(bf16[1024,1024]{1,0:T(8,128)(2,1)} %copy-done, bf16[352,2048]{1,0:T(8,128)(2,1)} %bitcast.19, bf16[176,2048]{1,0:T(8,128)(2,1)} %copy-done.5, bf16[176,2048]{1,0:T(8,128)(2,1)} %copy-done.6, f32[704,1024]{1,0:T(8,128)} %copy-done.2, f32[1,1024]{1,0:T(1,128)} %copy-done.8), custom_call_target="tpu_custom_call" | custom-call | tf_op jit(solution)/shard_map/raw/pallas_call | solution.py:422
  92.6 1.6 %grad_gates.1 = f32[6,128]{1,0:T(8,128)} custom-call(s32[6,128]{1,0:T(8,128)} %bitcast.22, bf16[128,1152]{1,0:T(8,128)(2,1)} %copy-done.4, f32[16,64]{1,0:T(8,128)} %bitcast.30), custom_call_target="tpu_custom_call" | custom-call | tf_op jit(solution)/shard_map/grad_gates/pallas_call | solution.py:503
  94.2 2.7 %collective-permute-done.20.got_ref = bf16[352,1024]{1,0:T(8,128)(2,1)S(1)} collective-permute-done((bf16[352,1024]{1,0:T(8,128)(2,1)}, bf16[352,1024]{1,0:T(8,128)(2,1)S(1)}, u32[]{:S(2)}, u32[]{:S(2)}) %collective-permute-start.20) | collective-permute-done | bytes 720928 | tf_op jit(solution)/shard_map/ppermute | solution.py:320
  (59 shorter events, 15.9 us)
Async XLA Ops:
  2.2 26.4 %collective-permute-start.11 = (bf16[176,2048]{1,0:T(8,128)(2,1)S(1)}, bf16[176,2048]{1,0:T(8,128)(2,1)S(1)}, u32[]{:S(2)}, u32[]{:S(2)}) collective-permute-start(bf16[176,2048]{1,0:T(8,128)(2,1)S(1)} %get-tuple-element.62), channel_id=1, source_target_pairs={{0,16},{16,0},{1,17},{17,1},{2,18},{18,2},{3,19},{19,3},{4,20},{20... | collective-permute-start | bytes 2162696 | tf_op jit(solution)/shard_map/ppermute | solution.py:320
  5.4 35.1 %copy-start.4 = (bf16[128,1152]{1,0:T(8,128)(2,1)}, bf16[128,1152]{1,0:T(8,128)(2,1)S(1)}, u32[]{:S(2)}) copy-start(bf16[128,1152]{1,0:T(8,128)(2,1)S(1)} %pack.1.refs_0_.slots_ref) | copy-start | bytes 884740
  5.4 9.8 %collective-permute-start.7 = (bf16[128,1152]{1,0:T(8,128)(2,1)S(1)}, bf16[128,1152]{1,0:T(8,128)(2,1)S(1)}, u32[]{:S(2)}, u32[]{:S(2)}) collective-permute-start(bf16[128,1152]{1,0:T(8,128)(2,1)S(1)} %pack.1.refs_0_.slots_ref), channel_id=1, source_target_pairs={{0,4},{1,5},{2,6},{3,7},{4,12},{5,13},{6,14},{7,15},{12,8},{13,9},... | collective-permute-start | bytes 884744 | tf_op jit(solution)/shard_map/ppermute | solution.py:308
  7.0 9.7 %collective-permute-start.1 = (bf16[128,1152]{1,0:T(8,128)(2,1)S(1)}, bf16[128,1152]{1,0:T(8,128)(2,1)S(1)}, u32[]{:S(2)}, u32[]{:S(2)}) collective-permute-start(bf16[128,1152]{1,0:T(8,128)(2,1)S(1)} %pack.1.refs_0_.slots_ref), channel_id=1, source_target_pairs={{0,2},{1,3},{2,0},{3,1},{4,6},{5,7},{6,4},{7,5},{8,10},{9,11},{10,... | collective-permute-start | bytes 884744 | tf_op jit(solution)/shard_map/ppermute | solution.py:314
  8.5 30.3 %collective-permute-start.13 = (bf16[176,2048]{1,0:T(8,128)(2,1)S(1)}, bf16[176,2048]{1,0:T(8,128)(2,1)S(1)}, u32[]{:S(2)}, u32[]{:S(2)}) collective-permute-start(bf16[176,2048]{1,0:T(8,128)(2,1)S(1)} %get-tuple-element.61), channel_id=1, source_target_pairs={{0,16},{16,0},{1,17},{17,1},{2,18},{18,2},{3,19},{19,3},{4,20},{20... | collective-permute-start | bytes 2162696 | tf_op jit(solution)/shard_map/ppermute | solution.py:320
  9.1 15.3 %collective-permute-start = (bf16[128,1152]{1,0:T(8,128)(2,1)S(1)}, bf16[128,1152]{1,0:T(8,128)(2,1)S(1)}, u32[]{:S(2)}, u32[]{:S(2)}) collective-permute-start(bf16[128,1152]{1,0:T(8,128)(2,1)S(1)} %pack.1.refs_0_.slots_ref), channel_id=1, source_target_pairs={{0,8},{1,9},{2,10},{3,11},{4,0},{5,1},{6,2},{7,3},{12,4},{13,5},{1... | collective-permute-start | bytes 884744 | tf_op jit(solution)/shard_map/ppermute | solution.py:311
  15.2 9.1 %collective-permute-start.10 = (bf16[128,1152]{1,0:T(8,128)(2,1)S(1)}, bf16[128,1152]{1,0:T(8,128)(2,1)S(1)}, u32[]{:S(2)}, u32[]{:S(2)}) collective-permute-start(bf16[128,1152]{1,0:T(8,128)(2,1)S(1)} %collective-permute-done.7.refs_2_), channel_id=1, source_target_pairs={{0,2},{1,3},{2,0},{3,1},{4,6},{5,7},{6,4},{7,5},{8,10},{9,11},{10,... | collective-permute-start | bytes 884744 | tf_op jit(solution)/shard_map/ppermute | solution.py:314
  16.8 11.8 %collective-permute-start.8 = (bf16[128,1152]{1,0:T(8,128)(2,1)S(1)}, bf16[128,1152]{1,0:T(8,128)(2,1)S(1)}, u32[]{:S(2)}, u32[]{:S(2)}) collective-permute-start(bf16[128,1152]{1,0:T(8,128)(2,1)S(1)} %collective-permute-done.7.refs_2_), channel_id=1, source_target_pairs={{0,4},{1,5},{2,6},{3,7},{4,12},{5,13},{6,14},{7,15},{12,8},{13,9},... | collective-permute-start | bytes 884744 | tf_op jit(solution)/shard_map/ppermute | solution.py:308
  24.3 14.5 %collective-permute-start.2 = (bf16[128,1152]{1,0:T(8,128)(2,1)S(1)}, bf16[128,1152]{1,0:T(8,128)(2,1)S(1)}, u32[]{:S(2)}, u32[]{:S(2)}) collective-permute-start(bf16[128,1152]{1,0:T(8,128)(2,1)S(1)} %collective-permute-done.after_ref.refs_6_), channel_id=1, source_target_pairs={{0,2},{1,3},{2,0},{3,1},{4,6},{5,7},{6,4},{7,5},{8,10},{9,11},{10,... | collective-permute-start | bytes 884744 | tf_op jit(solution)/shard_map/ppermute | solution.py:314
  28.6 36.2 %copy-start.5 = (bf16[176,2048]{1,0:T(8,128)(2,1)}, bf16[176,2048]{1,0:T(8,128)(2,1)S(1)}, u32[]{:S(2)}) copy-start(bf16[176,2048]{1,0:T(8,128)(2,1)S(1)} %collective-permute-done.11.refs_0_) | copy-start | bytes 2162692
  28.6 10.3 %collective-permute-start.12 = (bf16[128,1152]{1,0:T(8,128)(2,1)S(1)}, bf16[128,1152]{1,0:T(8,128)(2,1)S(1)}, u32[]{:S(2)}, u32[]{:S(2)}) collective-permute-start(bf16[128,1152]{1,0:T(8,128)(2,1)S(1)} %collective-permute-done.8.refs_4_), channel_id=1, source_target_pairs={{0,2},{1,3},{2,0},{3,1},{4,6},{5,7},{6,4},{7,5},{8,10},{9,11},{10,... | collective-permute-start | bytes 884744 | tf_op jit(solution)/shard_map/ppermute | solution.py:314
  30.1 8.8 %collective-permute-start.4 = (bf16[128,1024]{1,0:T(8,128)(2,1)S(1)}, bf16[128,1024]{1,0:T(8,128)(2,1)S(1)}, u32[]{:S(2)}, u32[]{:S(2)}) collective-permute-start(bf16[128,1024]{1,0:T(8,128)(2,1)S(1)} %later_pack.1.refs_0_), channel_id=1, source_target_pairs={{0,4},{1,5},{2,6},{3,7},{4,12},{5,13},{6,14},{7,15},{12,8},{13,9},... | collective-permute-start | bytes 786440 | tf_op jit(solution)/shard_map/ppermute | solution.py:308
  40.5 5.7 %collective-permute-start.14 = (bf16[528,1024]{1,0:T(8,128)(2,1)S(1)}, bf16[528,1024]{1,0:T(8,128)(2,1)S(1)}, u32[]{:S(2)}, u32[]{:S(2)}) collective-permute-start(bf16[528,1024]{1,0:T(8,128)(2,1)S(1)} %get-tuple-element.39), channel_id=1, source_target_pairs={{0,1},{1,0},{2,3},{3,2},{4,5},{5,4},{6,7},{7,6},{8,9},{9,8},{10,11... | collective-permute-start | bytes 3244040 | tf_op jit(solution)/shard_map/ppermute | solution.py:317
  40.6 19.8 %collective-permute-start.6 = (bf16[128,1024]{1,0:T(8,128)(2,1)S(1)}, bf16[128,1024]{1,0:T(8,128)(2,1)S(1)}, u32[]{:S(2)}, u32[]{:S(2)}) collective-permute-start(bf16[128,1024]{1,0:T(8,128)(2,1)S(1)} %collective-permute-done.4.refs_2_), channel_id=1, source_target_pairs={{0,4},{1,5},{2,6},{3,7},{4,12},{5,13},{6,14},{7,15},{12,8},{13,9},... | collective-permute-start | bytes 786440 | tf_op jit(solution)/shard_map/ppermute | solution.py:308
  43.6 13.0 %collective-permute-start.9 = (bf16[128,1024]{1,0:T(8,128)(2,1)S(1)}, bf16[128,1024]{1,0:T(8,128)(2,1)S(1)}, u32[]{:S(2)}, u32[]{:S(2)}) collective-permute-start(bf16[128,1024]{1,0:T(8,128)(2,1)S(1)} %later_pack.1.refs_0_), channel_id=1, source_target_pairs={{0,8},{1,9},{2,10},{3,11},{4,0},{5,1},{6,2},{7,3},{12,4},{13,5},{1... | collective-permute-start | bytes 786440 | tf_op jit(solution)/shard_map/ppermute | solution.py:311
  44.2 16.2 %collective-permute-start.3 = (bf16[128,1024]{1,0:T(8,128)(2,1)S(1)}, bf16[128,1024]{1,0:T(8,128)(2,1)S(1)}, u32[]{:S(2)}, u32[]{:S(2)}) collective-permute-start(bf16[128,1024]{1,0:T(8,128)(2,1)S(1)} %later_pack.1.refs_0_), channel_id=1, source_target_pairs={{0,2},{1,3},{2,0},{3,1},{4,6},{5,7},{6,4},{7,5},{8,10},{9,11},{10,... | collective-permute-start | bytes 786440 | tf_op jit(solution)/shard_map/ppermute | solution.py:314
  46.2 14.2 %collective-permute-start.5 = (bf16[128,1024]{1,0:T(8,128)(2,1)S(1)}, bf16[128,1024]{1,0:T(8,128)(2,1)S(1)}, u32[]{:S(2)}, u32[]{:S(2)}) collective-permute-start(bf16[128,1024]{1,0:T(8,128)(2,1)S(1)} %collective-permute-done.4.refs_2_), channel_id=1, source_target_pairs={{0,2},{1,3},{2,0},{3,1},{4,6},{5,7},{6,4},{7,5},{8,10},{9,11},{10,... | collective-permute-start | bytes 786440 | tf_op jit(solution)/shard_map/ppermute | solution.py:314
  49.2 23.2 %collective-permute-start.17 = (bf16[352,512]{1,0:T(8,128)(2,1)S(1)}, bf16[352,512]{1,0:T(8,128)(2,1)S(1)}, u32[]{:S(2)}, u32[]{:S(2)}) collective-permute-start(bf16[352,512]{1,0:T(8,128)(2,1)S(1)} %get-tuple-element.49), channel_id=1, source_target_pairs={{0,16},{16,0},{1,17},{17,1},{2,18},{18,2},{3,19},{19,3},{4,20},{20... | collective-permute-start | bytes 1081352 | tf_op jit(solution)/shard_map/ppermute | solution.py:320
  56.6 15.8 %collective-permute-start.18 = (bf16[352,512]{1,0:T(8,128)(2,1)S(1)}, bf16[352,512]{1,0:T(8,128)(2,1)S(1)}, u32[]{:S(2)}, u32[]{:S(2)}) collective-permute-start(bf16[352,512]{1,0:T(8,128)(2,1)S(1)} %get-tuple-element.50), channel_id=1, source_target_pairs={{0,16},{16,0},{1,17},{17,1},{2,18},{18,2},{3,19},{19,3},{4,20},{20... | collective-permute-start | bytes 1081352 | tf_op jit(solution)/shard_map/ppermute | solution.py:320
  60.4 8.3 %collective-permute-start.15 = (bf16[128,1024]{1,0:T(8,128)(2,1)S(1)}, bf16[128,1024]{1,0:T(8,128)(2,1)S(1)}, u32[]{:S(2)}, u32[]{:S(2)}) collective-permute-start(bf16[128,1024]{1,0:T(8,128)(2,1)S(1)} %collective-permute-done.6.refs_4_), channel_id=1, source_target_pairs={{0,2},{1,3},{2,0},{3,1},{4,6},{5,7},{6,4},{7,5},{8,10},{9,11},{10,... | collective-permute-start | bytes 786440 | tf_op jit(solution)/shard_map/ppermute | solution.py:314
  62.5 8.7 %collective-permute-start.16 = (bf16[128,1024]{1,0:T(8,128)(2,1)S(1)}, bf16[128,1024]{1,0:T(8,128)(2,1)S(1)}, u32[]{:S(2)}, u32[]{:S(2)}) collective-permute-start(bf16[128,1024]{1,0:T(8,128)(2,1)S(1)} %collective-permute-done.3.refs_1_), channel_id=1, source_target_pairs={{0,8},{1,9},{2,10},{3,11},{4,0},{5,1},{6,2},{7,3},{12,4},{13,5},{1... | collective-permute-start | bytes 786440 | tf_op jit(solution)/shard_map/ppermute | solution.py:311
  72.4 2.7 %collective-permute-start.19 = (bf16[512,1024]{1,0:T(8,128)(2,1)S(1)}, bf16[512,1024]{1,0:T(8,128)(2,1)S(1)}, u32[]{:S(2)}, u32[]{:S(2)}) collective-permute-start(bf16[512,1024]{1,0:T(8,128)(2,1)S(1)} %get-tuple-element.51), channel_id=1, source_target_pairs={{0,1},{1,0},{2,3},{3,2},{4,5},{5,4},{6,7},{7,6},{8,9},{9,8},{10,11... | collective-permute-start | bytes 3145736 | tf_op jit(solution)/shard_map/ppermute | solution.py:317
  78.5 18.4 %collective-permute-start.20 = (bf16[352,1024]{1,0:T(8,128)(2,1)}, bf16[352,1024]{1,0:T(8,128)(2,1)S(1)}, u32[]{:S(2)}, u32[]{:S(2)}) collective-permute-start(bf16[352,1024]{1,0:T(8,128)(2,1)} %get-tuple-element.57), channel_id=1, source_target_pairs={{0,16},{16,0},{1,17},{17,1},{2,18},{18,2},{3,19},{19,3},{4,20},{20... | collective-permute-start | bytes 2162696 | tf_op jit(solution)/shard_map/ppermute | solution.py:320
  81.3 10.7 %all-to-all-start = ((f32[16,1,64]{2,1,0:T(1,128)}), f32[16,1,64]{2,1,0:T(1,128)S(1)}, u32[]{:S(2)}, u32[]{:S(2)}) async-start(f32[16,1,64]{2,1,0:T(1,128)} %bitcast.12), calls=%async_computation | async-start | bytes 16384 | tf_op jit(solution)/shard_map/all_to_all | solution.py:502
  (10 other events, 86.5 us)

commit v12 on v11

--- a/solution.py
+++ b/solution.py
@@ -298,10 +298,7 @@
     hidden_t = hidden[0, 0].T
     routes_t, gates_t = routes.T, gates.T
     weight = down_weight[0]
-    split = half // 32 * 16
-    weight_specs = [
-        pl.BlockSpec((n, model), lambda i: (0, 0)) for n in (half, split, half - split)
-    ]
+    weight_specs = [pl.BlockSpec((half, model), lambda i: (0, 0))] * 2
     dma = pltpu.SemaphoreType.DMA
 
     def forward(x):
@@ -471,22 +468,21 @@
         )(own, got, *before)
 
     x0 = pack()
-    w = [swap(weight[:split]), swap(weight[split:])]
+    w = [swap(weight)]
     f0, r0, y0 = forward(x0), backward(x0), across(x0)
+    x1 = later_pack(f0)
     ff0, yf0 = forward(f0), across(f0)
-    x1 = later_pack(r0)
-    f1, yr0 = forward(x1), across(behind(r0, y0))
-    yff0 = across(behind(ff0, yf0, w[0]))
+    y1 = across(behind(x1, y0))
+    f1, r1, yr0 = forward(x1), backward(behind(x1, ff0)), across(behind(r0, y0))
+    yff0 = across(behind(ff0, yf0, y1))
     mine0, theirs0, pmat, gslot = first_pick(
-        [x0, y0, f0, yf0, ff0, yff0, r0, behind(yr0, f1, w[1])]
-    )
-    ff1, y1 = forward(f1), across(behind(x1, yr0))
-    r1, yf1 = backward(behind(x1, ff0)), across(behind(f1, yr0))
+        [x0, y0, f0, yf0, ff0, yff0, r0, behind(yr0, f1, r1, w[0])]
+    )
+    ff1, yf1 = forward(f1), across(behind(f1, yr0))
     got = sibling(theirs0)
     rows0, send0, own0, slot_gates, hs = first_products(mine0, got, gslot)
     got0 = [swap(part) for part in send0]
-    done = (yf1, r1, rows0)
-    yff1, ry1 = across(behind(ff1, y1, *done)), backward(behind(y1, *done))
+    yff1, ry1 = across(behind(ff1, rows0)), backward(behind(y1, ff1, rows0))
     forwarded = forward_columns(w)
     raw, part = raw_part(rows0, w)
     mine1, theirs1 = later_pick(

time: 98.1 us -> 100 us (1.019)
  waiting for transfers between devices: 27 us -> 31.3 us
  starting transfers between devices: 39.9 us -> 36.3 us
  local copies, waits for them, and re-layouts: 2.14 us -> 4.07 us
    ppermute x7, waiting for transfers between devices: 0.71 us -> 10 us  [across(): return lax.ppermute(x, 'expert', swap_pairs(2))]
    ppermute x3, waiting for transfers between devices: 9.21 us -> 3.61 us  [backward(): return lax.ppermute(x, 'expert', ring_pairs(-1))]
    ppermute x4, waiting for transfers between devices: 13.3 us -> 9.47 us  [forward(): return lax.ppermute(x, 'expert', ring_pairs(1))]
    ppermute x4, starting transfers between devices: 16.8 us -> 13.1 us  [forward(): return lax.ppermute(x, 'expert', ring_pairs(1))]
    ppermute x5 -> x4, waiting for transfers between devices: 2.67 us -> 6.25 us  [swap(): return lax.ppermute(x, 'dp', [(0, 1), (1, 0)])]
    unnamed x24, local copies, waits for them, and re-layouts: 0.64 us -> 4.07 us
    slice x1 -> x0, local copies, waits for them, and re-layouts: 1.5 us -> none  [ring_shards(): w = [swap(weight[:split]), swap(weight[split:])]]
    ppermute x5 -> x4, starting transfers between devices: 6.21 us -> 5.65 us  [swap(): return lax.ppermute(x, 'dp', [(0, 1), (1, 0)])]
  transfers between devices with their start and end apart: 22 -> 21, of which waited for: 8 -> 10; matrix products, arithmetic and copies ran while one was open for 0% -> 0% of each run, Pallas kernels for 23% -> 21%
where the time goes in v12:
time: 100 us; the launch traced here: 99.7 us
  starting transfers between devices  36.3 us (36%)
  waiting for transfers between devices  31.3 us (31%)
  Pallas kernels  27.2 us (27%)
  local copies, waits for them, and re-layouts  4.07 us (4%)
    ppermute x4, starting transfers between devices, forward(): return lax.ppermute(x, 'expert', ring_pairs(1))  13.1 us
    ppermute x7, waiting for transfers between devices, across(): return lax.ppermute(x, 'expert', swap_pairs(2))  10 us
    ppermute x4, waiting for transfers between devices, forward(): return lax.ppermute(x, 'expert', ring_pairs(1))  9.47 us
    ppermute x7, starting transfers between devices, across(): return lax.ppermute(x, 'expert', swap_pairs(2))  8.31 us
    pallas_call x1, Pallas kernels, raw_rest(): pl.pallas_call(functools.partial(raw_kernel, half, columns[1]), grid=(slo...  6.47 us
    ppermute x4, waiting for transfers between devices, swap(): return lax.ppermute(x, 'dp', [(0, 1), (1, 0)])  6.25 us
    ppermute x4, starting transfers between devices, swap(): return lax.ppermute(x, 'dp', [(0, 1), (1, 0)])  5.65 us
    all_to_all x1, starting transfers between devices, ring_shards(): lax.all_to_all(back, 'expert', split_axis=0, concat_axis=0, tiled=True)  4.61 us
  transfers between devices with their start and end apart: 21, of which 10 were waited for; matrix products, arithmetic and copies ran while one was open for 0% of the time, Pallas kernels for 21%

profile of v12, /device:TPU:0, one launch (start us, length us, event | category | flops | bytes accessed | tf_op | source)
XLA Modules:
  0.0 99.7 jit_solution(9786262934973360032)
XLA Ops:
  0.6 3.0 %collective-permute-start.12 = (bf16[352,2048]{1,0:T(8,128)(2,1)}, bf16[352,2048]{1,0:T(8,128)(2,1)S(1)}, u32[]{:S(2)}, u32[]{:S(2)}) collective-permute-start(bf16[352,2048]{1,0:T(8,128)(2,1)} %bitcast.15), channel_id=1, source_target_pairs={{0,16},{16,0},{1,17},{17,1},{2,18},{18,2},{3,19},{19,3},{4,20},{20... | collective-permute-start | bytes 4325384 | tf_op jit(solution)/shard_map/ppermute | solution.py:317
  6.3 1.6 %collective-permute-start = (bf16[128,1152]{1,0:T(8,128)(2,1)S(1)}, bf16[128,1152]{1,0:T(8,128)(2,1)S(1)}, u32[]{:S(2)}, u32[]{:S(2)}) collective-permute-start(bf16[128,1152]{1,0:T(8,128)(2,1)S(1)} %pack.1.refs_0_.slots_ref), channel_id=1, source_target_pairs={{0,4},{1,5},{2,6},{3,7},{4,12},{5,13},{6,14},{7,15},{12,8},{13,9},... | collective-permute-start | bytes 884744 | tf_op jit(solution)/shard_map/ppermute | solution.py:305
  7.9 1.5 %collective-permute-start.1 = (bf16[128,1152]{1,0:T(8,128)(2,1)S(1)}, bf16[128,1152]{1,0:T(8,128)(2,1)S(1)}, u32[]{:S(2)}, u32[]{:S(2)}) collective-permute-start(bf16[128,1152]{1,0:T(8,128)(2,1)S(1)} %pack.1.refs_0_.slots_ref), channel_id=1, source_target_pairs={{0,2},{1,3},{2,0},{3,1},{4,6},{5,7},{6,4},{7,5},{8,10},{9,11},{10,... | collective-permute-start | bytes 884744 | tf_op jit(solution)/shard_map/ppermute | solution.py:311
  10.8 5.3 %collective-permute-done.after_ref.refs_2_ = bf16[128,1152]{1,0:T(8,128)(2,1)S(1)} collective-permute-done((bf16[128,1152]{1,0:T(8,128)(2,1)S(1)}, bf16[128,1152]{1,0:T(8,128)(2,1)S(1)}, u32[]{:S(2)}, u32[]{:S(2)}) %collective-permute-start) | collective-permute-done | bytes 294944 | tf_op jit(solution)/shard_map/ppermute | solution.py:305
  16.1 7.6 %collective-permute-start.9 = (bf16[128,1152]{1,0:T(8,128)(2,1)S(1)}, bf16[128,1152]{1,0:T(8,128)(2,1)S(1)}, u32[]{:S(2)}, u32[]{:S(2)}) collective-permute-start(bf16[128,1152]{1,0:T(8,128)(2,1)S(1)} %collective-permute-done.after_ref.refs_2_), channel_id=1, source_target_pairs={{0,4},{1,5},{2,6},{3,7},{4,12},{5,13},{6,14},{7,15},{12,8},{13,9},... | collective-permute-start | bytes 884744 | tf_op jit(solution)/shard_map/ppermute | solution.py:305
  23.7 1.5 %collective-permute-start.8 = (bf16[128,1152]{1,0:T(8,128)(2,1)S(1)}, bf16[128,1152]{1,0:T(8,128)(2,1)S(1)}, u32[]{:S(2)}, u32[]{:S(2)}) collective-permute-start(bf16[128,1152]{1,0:T(8,128)(2,1)S(1)} %collective-permute-done.after_ref.refs_2_), channel_id=1, source_target_pairs={{0,2},{1,3},{2,0},{3,1},{4,6},{5,7},{6,4},{7,5},{8,10},{9,11},{10,... | collective-permute-start | bytes 884744 | tf_op jit(solution)/shard_map/ppermute | solution.py:311
  26.9 1.5 %collective-permute-start.5 = (bf16[128,1152]{1,0:T(8,128)(2,1)S(1)}, bf16[128,1152]{1,0:T(8,128)(2,1)S(1)}, u32[]{:S(2)}, u32[]{:S(2)}) collective-permute-start(bf16[128,1152]{1,0:T(8,128)(2,1)S(1)} %collective-permute-done.4.refs_6_), channel_id=1, source_target_pairs={{0,2},{1,3},{2,0},{3,1},{4,6},{5,7},{6,4},{7,5},{8,10},{9,11},{10,... | collective-permute-start | bytes 884744 | tf_op jit(solution)/shard_map/ppermute | solution.py:311
  28.4 8.7 %collective-permute-done.2.refs_1_ = bf16[128,1024]{1,0:T(8,128)(2,1)S(1)} collective-permute-done((bf16[128,1024]{1,0:T(8,128)(2,1)S(1)}, bf16[128,1024]{1,0:T(8,128)(2,1)S(1)}, u32[]{:S(2)}, u32[]{:S(2)}) %collective-permute-start.2) | collective-permute-done | bytes 262176 | tf_op jit(solution)/shard_map/ppermute | solution.py:311
  37.2 1.5 %collective-permute-start.10 = (bf16[128,1152]{1,0:T(8,128)(2,1)S(1)}, bf16[128,1152]{1,0:T(8,128)(2,1)S(1)}, u32[]{:S(2)}, u32[]{:S(2)}) collective-permute-start(bf16[128,1152]{1,0:T(8,128)(2,1)S(1)} %collective-permute-done.9.refs_4_), channel_id=1, source_target_pairs={{0,2},{1,3},{2,0},{3,1},{4,6},{5,7},{6,4},{7,5},{8,10},{9,11},{10,... | collective-permute-start | bytes 884744 | tf_op jit(solution)/shard_map/ppermute | solution.py:311
  38.7 3.2 %collective-permute-start.3 = (bf16[128,1024]{1,0:T(8,128)(2,1)S(1)}, bf16[128,1024]{1,0:T(8,128)(2,1)S(1)}, u32[]{:S(2)}, u32[]{:S(2)}) collective-permute-start(bf16[128,1024]{1,0:T(8,128)(2,1)S(1)} %later_pack.1.refs_0_), channel_id=1, source_target_pairs={{0,4},{1,5},{2,6},{3,7},{4,12},{5,13},{6,14},{7,15},{12,8},{13,9},... | collective-permute-start | bytes 786440 | tf_op jit(solution)/shard_map/ppermute | solution.py:305
  41.9 4.1 %collective-permute-done.3.refs_2_ = bf16[128,1024]{1,0:T(8,128)(2,1)S(1)} collective-permute-done((bf16[128,1024]{1,0:T(8,128)(2,1)S(1)}, bf16[128,1024]{1,0:T(8,128)(2,1)S(1)}, u32[]{:S(2)}, u32[]{:S(2)}) %collective-permute-start.3) | collective-permute-done | bytes 262176 | tf_op jit(solution)/shard_map/ppermute | solution.py:305
  46.0 2.8 %collective-permute-done.11.refs_6_ = bf16[128,1024]{1,0:T(8,128)(2,1)S(1)} collective-permute-done((bf16[128,1024]{1,0:T(8,128)(2,1)S(1)}, bf16[128,1024]{1,0:T(8,128)(2,1)S(1)}, u32[]{:S(2)}, u32[]{:S(2)}) %collective-permute-start.11) | collective-permute-done | bytes 262176 | tf_op jit(solution)/shard_map/ppermute | solution.py:308
  48.8 1.6 %first_pick.1 = (bf16[512,1024]{1,0:T(8,128)(2,1)S(1)}, bf16[528,1024]{1,0:T(8,128)(2,1)S(1)}, bf16[1024,128]{1,0:T(8,128)(2,1)S(1)}, f32[8,128]{1,0:T(8,128)S(1)}) custom-call(bf16[128,1152]{1,0:T(8,128)(2,1)S(1)} %pack.1.refs_0_.slots_ref, bf16[128,1152]{1,0:T(8,128)(2,1)S(1)} %collective-permute-done.1.refs_1_, ...), custom_call_target="tpu_custom_call" | custom-call | flops 3000000000 | bytes 9437184 | tf_op jit(solution)/shard_map/first_pick/pallas_call | solution.py:349
  53.2 3.0 %first_products.1 = (f32[1,1024]{1,0:T(1,128)S(1)}, bf16[704,1024]{1,0:T(8,128)(2,1)S(1)}, bf16[1024,1024]{1,0:T(8,128)(2,1)S(1)}, bf16[352,512]{1,0:T(8,128)(2,...) custom-call(bf16[512,1024]{1,0:T(8,128)(2,1)S(1)} %get-tuple-element.38.mine_ref, ...), custom_call_target="tpu_custom_call" | custom-call | flops 3000000000 | bytes 9437184 | tf_op jit(solution)/shard_map/first_products/pallas_call | solution.py:380
  56.8 1.5 %collective-permute-start.17 = (bf16[352,512]{1,0:T(8,128)(2,1)S(1)}, bf16[352,512]{1,0:T(8,128)(2,1)S(1)}, u32[]{:S(2)}, u32[]{:S(2)}) collective-permute-start(bf16[352,512]{1,0:T(8,128)(2,1)S(1)} %get-tuple-element.50), channel_id=1, source_target_pairs={{0,16},{16,0},{1,17},{17,1},{2,18},{18,2},{3,19},{19,3},{4,20},{20... | collective-permute-start | bytes 1081352 | tf_op jit(solution)/shard_map/ppermute | solution.py:317
  58.3 3.2 %hidden_weight.1.forward_ref = bf16[1024,1024]{1,0:T(8,128)(2,1)S(1)} custom-call(bf16[352,2048]{1,0:T(8,128)(2,1)S(1)} %bitcast.17, bf16[352,2048]{1,0:T(8,128)(2,1)S(1)} %collective-permute-done.12.refs_0_, bf16[704,1024]{1,0:T(8,128)(2,1)S(1)} %bitcast.23), custom_call_target="tpu_custom_call" | custom-call | flops 3000000000 | bytes 9437184 | tf_op jit(solution)/shard_map/hidden_weight/pallas_call | solution.py:435
  62.0 3.1 %collective-permute-start.15 = (bf16[128,1024]{1,0:T(8,128)(2,1)S(1)}, bf16[128,1024]{1,0:T(8,128)(2,1)S(1)}, u32[]{:S(2)}, u32[]{:S(2)}) collective-permute-start(bf16[128,1024]{1,0:T(8,128)(2,1)S(1)} %collective-permute-done.2.refs_1_), channel_id=1, source_target_pairs={{0,8},{1,9},{2,10},{3,11},{4,0},{5,1},{6,2},{7,3},{12,4},{13,5},{1... | collective-permute-start | bytes 786440 | tf_op jit(solution)/shard_map/ppermute | solution.py:308
  65.2 2.8 %raw_part.1 = (f32[704,1024]{1,0:T(8,128)S(1)}, f32[16,64]{1,0:T(8,128)S(1)}) custom-call(bf16[1024,1024]{1,0:T(8,128)(2,1)S(1)} %get-tuple-element.41.rows_ref, bf16[352,2048]{1,0:T(8,128)(2,1)S(1)} %bitcast.18, bf16[352,2048]{1,0:T(8,128)(2,1)S(1)} %collective-permute-done.12.refs_0_, bf16[704,1024]{1,0:T(8,128)(2,1)S(1)} %bitcast.24), custom_call_target="tpu_custom_call" | custom-call | flops 3000000000 | bytes 9437184 | tf_op jit(solution)/shard_map/raw_part/pallas_call | solution.py:407
  71.4 3.0 %collective-permute-done.17.got_ref = bf16[352,512]{1,0:T(8,128)(2,1)S(1)} collective-permute-done((bf16[352,512]{1,0:T(8,128)(2,1)S(1)}, bf16[352,512]{1,0:T(8,128)(2,1)S(1)}, u32[]{:S(2)}, u32[]{:S(2)}) %collective-permute-start.17) | collective-permute-done | bytes 360480 | tf_op jit(solution)/shard_map/ppermute | solution.py:317
  77.1 3.3 %products.1 = (bf16[1024,1024]{1,0:T(8,128)(2,1)S(1)}, bf16[352,1024]{1,0:T(8,128)(2,1)}, bf16[352,1024]{1,0:T(8,128)(2,1)S(1)}) custom-call(bf16[512,1024]{1,0:T(8,128)(2,1)S(1)} %get-tuple-element.47.mine_ref, bf16[512,1024]{1,0:T(8,128)(2,1)S(1)} %collective-permute-done.18.got_ref, bf16[704,1024]{1,0:T(8,128)(2,1)S(1)} %get-tuple-element.55.hs_ref), custom_call_target="tpu_custom_call" | custom-call | tf_op jit(solution)/shard_map/products/pallas_call | solution.py:392
  82.2 4.6 %all-to-all-start = ((f32[16,1,64]{2,1,0:T(1,128)}), f32[16,1,64]{2,1,0:T(1,128)S(1)}, u32[]{:S(2)}, u32[]{:S(2)}) async-start(f32[16,1,64]{2,1,0:T(1,128)} %bitcast.10), calls=%async_computation | async-start | bytes 16384 | tf_op jit(solution)/shard_map/all_to_all | solution.py:498
  86.8 6.5 %raw.1 = bf16[704,1024]{1,0:T(8,128)(2,1)} custom-call(bf16[1024,1024]{1,0:T(8,128)(2,1)} %copy-done, bf16[352,2048]{1,0:T(8,128)(2,1)} %bitcast.16, bf16[352,2048]{1,0:T(8,128)(2,1)} %copy-done.5, f32[704,1024]{1,0:T(8,128)} %copy-done.1, f32[1,1024]{1,0:T(1,128)} %copy-done.8), custom_call_target="tpu_custom_call" | custom-call | tf_op jit(solution)/shard_map/raw/pallas_call | solution.py:419
  93.9 1.6 %grad_gates.1 = f32[6,128]{1,0:T(8,128)} custom-call(s32[6,128]{1,0:T(8,128)} %bitcast.19, bf16[128,1152]{1,0:T(8,128)(2,1)} %copy-done.6, f32[16,64]{1,0:T(8,128)} %bitcast.27), custom_call_target="tpu_custom_call" | custom-call | tf_op jit(solution)/shard_map/grad_gates/pallas_call | solution.py:499
  95.5 3.3 %collective-permute-done.19.got_ref = bf16[352,1024]{1,0:T(8,128)(2,1)S(1)} collective-permute-done((bf16[352,1024]{1,0:T(8,128)(2,1)}, bf16[352,1024]{1,0:T(8,128)(2,1)S(1)}, u32[]{:S(2)}, u32[]{:S(2)}) %collective-permute-start.19) | collective-permute-done | bytes 720928 | tf_op jit(solution)/shard_map/ppermute | solution.py:317
  (56 shorter events, 18.9 us)
Async XLA Ops:
  0.6 48.1 %collective-permute-start.12 = (bf16[352,2048]{1,0:T(8,128)(2,1)}, bf16[352,2048]{1,0:T(8,128)(2,1)S(1)}, u32[]{:S(2)}, u32[]{:S(2)}) collective-permute-start(bf16[352,2048]{1,0:T(8,128)(2,1)} %bitcast.15), channel_id=1, source_target_pairs={{0,16},{16,0},{1,17},{17,1},{2,18},{18,2},{3,19},{19,3},{4,20},{20... | collective-permute-start | bytes 4325384 | tf_op jit(solution)/shard_map/ppermute | solution.py:317
  6.2 44.1 %copy-start.6 = (bf16[128,1152]{1,0:T(8,128)(2,1)}, bf16[128,1152]{1,0:T(8,128)(2,1)S(1)}, u32[]{:S(2)}) copy-start(bf16[128,1152]{1,0:T(8,128)(2,1)S(1)} %pack.1.refs_0_.slots_ref) | copy-start | bytes 884740
  6.3 9.8 %collective-permute-start = (bf16[128,1152]{1,0:T(8,128)(2,1)S(1)}, bf16[128,1152]{1,0:T(8,128)(2,1)S(1)}, u32[]{:S(2)}, u32[]{:S(2)}) collective-permute-start(bf16[128,1152]{1,0:T(8,128)(2,1)S(1)} %pack.1.refs_0_.slots_ref), channel_id=1, source_target_pairs={{0,4},{1,5},{2,6},{3,7},{4,12},{5,13},{6,14},{7,15},{12,8},{13,9},... | collective-permute-start | bytes 884744 | tf_op jit(solution)/shard_map/ppermute | solution.py:305
  7.9 18.4 %collective-permute-start.1 = (bf16[128,1152]{1,0:T(8,128)(2,1)S(1)}, bf16[128,1152]{1,0:T(8,128)(2,1)S(1)}, u32[]{:S(2)}, u32[]{:S(2)}) collective-permute-start(bf16[128,1152]{1,0:T(8,128)(2,1)S(1)} %pack.1.refs_0_.slots_ref), channel_id=1, source_target_pairs={{0,2},{1,3},{2,0},{3,1},{4,6},{5,7},{6,4},{7,5},{8,10},{9,11},{10,... | collective-permute-start | bytes 884744 | tf_op jit(solution)/shard_map/ppermute | solution.py:311
  9.4 17.5 %collective-permute-start.4 = (bf16[128,1152]{1,0:T(8,128)(2,1)S(1)}, bf16[128,1152]{1,0:T(8,128)(2,1)S(1)}, u32[]{:S(2)}, u32[]{:S(2)}) collective-permute-start(bf16[128,1152]{1,0:T(8,128)(2,1)S(1)} %pack.1.refs_0_.slots_ref), channel_id=1, source_target_pairs={{0,8},{1,9},{2,10},{3,11},{4,0},{5,1},{6,2},{7,3},{12,4},{13,5},{1... | collective-permute-start | bytes 884744 | tf_op jit(solution)/shard_map/ppermute | solution.py:308
  16.1 21.1 %collective-permute-start.9 = (bf16[128,1152]{1,0:T(8,128)(2,1)S(1)}, bf16[128,1152]{1,0:T(8,128)(2,1)S(1)}, u32[]{:S(2)}, u32[]{:S(2)}) collective-permute-start(bf16[128,1152]{1,0:T(8,128)(2,1)S(1)} %collective-permute-done.after_ref.refs_2_), channel_id=1, source_target_pairs={{0,4},{1,5},{2,6},{3,7},{4,12},{5,13},{6,14},{7,15},{12,8},{13,9},... | collective-permute-start | bytes 884744 | tf_op jit(solution)/shard_map/ppermute | solution.py:305
  23.7 13.5 %collective-permute-start.8 = (bf16[128,1152]{1,0:T(8,128)(2,1)S(1)}, bf16[128,1152]{1,0:T(8,128)(2,1)S(1)}, u32[]{:S(2)}, u32[]{:S(2)}) collective-permute-start(bf16[128,1152]{1,0:T(8,128)(2,1)S(1)} %collective-permute-done.after_ref.refs_2_), channel_id=1, source_target_pairs={{0,2},{1,3},{2,0},{3,1},{4,6},{5,7},{6,4},{7,5},{8,10},{9,11},{10,... | collective-permute-start | bytes 884744 | tf_op jit(solution)/shard_map/ppermute | solution.py:311
  26.3 26.9 %copy-start.10 = (bf16[1,1,1024,704]{2,3,1,0:T(8,128)(2,1)S(1)}, bf16[1,1,1024,704]{2,3,1,0:T(8,128)(2,1)}, u32[]{:S(2)}) copy-start(bf16[1,1,1024,704]{2,3,1,0:T(8,128)(2,1)} %param.8) | copy-start | bytes 4325380
  26.3 10.8 %collective-permute-start.2 = (bf16[128,1024]{1,0:T(8,128)(2,1)S(1)}, bf16[128,1024]{1,0:T(8,128)(2,1)S(1)}, u32[]{:S(2)}, u32[]{:S(2)}) collective-permute-start(bf16[128,1024]{1,0:T(8,128)(2,1)S(1)} %later_pack.1.refs_0_), channel_id=1, source_target_pairs={{0,2},{1,3},{2,0},{3,1},{4,6},{5,7},{6,4},{7,5},{8,10},{9,11},{10,... | collective-permute-start | bytes 786440 | tf_op jit(solution)/shard_map/ppermute | solution.py:311
  26.9 19.1 %collective-permute-start.5 = (bf16[128,1152]{1,0:T(8,128)(2,1)S(1)}, bf16[128,1152]{1,0:T(8,128)(2,1)S(1)}, u32[]{:S(2)}, u32[]{:S(2)}) collective-permute-start(bf16[128,1152]{1,0:T(8,128)(2,1)S(1)} %collective-permute-done.4.refs_6_), channel_id=1, source_target_pairs={{0,2},{1,3},{2,0},{3,1},{4,6},{5,7},{6,4},{7,5},{8,10},{9,11},{10,... | collective-permute-start | bytes 884744 | tf_op jit(solution)/shard_map/ppermute | solution.py:311
  37.2 11.6 %collective-permute-start.10 = (bf16[128,1152]{1,0:T(8,128)(2,1)S(1)}, bf16[128,1152]{1,0:T(8,128)(2,1)S(1)}, u32[]{:S(2)}, u32[]{:S(2)}) collective-permute-start(bf16[128,1152]{1,0:T(8,128)(2,1)S(1)} %collective-permute-done.9.refs_4_), channel_id=1, source_target_pairs={{0,2},{1,3},{2,0},{3,1},{4,6},{5,7},{6,4},{7,5},{8,10},{9,11},{10,... | collective-permute-start | bytes 884744 | tf_op jit(solution)/shard_map/ppermute | solution.py:311
  38.7 7.3 %collective-permute-start.3 = (bf16[128,1024]{1,0:T(8,128)(2,1)S(1)}, bf16[128,1024]{1,0:T(8,128)(2,1)S(1)}, u32[]{:S(2)}, u32[]{:S(2)}) collective-permute-start(bf16[128,1024]{1,0:T(8,128)(2,1)S(1)} %later_pack.1.refs_0_), channel_id=1, source_target_pairs={{0,4},{1,5},{2,6},{3,7},{4,12},{5,13},{6,14},{7,15},{12,8},{13,9},... | collective-permute-start | bytes 786440 | tf_op jit(solution)/shard_map/ppermute | solution.py:305
  41.9 6.9 %collective-permute-start.11 = (bf16[128,1024]{1,0:T(8,128)(2,1)S(1)}, bf16[128,1024]{1,0:T(8,128)(2,1)S(1)}, u32[]{:S(2)}, u32[]{:S(2)}) collective-permute-start(bf16[128,1024]{1,0:T(8,128)(2,1)S(1)} %later_pack.1.refs_0_), channel_id=1, source_target_pairs={{0,8},{1,9},{2,10},{3,11},{4,0},{5,1},{6,2},{7,3},{12,4},{13,5},{1... | collective-permute-start | bytes 786440 | tf_op jit(solution)/shard_map/ppermute | solution.py:308
  48.8 16.4 %copy-start.5 = (bf16[352,2048]{1,0:T(8,128)(2,1)}, bf16[352,2048]{1,0:T(8,128)(2,1)S(1)}, u32[]{:S(2)}) copy-start(bf16[352,2048]{1,0:T(8,128)(2,1)S(1)} %collective-permute-done.12.refs_0_) | copy-start | bytes 4325380
  50.4 2.8 %collective-permute-start.13 = (bf16[528,1024]{1,0:T(8,128)(2,1)S(1)}, bf16[528,1024]{1,0:T(8,128)(2,1)S(1)}, u32[]{:S(2)}, u32[]{:S(2)}) collective-permute-start(bf16[528,1024]{1,0:T(8,128)(2,1)S(1)} %get-tuple-element.39), channel_id=1, source_target_pairs={{0,1},{1,0},{2,3},{3,2},{4,5},{5,4},{6,7},{7,6},{8,9},{9,8},{10,11... | collective-permute-start | bytes 3244040 | tf_op jit(solution)/shard_map/ppermute | solution.py:314
  50.5 11.0 %collective-permute-start.7 = (bf16[128,1024]{1,0:T(8,128)(2,1)S(1)}, bf16[128,1024]{1,0:T(8,128)(2,1)S(1)}, u32[]{:S(2)}, u32[]{:S(2)}) collective-permute-start(bf16[128,1024]{1,0:T(8,128)(2,1)S(1)} %collective-permute-done.3.refs_2_), channel_id=1, source_target_pairs={{0,4},{1,5},{2,6},{3,7},{4,12},{5,13},{6,14},{7,15},{12,8},{13,9},... | collective-permute-start | bytes 786440 | tf_op jit(solution)/shard_map/ppermute | solution.py:305
  51.2 16.9 %collective-permute-start.6 = (bf16[128,1024]{1,0:T(8,128)(2,1)S(1)}, bf16[128,1024]{1,0:T(8,128)(2,1)S(1)}, u32[]{:S(2)}, u32[]{:S(2)}) collective-permute-start(bf16[128,1024]{1,0:T(8,128)(2,1)S(1)} %collective-permute-done.3.refs_2_), channel_id=1, source_target_pairs={{0,2},{1,3},{2,0},{3,1},{4,6},{5,7},{6,4},{7,5},{8,10},{9,11},{10,... | collective-permute-start | bytes 786440 | tf_op jit(solution)/shard_map/ppermute | solution.py:311
  56.2 15.2 %collective-permute-start.16 = (bf16[352,512]{1,0:T(8,128)(2,1)S(1)}, bf16[352,512]{1,0:T(8,128)(2,1)S(1)}, u32[]{:S(2)}, u32[]{:S(2)}) collective-permute-start(bf16[352,512]{1,0:T(8,128)(2,1)S(1)} %get-tuple-element.49), channel_id=1, source_target_pairs={{0,16},{16,0},{1,17},{17,1},{2,18},{18,2},{3,19},{19,3},{4,20},{20... | collective-permute-start | bytes 1081352 | tf_op jit(solution)/shard_map/ppermute | solution.py:317
  56.8 17.6 %collective-permute-start.17 = (bf16[352,512]{1,0:T(8,128)(2,1)S(1)}, bf16[352,512]{1,0:T(8,128)(2,1)S(1)}, u32[]{:S(2)}, u32[]{:S(2)}) collective-permute-start(bf16[352,512]{1,0:T(8,128)(2,1)S(1)} %get-tuple-element.50), channel_id=1, source_target_pairs={{0,16},{16,0},{1,17},{17,1},{2,18},{18,2},{3,19},{19,3},{4,20},{20... | collective-permute-start | bytes 1081352 | tf_op jit(solution)/shard_map/ppermute | solution.py:317
  61.5 7.8 %collective-permute-start.14 = (bf16[128,1024]{1,0:T(8,128)(2,1)S(1)}, bf16[128,1024]{1,0:T(8,128)(2,1)S(1)}, u32[]{:S(2)}, u32[]{:S(2)}) collective-permute-start(bf16[128,1024]{1,0:T(8,128)(2,1)S(1)} %collective-permute-done.7.refs_4_), channel_id=1, source_target_pairs={{0,2},{1,3},{2,0},{3,1},{4,6},{5,7},{6,4},{7,5},{8,10},{9,11},{10,... | collective-permute-start | bytes 786440 | tf_op jit(solution)/shard_map/ppermute | solution.py:311
  62.0 8.1 %collective-permute-start.15 = (bf16[128,1024]{1,0:T(8,128)(2,1)S(1)}, bf16[128,1024]{1,0:T(8,128)(2,1)S(1)}, u32[]{:S(2)}, u32[]{:S(2)}) collective-permute-start(bf16[128,1024]{1,0:T(8,128)(2,1)S(1)} %collective-permute-done.2.refs_1_), channel_id=1, source_target_pairs={{0,8},{1,9},{2,10},{3,11},{4,0},{5,1},{6,2},{7,3},{12,4},{13,5},{1... | collective-permute-start | bytes 786440 | tf_op jit(solution)/shard_map/ppermute | solution.py:308
  74.4 2.7 %collective-permute-start.18 = (bf16[512,1024]{1,0:T(8,128)(2,1)S(1)}, bf16[512,1024]{1,0:T(8,128)(2,1)S(1)}, u32[]{:S(2)}, u32[]{:S(2)}) collective-permute-start(bf16[512,1024]{1,0:T(8,128)(2,1)S(1)} %get-tuple-element.51), channel_id=1, source_target_pairs={{0,1},{1,0},{2,3},{3,2},{4,5},{5,4},{6,7},{7,6},{8,9},{9,8},{10,11... | collective-permute-start | bytes 3145736 | tf_op jit(solution)/shard_map/ppermute | solution.py:314
  80.4 18.4 %collective-permute-start.19 = (bf16[352,1024]{1,0:T(8,128)(2,1)}, bf16[352,1024]{1,0:T(8,128)(2,1)S(1)}, u32[]{:S(2)}, u32[]{:S(2)}) collective-permute-start(bf16[352,1024]{1,0:T(8,128)(2,1)} %get-tuple-element.57), channel_id=1, source_target_pairs={{0,16},{16,0},{1,17},{17,1},{2,18},{18,2},{3,19},{19,3},{4,20},{20... | collective-permute-start | bytes 2162696 | tf_op jit(solution)/shard_map/ppermute | solution.py:317
  82.2 11.1 %all-to-all-start = ((f32[16,1,64]{2,1,0:T(1,128)}), f32[16,1,64]{2,1,0:T(1,128)S(1)}, u32[]{:S(2)}, u32[]{:S(2)}) async-start(f32[16,1,64]{2,1,0:T(1,128)} %bitcast.10), calls=%async_computation | async-start | bytes 16384 | tf_op jit(solution)/shard_map/all_to_all | solution.py:498
  (9 other events, 23.5 us)

commit v13 on v12

--- a/solution.py
+++ b/solution.py
@@ -472,13 +472,12 @@
     f0, r0, y0 = forward(x0), backward(x0), across(x0)
     x1 = later_pack(f0)
     ff0, yf0 = forward(f0), across(f0)
-    y1 = across(behind(x1, y0))
     f1, r1, yr0 = forward(x1), backward(behind(x1, ff0)), across(behind(r0, y0))
-    yff0 = across(behind(ff0, yf0, y1))
+    yff0 = across(behind(ff0, yf0))
     mine0, theirs0, pmat, gslot = first_pick(
         [x0, y0, f0, yf0, ff0, yff0, r0, behind(yr0, f1, r1, w[0])]
     )
-    ff1, yf1 = forward(f1), across(behind(f1, yr0))
+    ff1, yf1, y1 = forward(f1), across(behind(f1, yr0)), across(behind(x1, yr0))
     got = sibling(theirs0)
     rows0, send0, own0, slot_gates, hs = first_products(mine0, got, gslot)
     got0 = [swap(part) for part in send0]

time: 100 us -> 97.5 us (0.975)
  starting transfers between devices: 36.3 us -> 34.4 us
    ppermute x4, waiting for transfers between devices: 9.47 us -> 17.3 us  [forward(): return lax.ppermute(x, 'expert', ring_pairs(1))]
    ppermute x7, waiting for transfers between devices: 10 us -> 5.6 us  [across(): return lax.ppermute(x, 'expert', swap_pairs(2))]
    ppermute x3, waiting for transfers between devices: 3.61 us -> 0.04 us  [backward(): return lax.ppermute(x, 'expert', ring_pairs(-1))]
    ppermute x3, starting transfers between devices: 4.5 us -> 3.34 us  [backward(): return lax.ppermute(x, 'expert', ring_pairs(-1))]
  transfers between devices with their start and end apart: 21 -> 21, of which waited for: 10 -> 9; matrix products, arithmetic and copies ran while one was open for 0% -> 0% of each run, Pallas kernels for 21% -> 22%
where the time goes in v13:
time: 97.5 us; the launch traced here: 97.1 us
  starting transfers between devices  34.4 us (35%)
  waiting for transfers between devices  30.6 us (31%)
  Pallas kernels  27.2 us (28%)
  local copies, waits for them, and re-layouts  4.07 us (4%)
    ppermute x4, waiting for transfers between devices, forward(): return lax.ppermute(x, 'expert', ring_pairs(1))  17.3 us
    ppermute x4, starting transfers between devices, forward(): return lax.ppermute(x, 'expert', ring_pairs(1))  12.9 us
    ppermute x7, starting transfers between devices, across(): return lax.ppermute(x, 'expert', swap_pairs(2))  7.92 us
    pallas_call x1, Pallas kernels, raw_rest(): pl.pallas_call(functools.partial(raw_kernel, half, columns[1]), grid=(slo...  6.46 us
    ppermute x4, waiting for transfers between devices, swap(): return lax.ppermute(x, 'dp', [(0, 1), (1, 0)])  6.05 us
    ppermute x4, starting transfers between devices, swap(): return lax.ppermute(x, 'dp', [(0, 1), (1, 0)])  5.66 us
    ppermute x7, waiting for transfers between devices, across(): return lax.ppermute(x, 'expert', swap_pairs(2))  5.6 us
    all_to_all x1, starting transfers between devices, ring_shards(): lax.all_to_all(back, 'expert', split_axis=0, concat_axis=0, tiled=True)  4.54 us
  transfers between devices with their start and end apart: 21, of which 9 were waited for; matrix products, arithmetic and copies ran while one was open for 0% of the time, Pallas kernels for 22%

profile of v13, /device:TPU:0, one launch (start us, length us, event | category | flops | bytes accessed | tf_op | source)
XLA Modules:
  0.0 97.1 jit_solution(14462184890545755854)
XLA Ops:
  0.6 3.0 %collective-permute-start.12 = (bf16[352,2048]{1,0:T(8,128)(2,1)}, bf16[352,2048]{1,0:T(8,128)(2,1)S(1)}, u32[]{:S(2)}, u32[]{:S(2)}) collective-permute-start(bf16[352,2048]{1,0:T(8,128)(2,1)} %bitcast.15), channel_id=1, source_target_pairs={{0,16},{16,0},{1,17},{17,1},{2,18},{18,2},{3,19},{19,3},{4,20},{20... | collective-permute-start | bytes 4325384 | tf_op jit(solution)/shard_map/ppermute | solution.py:317
  6.3 1.6 %collective-permute-start = (bf16[128,1152]{1,0:T(8,128)(2,1)S(1)}, bf16[128,1152]{1,0:T(8,128)(2,1)S(1)}, u32[]{:S(2)}, u32[]{:S(2)}) collective-permute-start(bf16[128,1152]{1,0:T(8,128)(2,1)S(1)} %pack.1.refs_0_.slots_ref), channel_id=1, source_target_pairs={{0,4},{1,5},{2,6},{3,7},{4,12},{5,13},{6,14},{7,15},{12,8},{13,9},... | collective-permute-start | bytes 884744 | tf_op jit(solution)/shard_map/ppermute | solution.py:305
  7.9 1.5 %collective-permute-start.2 = (bf16[128,1152]{1,0:T(8,128)(2,1)S(1)}, bf16[128,1152]{1,0:T(8,128)(2,1)S(1)}, u32[]{:S(2)}, u32[]{:S(2)}) collective-permute-start(bf16[128,1152]{1,0:T(8,128)(2,1)S(1)} %pack.1.refs_0_.slots_ref), channel_id=1, source_target_pairs={{0,2},{1,3},{2,0},{3,1},{4,6},{5,7},{6,4},{7,5},{8,10},{9,11},{10,... | collective-permute-start | bytes 884744 | tf_op jit(solution)/shard_map/ppermute | solution.py:311
  10.8 5.3 %collective-permute-done.after_ref.refs_2_ = bf16[128,1152]{1,0:T(8,128)(2,1)S(1)} collective-permute-done((bf16[128,1152]{1,0:T(8,128)(2,1)S(1)}, bf16[128,1152]{1,0:T(8,128)(2,1)S(1)}, u32[]{:S(2)}, u32[]{:S(2)}) %collective-permute-start) | collective-permute-done | bytes 294944 | tf_op jit(solution)/shard_map/ppermute | solution.py:305
  16.1 7.6 %collective-permute-start.9 = (bf16[128,1152]{1,0:T(8,128)(2,1)S(1)}, bf16[128,1152]{1,0:T(8,128)(2,1)S(1)}, u32[]{:S(2)}, u32[]{:S(2)}) collective-permute-start(bf16[128,1152]{1,0:T(8,128)(2,1)S(1)} %collective-permute-done.after_ref.refs_2_), channel_id=1, source_target_pairs={{0,4},{1,5},{2,6},{3,7},{4,12},{5,13},{6,14},{7,15},{12,8},{13,9},... | collective-permute-start | bytes 884744 | tf_op jit(solution)/shard_map/ppermute | solution.py:305
  23.7 1.5 %collective-permute-start.8 = (bf16[128,1152]{1,0:T(8,128)(2,1)S(1)}, bf16[128,1152]{1,0:T(8,128)(2,1)S(1)}, u32[]{:S(2)}, u32[]{:S(2)}) collective-permute-start(bf16[128,1152]{1,0:T(8,128)(2,1)S(1)} %collective-permute-done.after_ref.refs_2_), channel_id=1, source_target_pairs={{0,2},{1,3},{2,0},{3,1},{4,6},{5,7},{6,4},{7,5},{8,10},{9,11},{10,... | collective-permute-start | bytes 884744 | tf_op jit(solution)/shard_map/ppermute | solution.py:311
  25.7 3.5 %collective-permute-done.9.refs_4_ = bf16[128,1152]{1,0:T(8,128)(2,1)S(1)} collective-permute-done((bf16[128,1152]{1,0:T(8,128)(2,1)S(1)}, bf16[128,1152]{1,0:T(8,128)(2,1)S(1)}, u32[]{:S(2)}, u32[]{:S(2)}) %collective-permute-start.9) | collective-permute-done | bytes 294944 | tf_op jit(solution)/shard_map/ppermute | solution.py:305
  29.2 2.4 %collective-permute-done.8.refs_3_ = bf16[128,1152]{1,0:T(8,128)(2,1)S(1)} collective-permute-done((bf16[128,1152]{1,0:T(8,128)(2,1)S(1)}, bf16[128,1152]{1,0:T(8,128)(2,1)S(1)}, u32[]{:S(2)}, u32[]{:S(2)}) %collective-permute-start.8) | collective-permute-done | bytes 294944 | tf_op jit(solution)/shard_map/ppermute | solution.py:311
  31.6 1.5 %collective-permute-start.10 = (bf16[128,1152]{1,0:T(8,128)(2,1)S(1)}, bf16[128,1152]{1,0:T(8,128)(2,1)S(1)}, u32[]{:S(2)}, u32[]{:S(2)}) collective-permute-start(bf16[128,1152]{1,0:T(8,128)(2,1)S(1)} %collective-permute-done.9.refs_4_), channel_id=1, source_target_pairs={{0,2},{1,3},{2,0},{3,1},{4,6},{5,7},{6,4},{7,5},{8,10},{9,11},{10,... | collective-permute-start | bytes 884744 | tf_op jit(solution)/shard_map/ppermute | solution.py:311
  34.2 3.5 %collective-permute-start.5 = (bf16[128,1024]{1,0:T(8,128)(2,1)S(1)}, bf16[128,1024]{1,0:T(8,128)(2,1)S(1)}, u32[]{:S(2)}, u32[]{:S(2)}) collective-permute-start(bf16[128,1024]{1,0:T(8,128)(2,1)S(1)} %later_pack.1.refs_0_), channel_id=1, source_target_pairs={{0,4},{1,5},{2,6},{3,7},{4,12},{5,13},{6,14},{7,15},{12,8},{13,9},... | collective-permute-start | bytes 786440 | tf_op jit(solution)/shard_map/ppermute | solution.py:305
  37.7 8.5 %collective-permute-done.5.refs_2_ = bf16[128,1024]{1,0:T(8,128)(2,1)S(1)} collective-permute-done((bf16[128,1024]{1,0:T(8,128)(2,1)S(1)}, bf16[128,1024]{1,0:T(8,128)(2,1)S(1)}, u32[]{:S(2)}, u32[]{:S(2)}) %collective-permute-start.5) | collective-permute-done | bytes 262176 | tf_op jit(solution)/shard_map/ppermute | solution.py:305
  46.2 1.6 %first_pick.1 = (bf16[512,1024]{1,0:T(8,128)(2,1)S(1)}, bf16[528,1024]{1,0:T(8,128)(2,1)S(1)}, bf16[1024,128]{1,0:T(8,128)(2,1)S(1)}, f32[8,128]{1,0:T(8,128)S(1)}) custom-call(bf16[128,1152]{1,0:T(8,128)(2,1)S(1)} %pack.1.refs_0_.slots_ref, bf16[128,1152]{1,0:T(8,128)(2,1)S(1)} %collective-permute-done.2.refs_1_, ...), custom_call_target="tpu_custom_call" | custom-call | flops 3000000000 | bytes 9437184 | tf_op jit(solution)/shard_map/first_pick/pallas_call | solution.py:349
  50.6 3.0 %first_products.1 = (f32[1,1024]{1,0:T(1,128)S(1)}, bf16[704,1024]{1,0:T(8,128)(2,1)S(1)}, bf16[1024,1024]{1,0:T(8,128)(2,1)S(1)}, bf16[352,512]{1,0:T(8,128)(2,...) custom-call(bf16[512,1024]{1,0:T(8,128)(2,1)S(1)} %get-tuple-element.38.mine_ref, ...), custom_call_target="tpu_custom_call" | custom-call | flops 3000000000 | bytes 9437184 | tf_op jit(solution)/shard_map/first_products/pallas_call | solution.py:380
  54.2 1.5 %collective-permute-start.17 = (bf16[352,512]{1,0:T(8,128)(2,1)S(1)}, bf16[352,512]{1,0:T(8,128)(2,1)S(1)}, u32[]{:S(2)}, u32[]{:S(2)}) collective-permute-start(bf16[352,512]{1,0:T(8,128)(2,1)S(1)} %get-tuple-element.50), channel_id=1, source_target_pairs={{0,16},{16,0},{1,17},{17,1},{2,18},{18,2},{3,19},{19,3},{4,20},{20... | collective-permute-start | bytes 1081352 | tf_op jit(solution)/shard_map/ppermute | solution.py:317
  55.7 3.2 %hidden_weight.1.forward_ref = bf16[1024,1024]{1,0:T(8,128)(2,1)S(1)} custom-call(bf16[352,2048]{1,0:T(8,128)(2,1)S(1)} %bitcast.17, bf16[352,2048]{1,0:T(8,128)(2,1)S(1)} %collective-permute-done.12.refs_0_, bf16[704,1024]{1,0:T(8,128)(2,1)S(1)} %bitcast.23), custom_call_target="tpu_custom_call" | custom-call | flops 3000000000 | bytes 9437184 | tf_op jit(solution)/shard_map/hidden_weight/pallas_call | solution.py:435
  59.8 2.0 %collective-permute-start.15 = (bf16[128,1024]{1,0:T(8,128)(2,1)S(1)}, bf16[128,1024]{1,0:T(8,128)(2,1)S(1)}, u32[]{:S(2)}, u32[]{:S(2)}) collective-permute-start(bf16[128,1024]{1,0:T(8,128)(2,1)S(1)} %collective-permute-done.4.refs_1_), channel_id=1, source_target_pairs={{0,8},{1,9},{2,10},{3,11},{4,0},{5,1},{6,2},{7,3},{12,4},{13,5},{1... | collective-permute-start | bytes 786440 | tf_op jit(solution)/shard_map/ppermute | solution.py:308
  61.8 2.8 %raw_part.1 = (f32[704,1024]{1,0:T(8,128)S(1)}, f32[16,64]{1,0:T(8,128)S(1)}) custom-call(bf16[1024,1024]{1,0:T(8,128)(2,1)S(1)} %get-tuple-element.41.rows_ref, bf16[352,2048]{1,0:T(8,128)(2,1)S(1)} %bitcast.18, bf16[352,2048]{1,0:T(8,128)(2,1)S(1)} %collective-permute-done.12.refs_0_, bf16[704,1024]{1,0:T(8,128)(2,1)S(1)} %bitcast.24), custom_call_target="tpu_custom_call" | custom-call | flops 3000000000 | bytes 9437184 | tf_op jit(solution)/shard_map/raw_part/pallas_call | solution.py:407
  64.7 3.2 %collective-permute-done.14.refs_5_ = bf16[128,1024]{1,0:T(8,128)(2,1)S(1)} collective-permute-done((bf16[128,1024]{1,0:T(8,128)(2,1)S(1)}, bf16[128,1024]{1,0:T(8,128)(2,1)S(1)}, u32[]{:S(2)}, u32[]{:S(2)}) %collective-permute-start.14) | collective-permute-done | bytes 262176 | tf_op jit(solution)/shard_map/ppermute | solution.py:311
  69.1 2.7 %collective-permute-done.17.got_ref = bf16[352,512]{1,0:T(8,128)(2,1)S(1)} collective-permute-done((bf16[352,512]{1,0:T(8,128)(2,1)S(1)}, bf16[352,512]{1,0:T(8,128)(2,1)S(1)}, u32[]{:S(2)}, u32[]{:S(2)}) %collective-permute-start.17) | collective-permute-done | bytes 360480 | tf_op jit(solution)/shard_map/ppermute | solution.py:317
  74.5 3.3 %products.1 = (bf16[1024,1024]{1,0:T(8,128)(2,1)S(1)}, bf16[352,1024]{1,0:T(8,128)(2,1)}, bf16[352,1024]{1,0:T(8,128)(2,1)S(1)}) custom-call(bf16[512,1024]{1,0:T(8,128)(2,1)S(1)} %get-tuple-element.47.mine_ref, bf16[512,1024]{1,0:T(8,128)(2,1)S(1)} %collective-permute-done.18.got_ref, bf16[704,1024]{1,0:T(8,128)(2,1)S(1)} %get-tuple-element.55.hs_ref), custom_call_target="tpu_custom_call" | custom-call | tf_op jit(solution)/shard_map/products/pallas_call | solution.py:392
  79.6 4.5 %all-to-all-start = ((f32[16,1,64]{2,1,0:T(1,128)}), f32[16,1,64]{2,1,0:T(1,128)S(1)}, u32[]{:S(2)}, u32[]{:S(2)}) async-start(f32[16,1,64]{2,1,0:T(1,128)} %bitcast.10), calls=%async_computation | async-start | bytes 16384 | tf_op jit(solution)/shard_map/all_to_all | solution.py:497
  84.2 6.5 %raw.1 = bf16[704,1024]{1,0:T(8,128)(2,1)} custom-call(bf16[1024,1024]{1,0:T(8,128)(2,1)} %copy-done, bf16[352,2048]{1,0:T(8,128)(2,1)} %bitcast.16, bf16[352,2048]{1,0:T(8,128)(2,1)} %copy-done.5, f32[704,1024]{1,0:T(8,128)} %copy-done.1, f32[1,1024]{1,0:T(1,128)} %copy-done.8), custom_call_target="tpu_custom_call" | custom-call | tf_op jit(solution)/shard_map/raw/pallas_call | solution.py:419
  91.3 1.6 %grad_gates.1 = f32[6,128]{1,0:T(8,128)} custom-call(s32[6,128]{1,0:T(8,128)} %bitcast.19, bf16[128,1152]{1,0:T(8,128)(2,1)} %copy-done.6, f32[16,64]{1,0:T(8,128)} %bitcast.27), custom_call_target="tpu_custom_call" | custom-call | tf_op jit(solution)/shard_map/grad_gates/pallas_call | solution.py:498
  92.9 3.3 %collective-permute-done.19.got_ref = bf16[352,1024]{1,0:T(8,128)(2,1)S(1)} collective-permute-done((bf16[352,1024]{1,0:T(8,128)(2,1)}, bf16[352,1024]{1,0:T(8,128)(2,1)S(1)}, u32[]{:S(2)}, u32[]{:S(2)}) %collective-permute-start.19) | collective-permute-done | bytes 720928 | tf_op jit(solution)/shard_map/ppermute | solution.py:317
  (56 shorter events, 17.0 us)
Async XLA Ops:
  0.6 45.6 %collective-permute-start.12 = (bf16[352,2048]{1,0:T(8,128)(2,1)}, bf16[352,2048]{1,0:T(8,128)(2,1)S(1)}, u32[]{:S(2)}, u32[]{:S(2)}) collective-permute-start(bf16[352,2048]{1,0:T(8,128)(2,1)} %bitcast.15), channel_id=1, source_target_pairs={{0,16},{16,0},{1,17},{17,1},{2,18},{18,2},{3,19},{19,3},{4,20},{20... | collective-permute-start | bytes 4325384 | tf_op jit(solution)/shard_map/ppermute | solution.py:317
  6.2 41.6 %copy-start.6 = (bf16[128,1152]{1,0:T(8,128)(2,1)}, bf16[128,1152]{1,0:T(8,128)(2,1)S(1)}, u32[]{:S(2)}) copy-start(bf16[128,1152]{1,0:T(8,128)(2,1)S(1)} %pack.1.refs_0_.slots_ref) | copy-start | bytes 884740
  6.3 9.8 %collective-permute-start = (bf16[128,1152]{1,0:T(8,128)(2,1)S(1)}, bf16[128,1152]{1,0:T(8,128)(2,1)S(1)}, u32[]{:S(2)}, u32[]{:S(2)}) collective-permute-start(bf16[128,1152]{1,0:T(8,128)(2,1)S(1)} %pack.1.refs_0_.slots_ref), channel_id=1, source_target_pairs={{0,4},{1,5},{2,6},{3,7},{4,12},{5,13},{6,14},{7,15},{12,8},{13,9},... | collective-permute-start | bytes 884744 | tf_op jit(solution)/shard_map/ppermute | solution.py:305
  7.9 17.3 %collective-permute-start.2 = (bf16[128,1152]{1,0:T(8,128)(2,1)S(1)}, bf16[128,1152]{1,0:T(8,128)(2,1)S(1)}, u32[]{:S(2)}, u32[]{:S(2)}) collective-permute-start(bf16[128,1152]{1,0:T(8,128)(2,1)S(1)} %pack.1.refs_0_.slots_ref), channel_id=1, source_target_pairs={{0,2},{1,3},{2,0},{3,1},{4,6},{5,7},{6,4},{7,5},{8,10},{9,11},{10,... | collective-permute-start | bytes 884744 | tf_op jit(solution)/shard_map/ppermute | solution.py:311
  9.4 15.8 %collective-permute-start.1 = (bf16[128,1152]{1,0:T(8,128)(2,1)S(1)}, bf16[128,1152]{1,0:T(8,128)(2,1)S(1)}, u32[]{:S(2)}, u32[]{:S(2)}) collective-permute-start(bf16[128,1152]{1,0:T(8,128)(2,1)S(1)} %pack.1.refs_0_.slots_ref), channel_id=1, source_target_pairs={{0,8},{1,9},{2,10},{3,11},{4,0},{5,1},{6,2},{7,3},{12,4},{13,5},{1... | collective-permute-start | bytes 884744 | tf_op jit(solution)/shard_map/ppermute | solution.py:308
  16.1 13.1 %collective-permute-start.9 = (bf16[128,1152]{1,0:T(8,128)(2,1)S(1)}, bf16[128,1152]{1,0:T(8,128)(2,1)S(1)}, u32[]{:S(2)}, u32[]{:S(2)}) collective-permute-start(bf16[128,1152]{1,0:T(8,128)(2,1)S(1)} %collective-permute-done.after_ref.refs_2_), channel_id=1, source_target_pairs={{0,4},{1,5},{2,6},{3,7},{4,12},{5,13},{6,14},{7,15},{12,8},{13,9},... | collective-permute-start | bytes 884744 | tf_op jit(solution)/shard_map/ppermute | solution.py:305
  23.7 7.9 %collective-permute-start.8 = (bf16[128,1152]{1,0:T(8,128)(2,1)S(1)}, bf16[128,1152]{1,0:T(8,128)(2,1)S(1)}, u32[]{:S(2)}, u32[]{:S(2)}) collective-permute-start(bf16[128,1152]{1,0:T(8,128)(2,1)S(1)} %collective-permute-done.after_ref.refs_2_), channel_id=1, source_target_pairs={{0,2},{1,3},{2,0},{3,1},{4,6},{5,7},{6,4},{7,5},{8,10},{9,11},{10,... | collective-permute-start | bytes 884744 | tf_op jit(solution)/shard_map/ppermute | solution.py:311
  25.2 21.0 %collective-permute-start.3 = (bf16[128,1152]{1,0:T(8,128)(2,1)S(1)}, bf16[128,1152]{1,0:T(8,128)(2,1)S(1)}, u32[]{:S(2)}, u32[]{:S(2)}) collective-permute-start(bf16[128,1152]{1,0:T(8,128)(2,1)S(1)} %collective-permute-done.1.refs_6_), channel_id=1, source_target_pairs={{0,2},{1,3},{2,0},{3,1},{4,6},{5,7},{6,4},{7,5},{8,10},{9,11},{10,... | collective-permute-start | bytes 884744 | tf_op jit(solution)/shard_map/ppermute | solution.py:311
  31.6 14.6 %collective-permute-start.10 = (bf16[128,1152]{1,0:T(8,128)(2,1)S(1)}, bf16[128,1152]{1,0:T(8,128)(2,1)S(1)}, u32[]{:S(2)}, u32[]{:S(2)}) collective-permute-start(bf16[128,1152]{1,0:T(8,128)(2,1)S(1)} %collective-permute-done.9.refs_4_), channel_id=1, source_target_pairs={{0,2},{1,3},{2,0},{3,1},{4,6},{5,7},{6,4},{7,5},{8,10},{9,11},{10,... | collective-permute-start | bytes 884744 | tf_op jit(solution)/shard_map/ppermute | solution.py:311
  34.2 16.4 %copy-start.10 = (bf16[1,1,1024,704]{2,3,1,0:T(8,128)(2,1)S(1)}, bf16[1,1,1024,704]{2,3,1,0:T(8,128)(2,1)}, u32[]{:S(2)}) copy-start(bf16[1,1,1024,704]{2,3,1,0:T(8,128)(2,1)} %param.8) | copy-start | bytes 4325380
  34.2 11.9 %collective-permute-start.5 = (bf16[128,1024]{1,0:T(8,128)(2,1)S(1)}, bf16[128,1024]{1,0:T(8,128)(2,1)S(1)}, u32[]{:S(2)}, u32[]{:S(2)}) collective-permute-start(bf16[128,1024]{1,0:T(8,128)(2,1)S(1)} %later_pack.1.refs_0_), channel_id=1, source_target_pairs={{0,4},{1,5},{2,6},{3,7},{4,12},{5,13},{6,14},{7,15},{12,8},{13,9},... | collective-permute-start | bytes 786440 | tf_op jit(solution)/shard_map/ppermute | solution.py:305
  37.7 8.5 %collective-permute-start.11 = (bf16[128,1024]{1,0:T(8,128)(2,1)S(1)}, bf16[128,1024]{1,0:T(8,128)(2,1)S(1)}, u32[]{:S(2)}, u32[]{:S(2)}) collective-permute-start(bf16[128,1024]{1,0:T(8,128)(2,1)S(1)} %later_pack.1.refs_0_), channel_id=1, source_target_pairs={{0,8},{1,9},{2,10},{3,11},{4,0},{5,1},{6,2},{7,3},{12,4},{13,5},{1... | collective-permute-start | bytes 786440 | tf_op jit(solution)/shard_map/ppermute | solution.py:308
  46.2 15.6 %copy-start.5 = (bf16[352,2048]{1,0:T(8,128)(2,1)}, bf16[352,2048]{1,0:T(8,128)(2,1)S(1)}, u32[]{:S(2)}) copy-start(bf16[352,2048]{1,0:T(8,128)(2,1)S(1)} %collective-permute-done.12.refs_0_) | copy-start | bytes 4325380
  47.8 2.8 %collective-permute-start.13 = (bf16[528,1024]{1,0:T(8,128)(2,1)S(1)}, bf16[528,1024]{1,0:T(8,128)(2,1)S(1)}, u32[]{:S(2)}, u32[]{:S(2)}) collective-permute-start(bf16[528,1024]{1,0:T(8,128)(2,1)S(1)} %get-tuple-element.39), channel_id=1, source_target_pairs={{0,1},{1,0},{2,3},{3,2},{4,5},{5,4},{6,7},{7,6},{8,9},{9,8},{10,11... | collective-permute-start | bytes 3244040 | tf_op jit(solution)/shard_map/ppermute | solution.py:314
  47.9 11.0 %collective-permute-start.7 = (bf16[128,1024]{1,0:T(8,128)(2,1)S(1)}, bf16[128,1024]{1,0:T(8,128)(2,1)S(1)}, u32[]{:S(2)}, u32[]{:S(2)}) collective-permute-start(bf16[128,1024]{1,0:T(8,128)(2,1)S(1)} %collective-permute-done.5.refs_2_), channel_id=1, source_target_pairs={{0,4},{1,5},{2,6},{3,7},{4,12},{5,13},{6,14},{7,15},{12,8},{13,9},... | collective-permute-start | bytes 786440 | tf_op jit(solution)/shard_map/ppermute | solution.py:305
  48.1 10.8 %collective-permute-start.4 = (bf16[128,1024]{1,0:T(8,128)(2,1)S(1)}, bf16[128,1024]{1,0:T(8,128)(2,1)S(1)}, u32[]{:S(2)}, u32[]{:S(2)}) collective-permute-start(bf16[128,1024]{1,0:T(8,128)(2,1)S(1)} %later_pack.1.refs_0_), channel_id=1, source_target_pairs={{0,2},{1,3},{2,0},{3,1},{4,6},{5,7},{6,4},{7,5},{8,10},{9,11},{10,... | collective-permute-start | bytes 786440 | tf_op jit(solution)/shard_map/ppermute | solution.py:311
  49.4 15.3 %collective-permute-start.6 = (bf16[128,1024]{1,0:T(8,128)(2,1)S(1)}, bf16[128,1024]{1,0:T(8,128)(2,1)S(1)}, u32[]{:S(2)}, u32[]{:S(2)}) collective-permute-start(bf16[128,1024]{1,0:T(8,128)(2,1)S(1)} %collective-permute-done.5.refs_2_), channel_id=1, source_target_pairs={{0,2},{1,3},{2,0},{3,1},{4,6},{5,7},{6,4},{7,5},{8,10},{9,11},{10,... | collective-permute-start | bytes 786440 | tf_op jit(solution)/shard_map/ppermute | solution.py:311
  53.6 15.5 %collective-permute-start.16 = (bf16[352,512]{1,0:T(8,128)(2,1)S(1)}, bf16[352,512]{1,0:T(8,128)(2,1)S(1)}, u32[]{:S(2)}, u32[]{:S(2)}) collective-permute-start(bf16[352,512]{1,0:T(8,128)(2,1)S(1)} %get-tuple-element.49), channel_id=1, source_target_pairs={{0,16},{16,0},{1,17},{17,1},{2,18},{18,2},{3,19},{19,3},{4,20},{20... | collective-permute-start | bytes 1081352 | tf_op jit(solution)/shard_map/ppermute | solution.py:317
  54.2 17.6 %collective-permute-start.17 = (bf16[352,512]{1,0:T(8,128)(2,1)S(1)}, bf16[352,512]{1,0:T(8,128)(2,1)S(1)}, u32[]{:S(2)}, u32[]{:S(2)}) collective-permute-start(bf16[352,512]{1,0:T(8,128)(2,1)S(1)} %get-tuple-element.50), channel_id=1, source_target_pairs={{0,16},{16,0},{1,17},{17,1},{2,18},{18,2},{3,19},{19,3},{4,20},{20... | collective-permute-start | bytes 1081352 | tf_op jit(solution)/shard_map/ppermute | solution.py:317
  59.0 8.9 %collective-permute-start.14 = (bf16[128,1024]{1,0:T(8,128)(2,1)S(1)}, bf16[128,1024]{1,0:T(8,128)(2,1)S(1)}, u32[]{:S(2)}, u32[]{:S(2)}) collective-permute-start(bf16[128,1024]{1,0:T(8,128)(2,1)S(1)} %collective-permute-done.7.refs_4_), channel_id=1, source_target_pairs={{0,2},{1,3},{2,0},{3,1},{4,6},{5,7},{6,4},{7,5},{8,10},{9,11},{10,... | collective-permute-start | bytes 786440 | tf_op jit(solution)/shard_map/ppermute | solution.py:311
  59.8 8.1 %collective-permute-start.15 = (bf16[128,1024]{1,0:T(8,128)(2,1)S(1)}, bf16[128,1024]{1,0:T(8,128)(2,1)S(1)}, u32[]{:S(2)}, u32[]{:S(2)}) collective-permute-start(bf16[128,1024]{1,0:T(8,128)(2,1)S(1)} %collective-permute-done.4.refs_1_), channel_id=1, source_target_pairs={{0,8},{1,9},{2,10},{3,11},{4,0},{5,1},{6,2},{7,3},{12,4},{13,5},{1... | collective-permute-start | bytes 786440 | tf_op jit(solution)/shard_map/ppermute | solution.py:308
  71.8 2.7 %collective-permute-start.18 = (bf16[512,1024]{1,0:T(8,128)(2,1)S(1)}, bf16[512,1024]{1,0:T(8,128)(2,1)S(1)}, u32[]{:S(2)}, u32[]{:S(2)}) collective-permute-start(bf16[512,1024]{1,0:T(8,128)(2,1)S(1)} %get-tuple-element.51), channel_id=1, source_target_pairs={{0,1},{1,0},{2,3},{3,2},{4,5},{5,4},{6,7},{7,6},{8,9},{9,8},{10,11... | collective-permute-start | bytes 3145736 | tf_op jit(solution)/shard_map/ppermute | solution.py:314
  77.8 18.4 %collective-permute-start.19 = (bf16[352,1024]{1,0:T(8,128)(2,1)}, bf16[352,1024]{1,0:T(8,128)(2,1)S(1)}, u32[]{:S(2)}, u32[]{:S(2)}) collective-permute-start(bf16[352,1024]{1,0:T(8,128)(2,1)} %get-tuple-element.57), channel_id=1, source_target_pairs={{0,16},{16,0},{1,17},{17,1},{2,18},{18,2},{3,19},{19,3},{4,20},{20... | collective-permute-start | bytes 2162696 | tf_op jit(solution)/shard_map/ppermute | solution.py:317
  79.6 11.0 %all-to-all-start = ((f32[16,1,64]{2,1,0:T(1,128)}), f32[16,1,64]{2,1,0:T(1,128)S(1)}, u32[]{:S(2)}, u32[]{:S(2)}) async-start(f32[16,1,64]{2,1,0:T(1,128)} %bitcast.10), calls=%async_computation | async-start | bytes 16384 | tf_op jit(solution)/shard_map/all_to_all | solution.py:497
  (9 other events, 24.3 us)

commit v14 on v13

--- a/solution.py
+++ b/solution.py
@@ -43,7 +43,7 @@
     return [(i, i ^ bit) for i in range(NZ * NY * NC)]
 
 
-def pack_kernel(experts, width, routes_hbm, gates_hbm, grad_hbm, out_ref, *scratch):
+def pack_kernel(experts, width, routes_hbm, gates_hbm, grad_hbm, out_ref, later_ref, *scratch):
     routes_ref, gates_ref, sems = scratch
     copies = [
         pltpu.make_async_copy(src, dst, sems.at[i])
@@ -52,6 +52,7 @@
                 (routes_hbm, routes_ref),
                 (gates_hbm, gates_ref),
                 (grad_hbm.at[:, :width], out_ref.at[:, :width]),
+                (grad_hbm.at[:, width:], later_ref),
             )
         )
     ]
@@ -83,13 +84,7 @@
     out_ref[:experts, width:] = dense.astype(jnp.bfloat16)
     out_ref[experts : 2 * experts, width:] = slots.astype(jnp.bfloat16)
     copies[2].wait()
-
-
-def later_pack_kernel(low, grad_hbm, after_ref, out_ref, sem):
-    del after_ref
-    copy = pltpu.make_async_copy(grad_hbm.at[:, pl.ds(low, out_ref.shape[1])], out_ref, sem)
-    copy.start()
-    copy.wait()
+    copies[3].wait()
 
 
 def pair_place(arrival):
@@ -322,28 +317,20 @@
     def pack():
         return pl.pallas_call(
             functools.partial(pack_kernel, experts, widths[0]),
-            out_shape=shape((tokens, widths[0] + tokens), bf16),
+            out_shape=[
+                shape((tokens, widths[0] + tokens), bf16),
+                shape((tokens, widths[1]), bf16),
+            ],
             in_specs=[ANY] * 3,
-            out_specs=VMEM,
+            out_specs=[VMEM] * 2,
             scratch_shapes=[
                 pltpu.VMEM(routes_t.shape, routes_t.dtype),
                 pltpu.VMEM(gates_t.shape, gates_t.dtype),
-                dma((3,)),
+                dma((4,)),
             ],
-            compiler_params=params(48),
+            compiler_params=params(60),
             name="pack",
         )(routes_t, gates_t, grad_out)
-
-    def later_pack(after):
-        return pl.pallas_call(
-            functools.partial(later_pack_kernel, widths[0]),
-            out_shape=shape((tokens, widths[1]), bf16),
-            in_specs=[ANY] * 2,
-            out_specs=VMEM,
-            scratch_shapes=[dma],
-            compiler_params=params(48),
-            name="later_pack",
-        )(grad_out, after)
 
     def first_pick(blocks):
         return pl.pallas_call(
@@ -467,18 +454,19 @@
             name="finish",
         )(own, got, *before)
 
-    x0 = pack()
+    x0, x1 = pack()
     w = [swap(weight)]
-    f0, r0, y0 = forward(x0), backward(x0), across(x0)
-    x1 = later_pack(f0)
-    ff0, yf0 = forward(f0), across(f0)
-    f1, r1, yr0 = forward(x1), backward(behind(x1, ff0)), across(behind(r0, y0))
+    f0, y0 = forward(x0), across(x0)
+    ff0, yf0 = forward(behind(f0, y0)), across(behind(f0, y0))
+    r0 = backward(behind(x0, ff0, yf0))
     yff0 = across(behind(ff0, yf0))
+    f1, yr0 = forward(behind(x1, r0)), across(behind(r0, yff0))
+    r1 = backward(behind(x1, r0))
     mine0, theirs0, pmat, gslot = first_pick(
-        [x0, y0, f0, yf0, ff0, yff0, r0, behind(yr0, f1, r1, w[0])]
+        [x0, y0, f0, yf0, ff0, yff0, r0, behind(yr0, w[0])]
     )
     ff1, yf1, y1 = forward(f1), across(behind(f1, yr0)), across(behind(x1, yr0))
-    got = sibling(theirs0)
+    got = sibling(behind(theirs0, f1, r1))
     rows0, send0, own0, slot_gates, hs = first_products(mine0, got, gslot)
     got0 = [swap(part) for part in send0]
     yff1, ry1 = across(behind(ff1, rows0)), backward(behind(y1, ff1, rows0))

time: 97.5 us -> 96.6 us (level)
  waiting for transfers between devices: 30.6 us -> 38.2 us
  starting transfers between devices: 34.4 us -> 26.8 us
  local copies, waits for them, and re-layouts: 4.07 us -> 1.58 us
  Pallas kernels: 27.2 us -> 28.9 us
    ppermute x7, waiting for transfers between devices: 5.6 us -> 20.7 us  [across(): return lax.ppermute(x, 'expert', swap_pairs(2))]
    ppermute x4, waiting for transfers between devices: 17.3 us -> 6.11 us  [forward(): return lax.ppermute(x, 'expert', ring_pairs(1))]
    ppermute x4, starting transfers between devices: 12.9 us -> 4.41 us  [forward(): return lax.ppermute(x, 'expert', ring_pairs(1))]
    ppermute x3, waiting for transfers between devices: 0.04 us -> 3.94 us  [backward(): return lax.ppermute(x, 'expert', ring_pairs(-1))]
    unnamed x24 -> x18, local copies, waits for them, and re-layouts: 4.07 us -> 1.58 us
    ppermute x3, starting transfers between devices: 3.34 us -> 5.6 us  [backward(): return lax.ppermute(x, 'expert', ring_pairs(-1))]
    pallas_call x1, Pallas kernels: 0.19 us -> 1.89 us  [pack(): pl.pallas_call(functools.partial(pack_kernel, experts, widths[0]), out_sh...]
    all_to_all x1, starting transfers between devices: 4.54 us -> 3.48 us  [ring_shards(): lax.all_to_all(back, 'expert', split_axis=0, concat_axis=0, tiled=True)]
  transfers between devices with their start and end apart: 21 -> 21, of which waited for: 9 -> 12; matrix products, arithmetic and copies ran while one was open for 0% -> 0% of each run, Pallas kernels for 22% -> 26%
where the time goes in v14:
time: 96.6 us; the launch traced here: 96.3 us
  waiting for transfers between devices  38.2 us (40%)
  Pallas kernels  28.9 us (30%)
  starting transfers between devices  26.8 us (28%)
  local copies, waits for them, and re-layouts  1.58 us (2%)
    ppermute x7, waiting for transfers between devices, across(): return lax.ppermute(x, 'expert', swap_pairs(2))  20.7 us
    ppermute x7, starting transfers between devices, across(): return lax.ppermute(x, 'expert', swap_pairs(2))  7.73 us
    pallas_call x1, Pallas kernels, raw_rest(): pl.pallas_call(functools.partial(raw_kernel, half, columns[1]), grid=(slo...  6.46 us
    ppermute x4, waiting for transfers between devices, swap(): return lax.ppermute(x, 'dp', [(0, 1), (1, 0)])  6.3 us
    ppermute x4, waiting for transfers between devices, forward(): return lax.ppermute(x, 'expert', ring_pairs(1))  6.11 us
    ppermute x4, starting transfers between devices, swap(): return lax.ppermute(x, 'dp', [(0, 1), (1, 0)])  5.63 us
    ppermute x3, starting transfers between devices, backward(): return lax.ppermute(x, 'expert', ring_pairs(-1))  5.6 us
    ppermute x4, starting transfers between devices, forward(): return lax.ppermute(x, 'expert', ring_pairs(1))  4.41 us
  transfers between devices with their start and end apart: 21, of which 12 were waited for; matrix products, arithmetic and copies ran while one was open for 0% of the time, Pallas kernels for 26%

profile of v14, /device:TPU:0, one launch (start us, length us, event | category | flops | bytes accessed | tf_op | source)
XLA Modules:
  0.0 96.3 jit_solution(4458712090763240057)
XLA Ops:
  0.6 3.0 %collective-permute-start.11 = (bf16[352,2048]{1,0:T(8,128)(2,1)}, bf16[352,2048]{1,0:T(8,128)(2,1)S(1)}, u32[]{:S(2)}, u32[]{:S(2)}) collective-permute-start(bf16[352,2048]{1,0:T(8,128)(2,1)} %bitcast.15), channel_id=1, source_target_pairs={{0,16},{16,0},{1,17},{17,1},{2,18},{18,2},{3,19},{19,3},{4,20},{20... | collective-permute-start | bytes 4325384 | tf_op jit(solution)/shard_map/ppermute | solution.py:312
  3.6 1.9 %pack.1 = (bf16[128,1152]{1,0:T(8,128)(2,1)}, bf16[128,1024]{1,0:T(8,128)(2,1)}) custom-call(s32[6,128]{1,0:T(8,128)} %bitcast.25, bf16[6,128]{1,0:T(8,128)(2,1)} %bitcast.28, bf16[128,2048]{1,0:T(8,128)(2,1)} %grad_hbm.1), custom_call_target="tpu_custom_call" | custom-call | tf_op jit(solution)/shard_map/pack/pallas_call | solution.py:318
  5.5 1.6 %collective-permute-start.1 = (bf16[128,1152]{1,0:T(8,128)(2,1)}, bf16[128,1152]{1,0:T(8,128)(2,1)S(1)}, u32[]{:S(2)}, u32[]{:S(2)}) collective-permute-start(bf16[128,1152]{1,0:T(8,128)(2,1)} %get-tuple-element.40.refs_0_.slots_ref), channel_id=1, source_target_pairs={{0,2},{1,3},{2,0},{3,1},{4,6},{5,7},{6,4},{7,5},{8,10},{9,11},{10,... | collective-permute-start | bytes 884744 | tf_op jit(solution)/shard_map/ppermute | solution.py:306
  7.1 1.6 %collective-permute-start = (bf16[128,1152]{1,0:T(8,128)(2,1)}, bf16[128,1152]{1,0:T(8,128)(2,1)S(1)}, u32[]{:S(2)}, u32[]{:S(2)}) collective-permute-start(bf16[128,1152]{1,0:T(8,128)(2,1)} %get-tuple-element.40.refs_0_.slots_ref), channel_id=1, source_target_pairs={{0,4},{1,5},{2,6},{3,7},{4,12},{5,13},{6,14},{7,15},{12,8},{13,9},... | collective-permute-start | bytes 884744 | tf_op jit(solution)/shard_map/ppermute | solution.py:300
  8.7 5.6 %collective-permute-done.1.refs_1_ = bf16[128,1152]{1,0:T(8,128)(2,1)S(1)} collective-permute-done((bf16[128,1152]{1,0:T(8,128)(2,1)}, bf16[128,1152]{1,0:T(8,128)(2,1)S(1)}, u32[]{:S(2)}, u32[]{:S(2)}) %collective-permute-start.1) | collective-permute-done | bytes 294944 | tf_op jit(solution)/shard_map/ppermute | solution.py:306
  14.3 2.2 %collective-permute-done.refs_2_ = bf16[128,1152]{1,0:T(8,128)(2,1)S(1)} collective-permute-done((bf16[128,1152]{1,0:T(8,128)(2,1)}, bf16[128,1152]{1,0:T(8,128)(2,1)S(1)}, u32[]{:S(2)}, u32[]{:S(2)}) %collective-permute-start) | collective-permute-done | bytes 294944 | tf_op jit(solution)/shard_map/ppermute | solution.py:300
  17.8 5.9 %collective-permute-done.3.refs_3_ = bf16[128,1152]{1,0:T(8,128)(2,1)S(1)} collective-permute-done((bf16[128,1152]{1,0:T(8,128)(2,1)S(1)}, bf16[128,1152]{1,0:T(8,128)(2,1)S(1)}, u32[]{:S(2)}, u32[]{:S(2)}) %collective-permute-start.3) | collective-permute-done | bytes 294944 | tf_op jit(solution)/shard_map/ppermute | solution.py:306
  27.9 3.9 %collective-permute-done.4.refs_6_ = bf16[128,1152]{1,0:T(8,128)(2,1)S(1)} collective-permute-done((bf16[128,1152]{1,0:T(8,128)(2,1)}, bf16[128,1152]{1,0:T(8,128)(2,1)S(1)}, u32[]{:S(2)}, u32[]{:S(2)}) %collective-permute-start.4) | collective-permute-done | bytes 294944 | tf_op jit(solution)/shard_map/ppermute | solution.py:303
  31.8 2.3 %collective-permute-done.5.refs_5_ = bf16[128,1152]{1,0:T(8,128)(2,1)S(1)} collective-permute-done((bf16[128,1152]{1,0:T(8,128)(2,1)S(1)}, bf16[128,1152]{1,0:T(8,128)(2,1)S(1)}, u32[]{:S(2)}, u32[]{:S(2)}) %collective-permute-start.5) | collective-permute-done | bytes 294944 | tf_op jit(solution)/shard_map/ppermute | solution.py:306
  35.6 3.1 %collective-permute-start.12 = (bf16[128,1024]{1,0:T(8,128)(2,1)}, bf16[128,1024]{1,0:T(8,128)(2,1)S(1)}, u32[]{:S(2)}, u32[]{:S(2)}) collective-permute-start(bf16[128,1024]{1,0:T(8,128)(2,1)} %get-tuple-element.44.refs_0_), channel_id=1, source_target_pairs={{0,8},{1,9},{2,10},{3,11},{4,0},{5,1},{6,2},{7,3},{12,4},{13,5},{1... | collective-permute-start | bytes 786440 | tf_op jit(solution)/shard_map/ppermute | solution.py:303
  38.8 2.1 %collective-permute-done.6.refs_7_ = bf16[128,1152]{1,0:T(8,128)(2,1)S(1)} collective-permute-done((bf16[128,1152]{1,0:T(8,128)(2,1)S(1)}, bf16[128,1152]{1,0:T(8,128)(2,1)S(1)}, u32[]{:S(2)}, u32[]{:S(2)}) %collective-permute-start.6) | collective-permute-done | bytes 294944 | tf_op jit(solution)/shard_map/ppermute | solution.py:306
  41.8 1.6 %first_pick.1 = (bf16[512,1024]{1,0:T(8,128)(2,1)S(1)}, bf16[528,1024]{1,0:T(8,128)(2,1)S(1)}, bf16[1024,128]{1,0:T(8,128)(2,1)S(1)}, f32[8,128]{1,0:T(8,128)S(1)}) custom-call(bf16[128,1152]{1,0:T(8,128)(2,1)S(1)} %copy-done.4, bf16[128,1152]{1,0:T(8,128)(2,1)S(1)} %collective-permute-done.1.refs_1_, bf16[128,1152]{1,0:T(8,128)(2,1)S(1)} %collective-permute-done.refs_2_, ...), custom_call_target="tpu_custom_call" | custom-call | flops 3000000000 | bytes 9437184 | tf_op jit(solution)/shard_map/first_pick/pallas_call | solution.py:336
  43.4 2.8 %collective-permute-done.8.refs_2_ = bf16[128,1024]{1,0:T(8,128)(2,1)S(1)} collective-permute-done((bf16[128,1024]{1,0:T(8,128)(2,1)}, bf16[128,1024]{1,0:T(8,128)(2,1)S(1)}, u32[]{:S(2)}, u32[]{:S(2)}) %collective-permute-start.8) | collective-permute-done | bytes 262176 | tf_op jit(solution)/shard_map/ppermute | solution.py:300
  46.2 2.0 %collective-permute-start.10 = (bf16[128,1024]{1,0:T(8,128)(2,1)S(1)}, bf16[128,1024]{1,0:T(8,128)(2,1)S(1)}, u32[]{:S(2)}, u32[]{:S(2)}) collective-permute-start(bf16[128,1024]{1,0:T(8,128)(2,1)S(1)} %collective-permute-done.8.refs_2_), channel_id=1, source_target_pairs={{0,4},{1,5},{2,6},{3,7},{4,12},{5,13},{6,14},{7,15},{12,8},{13,9},... | collective-permute-start | bytes 786440 | tf_op jit(solution)/shard_map/ppermute | solution.py:300
  50.2 3.0 %first_products.1 = (f32[1,1024]{1,0:T(1,128)S(1)}, bf16[704,1024]{1,0:T(8,128)(2,1)S(1)}, bf16[1024,1024]{1,0:T(8,128)(2,1)S(1)}, bf16[352,512]{1,0:T(8,128)(2,...) custom-call(bf16[512,1024]{1,0:T(8,128)(2,1)S(1)} %get-tuple-element.47.mine_ref, ...), custom_call_target="tpu_custom_call" | custom-call | flops 3000000000 | bytes 9437184 | tf_op jit(solution)/shard_map/first_products/pallas_call | solution.py:367
  55.3 3.2 %hidden_weight.1.forward_ref = bf16[1024,1024]{1,0:T(8,128)(2,1)S(1)} custom-call(bf16[352,2048]{1,0:T(8,128)(2,1)S(1)} %bitcast.17, bf16[352,2048]{1,0:T(8,128)(2,1)S(1)} %collective-permute-done.11.refs_0_, bf16[704,1024]{1,0:T(8,128)(2,1)S(1)} %bitcast.20), custom_call_target="tpu_custom_call" | custom-call | flops 3000000000 | bytes 9437184 | tf_op jit(solution)/shard_map/hidden_weight/pallas_call | solution.py:422
  60.1 2.9 %raw_part.1 = (f32[704,1024]{1,0:T(8,128)S(1)}, f32[16,64]{1,0:T(8,128)S(1)}) custom-call(bf16[1024,1024]{1,0:T(8,128)(2,1)S(1)} %get-tuple-element.51.rows_ref, bf16[352,2048]{1,0:T(8,128)(2,1)S(1)} %bitcast.18, bf16[352,2048]{1,0:T(8,128)(2,1)S(1)} %collective-permute-done.11.refs_0_, bf16[704,1024]{1,0:T(8,128)(2,1)S(1)} %bitcast.21), custom_call_target="tpu_custom_call" | custom-call | flops 3000000000 | bytes 9437184 | tf_op jit(solution)/shard_map/raw_part/pallas_call | solution.py:394
  63.0 4.9 %collective-permute-done.14.refs_5_ = bf16[128,1024]{1,0:T(8,128)(2,1)S(1)} collective-permute-done((bf16[128,1024]{1,0:T(8,128)(2,1)S(1)}, bf16[128,1024]{1,0:T(8,128)(2,1)S(1)}, u32[]{:S(2)}, u32[]{:S(2)}) %collective-permute-start.14) | collective-permute-done | bytes 262176 | tf_op jit(solution)/shard_map/ppermute | solution.py:306
  69.1 1.9 %collective-permute-done.17.got_ref = bf16[352,512]{1,0:T(8,128)(2,1)S(1)} collective-permute-done((bf16[352,512]{1,0:T(8,128)(2,1)S(1)}, bf16[352,512]{1,0:T(8,128)(2,1)S(1)}, u32[]{:S(2)}, u32[]{:S(2)}) %collective-permute-start.17) | collective-permute-done | bytes 360480 | tf_op jit(solution)/shard_map/ppermute | solution.py:312
  73.7 3.3 %products.1 = (bf16[1024,1024]{1,0:T(8,128)(2,1)S(1)}, bf16[352,1024]{1,0:T(8,128)(2,1)}, bf16[352,1024]{1,0:T(8,128)(2,1)S(1)}) custom-call(bf16[512,1024]{1,0:T(8,128)(2,1)S(1)} %get-tuple-element.57.mine_ref, bf16[512,1024]{1,0:T(8,128)(2,1)S(1)} %collective-permute-done.18.got_ref, bf16[704,1024]{1,0:T(8,128)(2,1)S(1)} %get-tuple-element.65.hs_ref), custom_call_target="tpu_custom_call" | custom-call | tf_op jit(solution)/shard_map/products/pallas_call | solution.py:379
  78.8 3.5 %all-to-all-start = ((f32[16,1,64]{2,1,0:T(1,128)}), f32[16,1,64]{2,1,0:T(1,128)S(1)}, u32[]{:S(2)}, u32[]{:S(2)}) async-start(f32[16,1,64]{2,1,0:T(1,128)} %bitcast.10), calls=%async_computation | async-start | bytes 16384 | tf_op jit(solution)/shard_map/all_to_all | solution.py:485
  82.3 6.5 %raw.1 = bf16[704,1024]{1,0:T(8,128)(2,1)} custom-call(bf16[1024,1024]{1,0:T(8,128)(2,1)} %copy-done, bf16[352,2048]{1,0:T(8,128)(2,1)} %bitcast.16, bf16[352,2048]{1,0:T(8,128)(2,1)} %copy-done.3, f32[704,1024]{1,0:T(8,128)} %copy-done.1, f32[1,1024]{1,0:T(1,128)} %copy-done.6), custom_call_target="tpu_custom_call" | custom-call | tf_op jit(solution)/shard_map/raw/pallas_call | solution.py:406
  89.4 1.6 %grad_gates.1 = f32[6,128]{1,0:T(8,128)} custom-call(s32[6,128]{1,0:T(8,128)} %bitcast.26, bf16[128,1152]{1,0:T(8,128)(2,1)} %get-tuple-element.40.refs_0_.slots_ref, f32[16,64]{1,0:T(8,128)} %bitcast.24), custom_call_target="tpu_custom_call" | custom-call | tf_op jit(solution)/shard_map/grad_gates/pallas_call | solution.py:486
  91.0 4.4 %collective-permute-done.19.got_ref = bf16[352,1024]{1,0:T(8,128)(2,1)S(1)} collective-permute-done((bf16[352,1024]{1,0:T(8,128)(2,1)}, bf16[352,1024]{1,0:T(8,128)(2,1)S(1)}, u32[]{:S(2)}, u32[]{:S(2)}) %collective-permute-start.19) | collective-permute-done | bytes 720928 | tf_op jit(solution)/shard_map/ppermute | solution.py:312
  (49 shorter events, 20.9 us)
Async XLA Ops:
  0.6 40.2 %collective-permute-start.11 = (bf16[352,2048]{1,0:T(8,128)(2,1)}, bf16[352,2048]{1,0:T(8,128)(2,1)S(1)}, u32[]{:S(2)}, u32[]{:S(2)}) collective-permute-start(bf16[352,2048]{1,0:T(8,128)(2,1)} %bitcast.15), channel_id=1, source_target_pairs={{0,16},{16,0},{1,17},{17,1},{2,18},{18,2},{3,19},{19,3},{4,20},{20... | collective-permute-start | bytes 4325384 | tf_op jit(solution)/shard_map/ppermute | solution.py:312
  5.5 8.7 %collective-permute-start.1 = (bf16[128,1152]{1,0:T(8,128)(2,1)}, bf16[128,1152]{1,0:T(8,128)(2,1)S(1)}, u32[]{:S(2)}, u32[]{:S(2)}) collective-permute-start(bf16[128,1152]{1,0:T(8,128)(2,1)} %get-tuple-element.40.refs_0_.slots_ref), channel_id=1, source_target_pairs={{0,2},{1,3},{2,0},{3,1},{4,6},{5,7},{6,4},{7,5},{8,10},{9,11},{10,... | collective-permute-start | bytes 884744 | tf_op jit(solution)/shard_map/ppermute | solution.py:306
  7.1 9.3 %collective-permute-start = (bf16[128,1152]{1,0:T(8,128)(2,1)}, bf16[128,1152]{1,0:T(8,128)(2,1)S(1)}, u32[]{:S(2)}, u32[]{:S(2)}) collective-permute-start(bf16[128,1152]{1,0:T(8,128)(2,1)} %get-tuple-element.40.refs_0_.slots_ref), channel_id=1, source_target_pairs={{0,4},{1,5},{2,6},{3,7},{4,12},{5,13},{6,14},{7,15},{12,8},{13,9},... | collective-permute-start | bytes 884744 | tf_op jit(solution)/shard_map/ppermute | solution.py:300
  16.4 7.3 %collective-permute-start.3 = (bf16[128,1152]{1,0:T(8,128)(2,1)S(1)}, bf16[128,1152]{1,0:T(8,128)(2,1)S(1)}, u32[]{:S(2)}, u32[]{:S(2)}) collective-permute-start(bf16[128,1152]{1,0:T(8,128)(2,1)S(1)} %collective-permute-done.refs_2_), channel_id=1, source_target_pairs={{0,2},{1,3},{2,0},{3,1},{4,6},{5,7},{6,4},{7,5},{8,10},{9,11},{10,... | collective-permute-start | bytes 884744 | tf_op jit(solution)/shard_map/ppermute | solution.py:306
  16.9 7.9 %collective-permute-start.2 = (bf16[128,1152]{1,0:T(8,128)(2,1)S(1)}, bf16[128,1152]{1,0:T(8,128)(2,1)S(1)}, u32[]{:S(2)}, u32[]{:S(2)}) collective-permute-start(bf16[128,1152]{1,0:T(8,128)(2,1)S(1)} %collective-permute-done.refs_2_), channel_id=1, source_target_pairs={{0,4},{1,5},{2,6},{3,7},{4,12},{5,13},{6,14},{7,15},{12,8},{13,9},... | collective-permute-start | bytes 884744 | tf_op jit(solution)/shard_map/ppermute | solution.py:300
  24.8 6.9 %collective-permute-start.4 = (bf16[128,1152]{1,0:T(8,128)(2,1)}, bf16[128,1152]{1,0:T(8,128)(2,1)S(1)}, u32[]{:S(2)}, u32[]{:S(2)}) collective-permute-start(bf16[128,1152]{1,0:T(8,128)(2,1)} %get-tuple-element.40.refs_0_.slots_ref), channel_id=1, source_target_pairs={{0,8},{1,9},{2,10},{3,11},{4,0},{5,1},{6,2},{7,3},{12,4},{13,5},{1... | collective-permute-start | bytes 884744 | tf_op jit(solution)/shard_map/ppermute | solution.py:303
  26.3 7.8 %collective-permute-start.5 = (bf16[128,1152]{1,0:T(8,128)(2,1)S(1)}, bf16[128,1152]{1,0:T(8,128)(2,1)S(1)}, u32[]{:S(2)}, u32[]{:S(2)}) collective-permute-start(bf16[128,1152]{1,0:T(8,128)(2,1)S(1)} %collective-permute-done.2.refs_4_), channel_id=1, source_target_pairs={{0,2},{1,3},{2,0},{3,1},{4,6},{5,7},{6,4},{7,5},{8,10},{9,11},{10,... | collective-permute-start | bytes 884744 | tf_op jit(solution)/shard_map/ppermute | solution.py:306
  34.1 6.7 %collective-permute-start.6 = (bf16[128,1152]{1,0:T(8,128)(2,1)S(1)}, bf16[128,1152]{1,0:T(8,128)(2,1)S(1)}, u32[]{:S(2)}, u32[]{:S(2)}) collective-permute-start(bf16[128,1152]{1,0:T(8,128)(2,1)S(1)} %collective-permute-done.4.refs_6_), channel_id=1, source_target_pairs={{0,2},{1,3},{2,0},{3,1},{4,6},{5,7},{6,4},{7,5},{8,10},{9,11},{10,... | collective-permute-start | bytes 884744 | tf_op jit(solution)/shard_map/ppermute | solution.py:306
  35.6 7.8 %collective-permute-start.12 = (bf16[128,1024]{1,0:T(8,128)(2,1)}, bf16[128,1024]{1,0:T(8,128)(2,1)S(1)}, u32[]{:S(2)}, u32[]{:S(2)}) collective-permute-start(bf16[128,1024]{1,0:T(8,128)(2,1)} %get-tuple-element.44.refs_0_), channel_id=1, source_target_pairs={{0,8},{1,9},{2,10},{3,11},{4,0},{5,1},{6,2},{7,3},{12,4},{13,5},{1... | collective-permute-start | bytes 786440 | tf_op jit(solution)/shard_map/ppermute | solution.py:303
  38.8 7.5 %collective-permute-start.8 = (bf16[128,1024]{1,0:T(8,128)(2,1)}, bf16[128,1024]{1,0:T(8,128)(2,1)S(1)}, u32[]{:S(2)}, u32[]{:S(2)}) collective-permute-start(bf16[128,1024]{1,0:T(8,128)(2,1)} %get-tuple-element.44.refs_0_), channel_id=1, source_target_pairs={{0,4},{1,5},{2,6},{3,7},{4,12},{5,13},{6,14},{7,15},{12,8},{13,9},... | collective-permute-start | bytes 786440 | tf_op jit(solution)/shard_map/ppermute | solution.py:300
  41.8 18.3 %copy-start.3 = (bf16[352,2048]{1,0:T(8,128)(2,1)}, bf16[352,2048]{1,0:T(8,128)(2,1)S(1)}, u32[]{:S(2)}) copy-start(bf16[352,2048]{1,0:T(8,128)(2,1)S(1)} %collective-permute-done.11.refs_0_) | copy-start | bytes 4325380
  41.8 8.5 %copy-start.7 = (bf16[1,1,1024,704]{2,3,1,0:T(8,128)(2,1)S(1)}, bf16[1,1,1024,704]{2,3,1,0:T(8,128)(2,1)}, u32[]{:S(2)}) copy-start(bf16[1,1,1024,704]{2,3,1,0:T(8,128)(2,1)} %param.8) | copy-start | bytes 4325380
  46.2 4.0 %collective-permute-start.13 = (bf16[528,1024]{1,0:T(8,128)(2,1)S(1)}, bf16[528,1024]{1,0:T(8,128)(2,1)S(1)}, u32[]{:S(2)}, u32[]{:S(2)}) collective-permute-start(bf16[528,1024]{1,0:T(8,128)(2,1)S(1)} %get-tuple-element.49), channel_id=1, source_target_pairs={{0,1},{1,0},{2,3},{3,2},{4,5},{5,4},{6,7},{7,6},{8,9},{9,8},{10,11... | collective-permute-start | bytes 3244040 | tf_op jit(solution)/shard_map/ppermute | solution.py:309
  46.2 12.3 %collective-permute-start.10 = (bf16[128,1024]{1,0:T(8,128)(2,1)S(1)}, bf16[128,1024]{1,0:T(8,128)(2,1)S(1)}, u32[]{:S(2)}, u32[]{:S(2)}) collective-permute-start(bf16[128,1024]{1,0:T(8,128)(2,1)S(1)} %collective-permute-done.8.refs_2_), channel_id=1, source_target_pairs={{0,4},{1,5},{2,6},{3,7},{4,12},{5,13},{6,14},{7,15},{12,8},{13,9},... | collective-permute-start | bytes 786440 | tf_op jit(solution)/shard_map/ppermute | solution.py:300
  48.2 10.4 %collective-permute-start.7 = (bf16[128,1024]{1,0:T(8,128)(2,1)S(1)}, bf16[128,1024]{1,0:T(8,128)(2,1)S(1)}, u32[]{:S(2)}, u32[]{:S(2)}) collective-permute-start(bf16[128,1024]{1,0:T(8,128)(2,1)S(1)} %copy-done.5), channel_id=1, source_target_pairs={{0,2},{1,3},{2,0},{3,1},{4,6},{5,7},{6,4},{7,5},{8,10},{9,11},{10,... | collective-permute-start | bytes 786440 | tf_op jit(solution)/shard_map/ppermute | solution.py:306
  48.7 14.3 %collective-permute-start.9 = (bf16[128,1024]{1,0:T(8,128)(2,1)S(1)}, bf16[128,1024]{1,0:T(8,128)(2,1)S(1)}, u32[]{:S(2)}, u32[]{:S(2)}) collective-permute-start(bf16[128,1024]{1,0:T(8,128)(2,1)S(1)} %collective-permute-done.8.refs_2_), channel_id=1, source_target_pairs={{0,2},{1,3},{2,0},{3,1},{4,6},{5,7},{6,4},{7,5},{8,10},{9,11},{10,... | collective-permute-start | bytes 786440 | tf_op jit(solution)/shard_map/ppermute | solution.py:306
  53.2 15.9 %collective-permute-start.16 = (bf16[352,512]{1,0:T(8,128)(2,1)S(1)}, bf16[352,512]{1,0:T(8,128)(2,1)S(1)}, u32[]{:S(2)}, u32[]{:S(2)}) collective-permute-start(bf16[352,512]{1,0:T(8,128)(2,1)S(1)} %get-tuple-element.59), channel_id=1, source_target_pairs={{0,16},{16,0},{1,17},{17,1},{2,18},{18,2},{3,19},{19,3},{4,20},{20... | collective-permute-start | bytes 1081352 | tf_op jit(solution)/shard_map/ppermute | solution.py:312
  53.8 17.2 %collective-permute-start.17 = (bf16[352,512]{1,0:T(8,128)(2,1)S(1)}, bf16[352,512]{1,0:T(8,128)(2,1)S(1)}, u32[]{:S(2)}, u32[]{:S(2)}) collective-permute-start(bf16[352,512]{1,0:T(8,128)(2,1)S(1)} %get-tuple-element.60), channel_id=1, source_target_pairs={{0,16},{16,0},{1,17},{17,1},{2,18},{18,2},{3,19},{19,3},{4,20},{20... | collective-permute-start | bytes 1081352 | tf_op jit(solution)/shard_map/ppermute | solution.py:312
  58.6 9.3 %collective-permute-start.14 = (bf16[128,1024]{1,0:T(8,128)(2,1)S(1)}, bf16[128,1024]{1,0:T(8,128)(2,1)S(1)}, u32[]{:S(2)}, u32[]{:S(2)}) collective-permute-start(bf16[128,1024]{1,0:T(8,128)(2,1)S(1)} %collective-permute-done.10.refs_4_), channel_id=1, source_target_pairs={{0,2},{1,3},{2,0},{3,1},{4,6},{5,7},{6,4},{7,5},{8,10},{9,11},{10,... | collective-permute-start | bytes 786440 | tf_op jit(solution)/shard_map/ppermute | solution.py:306
  59.1 8.7 %collective-permute-start.15 = (bf16[128,1024]{1,0:T(8,128)(2,1)S(1)}, bf16[128,1024]{1,0:T(8,128)(2,1)S(1)}, u32[]{:S(2)}, u32[]{:S(2)}) collective-permute-start(bf16[128,1024]{1,0:T(8,128)(2,1)S(1)} %collective-permute-done.7.refs_1_), channel_id=1, source_target_pairs={{0,8},{1,9},{2,10},{3,11},{4,0},{5,1},{6,2},{7,3},{12,4},{13,5},{1... | collective-permute-start | bytes 786440 | tf_op jit(solution)/shard_map/ppermute | solution.py:303
  63.0 8.8 %copy-start.1 = (f32[704,1024]{1,0:T(8,128)}, f32[704,1024]{1,0:T(8,128)S(1)}, u32[]{:S(2)}) copy-start(f32[704,1024]{1,0:T(8,128)S(1)} %get-tuple-element.55.refs_1_) | copy-start | bytes 8650756
  71.0 2.7 %collective-permute-start.18 = (bf16[512,1024]{1,0:T(8,128)(2,1)S(1)}, bf16[512,1024]{1,0:T(8,128)(2,1)S(1)}, u32[]{:S(2)}, u32[]{:S(2)}) collective-permute-start(bf16[512,1024]{1,0:T(8,128)(2,1)S(1)} %get-tuple-element.61), channel_id=1, source_target_pairs={{0,1},{1,0},{2,3},{3,2},{4,5},{5,4},{6,7},{7,6},{8,9},{9,8},{10,11... | collective-permute-start | bytes 3145736 | tf_op jit(solution)/shard_map/ppermute | solution.py:309
  77.0 18.4 %collective-permute-start.19 = (bf16[352,1024]{1,0:T(8,128)(2,1)}, bf16[352,1024]{1,0:T(8,128)(2,1)S(1)}, u32[]{:S(2)}, u32[]{:S(2)}) collective-permute-start(bf16[352,1024]{1,0:T(8,128)(2,1)} %get-tuple-element.67), channel_id=1, source_target_pairs={{0,16},{16,0},{1,17},{17,1},{2,18},{18,2},{3,19},{19,3},{4,20},{20... | collective-permute-start | bytes 2162696 | tf_op jit(solution)/shard_map/ppermute | solution.py:312
  78.8 10.0 %all-to-all-start = ((f32[16,1,64]{2,1,0:T(1,128)}), f32[16,1,64]{2,1,0:T(1,128)S(1)}, u32[]{:S(2)}, u32[]{:S(2)}) async-start(f32[16,1,64]{2,1,0:T(1,128)} %bitcast.10), calls=%async_computation | async-start | bytes 16384 | tf_op jit(solution)/shard_map/all_to_all | solution.py:485
  (6 other events, 20.2 us)

commit v15 on v14

--- a/solution.py
+++ b/solution.py
@@ -461,24 +461,23 @@
     r0 = backward(behind(x0, ff0, yf0))
     yff0 = across(behind(ff0, yf0))
     f1, yr0 = forward(behind(x1, r0)), across(behind(r0, yff0))
-    r1 = backward(behind(x1, r0))
     mine0, theirs0, pmat, gslot = first_pick(
         [x0, y0, f0, yf0, ff0, yff0, r0, behind(yr0, w[0])]
     )
     ff1, yf1, y1 = forward(f1), across(behind(f1, yr0)), across(behind(x1, yr0))
-    got = sibling(behind(theirs0, f1, r1))
+    r1 = backward(behind(x1, yr0))
+    got = sibling(behind(theirs0, f1))
     rows0, send0, own0, slot_gates, hs = first_products(mine0, got, gslot)
     got0 = [swap(part) for part in send0]
-    yff1, ry1 = across(behind(ff1, rows0)), backward(behind(y1, ff1, rows0))
-    forwarded = forward_columns(w)
+    done = (r1, yf1, rows0)
+    yff1, ry1 = across(behind(ff1, *done)), backward(behind(y1, *done))
     raw, part = raw_part(rows0, w)
     mine1, theirs1 = later_pick(
-        [x1, y1, f1, yf1, ff1, yff1, r1, ry1], behind(pmat, raw, forwarded)
-    )
-    grad_weight = finish(0, own0[0], got0[0])
-    grad_weight = finish(widths[0] // 2, own0[1], got0[1], grad_weight)
+        [x1, y1, f1, yf1, ff1, yff1, r1, ry1], behind(pmat, raw)
+    )
     got = sibling(behind(theirs1, *got0))
-    rows1, send1, own1 = later_products(mine1, got, behind(hs, grad_weight))
+    forwarded = forward_columns([behind(w[0], theirs1)])
+    rows1, send1, own1 = later_products(mine1, got, behind(hs, forwarded))
     got1 = [swap(part) for part in send1]
 
     back = slot_grads(rows1, forwarded, part)
@@ -497,6 +496,8 @@
     )(routes_t, x0, returned)
 
     grad_hidden = raw_rest(rows1, w, raw, slot_gates)
+    grad_weight = finish(0, behind(own0[0], back), got0[0])
+    grad_weight = finish(widths[0] // 2, own0[1], got0[1], grad_weight)
     grad_weight = finish(widths[0], own1[0], got1[0], grad_weight)
     return grad_weight[None], grad_hidden.T[None, None], grad_gates.T
 

time: 96.6 us -> 97.3 us (level)
  local copies, waits for them, and re-layouts: 1.58 us -> 2.74 us
    ppermute x3, waiting for transfers between devices: 3.94 us -> 10.5 us  [backward(): return lax.ppermute(x, 'expert', ring_pairs(-1))]
    ppermute x4, waiting for transfers between devices: 6.3 us -> 1.9 us  [swap(): return lax.ppermute(x, 'dp', [(0, 1), (1, 0)])]
    ppermute x4, waiting for transfers between devices: 6.11 us -> 3.29 us  [forward(): return lax.ppermute(x, 'expert', ring_pairs(1))]
    ppermute x4, starting transfers between devices: 4.41 us -> 3.04 us  [forward(): return lax.ppermute(x, 'expert', ring_pairs(1))]
    unnamed x18 -> x34, local copies, waits for them, and re-layouts: 1.58 us -> 2.74 us
    ppermute x2, waiting for transfers between devices: 1.11 us -> 0.01 us  [sibling(): return lax.ppermute(x, 'expert', swap_pairs(1))]
    ppermute x7, waiting for transfers between devices: 20.7 us -> 21.8 us  [across(): return lax.ppermute(x, 'expert', swap_pairs(2))]
  transfers between devices with their start and end apart: 21 -> 21, of which waited for: 12 -> 12; matrix products, arithmetic and copies ran while one was open for 0% -> 0% of each run, Pallas kernels for 26% -> 25%
where the time goes in v15:
time: 97.3 us; the launch traced here: 97 us
  waiting for transfers between devices  37.5 us (39%)
  Pallas kernels  29 us (30%)
  starting transfers between devices  26.9 us (28%)
  local copies, waits for them, and re-layouts  2.74 us (3%)
    ppermute x7, waiting for transfers between devices, across(): return lax.ppermute(x, 'expert', swap_pairs(2))  21.8 us
    ppermute x3, waiting for transfers between devices, backward(): return lax.ppermute(x, 'expert', ring_pairs(-1))  10.5 us
    ppermute x7, starting transfers between devices, across(): return lax.ppermute(x, 'expert', swap_pairs(2))  8.67 us
    pallas_call x1, Pallas kernels, raw_rest(): pl.pallas_call(functools.partial(raw_kernel, half, columns[1]), grid=(slo...  6.51 us
    ppermute x3, starting transfers between devices, backward(): return lax.ppermute(x, 'expert', ring_pairs(-1))  6.19 us
    ppermute x4, starting transfers between devices, swap(): return lax.ppermute(x, 'dp', [(0, 1), (1, 0)])  4.83 us
    all_to_all x1, starting transfers between devices, ring_shards(): lax.all_to_all(back, 'expert', split_axis=0, concat_axis=0, tiled=True)  4.03 us
    pallas_call x1, Pallas kernels, later_products(): pl.pallas_call(functools.partial(products, half, capacity), out_shape=pro...  3.33 us
  transfers between devices with their start and end apart: 21, of which 12 were waited for; matrix products, arithmetic and copies ran while one was open for 0% of the time, Pallas kernels for 25%

profile of v15, /device:TPU:0, one launch (start us, length us, event | category | flops | bytes accessed | tf_op | source)
XLA Modules:
  0.0 97.0 jit_solution(8789679159976569049)
XLA Ops:
  0.6 3.0 %collective-permute-start.12 = (bf16[352,2048]{1,0:T(8,128)(2,1)}, bf16[352,2048]{1,0:T(8,128)(2,1)S(1)}, u32[]{:S(2)}, u32[]{:S(2)}) collective-permute-start(bf16[352,2048]{1,0:T(8,128)(2,1)} %bitcast.15), channel_id=1, source_target_pairs={{0,16},{16,0},{1,17},{17,1},{2,18},{18,2},{3,19},{19,3},{4,20},{20... | collective-permute-start | bytes 4325384 | tf_op jit(solution)/shard_map/ppermute | solution.py:312
  3.6 1.9 %pack.1 = (bf16[128,1152]{1,0:T(8,128)(2,1)}, bf16[128,1024]{1,0:T(8,128)(2,1)}) custom-call(s32[6,128]{1,0:T(8,128)} %bitcast.25, bf16[6,128]{1,0:T(8,128)(2,1)} %bitcast.28, bf16[128,2048]{1,0:T(8,128)(2,1)} %grad_hbm.1), custom_call_target="tpu_custom_call" | custom-call | tf_op jit(solution)/shard_map/pack/pallas_call | solution.py:318
  5.5 1.6 %collective-permute-start.1 = (bf16[128,1152]{1,0:T(8,128)(2,1)}, bf16[128,1152]{1,0:T(8,128)(2,1)S(1)}, u32[]{:S(2)}, u32[]{:S(2)}) collective-permute-start(bf16[128,1152]{1,0:T(8,128)(2,1)} %get-tuple-element.42.refs_0_.slots_ref), channel_id=1, source_target_pairs={{0,2},{1,3},{2,0},{3,1},{4,6},{5,7},{6,4},{7,5},{8,10},{9,11},{10,... | collective-permute-start | bytes 884744 | tf_op jit(solution)/shard_map/ppermute | solution.py:306
  7.1 1.6 %collective-permute-start = (bf16[128,1152]{1,0:T(8,128)(2,1)}, bf16[128,1152]{1,0:T(8,128)(2,1)S(1)}, u32[]{:S(2)}, u32[]{:S(2)}) collective-permute-start(bf16[128,1152]{1,0:T(8,128)(2,1)} %get-tuple-element.42.refs_0_.slots_ref), channel_id=1, source_target_pairs={{0,4},{1,5},{2,6},{3,7},{4,12},{5,13},{6,14},{7,15},{12,8},{13,9},... | collective-permute-start | bytes 884744 | tf_op jit(solution)/shard_map/ppermute | solution.py:300
  8.7 5.6 %collective-permute-done.1.refs_1_ = bf16[128,1152]{1,0:T(8,128)(2,1)S(1)} collective-permute-done((bf16[128,1152]{1,0:T(8,128)(2,1)}, bf16[128,1152]{1,0:T(8,128)(2,1)S(1)}, u32[]{:S(2)}, u32[]{:S(2)}) %collective-permute-start.1) | collective-permute-done | bytes 294944 | tf_op jit(solution)/shard_map/ppermute | solution.py:306
  14.3 2.2 %collective-permute-done.refs_2_ = bf16[128,1152]{1,0:T(8,128)(2,1)S(1)} collective-permute-done((bf16[128,1152]{1,0:T(8,128)(2,1)}, bf16[128,1152]{1,0:T(8,128)(2,1)S(1)}, u32[]{:S(2)}, u32[]{:S(2)}) %collective-permute-start) | collective-permute-done | bytes 294944 | tf_op jit(solution)/shard_map/ppermute | solution.py:300
  17.8 5.9 %collective-permute-done.3.refs_3_ = bf16[128,1152]{1,0:T(8,128)(2,1)S(1)} collective-permute-done((bf16[128,1152]{1,0:T(8,128)(2,1)S(1)}, bf16[128,1152]{1,0:T(8,128)(2,1)S(1)}, u32[]{:S(2)}, u32[]{:S(2)}) %collective-permute-start.3) | collective-permute-done | bytes 294944 | tf_op jit(solution)/shard_map/ppermute | solution.py:306
  26.3 1.5 %collective-permute-start.5 = (bf16[128,1152]{1,0:T(8,128)(2,1)S(1)}, bf16[128,1152]{1,0:T(8,128)(2,1)S(1)}, u32[]{:S(2)}, u32[]{:S(2)}) collective-permute-start(bf16[128,1152]{1,0:T(8,128)(2,1)S(1)} %collective-permute-done.2.refs_4_), channel_id=1, source_target_pairs={{0,2},{1,3},{2,0},{3,1},{4,6},{5,7},{6,4},{7,5},{8,10},{9,11},{10,... | collective-permute-start | bytes 884744 | tf_op jit(solution)/shard_map/ppermute | solution.py:306
  27.9 3.9 %collective-permute-done.4.refs_6_ = bf16[128,1152]{1,0:T(8,128)(2,1)S(1)} collective-permute-done((bf16[128,1152]{1,0:T(8,128)(2,1)}, bf16[128,1152]{1,0:T(8,128)(2,1)S(1)}, u32[]{:S(2)}, u32[]{:S(2)}) %collective-permute-start.4) | collective-permute-done | bytes 294944 | tf_op jit(solution)/shard_map/ppermute | solution.py:303
  31.8 2.3 %collective-permute-done.5.refs_5_ = bf16[128,1152]{1,0:T(8,128)(2,1)S(1)} collective-permute-done((bf16[128,1152]{1,0:T(8,128)(2,1)S(1)}, bf16[128,1152]{1,0:T(8,128)(2,1)S(1)}, u32[]{:S(2)}, u32[]{:S(2)}) %collective-permute-start.5) | collective-permute-done | bytes 294944 | tf_op jit(solution)/shard_map/ppermute | solution.py:306
  35.9 4.9 %collective-permute-done.6.refs_7_ = bf16[128,1152]{1,0:T(8,128)(2,1)S(1)} collective-permute-done((bf16[128,1152]{1,0:T(8,128)(2,1)S(1)}, bf16[128,1152]{1,0:T(8,128)(2,1)S(1)}, u32[]{:S(2)}, u32[]{:S(2)}) %collective-permute-start.6) | collective-permute-done | bytes 294944 | tf_op jit(solution)/shard_map/ppermute | solution.py:306
  41.8 1.6 %first_pick.1 = (bf16[512,1024]{1,0:T(8,128)(2,1)S(1)}, bf16[528,1024]{1,0:T(8,128)(2,1)S(1)}, bf16[1024,128]{1,0:T(8,128)(2,1)S(1)}, f32[8,128]{1,0:T(8,128)S(1)}) custom-call(bf16[128,1152]{1,0:T(8,128)(2,1)S(1)} %copy-done.12, bf16[128,1152]{1,0:T(8,128)(2,1)S(1)} %collective-permute-done.1.refs_1_, bf16[128,1152]{1,0:T(8,128)(2,1)S(1)} %collective-permute-done.refs_2_, ...), custom_call_target="tpu_custom_call" | custom-call | flops 3000000000 | bytes 9437184 | tf_op jit(solution)/shard_map/first_pick/pallas_call | solution.py:336
  43.8 3.0 %collective-permute-start.11 = (bf16[128,1024]{1,0:T(8,128)(2,1)S(1)}, bf16[128,1024]{1,0:T(8,128)(2,1)S(1)}, u32[]{:S(2)}, u32[]{:S(2)}) collective-permute-start(bf16[128,1024]{1,0:T(8,128)(2,1)S(1)} %copy-done.13), channel_id=1, source_target_pairs={{0,8},{1,9},{2,10},{3,11},{4,0},{5,1},{6,2},{7,3},{12,4},{13,5},{1... | collective-permute-start | bytes 786440 | tf_op jit(solution)/shard_map/ppermute | solution.py:303
  48.8 3.0 %first_products.1 = (f32[1,1024]{1,0:T(1,128)S(1)}, bf16[704,1024]{1,0:T(8,128)(2,1)S(1)}, bf16[1024,1024]{1,0:T(8,128)(2,1)S(1)}, bf16[352,512]{1,0:T(8,128)(2,...) custom-call(bf16[512,1024]{1,0:T(8,128)(2,1)S(1)} %get-tuple-element.49.mine_ref, ...), custom_call_target="tpu_custom_call" | custom-call | flops 3000000000 | bytes 9437184 | tf_op jit(solution)/shard_map/first_products/pallas_call | solution.py:367
  53.1 5.3 %collective-permute-done.11.refs_6_ = bf16[128,1024]{1,0:T(8,128)(2,1)S(1)} collective-permute-done((bf16[128,1024]{1,0:T(8,128)(2,1)S(1)}, bf16[128,1024]{1,0:T(8,128)(2,1)S(1)}, u32[]{:S(2)}, u32[]{:S(2)}) %collective-permute-start.11) | collective-permute-done | bytes 262176 | tf_op jit(solution)/shard_map/ppermute | solution.py:303
  59.0 1.7 %collective-permute-done.9.refs_3_ = bf16[128,1024]{1,0:T(8,128)(2,1)S(1)} collective-permute-done((bf16[128,1024]{1,0:T(8,128)(2,1)S(1)}, bf16[128,1024]{1,0:T(8,128)(2,1)S(1)}, u32[]{:S(2)}, u32[]{:S(2)}) %collective-permute-start.9) | collective-permute-done | bytes 262176 | tf_op jit(solution)/shard_map/ppermute | solution.py:306
  62.2 1.7 %collective-permute-start.15 = (bf16[128,1024]{1,0:T(8,128)(2,1)S(1)}, bf16[128,1024]{1,0:T(8,128)(2,1)S(1)}, u32[]{:S(2)}, u32[]{:S(2)}) collective-permute-start(bf16[128,1024]{1,0:T(8,128)(2,1)S(1)} %collective-permute-done.7.refs_1_), channel_id=1, source_target_pairs={{0,8},{1,9},{2,10},{3,11},{4,0},{5,1},{6,2},{7,3},{12,4},{13,5},{1... | collective-permute-start | bytes 786440 | tf_op jit(solution)/shard_map/ppermute | solution.py:303
  64.0 2.9 %raw_part.1 = (f32[704,1024]{1,0:T(8,128)S(1)}, f32[16,64]{1,0:T(8,128)S(1)}) custom-call(bf16[1024,1024]{1,0:T(8,128)(2,1)S(1)} %get-tuple-element.53.rows_ref, bf16[352,2048]{1,0:T(8,128)(2,1)S(1)} %bitcast.17, bf16[352,2048]{1,0:T(8,128)(2,1)S(1)} %collective-permute-done.12.refs_0_, bf16[704,1024]{1,0:T(8,128)(2,1)S(1)} %bitcast.20), custom_call_target="tpu_custom_call" | custom-call | flops 3000000000 | bytes 9437184 | tf_op jit(solution)/shard_map/raw_part/pallas_call | solution.py:394
  70.7 3.2 %hidden_weight.1.forward_ref = bf16[1024,1024]{1,0:T(8,128)(2,1)S(1)} custom-call(bf16[352,2048]{1,0:T(8,128)(2,1)S(1)} %bitcast.18, bf16[352,2048]{1,0:T(8,128)(2,1)S(1)} %collective-permute-done.12.refs_0_, bf16[704,1024]{1,0:T(8,128)(2,1)S(1)} %bitcast.21), custom_call_target="tpu_custom_call" | custom-call | flops 3000000000 | bytes 9437184 | tf_op jit(solution)/shard_map/hidden_weight/pallas_call | solution.py:422
  74.0 3.3 %products.1 = (bf16[1024,1024]{1,0:T(8,128)(2,1)S(1)}, bf16[352,1024]{1,0:T(8,128)(2,1)}, bf16[352,1024]{1,0:T(8,128)(2,1)S(1)}) custom-call(bf16[512,1024]{1,0:T(8,128)(2,1)S(1)} %get-tuple-element.59.mine_ref, bf16[512,1024]{1,0:T(8,128)(2,1)S(1)} %collective-permute-done.18.got_ref, bf16[704,1024]{1,0:T(8,128)(2,1)S(1)} %get-tuple-element.66.hs_ref), custom_call_target="tpu_custom_call" | custom-call | tf_op jit(solution)/shard_map/products/pallas_call | solution.py:379
  79.4 4.0 %all-to-all-start = ((f32[16,1,64]{2,1,0:T(1,128)}), f32[16,1,64]{2,1,0:T(1,128)S(1)}, u32[]{:S(2)}, u32[]{:S(2)}) async-start(f32[16,1,64]{2,1,0:T(1,128)} %bitcast.10), calls=%async_computation | async-start | bytes 16384 | tf_op jit(solution)/shard_map/all_to_all | solution.py:484
  83.4 6.5 %raw.1 = bf16[704,1024]{1,0:T(8,128)(2,1)} custom-call(bf16[1024,1024]{1,0:T(8,128)(2,1)} %copy-done, bf16[352,2048]{1,0:T(8,128)(2,1)} %bitcast.16, bf16[352,2048]{1,0:T(8,128)(2,1)} %copy-done.3, f32[704,1024]{1,0:T(8,128)} %copy-done.1, f32[1,1024]{1,0:T(1,128)} %copy-done.14), custom_call_target="tpu_custom_call" | custom-call | tf_op jit(solution)/shard_map/raw/pallas_call | solution.py:406
  92.5 1.6 %grad_gates.1 = f32[6,128]{1,0:T(8,128)} custom-call(s32[6,128]{1,0:T(8,128)} %bitcast.26, bf16[128,1152]{1,0:T(8,128)(2,1)} %get-tuple-element.42.refs_0_.slots_ref, f32[16,64]{1,0:T(8,128)} %bitcast.24), custom_call_target="tpu_custom_call" | custom-call | tf_op jit(solution)/shard_map/grad_gates/pallas_call | solution.py:485
  94.2 1.9 %collective-permute-done.19.got_ref = bf16[352,1024]{1,0:T(8,128)(2,1)S(1)} collective-permute-done((bf16[352,1024]{1,0:T(8,128)(2,1)}, bf16[352,1024]{1,0:T(8,128)(2,1)S(1)}, u32[]{:S(2)}, u32[]{:S(2)}) %collective-permute-start.19) | collective-permute-done | bytes 720928 | tf_op jit(solution)/shard_map/ppermute | solution.py:312
  (65 shorter events, 21.9 us)
Async XLA Ops:
  0.6 40.2 %collective-permute-start.12 = (bf16[352,2048]{1,0:T(8,128)(2,1)}, bf16[352,2048]{1,0:T(8,128)(2,1)S(1)}, u32[]{:S(2)}, u32[]{:S(2)}) collective-permute-start(bf16[352,2048]{1,0:T(8,128)(2,1)} %bitcast.15), channel_id=1, source_target_pairs={{0,16},{16,0},{1,17},{17,1},{2,18},{18,2},{3,19},{19,3},{4,20},{20... | collective-permute-start | bytes 4325384 | tf_op jit(solution)/shard_map/ppermute | solution.py:312
  5.5 8.7 %collective-permute-start.1 = (bf16[128,1152]{1,0:T(8,128)(2,1)}, bf16[128,1152]{1,0:T(8,128)(2,1)S(1)}, u32[]{:S(2)}, u32[]{:S(2)}) collective-permute-start(bf16[128,1152]{1,0:T(8,128)(2,1)} %get-tuple-element.42.refs_0_.slots_ref), channel_id=1, source_target_pairs={{0,2},{1,3},{2,0},{3,1},{4,6},{5,7},{6,4},{7,5},{8,10},{9,11},{10,... | collective-permute-start | bytes 884744 | tf_op jit(solution)/shard_map/ppermute | solution.py:306
  7.1 9.3 %collective-permute-start = (bf16[128,1152]{1,0:T(8,128)(2,1)}, bf16[128,1152]{1,0:T(8,128)(2,1)S(1)}, u32[]{:S(2)}, u32[]{:S(2)}) collective-permute-start(bf16[128,1152]{1,0:T(8,128)(2,1)} %get-tuple-element.42.refs_0_.slots_ref), channel_id=1, source_target_pairs={{0,4},{1,5},{2,6},{3,7},{4,12},{5,13},{6,14},{7,15},{12,8},{13,9},... | collective-permute-start | bytes 884744 | tf_op jit(solution)/shard_map/ppermute | solution.py:300
  16.4 7.3 %collective-permute-start.3 = (bf16[128,1152]{1,0:T(8,128)(2,1)S(1)}, bf16[128,1152]{1,0:T(8,128)(2,1)S(1)}, u32[]{:S(2)}, u32[]{:S(2)}) collective-permute-start(bf16[128,1152]{1,0:T(8,128)(2,1)S(1)} %collective-permute-done.refs_2_), channel_id=1, source_target_pairs={{0,2},{1,3},{2,0},{3,1},{4,6},{5,7},{6,4},{7,5},{8,10},{9,11},{10,... | collective-permute-start | bytes 884744 | tf_op jit(solution)/shard_map/ppermute | solution.py:306
  16.9 7.9 %collective-permute-start.2 = (bf16[128,1152]{1,0:T(8,128)(2,1)S(1)}, bf16[128,1152]{1,0:T(8,128)(2,1)S(1)}, u32[]{:S(2)}, u32[]{:S(2)}) collective-permute-start(bf16[128,1152]{1,0:T(8,128)(2,1)S(1)} %collective-permute-done.refs_2_), channel_id=1, source_target_pairs={{0,4},{1,5},{2,6},{3,7},{4,12},{5,13},{6,14},{7,15},{12,8},{13,9},... | collective-permute-start | bytes 884744 | tf_op jit(solution)/shard_map/ppermute | solution.py:300
  24.8 6.9 %collective-permute-start.4 = (bf16[128,1152]{1,0:T(8,128)(2,1)}, bf16[128,1152]{1,0:T(8,128)(2,1)S(1)}, u32[]{:S(2)}, u32[]{:S(2)}) collective-permute-start(bf16[128,1152]{1,0:T(8,128)(2,1)} %get-tuple-element.42.refs_0_.slots_ref), channel_id=1, source_target_pairs={{0,8},{1,9},{2,10},{3,11},{4,0},{5,1},{6,2},{7,3},{12,4},{13,5},{1... | collective-permute-start | bytes 884744 | tf_op jit(solution)/shard_map/ppermute | solution.py:303
  26.3 7.8 %collective-permute-start.5 = (bf16[128,1152]{1,0:T(8,128)(2,1)S(1)}, bf16[128,1152]{1,0:T(8,128)(2,1)S(1)}, u32[]{:S(2)}, u32[]{:S(2)}) collective-permute-start(bf16[128,1152]{1,0:T(8,128)(2,1)S(1)} %collective-permute-done.2.refs_4_), channel_id=1, source_target_pairs={{0,2},{1,3},{2,0},{3,1},{4,6},{5,7},{6,4},{7,5},{8,10},{9,11},{10,... | collective-permute-start | bytes 884744 | tf_op jit(solution)/shard_map/ppermute | solution.py:306
  34.1 6.7 %collective-permute-start.6 = (bf16[128,1152]{1,0:T(8,128)(2,1)S(1)}, bf16[128,1152]{1,0:T(8,128)(2,1)S(1)}, u32[]{:S(2)}, u32[]{:S(2)}) collective-permute-start(bf16[128,1152]{1,0:T(8,128)(2,1)S(1)} %collective-permute-done.4.refs_6_), channel_id=1, source_target_pairs={{0,2},{1,3},{2,0},{3,1},{4,6},{5,7},{6,4},{7,5},{8,10},{9,11},{10,... | collective-permute-start | bytes 884744 | tf_op jit(solution)/shard_map/ppermute | solution.py:306
  35.6 7.8 %collective-permute-start.8 = (bf16[128,1024]{1,0:T(8,128)(2,1)}, bf16[128,1024]{1,0:T(8,128)(2,1)S(1)}, u32[]{:S(2)}, u32[]{:S(2)}) collective-permute-start(bf16[128,1024]{1,0:T(8,128)(2,1)} %get-tuple-element.46.refs_0_), channel_id=1, source_target_pairs={{0,4},{1,5},{2,6},{3,7},{4,12},{5,13},{6,14},{7,15},{12,8},{13,9},... | collective-permute-start | bytes 786440 | tf_op jit(solution)/shard_map/ppermute | solution.py:300
  41.8 28.9 %copy-start.3 = (bf16[352,2048]{1,0:T(8,128)(2,1)}, bf16[352,2048]{1,0:T(8,128)(2,1)S(1)}, u32[]{:S(2)}) copy-start(bf16[352,2048]{1,0:T(8,128)(2,1)S(1)} %collective-permute-done.12.refs_0_) | copy-start | bytes 4325380
  43.4 5.4 %collective-permute-start.13 = (bf16[528,1024]{1,0:T(8,128)(2,1)S(1)}, bf16[528,1024]{1,0:T(8,128)(2,1)S(1)}, u32[]{:S(2)}, u32[]{:S(2)}) collective-permute-start(bf16[528,1024]{1,0:T(8,128)(2,1)S(1)} %get-tuple-element.51), channel_id=1, source_target_pairs={{0,1},{1,0},{2,3},{3,2},{4,5},{5,4},{6,7},{7,6},{8,9},{9,8},{10,11... | collective-permute-start | bytes 3244040 | tf_op jit(solution)/shard_map/ppermute | solution.py:309
  43.5 17.2 %collective-permute-start.10 = (bf16[128,1024]{1,0:T(8,128)(2,1)S(1)}, bf16[128,1024]{1,0:T(8,128)(2,1)S(1)}, u32[]{:S(2)}, u32[]{:S(2)}) collective-permute-start(bf16[128,1024]{1,0:T(8,128)(2,1)S(1)} %collective-permute-done.8.refs_2_), channel_id=1, source_target_pairs={{0,4},{1,5},{2,6},{3,7},{4,12},{5,13},{6,14},{7,15},{12,8},{13,9},... | collective-permute-start | bytes 786440 | tf_op jit(solution)/shard_map/ppermute | solution.py:300
  43.8 14.6 %collective-permute-start.11 = (bf16[128,1024]{1,0:T(8,128)(2,1)S(1)}, bf16[128,1024]{1,0:T(8,128)(2,1)S(1)}, u32[]{:S(2)}, u32[]{:S(2)}) collective-permute-start(bf16[128,1024]{1,0:T(8,128)(2,1)S(1)} %copy-done.13), channel_id=1, source_target_pairs={{0,8},{1,9},{2,10},{3,11},{4,0},{5,1},{6,2},{7,3},{12,4},{13,5},{1... | collective-permute-start | bytes 786440 | tf_op jit(solution)/shard_map/ppermute | solution.py:303
  46.8 12.2 %collective-permute-start.7 = (bf16[128,1024]{1,0:T(8,128)(2,1)S(1)}, bf16[128,1024]{1,0:T(8,128)(2,1)S(1)}, u32[]{:S(2)}, u32[]{:S(2)}) collective-permute-start(bf16[128,1024]{1,0:T(8,128)(2,1)S(1)} %copy-done.13), channel_id=1, source_target_pairs={{0,2},{1,3},{2,0},{3,1},{4,6},{5,7},{6,4},{7,5},{8,10},{9,11},{10,... | collective-permute-start | bytes 786440 | tf_op jit(solution)/shard_map/ppermute | solution.py:306
  48.3 12.4 %collective-permute-start.9 = (bf16[128,1024]{1,0:T(8,128)(2,1)S(1)}, bf16[128,1024]{1,0:T(8,128)(2,1)S(1)}, u32[]{:S(2)}, u32[]{:S(2)}) collective-permute-start(bf16[128,1024]{1,0:T(8,128)(2,1)S(1)} %collective-permute-done.8.refs_2_), channel_id=1, source_target_pairs={{0,2},{1,3},{2,0},{3,1},{4,6},{5,7},{6,4},{7,5},{8,10},{9,11},{10,... | collective-permute-start | bytes 786440 | tf_op jit(solution)/shard_map/ppermute | solution.py:306
  48.8 15.1 %copy-start.2 = (bf16[1,352,2048]{2,1,0:T(8,128)(2,1)S(1)}, bf16[1,352,2048]{2,1,0:T(8,128)(2,1)}, u32[]{:S(2)}) copy-start(bf16[1,352,2048]{2,1,0:T(8,128)(2,1)} %param.9) | copy-start | bytes 4325380
  52.6 14.3 %copy-start.14 = (f32[1,1024]{1,0:T(1,128)}, f32[1,1024]{1,0:T(1,128)S(1)}, u32[]{:S(2)}) copy-start(f32[1,1024]{1,0:T(1,128)S(1)} %get-tuple-element.74.refs_2_) | copy-start | bytes 12292
  52.6 18.0 %collective-permute-start.16 = (bf16[352,512]{1,0:T(8,128)(2,1)S(1)}, bf16[352,512]{1,0:T(8,128)(2,1)S(1)}, u32[]{:S(2)}, u32[]{:S(2)}) collective-permute-start(bf16[352,512]{1,0:T(8,128)(2,1)S(1)} %get-tuple-element.61), channel_id=1, source_target_pairs={{0,16},{16,0},{1,17},{17,1},{2,18},{18,2},{3,19},{19,3},{4,20},{20... | collective-permute-start | bytes 1081352 | tf_op jit(solution)/shard_map/ppermute | solution.py:312
  58.4 12.2 %collective-permute-start.17 = (bf16[352,512]{1,0:T(8,128)(2,1)S(1)}, bf16[352,512]{1,0:T(8,128)(2,1)S(1)}, u32[]{:S(2)}, u32[]{:S(2)}) collective-permute-start(bf16[352,512]{1,0:T(8,128)(2,1)S(1)} %get-tuple-element.62), channel_id=1, source_target_pairs={{0,16},{16,0},{1,17},{17,1},{2,18},{18,2},{3,19},{19,3},{4,20},{20... | collective-permute-start | bytes 1081352 | tf_op jit(solution)/shard_map/ppermute | solution.py:312
  60.7 7.4 %collective-permute-start.14 = (bf16[128,1024]{1,0:T(8,128)(2,1)S(1)}, bf16[128,1024]{1,0:T(8,128)(2,1)S(1)}, u32[]{:S(2)}, u32[]{:S(2)}) collective-permute-start(bf16[128,1024]{1,0:T(8,128)(2,1)S(1)} %collective-permute-done.10.refs_4_), channel_id=1, source_target_pairs={{0,2},{1,3},{2,0},{3,1},{4,6},{5,7},{6,4},{7,5},{8,10},{9,11},{10,... | collective-permute-start | bytes 786440 | tf_op jit(solution)/shard_map/ppermute | solution.py:306
  62.2 7.2 %collective-permute-start.15 = (bf16[128,1024]{1,0:T(8,128)(2,1)S(1)}, bf16[128,1024]{1,0:T(8,128)(2,1)S(1)}, u32[]{:S(2)}, u32[]{:S(2)}) collective-permute-start(bf16[128,1024]{1,0:T(8,128)(2,1)S(1)} %collective-permute-done.7.refs_1_), channel_id=1, source_target_pairs={{0,8},{1,9},{2,10},{3,11},{4,0},{5,1},{6,2},{7,3},{12,4},{13,5},{1... | collective-permute-start | bytes 786440 | tf_op jit(solution)/shard_map/ppermute | solution.py:303
  70.6 3.3 %collective-permute-start.18 = (bf16[512,1024]{1,0:T(8,128)(2,1)S(1)}, bf16[512,1024]{1,0:T(8,128)(2,1)S(1)}, u32[]{:S(2)}, u32[]{:S(2)}) collective-permute-start(bf16[512,1024]{1,0:T(8,128)(2,1)S(1)} %get-tuple-element.63), channel_id=1, source_target_pairs={{0,1},{1,0},{2,3},{3,2},{4,5},{5,4},{6,7},{7,6},{8,9},{9,8},{10,11... | collective-permute-start | bytes 3145736 | tf_op jit(solution)/shard_map/ppermute | solution.py:309
  77.3 18.7 %collective-permute-start.19 = (bf16[352,1024]{1,0:T(8,128)(2,1)}, bf16[352,1024]{1,0:T(8,128)(2,1)S(1)}, u32[]{:S(2)}, u32[]{:S(2)}) collective-permute-start(bf16[352,1024]{1,0:T(8,128)(2,1)} %get-tuple-element.68), channel_id=1, source_target_pairs={{0,16},{16,0},{1,17},{17,1},{2,18},{18,2},{3,19},{19,3},{4,20},{20... | collective-permute-start | bytes 2162696 | tf_op jit(solution)/shard_map/ppermute | solution.py:312
  79.4 12.6 %all-to-all-start = ((f32[16,1,64]{2,1,0:T(1,128)}), f32[16,1,64]{2,1,0:T(1,128)S(1)}, u32[]{:S(2)}, u32[]{:S(2)}) async-start(f32[16,1,64]{2,1,0:T(1,128)} %bitcast.10), calls=%async_computation | async-start | bytes 16384 | tf_op jit(solution)/shard_map/all_to_all | solution.py:484
  (14 other events, 56.8 us)

commit v16 on v14

--- a/solution.py
+++ b/solution.py
@@ -9,7 +9,7 @@
 
 NZ, NY, NC = 4, 2, 2
 CHUNKS = (4, 4)
-PIECES = (2, 1)
+PIECES = 2
 LANES = 128
 NT = (((1,), (1,)), ((), ()))
 VMEM = pl.BlockSpec(memory_space=pltpu.VMEM)
@@ -94,16 +94,17 @@
     return z * NY + (y ^ (arrival % NY))
 
 
-def pick(xs, pmat_ref, mine_ref, theirs_ref):
+def pick(low, xs, pmat_ref, mine_ref, theirs_ref):
     capacity = mine_ref.shape[0] // len(xs)
 
     @pl.loop(0, mine_ref.shape[1] // 256)
     def _(n):
         cols = pl.ds(pl.multiple_of(n * 256, 256), 256)
+        x_cols = pl.ds(pl.multiple_of(low + n * 256, 256), 256)
         for a, x_ref in enumerate(xs):
             rows = jnp.dot(
                 pmat_ref[a * 2 * capacity : (a + 1) * 2 * capacity, :],
-                x_ref[:, cols],
+                x_ref[:, x_cols],
                 preferred_element_type=jnp.float32,
             ).astype(jnp.bfloat16)
             where = pl.ds(pl.multiple_of(pair_place(a) * capacity, capacity), capacity)
@@ -144,11 +145,11 @@
         pmat_ref[a * 2 * capacity : (a + 1) * 2 * capacity, :] = one_hot.astype(jnp.bfloat16)
     theirs_ref[pairs * capacity :, :] = jnp.zeros((16, width), jnp.bfloat16)
     theirs_ref[pairs * capacity :, : 2 * capacity] = other_ref[...].astype(jnp.bfloat16)
-    pick(xs, pmat_ref, mine_ref, theirs_ref)
-
-
-def pick_kernel(*refs):
-    pick(refs[:-3], *refs[-3:])
+    pick(0, xs, pmat_ref, mine_ref, theirs_ref)
+
+
+def pick_kernel(low, *refs):
+    pick(low, refs[:-3], *refs[-3:])
 
 
 def products(half, capacity, mine_ref, got_ref, hs_ref, rows_ref, *outs):
@@ -216,10 +217,15 @@
         back_ref[to, :] = total[:, i * capacity : (i + 1) * capacity]
 
 
-def raw_kernel(half, cols, rows_ref, own_ref, *refs):
+def raw_kernel(half, cols, first_ref, second_ref, own_ref, *refs):
     *got_refs, sum_ref, gates_ref, grad_ref = refs
-    for units, raw in raw_parts(half, cols, rows_ref, own_ref, got_refs):
-        grad_ref[units, :] = ((raw + sum_ref[units, :]) * gates_ref[...]).astype(jnp.bfloat16)
+    parts = zip(
+        raw_parts(half, cols[0], first_ref, own_ref, got_refs),
+        raw_parts(half, cols[1], second_ref, own_ref, got_refs),
+    )
+    for (units, first), (_, second) in parts:
+        raw = first + second + sum_ref[units, :]
+        grad_ref[units, :] = (raw * gates_ref[...]).astype(jnp.bfloat16)
 
 
 def forward_kernel(half, cols, own_ref, *refs):
@@ -235,17 +241,18 @@
     ).astype(out_ref.dtype)
 
 
-def slot_grads_kernel(rows_ref, forward_ref, part_ref, back_ref):
+def slot_grads_kernel(first_ref, second_ref, forward_ref, part_ref, back_ref):
     capacity = back_ref.shape[1]
     pair = 2 * capacity
-    for p in range(rows_ref.shape[0] // pair):
+    width = first_ref.shape[1]
+    for p in range(first_ref.shape[0] // pair):
         at = slice(p * pair, (p + 1) * pair)
         some = jnp.zeros((pair, LANES), jnp.float32)
-        for n in range(0, rows_ref.shape[1], LANES):
-            cols = slice(n, n + LANES)
-            some += rows_ref[at, cols].astype(jnp.float32) * forward_ref[at, cols].astype(
-                jnp.float32
-            )
+        for n in range(0, 2 * width, LANES):
+            rows_ref, low = (first_ref, n) if n < width else (second_ref, n - width)
+            some += rows_ref[at, low : low + LANES].astype(jnp.float32) * forward_ref[
+                at, n : n + LANES
+            ].astype(jnp.float32)
         total = jnp.sum(some.T, axis=0, keepdims=True)
         for i in range(2):
             to = slice(2 * p + i, 2 * p + i + 1)
@@ -349,42 +356,44 @@
             name="first_pick",
         )(*blocks)
 
-    def later_pick(blocks, pmat):
-        return pl.pallas_call(
-            pick_kernel,
-            out_shape=[shape((slots // 2, widths[1]), bf16)] * 2,
+    piece = widths[1] // 2
+    halves = [slice(widths[0] + low, widths[0] + low + piece) for low in (0, piece)]
+
+    def later_pick(low, blocks, pmat):
+        return pl.pallas_call(
+            functools.partial(pick_kernel, low),
+            out_shape=[shape((slots // 2, piece), bf16)] * 2,
             in_specs=[VMEM] * (len(blocks) + 1),
             out_specs=[VMEM] * 2,
             compiler_params=params(24),
             name="pick",
         )(*blocks, pmat)
 
-    def product_shapes(c):
-        piece = shape((half, widths[c] // PIECES[c]), bf16)
-        return [shape((slots, widths[c]), bf16)] + [piece] * (2 * PIECES[c])
+    product_shapes = [shape((slots, widths[0]), bf16)] + [
+        shape((half, widths[0] // PIECES), bf16)
+    ] * (2 * PIECES)
 
     def first_products(mine, got, gslot):
         slot_gates, hs, rows, *halves = pl.pallas_call(
             functools.partial(first_products_kernel, half, capacity),
-            out_shape=[shape((1, slots), f32), shape((units, slots), bf16)] + product_shapes(0),
+            out_shape=[shape((1, slots), f32), shape((units, slots), bf16)] + product_shapes,
             in_specs=[VMEM] * 4,
-            out_specs=[VMEM] * (3 + 2 * PIECES[0]),
+            out_specs=[VMEM] * (3 + 2 * PIECES),
             compiler_params=params(24),
             cost_estimate=cost(3),
             name="first_products",
         )(mine, got, gslot, hidden_t)
-        return rows, halves[: PIECES[0]], halves[PIECES[0] :], slot_gates, hs
+        return rows, halves[: PIECES], halves[PIECES :], slot_gates, hs
 
     def later_products(mine, got, hs):
-        rows, *halves = pl.pallas_call(
+        return pl.pallas_call(
             functools.partial(products, half, capacity),
-            out_shape=product_shapes(1),
+            out_shape=[shape((slots, piece), bf16)] + [shape((half, piece), bf16)] * 2,
             in_specs=[VMEM] * 3,
-            out_specs=[VMEM] * (1 + 2 * PIECES[1]),
+            out_specs=[VMEM] * 3,
             compiler_params=params(24),
             name="products",
         )(mine, got, hs)
-        return rows, halves[: PIECES[1]], halves[PIECES[1] :]
 
     by_slot = pl.BlockSpec((units, tile), lambda i: (0, i))
     by_row = [pl.BlockSpec((tile, n), lambda i: (i, 0)) for n in widths]
@@ -404,11 +413,11 @@
 
     def raw_rest(rows, got_weight, raw, slot_gates):
         return pl.pallas_call(
-            functools.partial(raw_kernel, half, columns[1]),
+            functools.partial(raw_kernel, half, halves),
             grid=(slots // tile,),
             out_shape=shape((units, slots), bf16),
             in_specs=[
-                by_row[1],
+                *[pl.BlockSpec((tile, piece), lambda i: (i, 0))] * 2,
                 *weight_specs,
                 by_slot,
                 pl.BlockSpec((1, tile), lambda i: (0, i)),
@@ -416,7 +425,7 @@
             out_specs=by_slot,
             compiler_params=params(60),
             name="raw",
-        )(rows, weight, *got_weight, raw, slot_gates)
+        )(*rows, weight, *got_weight, raw, slot_gates)
 
     def forward_columns(got_weight):
         return pl.pallas_call(
@@ -434,11 +443,11 @@
         return pl.pallas_call(
             slot_grads_kernel,
             out_shape=back_shape,
-            in_specs=[VMEM] * 3,
+            in_specs=[VMEM] * 4,
             out_specs=VMEM,
             compiler_params=params(24),
             name="slot_grads",
-        )(rows, forwarded, part)
+        )(*rows, forwarded, part)
 
     def finish(low, own, got, *before):
         piece = own.shape[1]
@@ -472,14 +481,16 @@
     yff1, ry1 = across(behind(ff1, rows0)), backward(behind(y1, ff1, rows0))
     forwarded = forward_columns(w)
     raw, part = raw_part(rows0, w)
-    mine1, theirs1 = later_pick(
-        [x1, y1, f1, yf1, ff1, yff1, r1, ry1], behind(pmat, raw, forwarded)
-    )
-    grad_weight = finish(0, own0[0], got0[0])
-    grad_weight = finish(widths[0] // 2, own0[1], got0[1], grad_weight)
-    got = sibling(behind(theirs1, *got0))
-    rows1, send1, own1 = later_products(mine1, got, behind(hs, grad_weight))
-    got1 = [swap(part) for part in send1]
+    blocks = [x1, y1, f1, yf1, ff1, yff1, r1, ry1]
+    rows1, own1, got1 = [], [], []
+    for low in (0, piece):
+        mine, theirs = later_pick(low, blocks, behind(pmat, raw, forwarded))
+        if low > 0:
+            theirs = behind(theirs, *got0)
+        rows, send, own = later_products(mine, sibling(theirs), hs)
+        rows1.append(rows)
+        own1.append(own)
+        got1.append(swap(send))
 
     back = slot_grads(rows1, forwarded, part)
     returned = lax.all_to_all(back, "expert", split_axis=0, concat_axis=0, tiled=True)
@@ -497,7 +508,10 @@
     )(routes_t, x0, returned)
 
     grad_hidden = raw_rest(rows1, w, raw, slot_gates)
+    grad_weight = finish(0, behind(own0[0], back), got0[0])
+    grad_weight = finish(widths[0] // 2, own0[1], got0[1], grad_weight)
     grad_weight = finish(widths[0], own1[0], got1[0], grad_weight)
+    grad_weight = finish(widths[0] + piece, own1[1], got1[1], grad_weight)
     return grad_weight[None], grad_hidden.T[None, None], grad_gates.T
 
 

time: 96.6 us -> 94.2 us (0.975)
  waiting for transfers between devices: 38.2 us -> 32.6 us
  starting transfers between devices: 26.8 us -> 28.3 us
  Pallas kernels: 28.9 us -> 30 us
    ppermute x4 -> x5, waiting for transfers between devices: 6.3 us -> 1.83 us  [swap(): return lax.ppermute(x, 'dp', [(0, 1), (1, 0)])]
    ppermute x4 -> x5, starting transfers between devices: 5.63 us -> 7.12 us  [swap(): return lax.ppermute(x, 'dp', [(0, 1), (1, 0)])]
    ppermute x2 -> x3, waiting for transfers between devices: 1.11 us -> 0.01 us  [sibling(): return lax.ppermute(x, 'expert', swap_pairs(1))]
    pallas_call x3 -> x4, Pallas kernels: 2.49 us -> 3.13 us  [finish(): pl.pallas_call(finish_kernel, grid=(2,), out_shape=shape((half, model), b...]
    pallas_call x3 -> x5, Pallas kernels: 11 us -> 11.4 us  [the longest x1 6.43 us: raw_rest(): pl.pallas_call(functools.partial(raw_kernel, half, halves), grid=(slots /...]
    unnamed x18 -> x36, local copies, waits for them, and re-layouts: 1.58 us -> 2.02 us
  transfers between devices with their start and end apart: 21 -> 23, of which waited for: 12 -> 10; matrix products, arithmetic and copies ran while one was open for 0% -> 0% of each run, Pallas kernels for 26% -> 31%
where the time goes in v16:
time: 94.2 us; the launch traced here: 93.9 us
  waiting for transfers between devices  32.6 us (35%)
  Pallas kernels  30 us (32%)
  starting transfers between devices  28.3 us (30%)
  local copies, waits for them, and re-layouts  2.02 us (2%)
    ppermute x7, waiting for transfers between devices, across(): return lax.ppermute(x, 'expert', swap_pairs(2))  20.7 us
    ppermute x7, starting transfers between devices, across(): return lax.ppermute(x, 'expert', swap_pairs(2))  7.73 us
    ppermute x5, starting transfers between devices, swap(): return lax.ppermute(x, 'dp', [(0, 1), (1, 0)])  7.12 us
    pallas_call x1, Pallas kernels, raw_rest(): pl.pallas_call(functools.partial(raw_kernel, half, halves), grid=(slots /...  6.43 us
    ppermute x4, waiting for transfers between devices, forward(): return lax.ppermute(x, 'expert', ring_pairs(1))  6.13 us
    ppermute x3, starting transfers between devices, backward(): return lax.ppermute(x, 'expert', ring_pairs(-1))  5.6 us
    ppermute x4, starting transfers between devices, forward(): return lax.ppermute(x, 'expert', ring_pairs(1))  4.41 us
    ppermute x3, waiting for transfers between devices, backward(): return lax.ppermute(x, 'expert', ring_pairs(-1))  3.94 us
  transfers between devices with their start and end apart: 23, of which 10 were waited for; matrix products, arithmetic and copies ran while one was open for 0% of the time, Pallas kernels for 31%

profile of v16, /device:TPU:0, one launch (start us, length us, event | category | flops | bytes accessed | tf_op | source)
XLA Modules:
  0.0 93.9 jit_solution(5074326681025855378)
XLA Ops:
  0.6 3.0 %collective-permute-start.11 = (bf16[352,2048]{1,0:T(8,128)(2,1)}, bf16[352,2048]{1,0:T(8,128)(2,1)S(1)}, u32[]{:S(2)}, u32[]{:S(2)}) collective-permute-start(bf16[352,2048]{1,0:T(8,128)(2,1)} %bitcast.15), channel_id=1, source_target_pairs={{0,16},{16,0},{1,17},{17,1},{2,18},{18,2},{3,19},{19,3},{4,20},{20... | collective-permute-start | bytes 4325384 | tf_op jit(solution)/shard_map/ppermute | solution.py:319
  3.6 1.9 %pack.1 = (bf16[128,1152]{1,0:T(8,128)(2,1)}, bf16[128,1024]{1,0:T(8,128)(2,1)}) custom-call(s32[6,128]{1,0:T(8,128)} %bitcast.25, bf16[6,128]{1,0:T(8,128)(2,1)} %bitcast.28, bf16[128,2048]{1,0:T(8,128)(2,1)} %grad_hbm.1), custom_call_target="tpu_custom_call" | custom-call | tf_op jit(solution)/shard_map/pack/pallas_call | solution.py:325
  5.5 1.6 %collective-permute-start.1 = (bf16[128,1152]{1,0:T(8,128)(2,1)}, bf16[128,1152]{1,0:T(8,128)(2,1)S(1)}, u32[]{:S(2)}, u32[]{:S(2)}) collective-permute-start(bf16[128,1152]{1,0:T(8,128)(2,1)} %get-tuple-element.45.refs_0_.slots_ref), channel_id=1, source_target_pairs={{0,2},{1,3},{2,0},{3,1},{4,6},{5,7},{6,4},{7,5},{8,10},{9,11},{10,... | collective-permute-start | bytes 884744 | tf_op jit(solution)/shard_map/ppermute | solution.py:313
  7.1 1.6 %collective-permute-start = (bf16[128,1152]{1,0:T(8,128)(2,1)}, bf16[128,1152]{1,0:T(8,128)(2,1)S(1)}, u32[]{:S(2)}, u32[]{:S(2)}) collective-permute-start(bf16[128,1152]{1,0:T(8,128)(2,1)} %get-tuple-element.45.refs_0_.slots_ref), channel_id=1, source_target_pairs={{0,4},{1,5},{2,6},{3,7},{4,12},{5,13},{6,14},{7,15},{12,8},{13,9},... | collective-permute-start | bytes 884744 | tf_op jit(solution)/shard_map/ppermute | solution.py:307
  8.7 5.6 %collective-permute-done.1.refs_1_ = bf16[128,1152]{1,0:T(8,128)(2,1)S(1)} collective-permute-done((bf16[128,1152]{1,0:T(8,128)(2,1)}, bf16[128,1152]{1,0:T(8,128)(2,1)S(1)}, u32[]{:S(2)}, u32[]{:S(2)}) %collective-permute-start.1) | collective-permute-done | bytes 294944 | tf_op jit(solution)/shard_map/ppermute | solution.py:313
  14.3 2.2 %collective-permute-done.refs_2_ = bf16[128,1152]{1,0:T(8,128)(2,1)S(1)} collective-permute-done((bf16[128,1152]{1,0:T(8,128)(2,1)}, bf16[128,1152]{1,0:T(8,128)(2,1)S(1)}, u32[]{:S(2)}, u32[]{:S(2)}) %collective-permute-start) | collective-permute-done | bytes 294944 | tf_op jit(solution)/shard_map/ppermute | solution.py:307
  17.8 5.9 %collective-permute-done.3.refs_3_ = bf16[128,1152]{1,0:T(8,128)(2,1)S(1)} collective-permute-done((bf16[128,1152]{1,0:T(8,128)(2,1)S(1)}, bf16[128,1152]{1,0:T(8,128)(2,1)S(1)}, u32[]{:S(2)}, u32[]{:S(2)}) %collective-permute-start.3) | collective-permute-done | bytes 294944 | tf_op jit(solution)/shard_map/ppermute | solution.py:313
  27.9 3.9 %collective-permute-done.4.refs_6_ = bf16[128,1152]{1,0:T(8,128)(2,1)S(1)} collective-permute-done((bf16[128,1152]{1,0:T(8,128)(2,1)}, bf16[128,1152]{1,0:T(8,128)(2,1)S(1)}, u32[]{:S(2)}, u32[]{:S(2)}) %collective-permute-start.4) | collective-permute-done | bytes 294944 | tf_op jit(solution)/shard_map/ppermute | solution.py:310
  31.8 2.3 %collective-permute-done.5.refs_5_ = bf16[128,1152]{1,0:T(8,128)(2,1)S(1)} collective-permute-done((bf16[128,1152]{1,0:T(8,128)(2,1)S(1)}, bf16[128,1152]{1,0:T(8,128)(2,1)S(1)}, u32[]{:S(2)}, u32[]{:S(2)}) %collective-permute-start.5) | collective-permute-done | bytes 294944 | tf_op jit(solution)/shard_map/ppermute | solution.py:313
  35.6 3.1 %collective-permute-start.12 = (bf16[128,1024]{1,0:T(8,128)(2,1)}, bf16[128,1024]{1,0:T(8,128)(2,1)S(1)}, u32[]{:S(2)}, u32[]{:S(2)}) collective-permute-start(bf16[128,1024]{1,0:T(8,128)(2,1)} %get-tuple-element.49.refs_0_), channel_id=1, source_target_pairs={{0,8},{1,9},{2,10},{3,11},{4,0},{5,1},{6,2},{7,3},{12,4},{13,5},{1... | collective-permute-start | bytes 786440 | tf_op jit(solution)/shard_map/ppermute | solution.py:310
  38.8 2.1 %collective-permute-done.6.refs_7_ = bf16[128,1152]{1,0:T(8,128)(2,1)S(1)} collective-permute-done((bf16[128,1152]{1,0:T(8,128)(2,1)S(1)}, bf16[128,1152]{1,0:T(8,128)(2,1)S(1)}, u32[]{:S(2)}, u32[]{:S(2)}) %collective-permute-start.6) | collective-permute-done | bytes 294944 | tf_op jit(solution)/shard_map/ppermute | solution.py:313
  41.8 1.6 %first_pick.1 = (bf16[512,1024]{1,0:T(8,128)(2,1)S(1)}, bf16[528,1024]{1,0:T(8,128)(2,1)S(1)}, bf16[1024,128]{1,0:T(8,128)(2,1)S(1)}, f32[8,128]{1,0:T(8,128)S(1)}) custom-call(bf16[128,1152]{1,0:T(8,128)(2,1)S(1)} %copy-done.14, bf16[128,1152]{1,0:T(8,128)(2,1)S(1)} %collective-permute-done.1.refs_1_, bf16[128,1152]{1,0:T(8,128)(2,1)S(1)} %collective-permute-done.refs_2_, ...), custom_call_target="tpu_custom_call" | custom-call | flops 3000000000 | bytes 9437184 | tf_op jit(solution)/shard_map/first_pick/pallas_call | solution.py:343
  43.4 2.8 %collective-permute-done.8.refs_2_ = bf16[128,1024]{1,0:T(8,128)(2,1)S(1)} collective-permute-done((bf16[128,1024]{1,0:T(8,128)(2,1)}, bf16[128,1024]{1,0:T(8,128)(2,1)S(1)}, u32[]{:S(2)}, u32[]{:S(2)}) %collective-permute-start.8) | collective-permute-done | bytes 262176 | tf_op jit(solution)/shard_map/ppermute | solution.py:307
  46.3 2.0 %collective-permute-start.10 = (bf16[128,1024]{1,0:T(8,128)(2,1)S(1)}, bf16[128,1024]{1,0:T(8,128)(2,1)S(1)}, u32[]{:S(2)}, u32[]{:S(2)}) collective-permute-start(bf16[128,1024]{1,0:T(8,128)(2,1)S(1)} %collective-permute-done.8.refs_2_), channel_id=1, source_target_pairs={{0,4},{1,5},{2,6},{3,7},{4,12},{5,13},{6,14},{7,15},{12,8},{13,9},... | collective-permute-start | bytes 786440 | tf_op jit(solution)/shard_map/ppermute | solution.py:307
  50.2 3.0 %first_products.1 = (f32[1,1024]{1,0:T(1,128)S(1)}, bf16[704,1024]{1,0:T(8,128)(2,1)S(1)}, bf16[1024,1024]{1,0:T(8,128)(2,1)S(1)}, bf16[352,512]{1,0:T(8,128)(2,...) custom-call(bf16[512,1024]{1,0:T(8,128)(2,1)S(1)} %get-tuple-element.52.mine_ref, ...), custom_call_target="tpu_custom_call" | custom-call | flops 3000000000 | bytes 9437184 | tf_op jit(solution)/shard_map/first_products/pallas_call | solution.py:377
  55.3 3.2 %hidden_weight.1.forward_ref = bf16[1024,1024]{1,0:T(8,128)(2,1)S(1)} custom-call(bf16[352,2048]{1,0:T(8,128)(2,1)S(1)} %bitcast.17, bf16[352,2048]{1,0:T(8,128)(2,1)S(1)} %collective-permute-done.11.refs_0_, bf16[704,1024]{1,0:T(8,128)(2,1)S(1)} %bitcast.20), custom_call_target="tpu_custom_call" | custom-call | flops 3000000000 | bytes 9437184 | tf_op jit(solution)/shard_map/hidden_weight/pallas_call | solution.py:431
  60.2 2.9 %raw_part.1 = (f32[704,1024]{1,0:T(8,128)S(1)}, f32[16,64]{1,0:T(8,128)S(1)}) custom-call(bf16[1024,1024]{1,0:T(8,128)(2,1)S(1)} %get-tuple-element.56.rows_ref, bf16[352,2048]{1,0:T(8,128)(2,1)S(1)} %bitcast.18, bf16[352,2048]{1,0:T(8,128)(2,1)S(1)} %collective-permute-done.11.refs_0_, bf16[704,1024]{1,0:T(8,128)(2,1)S(1)} %bitcast.21), custom_call_target="tpu_custom_call" | custom-call | flops 3000000000 | bytes 9437184 | tf_op jit(solution)/shard_map/raw_part/pallas_call | solution.py:403
  63.0 4.9 %collective-permute-done.14.refs_5_ = bf16[128,1024]{1,0:T(8,128)(2,1)S(1)} collective-permute-done((bf16[128,1024]{1,0:T(8,128)(2,1)S(1)}, bf16[128,1024]{1,0:T(8,128)(2,1)S(1)}, u32[]{:S(2)}, u32[]{:S(2)}) %collective-permute-start.14) | collective-permute-done | bytes 262176 | tf_op jit(solution)/shard_map/ppermute | solution.py:313
  69.2 1.8 %collective-permute-done.17.got_ref = bf16[352,512]{1,0:T(8,128)(2,1)S(1)} collective-permute-done((bf16[352,512]{1,0:T(8,128)(2,1)S(1)}, bf16[352,512]{1,0:T(8,128)(2,1)S(1)}, u32[]{:S(2)}, u32[]{:S(2)}) %collective-permute-start.17) | collective-permute-done | bytes 360480 | tf_op jit(solution)/shard_map/ppermute | solution.py:319
  71.0 1.9 %products.3 = (bf16[1024,512]{1,0:T(8,128)(2,1)S(1)}, bf16[352,512]{1,0:T(8,128)(2,1)}, bf16[352,512]{1,0:T(8,128)(2,1)S(1)}) custom-call(bf16[512,512]{1,0:T(8,128)(2,1)S(1)} %get-tuple-element.70.mine_ref, bf16[512,512]{1,0:T(8,128)(2,1)S(1)} %collective-permute-done.20.got_ref, bf16[704,1024]{1,0:T(8,128)(2,1)S(1)} %get-tuple-element.67.hs_ref), custom_call_target="tpu_custom_call" | custom-call | tf_op jit(solution)/shard_map/products/pallas_call | solution.py:389
  73.5 1.9 %products.2 = (bf16[1024,512]{1,0:T(8,128)(2,1)S(1)}, bf16[352,512]{1,0:T(8,128)(2,1)}, bf16[352,512]{1,0:T(8,128)(2,1)S(1)}) custom-call(bf16[512,512]{1,0:T(8,128)(2,1)S(1)} %get-tuple-element.62.mine_ref, bf16[512,512]{1,0:T(8,128)(2,1)S(1)} %collective-permute-done.18.got_ref, bf16[704,1024]{1,0:T(8,128)(2,1)S(1)} %get-tuple-element.67.hs_ref), custom_call_target="tpu_custom_call" | custom-call | tf_op jit(solution)/shard_map/products/pallas_call | solution.py:389
  78.2 3.4 %all-to-all-start = ((f32[16,1,64]{2,1,0:T(1,128)}), f32[16,1,64]{2,1,0:T(1,128)S(1)}, u32[]{:S(2)}, u32[]{:S(2)}) async-start(f32[16,1,64]{2,1,0:T(1,128)} %bitcast.10), calls=%async_computation | async-start | bytes 16384 | tf_op jit(solution)/shard_map/all_to_all | solution.py:496
  81.7 6.4 %raw.1 = bf16[704,1024]{1,0:T(8,128)(2,1)} custom-call(bf16[1024,512]{1,0:T(8,128)(2,1)} %copy-done, bf16[1024,512]{1,0:T(8,128)(2,1)} %copy-done.1, bf16[352,2048]{1,0:T(8,128)(2,1)} %bitcast.16, bf16[352,2048]{1,0:T(8,128)(2,1)} %copy-done.4, f32[704,1024]{1,0:T(8,128)} %copy-done.2, f32[1,1024]{1,0:T(1,128)} %copy-done.15), custom_call_target="tpu_custom_call" | custom-call | tf_op jit(solution)/shard_map/raw/pallas_call | solution.py:415
  90.7 1.6 %grad_gates.1 = f32[6,128]{1,0:T(8,128)} custom-call(s32[6,128]{1,0:T(8,128)} %bitcast.26, bf16[128,1152]{1,0:T(8,128)(2,1)} %get-tuple-element.45.refs_0_.slots_ref, f32[16,64]{1,0:T(8,128)} %bitcast.24), custom_call_target="tpu_custom_call" | custom-call | tf_op jit(solution)/shard_map/grad_gates/pallas_call | solution.py:497
  (74 shorter events, 22.5 us)
Async XLA Ops:
  0.6 40.2 %collective-permute-start.11 = (bf16[352,2048]{1,0:T(8,128)(2,1)}, bf16[352,2048]{1,0:T(8,128)(2,1)S(1)}, u32[]{:S(2)}, u32[]{:S(2)}) collective-permute-start(bf16[352,2048]{1,0:T(8,128)(2,1)} %bitcast.15), channel_id=1, source_target_pairs={{0,16},{16,0},{1,17},{17,1},{2,18},{18,2},{3,19},{19,3},{4,20},{20... | collective-permute-start | bytes 4325384 | tf_op jit(solution)/shard_map/ppermute | solution.py:319
  5.5 8.7 %collective-permute-start.1 = (bf16[128,1152]{1,0:T(8,128)(2,1)}, bf16[128,1152]{1,0:T(8,128)(2,1)S(1)}, u32[]{:S(2)}, u32[]{:S(2)}) collective-permute-start(bf16[128,1152]{1,0:T(8,128)(2,1)} %get-tuple-element.45.refs_0_.slots_ref), channel_id=1, source_target_pairs={{0,2},{1,3},{2,0},{3,1},{4,6},{5,7},{6,4},{7,5},{8,10},{9,11},{10,... | collective-permute-start | bytes 884744 | tf_op jit(solution)/shard_map/ppermute | solution.py:313
  7.1 9.3 %collective-permute-start = (bf16[128,1152]{1,0:T(8,128)(2,1)}, bf16[128,1152]{1,0:T(8,128)(2,1)S(1)}, u32[]{:S(2)}, u32[]{:S(2)}) collective-permute-start(bf16[128,1152]{1,0:T(8,128)(2,1)} %get-tuple-element.45.refs_0_.slots_ref), channel_id=1, source_target_pairs={{0,4},{1,5},{2,6},{3,7},{4,12},{5,13},{6,14},{7,15},{12,8},{13,9},... | collective-permute-start | bytes 884744 | tf_op jit(solution)/shard_map/ppermute | solution.py:307
  16.4 7.3 %collective-permute-start.3 = (bf16[128,1152]{1,0:T(8,128)(2,1)S(1)}, bf16[128,1152]{1,0:T(8,128)(2,1)S(1)}, u32[]{:S(2)}, u32[]{:S(2)}) collective-permute-start(bf16[128,1152]{1,0:T(8,128)(2,1)S(1)} %collective-permute-done.refs_2_), channel_id=1, source_target_pairs={{0,2},{1,3},{2,0},{3,1},{4,6},{5,7},{6,4},{7,5},{8,10},{9,11},{10,... | collective-permute-start | bytes 884744 | tf_op jit(solution)/shard_map/ppermute | solution.py:313
  16.9 7.9 %collective-permute-start.2 = (bf16[128,1152]{1,0:T(8,128)(2,1)S(1)}, bf16[128,1152]{1,0:T(8,128)(2,1)S(1)}, u32[]{:S(2)}, u32[]{:S(2)}) collective-permute-start(bf16[128,1152]{1,0:T(8,128)(2,1)S(1)} %collective-permute-done.refs_2_), channel_id=1, source_target_pairs={{0,4},{1,5},{2,6},{3,7},{4,12},{5,13},{6,14},{7,15},{12,8},{13,9},... | collective-permute-start | bytes 884744 | tf_op jit(solution)/shard_map/ppermute | solution.py:307
  24.8 6.9 %collective-permute-start.4 = (bf16[128,1152]{1,0:T(8,128)(2,1)}, bf16[128,1152]{1,0:T(8,128)(2,1)S(1)}, u32[]{:S(2)}, u32[]{:S(2)}) collective-permute-start(bf16[128,1152]{1,0:T(8,128)(2,1)} %get-tuple-element.45.refs_0_.slots_ref), channel_id=1, source_target_pairs={{0,8},{1,9},{2,10},{3,11},{4,0},{5,1},{6,2},{7,3},{12,4},{13,5},{1... | collective-permute-start | bytes 884744 | tf_op jit(solution)/shard_map/ppermute | solution.py:310
  26.3 7.8 %collective-permute-start.5 = (bf16[128,1152]{1,0:T(8,128)(2,1)S(1)}, bf16[128,1152]{1,0:T(8,128)(2,1)S(1)}, u32[]{:S(2)}, u32[]{:S(2)}) collective-permute-start(bf16[128,1152]{1,0:T(8,128)(2,1)S(1)} %collective-permute-done.2.refs_4_), channel_id=1, source_target_pairs={{0,2},{1,3},{2,0},{3,1},{4,6},{5,7},{6,4},{7,5},{8,10},{9,11},{10,... | collective-permute-start | bytes 884744 | tf_op jit(solution)/shard_map/ppermute | solution.py:313
  34.1 6.7 %collective-permute-start.6 = (bf16[128,1152]{1,0:T(8,128)(2,1)S(1)}, bf16[128,1152]{1,0:T(8,128)(2,1)S(1)}, u32[]{:S(2)}, u32[]{:S(2)}) collective-permute-start(bf16[128,1152]{1,0:T(8,128)(2,1)S(1)} %collective-permute-done.4.refs_6_), channel_id=1, source_target_pairs={{0,2},{1,3},{2,0},{3,1},{4,6},{5,7},{6,4},{7,5},{8,10},{9,11},{10,... | collective-permute-start | bytes 884744 | tf_op jit(solution)/shard_map/ppermute | solution.py:313
  35.6 7.8 %collective-permute-start.12 = (bf16[128,1024]{1,0:T(8,128)(2,1)}, bf16[128,1024]{1,0:T(8,128)(2,1)S(1)}, u32[]{:S(2)}, u32[]{:S(2)}) collective-permute-start(bf16[128,1024]{1,0:T(8,128)(2,1)} %get-tuple-element.49.refs_0_), channel_id=1, source_target_pairs={{0,8},{1,9},{2,10},{3,11},{4,0},{5,1},{6,2},{7,3},{12,4},{13,5},{1... | collective-permute-start | bytes 786440 | tf_op jit(solution)/shard_map/ppermute | solution.py:310
  38.8 7.5 %collective-permute-start.8 = (bf16[128,1024]{1,0:T(8,128)(2,1)}, bf16[128,1024]{1,0:T(8,128)(2,1)S(1)}, u32[]{:S(2)}, u32[]{:S(2)}) collective-permute-start(bf16[128,1024]{1,0:T(8,128)(2,1)} %get-tuple-element.49.refs_0_), channel_id=1, source_target_pairs={{0,4},{1,5},{2,6},{3,7},{4,12},{5,13},{6,14},{7,15},{12,8},{13,9},... | collective-permute-start | bytes 786440 | tf_op jit(solution)/shard_map/ppermute | solution.py:307
  41.8 18.4 %copy-start.4 = (bf16[352,2048]{1,0:T(8,128)(2,1)}, bf16[352,2048]{1,0:T(8,128)(2,1)S(1)}, u32[]{:S(2)}) copy-start(bf16[352,2048]{1,0:T(8,128)(2,1)S(1)} %collective-permute-done.11.refs_0_) | copy-start | bytes 4325380
  46.2 4.0 %collective-permute-start.13 = (bf16[528,1024]{1,0:T(8,128)(2,1)S(1)}, bf16[528,1024]{1,0:T(8,128)(2,1)S(1)}, u32[]{:S(2)}, u32[]{:S(2)}) collective-permute-start(bf16[528,1024]{1,0:T(8,128)(2,1)S(1)} %get-tuple-element.54), channel_id=1, source_target_pairs={{0,1},{1,0},{2,3},{3,2},{4,5},{5,4},{6,7},{7,6},{8,9},{9,8},{10,11... | collective-permute-start | bytes 3244040 | tf_op jit(solution)/shard_map/ppermute | solution.py:316
  46.3 12.3 %collective-permute-start.10 = (bf16[128,1024]{1,0:T(8,128)(2,1)S(1)}, bf16[128,1024]{1,0:T(8,128)(2,1)S(1)}, u32[]{:S(2)}, u32[]{:S(2)}) collective-permute-start(bf16[128,1024]{1,0:T(8,128)(2,1)S(1)} %collective-permute-done.8.refs_2_), channel_id=1, source_target_pairs={{0,4},{1,5},{2,6},{3,7},{4,12},{5,13},{6,14},{7,15},{12,8},{13,9},... | collective-permute-start | bytes 786440 | tf_op jit(solution)/shard_map/ppermute | solution.py:307
  48.2 10.4 %collective-permute-start.7 = (bf16[128,1024]{1,0:T(8,128)(2,1)S(1)}, bf16[128,1024]{1,0:T(8,128)(2,1)S(1)}, u32[]{:S(2)}, u32[]{:S(2)}) collective-permute-start(bf16[128,1024]{1,0:T(8,128)(2,1)S(1)} %copy-done.5), channel_id=1, source_target_pairs={{0,2},{1,3},{2,0},{3,1},{4,6},{5,7},{6,4},{7,5},{8,10},{9,11},{10,... | collective-permute-start | bytes 786440 | tf_op jit(solution)/shard_map/ppermute | solution.py:313
  48.7 14.3 %collective-permute-start.9 = (bf16[128,1024]{1,0:T(8,128)(2,1)S(1)}, bf16[128,1024]{1,0:T(8,128)(2,1)S(1)}, u32[]{:S(2)}, u32[]{:S(2)}) collective-permute-start(bf16[128,1024]{1,0:T(8,128)(2,1)S(1)} %collective-permute-done.8.refs_2_), channel_id=1, source_target_pairs={{0,2},{1,3},{2,0},{3,1},{4,6},{5,7},{6,4},{7,5},{8,10},{9,11},{10,... | collective-permute-start | bytes 786440 | tf_op jit(solution)/shard_map/ppermute | solution.py:313
  53.3 15.9 %collective-permute-start.16 = (bf16[352,512]{1,0:T(8,128)(2,1)S(1)}, bf16[352,512]{1,0:T(8,128)(2,1)S(1)}, u32[]{:S(2)}, u32[]{:S(2)}) collective-permute-start(bf16[352,512]{1,0:T(8,128)(2,1)S(1)} %get-tuple-element.64), channel_id=1, source_target_pairs={{0,16},{16,0},{1,17},{17,1},{2,18},{18,2},{3,19},{19,3},{4,20},{20... | collective-permute-start | bytes 1081352 | tf_op jit(solution)/shard_map/ppermute | solution.py:319
  53.9 17.2 %collective-permute-start.17 = (bf16[352,512]{1,0:T(8,128)(2,1)S(1)}, bf16[352,512]{1,0:T(8,128)(2,1)S(1)}, u32[]{:S(2)}, u32[]{:S(2)}) collective-permute-start(bf16[352,512]{1,0:T(8,128)(2,1)S(1)} %get-tuple-element.65), channel_id=1, source_target_pairs={{0,16},{16,0},{1,17},{17,1},{2,18},{18,2},{3,19},{19,3},{4,20},{20... | collective-permute-start | bytes 1081352 | tf_op jit(solution)/shard_map/ppermute | solution.py:319
  58.6 9.3 %collective-permute-start.14 = (bf16[128,1024]{1,0:T(8,128)(2,1)S(1)}, bf16[128,1024]{1,0:T(8,128)(2,1)S(1)}, u32[]{:S(2)}, u32[]{:S(2)}) collective-permute-start(bf16[128,1024]{1,0:T(8,128)(2,1)S(1)} %collective-permute-done.10.refs_4_), channel_id=1, source_target_pairs={{0,2},{1,3},{2,0},{3,1},{4,6},{5,7},{6,4},{7,5},{8,10},{9,11},{10,... | collective-permute-start | bytes 786440 | tf_op jit(solution)/shard_map/ppermute | solution.py:313
  59.2 8.7 %collective-permute-start.15 = (bf16[128,1024]{1,0:T(8,128)(2,1)S(1)}, bf16[128,1024]{1,0:T(8,128)(2,1)S(1)}, u32[]{:S(2)}, u32[]{:S(2)}) collective-permute-start(bf16[128,1024]{1,0:T(8,128)(2,1)S(1)} %collective-permute-done.7.refs_1_), channel_id=1, source_target_pairs={{0,8},{1,9},{2,10},{3,11},{4,0},{5,1},{6,2},{7,3},{12,4},{13,5},{1... | collective-permute-start | bytes 786440 | tf_op jit(solution)/shard_map/ppermute | solution.py:310
  68.5 2.5 %collective-permute-start.20 = (bf16[512,512]{1,0:T(8,128)(2,1)S(1)}, bf16[512,512]{1,0:T(8,128)(2,1)S(1)}, u32[]{:S(2)}, u32[]{:S(2)}) collective-permute-start(bf16[512,512]{1,0:T(8,128)(2,1)S(1)} %get-tuple-element.71), channel_id=1, source_target_pairs={{0,1},{1,0},{2,3},{3,2},{4,5},{5,4},{6,7},{7,6},{8,9},{9,8},{10,11... | collective-permute-start | bytes 1572872 | tf_op jit(solution)/shard_map/ppermute | solution.py:316
  71.0 2.5 %collective-permute-start.18 = (bf16[512,512]{1,0:T(8,128)(2,1)S(1)}, bf16[512,512]{1,0:T(8,128)(2,1)S(1)}, u32[]{:S(2)}, u32[]{:S(2)}) collective-permute-start(bf16[512,512]{1,0:T(8,128)(2,1)S(1)} %get-tuple-element.66), channel_id=1, source_target_pairs={{0,1},{1,0},{2,3},{3,2},{4,5},{5,4},{6,7},{7,6},{8,9},{9,8},{10,11... | collective-permute-start | bytes 1572872 | tf_op jit(solution)/shard_map/ppermute | solution.py:316
  73.0 19.4 %collective-permute-start.21 = (bf16[352,512]{1,0:T(8,128)(2,1)}, bf16[352,512]{1,0:T(8,128)(2,1)S(1)}, u32[]{:S(2)}, u32[]{:S(2)}) collective-permute-start(bf16[352,512]{1,0:T(8,128)(2,1)} %get-tuple-element.73), channel_id=1, source_target_pairs={{0,16},{16,0},{1,17},{17,1},{2,18},{18,2},{3,19},{19,3},{4,20},{20... | collective-permute-start | bytes 1081352 | tf_op jit(solution)/shard_map/ppermute | solution.py:319
  75.4 17.7 %collective-permute-start.19 = (bf16[352,512]{1,0:T(8,128)(2,1)}, bf16[352,512]{1,0:T(8,128)(2,1)S(1)}, u32[]{:S(2)}, u32[]{:S(2)}) collective-permute-start(bf16[352,512]{1,0:T(8,128)(2,1)} %get-tuple-element.69), channel_id=1, source_target_pairs={{0,16},{16,0},{1,17},{17,1},{2,18},{18,2},{3,19},{19,3},{4,20},{20... | collective-permute-start | bytes 1081352 | tf_op jit(solution)/shard_map/ppermute | solution.py:319
  78.2 11.9 %all-to-all-start = ((f32[16,1,64]{2,1,0:T(1,128)}), f32[16,1,64]{2,1,0:T(1,128)S(1)}, u32[]{:S(2)}, u32[]{:S(2)}) async-start(f32[16,1,64]{2,1,0:T(1,128)} %bitcast.10), calls=%async_computation | async-start | bytes 16384 | tf_op jit(solution)/shard_map/all_to_all | solution.py:496
  (17 other events, 83.6 us)

commit v17 on v16

--- a/solution.py
+++ b/solution.py
@@ -260,29 +260,42 @@
 
 
 def gates_kernel(routes_ref, slots_ref, back_ref, out_ref):
-    back = back_ref[...]
+    rest = back_ref[...]
     routes = routes_ref[...]
-    experts, capacity = back.shape
-    tokens = routes.shape[1]
+    experts, capacity = rest.shape
+    chosen, tokens = routes.shape
+    pieces = []
+    for _ in range(3):
+        pieces.append(rest.astype(jnp.bfloat16))
+        rest = rest - pieces[-1].astype(jnp.float32)
     slots = slots_ref[experts : 2 * experts, :].astype(jnp.float32)
     expert = lax.broadcasted_iota(jnp.int32, (experts, tokens), 0)
     slot = lax.broadcasted_iota(jnp.int32, (capacity, tokens), 0).astype(jnp.float32)
-    for k in range(out_ref.shape[0]):
-        hit = expert == routes[k : k + 1, :]
+    hits = [expert == routes[k : k + 1, :] for k in range(chosen)]
+    one_hots = []
+    for hit in hits:
         number = jnp.sum(jnp.where(hit, slots, 0.0), axis=0, keepdims=True)
-        by_expert = jnp.dot(
-            back,
-            jnp.where(slot == number, 1.0, 0.0),
-            preferred_element_type=jnp.float32,
-            precision=lax.Precision.HIGHEST,
-        )
-        out_ref[k : k + 1, :] = jnp.sum(jnp.where(hit, by_expert, 0.0), axis=0, keepdims=True)
-
-
-def finish_kernel(own_ref, got_ref, *refs):
-    refs[-1][...] = (
-        own_ref[...].astype(jnp.float32) + got_ref[...].astype(jnp.float32)
-    ).astype(jnp.bfloat16)
+        one_hots.append(jnp.where(slot == number, 1.0, 0.0).astype(jnp.bfloat16))
+    by_expert = jnp.dot(
+        jnp.concatenate(pieces, axis=0),
+        jnp.concatenate(one_hots, axis=1),
+        preferred_element_type=jnp.float32,
+    )
+    by_expert = by_expert[:experts] + (
+        by_expert[experts : 2 * experts] + by_expert[2 * experts :]
+    )
+    for k, hit in enumerate(hits):
+        mine = by_expert[:, k * tokens : (k + 1) * tokens]
+        out_ref[k : k + 1, :] = jnp.sum(jnp.where(hit, mine, 0.0), axis=0, keepdims=True)
+
+
+def finish_kernel(*refs):
+    own_refs, got_refs, out_ref = refs[:2], refs[2:4], refs[-1]
+    piece = own_refs[0].shape[1]
+    for q in range(2):
+        out_ref[:, q * piece : (q + 1) * piece] = (
+            own_refs[q][...].astype(jnp.float32) + got_refs[q][...].astype(jnp.float32)
+        ).astype(jnp.bfloat16)
 
 
 def ring_shards(grad_out, gates, routes, hidden, down_weight):
@@ -449,19 +462,18 @@
             name="slot_grads",
         )(*rows, forwarded, part)
 
-    def finish(low, own, got, *before):
-        piece = own.shape[1]
-        spec = pl.BlockSpec((half // 2, piece), lambda i: (i, 0))
+    def finish(c, own, got, *before):
+        spec = pl.BlockSpec((half // 2, widths[c] // 2), lambda i: (i, 0))
         return pl.pallas_call(
             finish_kernel,
             grid=(2,),
             out_shape=shape((half, model), bf16),
-            in_specs=[spec, spec] + [ANY] * len(before),
-            out_specs=pl.BlockSpec((half // 2, piece), lambda i: (i, low // piece)),
-            input_output_aliases={2: 0} if before else {},
+            in_specs=[spec] * 4 + [ANY] * len(before),
+            out_specs=pl.BlockSpec((half // 2, widths[c]), lambda i: (i, c)),
+            input_output_aliases={4: 0} if before else {},
             compiler_params=params(8),
             name="finish",
-        )(own, got, *before)
+        )(*own, *got, *before)
 
     x0, x1 = pack()
     w = [swap(weight)]
@@ -508,10 +520,8 @@
     )(routes_t, x0, returned)
 
     grad_hidden = raw_rest(rows1, w, raw, slot_gates)
-    grad_weight = finish(0, behind(own0[0], back), got0[0])
-    grad_weight = finish(widths[0] // 2, own0[1], got0[1], grad_weight)
-    grad_weight = finish(widths[0], own1[0], got1[0], grad_weight)
-    grad_weight = finish(widths[0] + piece, own1[1], got1[1], grad_weight)
+    grad_weight = finish(0, [behind(own0[0], back), own0[1]], got0)
+    grad_weight = finish(1, own1, got1, grad_weight)
     return grad_weight[None], grad_hidden.T[None, None], grad_gates.T
 
 

time: 94.2 us -> 92.9 us (0.986)
  Pallas kernels: 30 us -> 28.7 us
    pallas_call x4 -> x2, Pallas kernels: 3.13 us -> 1.91 us  [finish(): pl.pallas_call(finish_kernel, grid=(2,), out_shape=shape((half, model), b...]
  transfers between devices with their start and end apart: 23 -> 23, of which waited for: 10 -> 11; matrix products, arithmetic and copies ran while one was open for 0% -> 0% of each run, Pallas kernels for 31% -> 30%
where the time goes in v17:
time: 92.9 us; the launch traced here: 92.6 us
  waiting for transfers between devices  33.1 us (36%)
  Pallas kernels  28.7 us (31%)
  starting transfers between devices  28.3 us (30%)
  local copies, waits for them, and re-layouts  1.62 us (2%)
    ppermute x7, waiting for transfers between devices, across(): return lax.ppermute(x, 'expert', swap_pairs(2))  20.7 us
    ppermute x7, starting transfers between devices, across(): return lax.ppermute(x, 'expert', swap_pairs(2))  7.73 us
    ppermute x5, starting transfers between devices, swap(): return lax.ppermute(x, 'dp', [(0, 1), (1, 0)])  7.12 us
    pallas_call x1, Pallas kernels, raw_rest(): pl.pallas_call(functools.partial(raw_kernel, half, halves), grid=(slots /...  6.47 us
    ppermute x4, waiting for transfers between devices, forward(): return lax.ppermute(x, 'expert', ring_pairs(1))  6.13 us
    ppermute x3, starting transfers between devices, backward(): return lax.ppermute(x, 'expert', ring_pairs(-1))  5.6 us
    ppermute x4, starting transfers between devices, forward(): return lax.ppermute(x, 'expert', ring_pairs(1))  4.41 us
    ppermute x3, waiting for transfers between devices, backward(): return lax.ppermute(x, 'expert', ring_pairs(-1))  3.94 us
  transfers between devices with their start and end apart: 23, of which 11 were waited for; matrix products, arithmetic and copies ran while one was open for 0% of the time, Pallas kernels for 30%

profile of v17, /device:TPU:0, one launch (start us, length us, event | category | flops | bytes accessed | tf_op | source)
XLA Modules:
  0.0 92.6 jit_solution(15222728378991113304)
XLA Ops:
  0.6 3.0 %collective-permute-start.11 = (bf16[352,2048]{1,0:T(8,128)(2,1)}, bf16[352,2048]{1,0:T(8,128)(2,1)S(1)}, u32[]{:S(2)}, u32[]{:S(2)}) collective-permute-start(bf16[352,2048]{1,0:T(8,128)(2,1)} %bitcast.15), channel_id=1, source_target_pairs={{0,16},{16,0},{1,17},{17,1},{2,18},{18,2},{3,19},{19,3},{4,20},{20... | collective-permute-start | bytes 4325384 | tf_op jit(solution)/shard_map/ppermute | solution.py:332
  3.6 1.9 %pack.1 = (bf16[128,1152]{1,0:T(8,128)(2,1)}, bf16[128,1024]{1,0:T(8,128)(2,1)}) custom-call(s32[6,128]{1,0:T(8,128)} %bitcast.25, bf16[6,128]{1,0:T(8,128)(2,1)} %bitcast.28, bf16[128,2048]{1,0:T(8,128)(2,1)} %grad_hbm.1), custom_call_target="tpu_custom_call" | custom-call | tf_op jit(solution)/shard_map/pack/pallas_call | solution.py:338
  5.5 1.6 %collective-permute-start.1 = (bf16[128,1152]{1,0:T(8,128)(2,1)}, bf16[128,1152]{1,0:T(8,128)(2,1)S(1)}, u32[]{:S(2)}, u32[]{:S(2)}) collective-permute-start(bf16[128,1152]{1,0:T(8,128)(2,1)} %get-tuple-element.45.refs_0_.slots_ref), channel_id=1, source_target_pairs={{0,2},{1,3},{2,0},{3,1},{4,6},{5,7},{6,4},{7,5},{8,10},{9,11},{10,... | collective-permute-start | bytes 884744 | tf_op jit(solution)/shard_map/ppermute | solution.py:326
  7.1 1.6 %collective-permute-start = (bf16[128,1152]{1,0:T(8,128)(2,1)}, bf16[128,1152]{1,0:T(8,128)(2,1)S(1)}, u32[]{:S(2)}, u32[]{:S(2)}) collective-permute-start(bf16[128,1152]{1,0:T(8,128)(2,1)} %get-tuple-element.45.refs_0_.slots_ref), channel_id=1, source_target_pairs={{0,4},{1,5},{2,6},{3,7},{4,12},{5,13},{6,14},{7,15},{12,8},{13,9},... | collective-permute-start | bytes 884744 | tf_op jit(solution)/shard_map/ppermute | solution.py:320
  8.7 5.6 %collective-permute-done.1.refs_1_ = bf16[128,1152]{1,0:T(8,128)(2,1)S(1)} collective-permute-done((bf16[128,1152]{1,0:T(8,128)(2,1)}, bf16[128,1152]{1,0:T(8,128)(2,1)S(1)}, u32[]{:S(2)}, u32[]{:S(2)}) %collective-permute-start.1) | collective-permute-done | bytes 294944 | tf_op jit(solution)/shard_map/ppermute | solution.py:326
  14.3 2.2 %collective-permute-done.refs_2_ = bf16[128,1152]{1,0:T(8,128)(2,1)S(1)} collective-permute-done((bf16[128,1152]{1,0:T(8,128)(2,1)}, bf16[128,1152]{1,0:T(8,128)(2,1)S(1)}, u32[]{:S(2)}, u32[]{:S(2)}) %collective-permute-start) | collective-permute-done | bytes 294944 | tf_op jit(solution)/shard_map/ppermute | solution.py:320
  17.8 5.9 %collective-permute-done.3.refs_3_ = bf16[128,1152]{1,0:T(8,128)(2,1)S(1)} collective-permute-done((bf16[128,1152]{1,0:T(8,128)(2,1)S(1)}, bf16[128,1152]{1,0:T(8,128)(2,1)S(1)}, u32[]{:S(2)}, u32[]{:S(2)}) %collective-permute-start.3) | collective-permute-done | bytes 294944 | tf_op jit(solution)/shard_map/ppermute | solution.py:326
  26.3 1.5 %collective-permute-start.5 = (bf16[128,1152]{1,0:T(8,128)(2,1)S(1)}, bf16[128,1152]{1,0:T(8,128)(2,1)S(1)}, u32[]{:S(2)}, u32[]{:S(2)}) collective-permute-start(bf16[128,1152]{1,0:T(8,128)(2,1)S(1)} %collective-permute-done.2.refs_4_), channel_id=1, source_target_pairs={{0,2},{1,3},{2,0},{3,1},{4,6},{5,7},{6,4},{7,5},{8,10},{9,11},{10,... | collective-permute-start | bytes 884744 | tf_op jit(solution)/shard_map/ppermute | solution.py:326
  27.9 3.9 %collective-permute-done.4.refs_6_ = bf16[128,1152]{1,0:T(8,128)(2,1)S(1)} collective-permute-done((bf16[128,1152]{1,0:T(8,128)(2,1)}, bf16[128,1152]{1,0:T(8,128)(2,1)S(1)}, u32[]{:S(2)}, u32[]{:S(2)}) %collective-permute-start.4) | collective-permute-done | bytes 294944 | tf_op jit(solution)/shard_map/ppermute | solution.py:323
  31.8 2.3 %collective-permute-done.5.refs_5_ = bf16[128,1152]{1,0:T(8,128)(2,1)S(1)} collective-permute-done((bf16[128,1152]{1,0:T(8,128)(2,1)S(1)}, bf16[128,1152]{1,0:T(8,128)(2,1)S(1)}, u32[]{:S(2)}, u32[]{:S(2)}) %collective-permute-start.5) | collective-permute-done | bytes 294944 | tf_op jit(solution)/shard_map/ppermute | solution.py:326
  35.6 3.1 %collective-permute-start.12 = (bf16[128,1024]{1,0:T(8,128)(2,1)}, bf16[128,1024]{1,0:T(8,128)(2,1)S(1)}, u32[]{:S(2)}, u32[]{:S(2)}) collective-permute-start(bf16[128,1024]{1,0:T(8,128)(2,1)} %get-tuple-element.49.refs_0_), channel_id=1, source_target_pairs={{0,8},{1,9},{2,10},{3,11},{4,0},{5,1},{6,2},{7,3},{12,4},{13,5},{1... | collective-permute-start | bytes 786440 | tf_op jit(solution)/shard_map/ppermute | solution.py:323
  38.8 2.1 %collective-permute-done.6.refs_7_ = bf16[128,1152]{1,0:T(8,128)(2,1)S(1)} collective-permute-done((bf16[128,1152]{1,0:T(8,128)(2,1)S(1)}, bf16[128,1152]{1,0:T(8,128)(2,1)S(1)}, u32[]{:S(2)}, u32[]{:S(2)}) %collective-permute-start.6) | collective-permute-done | bytes 294944 | tf_op jit(solution)/shard_map/ppermute | solution.py:326
  41.8 1.6 %first_pick.1 = (bf16[512,1024]{1,0:T(8,128)(2,1)S(1)}, bf16[528,1024]{1,0:T(8,128)(2,1)S(1)}, bf16[1024,128]{1,0:T(8,128)(2,1)S(1)}, f32[8,128]{1,0:T(8,128)S(1)}) custom-call(bf16[128,1152]{1,0:T(8,128)(2,1)S(1)} %copy-done.14, bf16[128,1152]{1,0:T(8,128)(2,1)S(1)} %collective-permute-done.1.refs_1_, bf16[128,1152]{1,0:T(8,128)(2,1)S(1)} %collective-permute-done.refs_2_, ...), custom_call_target="tpu_custom_call" | custom-call | flops 3000000000 | bytes 9437184 | tf_op jit(solution)/shard_map/first_pick/pallas_call | solution.py:356
  43.4 2.8 %collective-permute-done.8.refs_2_ = bf16[128,1024]{1,0:T(8,128)(2,1)S(1)} collective-permute-done((bf16[128,1024]{1,0:T(8,128)(2,1)}, bf16[128,1024]{1,0:T(8,128)(2,1)S(1)}, u32[]{:S(2)}, u32[]{:S(2)}) %collective-permute-start.8) | collective-permute-done | bytes 262176 | tf_op jit(solution)/shard_map/ppermute | solution.py:320
  46.3 2.0 %collective-permute-start.10 = (bf16[128,1024]{1,0:T(8,128)(2,1)S(1)}, bf16[128,1024]{1,0:T(8,128)(2,1)S(1)}, u32[]{:S(2)}, u32[]{:S(2)}) collective-permute-start(bf16[128,1024]{1,0:T(8,128)(2,1)S(1)} %collective-permute-done.8.refs_2_), channel_id=1, source_target_pairs={{0,4},{1,5},{2,6},{3,7},{4,12},{5,13},{6,14},{7,15},{12,8},{13,9},... | collective-permute-start | bytes 786440 | tf_op jit(solution)/shard_map/ppermute | solution.py:320
  50.2 3.0 %first_products.1 = (f32[1,1024]{1,0:T(1,128)S(1)}, bf16[704,1024]{1,0:T(8,128)(2,1)S(1)}, bf16[1024,1024]{1,0:T(8,128)(2,1)S(1)}, bf16[352,512]{1,0:T(8,128)(2,...) custom-call(bf16[512,1024]{1,0:T(8,128)(2,1)S(1)} %get-tuple-element.52.mine_ref, ...), custom_call_target="tpu_custom_call" | custom-call | flops 3000000000 | bytes 9437184 | tf_op jit(solution)/shard_map/first_products/pallas_call | solution.py:390
  55.3 3.2 %hidden_weight.1.forward_ref = bf16[1024,1024]{1,0:T(8,128)(2,1)S(1)} custom-call(bf16[352,2048]{1,0:T(8,128)(2,1)S(1)} %bitcast.17, bf16[352,2048]{1,0:T(8,128)(2,1)S(1)} %collective-permute-done.11.refs_0_, bf16[704,1024]{1,0:T(8,128)(2,1)S(1)} %bitcast.20), custom_call_target="tpu_custom_call" | custom-call | flops 3000000000 | bytes 9437184 | tf_op jit(solution)/shard_map/hidden_weight/pallas_call | solution.py:444
  60.2 2.9 %raw_part.1 = (f32[704,1024]{1,0:T(8,128)S(1)}, f32[16,64]{1,0:T(8,128)S(1)}) custom-call(bf16[1024,1024]{1,0:T(8,128)(2,1)S(1)} %get-tuple-element.56.rows_ref, bf16[352,2048]{1,0:T(8,128)(2,1)S(1)} %bitcast.18, bf16[352,2048]{1,0:T(8,128)(2,1)S(1)} %collective-permute-done.11.refs_0_, bf16[704,1024]{1,0:T(8,128)(2,1)S(1)} %bitcast.21), custom_call_target="tpu_custom_call" | custom-call | flops 3000000000 | bytes 9437184 | tf_op jit(solution)/shard_map/raw_part/pallas_call | solution.py:416
  63.0 4.9 %collective-permute-done.14.refs_5_ = bf16[128,1024]{1,0:T(8,128)(2,1)S(1)} collective-permute-done((bf16[128,1024]{1,0:T(8,128)(2,1)S(1)}, bf16[128,1024]{1,0:T(8,128)(2,1)S(1)}, u32[]{:S(2)}, u32[]{:S(2)}) %collective-permute-start.14) | collective-permute-done | bytes 262176 | tf_op jit(solution)/shard_map/ppermute | solution.py:326
  69.2 1.8 %collective-permute-done.18.refs_3_ = bf16[352,512]{1,0:T(8,128)(2,1)S(1)} collective-permute-done((bf16[352,512]{1,0:T(8,128)(2,1)S(1)}, bf16[352,512]{1,0:T(8,128)(2,1)S(1)}, u32[]{:S(2)}, u32[]{:S(2)}) %collective-permute-start.18) | collective-permute-done | bytes 360480 | tf_op jit(solution)/shard_map/ppermute | solution.py:332
  71.0 1.9 %products.2 = (bf16[1024,512]{1,0:T(8,128)(2,1)S(1)}, bf16[352,512]{1,0:T(8,128)(2,1)}, bf16[352,512]{1,0:T(8,128)(2,1)S(1)}) custom-call(bf16[512,512]{1,0:T(8,128)(2,1)S(1)} %get-tuple-element.62.mine_ref, bf16[512,512]{1,0:T(8,128)(2,1)S(1)} %collective-permute-done.16.got_ref, bf16[704,1024]{1,0:T(8,128)(2,1)S(1)} %get-tuple-element.64.hs_ref), custom_call_target="tpu_custom_call" | custom-call | tf_op jit(solution)/shard_map/products/pallas_call | solution.py:402
  73.5 1.9 %products.3 = (bf16[1024,512]{1,0:T(8,128)(2,1)S(1)}, bf16[352,512]{1,0:T(8,128)(2,1)}, bf16[352,512]{1,0:T(8,128)(2,1)S(1)}) custom-call(bf16[512,512]{1,0:T(8,128)(2,1)S(1)} %get-tuple-element.66.mine_ref, bf16[512,512]{1,0:T(8,128)(2,1)S(1)} %collective-permute-done.19.got_ref, bf16[704,1024]{1,0:T(8,128)(2,1)S(1)} %get-tuple-element.64.hs_ref), custom_call_target="tpu_custom_call" | custom-call | tf_op jit(solution)/shard_map/products/pallas_call | solution.py:402
  78.2 3.4 %all-to-all-start = ((f32[16,1,64]{2,1,0:T(1,128)}), f32[16,1,64]{2,1,0:T(1,128)S(1)}, u32[]{:S(2)}, u32[]{:S(2)}) async-start(f32[16,1,64]{2,1,0:T(1,128)} %bitcast.10), calls=%async_computation | async-start | bytes 16384 | tf_op jit(solution)/shard_map/all_to_all | solution.py:508
  81.7 6.5 %raw.1 = bf16[704,1024]{1,0:T(8,128)(2,1)} custom-call(bf16[1024,512]{1,0:T(8,128)(2,1)} %copy-done, bf16[1024,512]{1,0:T(8,128)(2,1)} %copy-done.1, bf16[352,2048]{1,0:T(8,128)(2,1)} %bitcast.16, bf16[352,2048]{1,0:T(8,128)(2,1)} %copy-done.4, f32[704,1024]{1,0:T(8,128)} %copy-done.2, f32[1,1024]{1,0:T(1,128)} %copy-done.15), custom_call_target="tpu_custom_call" | custom-call | tf_op jit(solution)/shard_map/raw/pallas_call | solution.py:428
  (72 shorter events, 21.3 us)
Async XLA Ops:
  0.6 40.2 %collective-permute-start.11 = (bf16[352,2048]{1,0:T(8,128)(2,1)}, bf16[352,2048]{1,0:T(8,128)(2,1)S(1)}, u32[]{:S(2)}, u32[]{:S(2)}) collective-permute-start(bf16[352,2048]{1,0:T(8,128)(2,1)} %bitcast.15), channel_id=1, source_target_pairs={{0,16},{16,0},{1,17},{17,1},{2,18},{18,2},{3,19},{19,3},{4,20},{20... | collective-permute-start | bytes 4325384 | tf_op jit(solution)/shard_map/ppermute | solution.py:332
  5.5 8.7 %collective-permute-start.1 = (bf16[128,1152]{1,0:T(8,128)(2,1)}, bf16[128,1152]{1,0:T(8,128)(2,1)S(1)}, u32[]{:S(2)}, u32[]{:S(2)}) collective-permute-start(bf16[128,1152]{1,0:T(8,128)(2,1)} %get-tuple-element.45.refs_0_.slots_ref), channel_id=1, source_target_pairs={{0,2},{1,3},{2,0},{3,1},{4,6},{5,7},{6,4},{7,5},{8,10},{9,11},{10,... | collective-permute-start | bytes 884744 | tf_op jit(solution)/shard_map/ppermute | solution.py:326
  7.1 9.3 %collective-permute-start = (bf16[128,1152]{1,0:T(8,128)(2,1)}, bf16[128,1152]{1,0:T(8,128)(2,1)S(1)}, u32[]{:S(2)}, u32[]{:S(2)}) collective-permute-start(bf16[128,1152]{1,0:T(8,128)(2,1)} %get-tuple-element.45.refs_0_.slots_ref), channel_id=1, source_target_pairs={{0,4},{1,5},{2,6},{3,7},{4,12},{5,13},{6,14},{7,15},{12,8},{13,9},... | collective-permute-start | bytes 884744 | tf_op jit(solution)/shard_map/ppermute | solution.py:320
  16.4 7.3 %collective-permute-start.3 = (bf16[128,1152]{1,0:T(8,128)(2,1)S(1)}, bf16[128,1152]{1,0:T(8,128)(2,1)S(1)}, u32[]{:S(2)}, u32[]{:S(2)}) collective-permute-start(bf16[128,1152]{1,0:T(8,128)(2,1)S(1)} %collective-permute-done.refs_2_), channel_id=1, source_target_pairs={{0,2},{1,3},{2,0},{3,1},{4,6},{5,7},{6,4},{7,5},{8,10},{9,11},{10,... | collective-permute-start | bytes 884744 | tf_op jit(solution)/shard_map/ppermute | solution.py:326
  16.9 7.9 %collective-permute-start.2 = (bf16[128,1152]{1,0:T(8,128)(2,1)S(1)}, bf16[128,1152]{1,0:T(8,128)(2,1)S(1)}, u32[]{:S(2)}, u32[]{:S(2)}) collective-permute-start(bf16[128,1152]{1,0:T(8,128)(2,1)S(1)} %collective-permute-done.refs_2_), channel_id=1, source_target_pairs={{0,4},{1,5},{2,6},{3,7},{4,12},{5,13},{6,14},{7,15},{12,8},{13,9},... | collective-permute-start | bytes 884744 | tf_op jit(solution)/shard_map/ppermute | solution.py:320
  24.8 6.9 %collective-permute-start.4 = (bf16[128,1152]{1,0:T(8,128)(2,1)}, bf16[128,1152]{1,0:T(8,128)(2,1)S(1)}, u32[]{:S(2)}, u32[]{:S(2)}) collective-permute-start(bf16[128,1152]{1,0:T(8,128)(2,1)} %get-tuple-element.45.refs_0_.slots_ref), channel_id=1, source_target_pairs={{0,8},{1,9},{2,10},{3,11},{4,0},{5,1},{6,2},{7,3},{12,4},{13,5},{1... | collective-permute-start | bytes 884744 | tf_op jit(solution)/shard_map/ppermute | solution.py:323
  26.3 7.8 %collective-permute-start.5 = (bf16[128,1152]{1,0:T(8,128)(2,1)S(1)}, bf16[128,1152]{1,0:T(8,128)(2,1)S(1)}, u32[]{:S(2)}, u32[]{:S(2)}) collective-permute-start(bf16[128,1152]{1,0:T(8,128)(2,1)S(1)} %collective-permute-done.2.refs_4_), channel_id=1, source_target_pairs={{0,2},{1,3},{2,0},{3,1},{4,6},{5,7},{6,4},{7,5},{8,10},{9,11},{10,... | collective-permute-start | bytes 884744 | tf_op jit(solution)/shard_map/ppermute | solution.py:326
  34.1 6.7 %collective-permute-start.6 = (bf16[128,1152]{1,0:T(8,128)(2,1)S(1)}, bf16[128,1152]{1,0:T(8,128)(2,1)S(1)}, u32[]{:S(2)}, u32[]{:S(2)}) collective-permute-start(bf16[128,1152]{1,0:T(8,128)(2,1)S(1)} %collective-permute-done.4.refs_6_), channel_id=1, source_target_pairs={{0,2},{1,3},{2,0},{3,1},{4,6},{5,7},{6,4},{7,5},{8,10},{9,11},{10,... | collective-permute-start | bytes 884744 | tf_op jit(solution)/shard_map/ppermute | solution.py:326
  35.6 7.8 %collective-permute-start.12 = (bf16[128,1024]{1,0:T(8,128)(2,1)}, bf16[128,1024]{1,0:T(8,128)(2,1)S(1)}, u32[]{:S(2)}, u32[]{:S(2)}) collective-permute-start(bf16[128,1024]{1,0:T(8,128)(2,1)} %get-tuple-element.49.refs_0_), channel_id=1, source_target_pairs={{0,8},{1,9},{2,10},{3,11},{4,0},{5,1},{6,2},{7,3},{12,4},{13,5},{1... | collective-permute-start | bytes 786440 | tf_op jit(solution)/shard_map/ppermute | solution.py:323
  38.8 7.5 %collective-permute-start.8 = (bf16[128,1024]{1,0:T(8,128)(2,1)}, bf16[128,1024]{1,0:T(8,128)(2,1)S(1)}, u32[]{:S(2)}, u32[]{:S(2)}) collective-permute-start(bf16[128,1024]{1,0:T(8,128)(2,1)} %get-tuple-element.49.refs_0_), channel_id=1, source_target_pairs={{0,4},{1,5},{2,6},{3,7},{4,12},{5,13},{6,14},{7,15},{12,8},{13,9},... | collective-permute-start | bytes 786440 | tf_op jit(solution)/shard_map/ppermute | solution.py:320
  41.8 18.4 %copy-start.4 = (bf16[352,2048]{1,0:T(8,128)(2,1)}, bf16[352,2048]{1,0:T(8,128)(2,1)S(1)}, u32[]{:S(2)}) copy-start(bf16[352,2048]{1,0:T(8,128)(2,1)S(1)} %collective-permute-done.11.refs_0_) | copy-start | bytes 4325380
  46.2 4.0 %collective-permute-start.13 = (bf16[528,1024]{1,0:T(8,128)(2,1)S(1)}, bf16[528,1024]{1,0:T(8,128)(2,1)S(1)}, u32[]{:S(2)}, u32[]{:S(2)}) collective-permute-start(bf16[528,1024]{1,0:T(8,128)(2,1)S(1)} %get-tuple-element.54), channel_id=1, source_target_pairs={{0,1},{1,0},{2,3},{3,2},{4,5},{5,4},{6,7},{7,6},{8,9},{9,8},{10,11... | collective-permute-start | bytes 3244040 | tf_op jit(solution)/shard_map/ppermute | solution.py:329
  46.3 12.3 %collective-permute-start.10 = (bf16[128,1024]{1,0:T(8,128)(2,1)S(1)}, bf16[128,1024]{1,0:T(8,128)(2,1)S(1)}, u32[]{:S(2)}, u32[]{:S(2)}) collective-permute-start(bf16[128,1024]{1,0:T(8,128)(2,1)S(1)} %collective-permute-done.8.refs_2_), channel_id=1, source_target_pairs={{0,4},{1,5},{2,6},{3,7},{4,12},{5,13},{6,14},{7,15},{12,8},{13,9},... | collective-permute-start | bytes 786440 | tf_op jit(solution)/shard_map/ppermute | solution.py:320
  48.2 10.4 %collective-permute-start.7 = (bf16[128,1024]{1,0:T(8,128)(2,1)S(1)}, bf16[128,1024]{1,0:T(8,128)(2,1)S(1)}, u32[]{:S(2)}, u32[]{:S(2)}) collective-permute-start(bf16[128,1024]{1,0:T(8,128)(2,1)S(1)} %copy-done.5), channel_id=1, source_target_pairs={{0,2},{1,3},{2,0},{3,1},{4,6},{5,7},{6,4},{7,5},{8,10},{9,11},{10,... | collective-permute-start | bytes 786440 | tf_op jit(solution)/shard_map/ppermute | solution.py:326
  48.7 14.3 %collective-permute-start.9 = (bf16[128,1024]{1,0:T(8,128)(2,1)S(1)}, bf16[128,1024]{1,0:T(8,128)(2,1)S(1)}, u32[]{:S(2)}, u32[]{:S(2)}) collective-permute-start(bf16[128,1024]{1,0:T(8,128)(2,1)S(1)} %collective-permute-done.8.refs_2_), channel_id=1, source_target_pairs={{0,2},{1,3},{2,0},{3,1},{4,6},{5,7},{6,4},{7,5},{8,10},{9,11},{10,... | collective-permute-start | bytes 786440 | tf_op jit(solution)/shard_map/ppermute | solution.py:326
  53.3 15.9 %collective-permute-start.17 = (bf16[352,512]{1,0:T(8,128)(2,1)S(1)}, bf16[352,512]{1,0:T(8,128)(2,1)S(1)}, u32[]{:S(2)}, u32[]{:S(2)}) collective-permute-start(bf16[352,512]{1,0:T(8,128)(2,1)S(1)} %get-tuple-element.68), channel_id=1, source_target_pairs={{0,16},{16,0},{1,17},{17,1},{2,18},{18,2},{3,19},{19,3},{4,20},{20... | collective-permute-start | bytes 1081352 | tf_op jit(solution)/shard_map/ppermute | solution.py:332
  53.9 17.2 %collective-permute-start.18 = (bf16[352,512]{1,0:T(8,128)(2,1)S(1)}, bf16[352,512]{1,0:T(8,128)(2,1)S(1)}, u32[]{:S(2)}, u32[]{:S(2)}) collective-permute-start(bf16[352,512]{1,0:T(8,128)(2,1)S(1)} %get-tuple-element.69), channel_id=1, source_target_pairs={{0,16},{16,0},{1,17},{17,1},{2,18},{18,2},{3,19},{19,3},{4,20},{20... | collective-permute-start | bytes 1081352 | tf_op jit(solution)/shard_map/ppermute | solution.py:332
  58.6 9.3 %collective-permute-start.14 = (bf16[128,1024]{1,0:T(8,128)(2,1)S(1)}, bf16[128,1024]{1,0:T(8,128)(2,1)S(1)}, u32[]{:S(2)}, u32[]{:S(2)}) collective-permute-start(bf16[128,1024]{1,0:T(8,128)(2,1)S(1)} %collective-permute-done.10.refs_4_), channel_id=1, source_target_pairs={{0,2},{1,3},{2,0},{3,1},{4,6},{5,7},{6,4},{7,5},{8,10},{9,11},{10,... | collective-permute-start | bytes 786440 | tf_op jit(solution)/shard_map/ppermute | solution.py:326
  59.2 8.7 %collective-permute-start.15 = (bf16[128,1024]{1,0:T(8,128)(2,1)S(1)}, bf16[128,1024]{1,0:T(8,128)(2,1)S(1)}, u32[]{:S(2)}, u32[]{:S(2)}) collective-permute-start(bf16[128,1024]{1,0:T(8,128)(2,1)S(1)} %collective-permute-done.7.refs_1_), channel_id=1, source_target_pairs={{0,8},{1,9},{2,10},{3,11},{4,0},{5,1},{6,2},{7,3},{12,4},{13,5},{1... | collective-permute-start | bytes 786440 | tf_op jit(solution)/shard_map/ppermute | solution.py:323
  68.5 2.5 %collective-permute-start.16 = (bf16[512,512]{1,0:T(8,128)(2,1)S(1)}, bf16[512,512]{1,0:T(8,128)(2,1)S(1)}, u32[]{:S(2)}, u32[]{:S(2)}) collective-permute-start(bf16[512,512]{1,0:T(8,128)(2,1)S(1)} %get-tuple-element.63), channel_id=1, source_target_pairs={{0,1},{1,0},{2,3},{3,2},{4,5},{5,4},{6,7},{7,6},{8,9},{9,8},{10,11... | collective-permute-start | bytes 1572872 | tf_op jit(solution)/shard_map/ppermute | solution.py:329
  71.0 2.5 %collective-permute-start.19 = (bf16[512,512]{1,0:T(8,128)(2,1)S(1)}, bf16[512,512]{1,0:T(8,128)(2,1)S(1)}, u32[]{:S(2)}, u32[]{:S(2)}) collective-permute-start(bf16[512,512]{1,0:T(8,128)(2,1)S(1)} %get-tuple-element.70), channel_id=1, source_target_pairs={{0,1},{1,0},{2,3},{3,2},{4,5},{5,4},{6,7},{7,6},{8,9},{9,8},{10,11... | collective-permute-start | bytes 1572872 | tf_op jit(solution)/shard_map/ppermute | solution.py:329
  73.0 18.3 %collective-permute-start.20 = (bf16[352,512]{1,0:T(8,128)(2,1)}, bf16[352,512]{1,0:T(8,128)(2,1)S(1)}, u32[]{:S(2)}, u32[]{:S(2)}) collective-permute-start(bf16[352,512]{1,0:T(8,128)(2,1)} %get-tuple-element.72), channel_id=1, source_target_pairs={{0,16},{16,0},{1,17},{17,1},{2,18},{18,2},{3,19},{19,3},{4,20},{20... | collective-permute-start | bytes 1081352 | tf_op jit(solution)/shard_map/ppermute | solution.py:332
  75.4 16.3 %collective-permute-start.21 = (bf16[352,512]{1,0:T(8,128)(2,1)}, bf16[352,512]{1,0:T(8,128)(2,1)S(1)}, u32[]{:S(2)}, u32[]{:S(2)}) collective-permute-start(bf16[352,512]{1,0:T(8,128)(2,1)} %get-tuple-element.73), channel_id=1, source_target_pairs={{0,16},{16,0},{1,17},{17,1},{2,18},{18,2},{3,19},{19,3},{4,20},{20... | collective-permute-start | bytes 1081352 | tf_op jit(solution)/shard_map/ppermute | solution.py:332
  78.2 10.9 %all-to-all-start = ((f32[16,1,64]{2,1,0:T(1,128)}), f32[16,1,64]{2,1,0:T(1,128)S(1)}, u32[]{:S(2)}, u32[]{:S(2)}) async-start(f32[16,1,64]{2,1,0:T(1,128)} %bitcast.10), calls=%async_computation | async-start | bytes 16384 | tf_op jit(solution)/shard_map/all_to_all | solution.py:508
  (17 other events, 94.6 us)

commit v18 on v17

--- a/solution.py
+++ b/solution.py
@@ -9,7 +9,6 @@
 
 NZ, NY, NC = 4, 2, 2
 CHUNKS = (4, 4)
-PIECES = 2
 LANES = 128
 NT = (((1,), (1,)), ((), ()))
 VMEM = pl.BlockSpec(memory_space=pltpu.VMEM)
@@ -152,28 +151,26 @@
     pick(low, refs[:-3], *refs[-3:])
 
 
-def products(half, capacity, mine_ref, got_ref, hs_ref, rows_ref, *outs):
+def products(low, half, capacity, mine_ref, got_ref, hs_ref, rows_ref, *outs):
     mine = lax.axis_index("dp")
     core = lax.axis_index("expert") & 1
     pairs = mine_ref.shape[0] // capacity
-    pieces = len(outs) // 2
-    piece = mine_ref.shape[1] // pieces
-    for q in range(pieces):
-
-        @pl.loop(0, piece // 256)
-        def _(n, q=q):
-            cols = pl.ds(pl.multiple_of(q * piece + n * 256, 256), 256)
-            out = pl.ds(pl.multiple_of(n * 256, 256), 256)
-            for p in range(pairs):
-                for c, ref in ((core, mine_ref), (1 - core, got_ref)):
-                    to = pl.ds(pl.multiple_of((2 * p + c) * capacity, capacity), capacity)
-                    rows_ref[to, cols] = ref[p * capacity : (p + 1) * capacity, cols]
-            block = rows_ref[:, cols]
-            for d, ref in ((1 - mine, outs[q]), (mine, outs[pieces + q])):
-                units = pl.ds(pl.multiple_of(d * half, 16), half)
-                ref[:, out] = jnp.dot(
-                    hs_ref[units, :], block, preferred_element_type=jnp.float32
-                ).astype(jnp.bfloat16)
+    send_ref, own_ref = outs
+
+    @pl.loop(0, rows_ref.shape[1] // 256)
+    def _(n):
+        cols = pl.ds(pl.multiple_of(n * 256, 256), 256)
+        from_cols = pl.ds(pl.multiple_of(low + n * 256, 256), 256)
+        for p in range(pairs):
+            for c, ref in ((core, mine_ref), (1 - core, got_ref)):
+                to = pl.ds(pl.multiple_of((2 * p + c) * capacity, capacity), capacity)
+                rows_ref[to, cols] = ref[p * capacity : (p + 1) * capacity, from_cols]
+        block = rows_ref[:, cols]
+        for d, ref in ((1 - mine, send_ref), (mine, own_ref)):
+            units = pl.ds(pl.multiple_of(d * half, 16), half)
+            ref[:, cols] = jnp.dot(
+                hs_ref[units, :], block, preferred_element_type=jnp.float32
+            ).astype(jnp.bfloat16)
 
 
 def first_products_kernel(half, capacity, mine_ref, got_ref, gslot_ref, hidden_ref, *outs):
@@ -184,7 +181,7 @@
     for p in range(pairs):
         gates_ref[:, p * 2 * capacity : (p + 1) * 2 * capacity] = by_pair[p : p + 1, :]
     hs_ref[...] = (hidden_ref[...].astype(jnp.float32) * gates_ref[...]).astype(jnp.bfloat16)
-    products(half, capacity, mine_ref, got_ref, hs_ref, *outs[2:])
+    products(0, half, capacity, mine_ref, got_ref, hs_ref, *outs[2:])
 
 
 def weight_parts(half, own_ref, got_refs):
@@ -203,10 +200,15 @@
         )
 
 
-def raw_part_kernel(half, capacity, cols, rows_ref, own_ref, *refs):
+def raw_part_kernel(half, capacity, cols, first_ref, second_ref, own_ref, *refs):
     *got_refs, hidden_ref, raw_ref, back_ref = refs
-    total = jnp.zeros((1, rows_ref.shape[0]), jnp.float32)
-    for units, raw in raw_parts(half, cols, rows_ref, own_ref, got_refs):
+    total = jnp.zeros((1, first_ref.shape[0]), jnp.float32)
+    terms = zip(
+        raw_parts(half, cols[0], first_ref, own_ref, got_refs),
+        raw_parts(half, cols[1], second_ref, own_ref, got_refs),
+    )
+    for (units, first), (_, second) in terms:
+        raw = first + second
         raw_ref[units, :] = raw
         total += jnp.sum(
             raw * hidden_ref[units, :].astype(jnp.float32), axis=0, keepdims=True
@@ -382,26 +384,23 @@
             name="pick",
         )(*blocks, pmat)
 
-    product_shapes = [shape((slots, widths[0]), bf16)] + [
-        shape((half, widths[0] // PIECES), bf16)
-    ] * (2 * PIECES)
+    product_shapes = [shape((slots, piece), bf16)] + [shape((half, piece), bf16)] * 2
 
     def first_products(mine, got, gslot):
-        slot_gates, hs, rows, *halves = pl.pallas_call(
+        return pl.pallas_call(
             functools.partial(first_products_kernel, half, capacity),
             out_shape=[shape((1, slots), f32), shape((units, slots), bf16)] + product_shapes,
             in_specs=[VMEM] * 4,
-            out_specs=[VMEM] * (3 + 2 * PIECES),
-            compiler_params=params(24),
-            cost_estimate=cost(3),
+            out_specs=[VMEM] * 5,
+            compiler_params=params(24),
+            cost_estimate=cost(2),
             name="first_products",
         )(mine, got, gslot, hidden_t)
-        return rows, halves[: PIECES], halves[PIECES :], slot_gates, hs
-
-    def later_products(mine, got, hs):
-        return pl.pallas_call(
-            functools.partial(products, half, capacity),
-            out_shape=[shape((slots, piece), bf16)] + [shape((half, piece), bf16)] * 2,
+
+    def later_products(low, mine, got, hs):
+        return pl.pallas_call(
+            functools.partial(products, low, half, capacity),
+            out_shape=product_shapes,
             in_specs=[VMEM] * 3,
             out_specs=[VMEM] * 3,
             compiler_params=params(24),
@@ -414,15 +413,19 @@
 
     def raw_part(rows, got_weight):
         return pl.pallas_call(
-            functools.partial(raw_part_kernel, half, capacity, columns[0]),
+            functools.partial(raw_part_kernel, half, capacity, [slice(0, piece), slice(piece, 2 * piece)]),
             grid=(slots // tile,),
             out_shape=[shape((units, slots), f32), back_shape],
-            in_specs=[by_row[0], *weight_specs, by_slot],
+            in_specs=[
+                *[pl.BlockSpec((tile, piece), lambda i: (i, 0))] * 2,
+                *weight_specs,
+                by_slot,
+            ],
             out_specs=[by_slot, pl.BlockSpec((experts, capacity), lambda i: (0, 0))],
             compiler_params=params(24),
             cost_estimate=cost(3),
             name="raw_part",
-        )(rows, weight, *got_weight, hidden_t)
+        )(*rows, weight, *got_weight, hidden_t)
 
     def raw_rest(rows, got_weight, raw, slot_gates):
         return pl.pallas_call(
@@ -487,11 +490,13 @@
         [x0, y0, f0, yf0, ff0, yff0, r0, behind(yr0, w[0])]
     )
     ff1, yf1, y1 = forward(f1), across(behind(f1, yr0)), across(behind(x1, yr0))
-    got = sibling(behind(theirs0, f1, r1))
-    rows0, send0, own0, slot_gates, hs = first_products(mine0, got, gslot)
+    forwarded = forward_columns(w)
+    got = sibling(behind(theirs0, f1, r1, forwarded))
+    slot_gates, hs, rows_a, send_a, own_a = first_products(mine0, got, gslot)
+    rows_b, send_b, own_b = later_products(piece, mine0, got, hs)
+    rows0, send0, own0 = [rows_a, rows_b], [send_a, send_b], [own_a, own_b]
     got0 = [swap(part) for part in send0]
-    yff1, ry1 = across(behind(ff1, rows0)), backward(behind(y1, ff1, rows0))
-    forwarded = forward_columns(w)
+    yff1, ry1 = across(behind(ff1, *rows0)), backward(behind(y1, ff1, *rows0))
     raw, part = raw_part(rows0, w)
     blocks = [x1, y1, f1, yf1, ff1, yff1, r1, ry1]
     rows1, own1, got1 = [], [], []
@@ -499,7 +504,7 @@
         mine, theirs = later_pick(low, blocks, behind(pmat, raw, forwarded))
         if low > 0:
             theirs = behind(theirs, *got0)
-        rows, send, own = later_products(mine, sibling(theirs), hs)
+        rows, send, own = later_products(0, mine, sibling(theirs), hs)
         rows1.append(rows)
         own1.append(own)
         got1.append(swap(send))

time: 92.9 us -> 94.5 us (1.017)
  starting transfers between devices: 28.3 us -> 32.1 us
  waiting for transfers between devices: 33.1 us -> 30.5 us
    ppermute x5, waiting for transfers between devices: 2.28 us -> 0.11 us  [swap(): return lax.ppermute(x, 'dp', [(0, 1), (1, 0)])]
    ppermute x4, waiting for transfers between devices: 6.13 us -> 4 us  [forward(): return lax.ppermute(x, 'expert', ring_pairs(1))]
    all_to_all x1, starting transfers between devices: 3.41 us -> 5.48 us  [ring_shards(): lax.all_to_all(back, 'expert', split_axis=0, concat_axis=0, tiled=True)]
    ppermute x3, waiting for transfers between devices: 0.01 us -> 1.53 us  [sibling(): return lax.ppermute(x, 'expert', swap_pairs(1))]
    pallas_call x1, Pallas kernels: 2.97 us -> 1.74 us  [first_products(): pl.pallas_call(functools.partial(first_products_kernel, half, capacity),...]
    pallas_call x3 -> x4, Pallas kernels: 6.66 us -> 7.85 us  [the longest x3 5.03 us: later_products(): pl.pallas_call(functools.partial(products, low, half, capacity), out_shap...]
    ppermute x7, starting transfers between devices: 7.73 us -> 8.78 us  [across(): return lax.ppermute(x, 'expert', swap_pairs(2))]
  transfers between devices with their start and end apart: 23 -> 23, of which waited for: 11 -> 13; matrix products, arithmetic and copies ran while one was open for 0% -> 0% of each run, Pallas kernels for 30% -> 29%
where the time goes in v18:
time: 94.5 us; the launch traced here: 94.1 us
  starting transfers between devices  32.1 us (34%)
  waiting for transfers between devices  30.5 us (32%)
  Pallas kernels  28.7 us (30%)
  local copies, waits for them, and re-layouts  1.88 us (2%)
    ppermute x7, waiting for transfers between devices, across(): return lax.ppermute(x, 'expert', swap_pairs(2))  20.9 us
    ppermute x7, starting transfers between devices, across(): return lax.ppermute(x, 'expert', swap_pairs(2))  8.78 us
    ppermute x5, starting transfers between devices, swap(): return lax.ppermute(x, 'dp', [(0, 1), (1, 0)])  7.19 us
    pallas_call x1, Pallas kernels, raw_rest(): pl.pallas_call(functools.partial(raw_kernel, half, halves), grid=(slots /...  6.47 us
    ppermute x3, starting transfers between devices, backward(): return lax.ppermute(x, 'expert', ring_pairs(-1))  6.38 us
    all_to_all x1, starting transfers between devices, ring_shards(): lax.all_to_all(back, 'expert', split_axis=0, concat_axis=0, tiled=True)  5.48 us
    pallas_call x3, Pallas kernels, later_products(): pl.pallas_call(functools.partial(products, low, half, capacity), out_shap...  5.03 us
    ppermute x4, waiting for transfers between devices, forward(): return lax.ppermute(x, 'expert', ring_pairs(1))  4 us
  transfers between devices with their start and end apart: 23, of which 13 were waited for; matrix products, arithmetic and copies ran while one was open for 0% of the time, Pallas kernels for 29%

profile of v18, /device:TPU:0, one launch (start us, length us, event | category | flops | bytes accessed | tf_op | source)
XLA Modules:
  0.0 94.1 jit_solution(6176574289036531743)
XLA Ops:
  0.6 3.0 %collective-permute-start.11 = (bf16[352,2048]{1,0:T(8,128)(2,1)}, bf16[352,2048]{1,0:T(8,128)(2,1)S(1)}, u32[]{:S(2)}, u32[]{:S(2)}) collective-permute-start(bf16[352,2048]{1,0:T(8,128)(2,1)} %bitcast.15), channel_id=1, source_target_pairs={{0,16},{16,0},{1,17},{17,1},{2,18},{18,2},{3,19},{19,3},{4,20},{20... | collective-permute-start | bytes 4325384 | tf_op jit(solution)/shard_map/ppermute | solution.py:334
  3.6 1.9 %pack.1 = (bf16[128,1152]{1,0:T(8,128)(2,1)}, bf16[128,1024]{1,0:T(8,128)(2,1)}) custom-call(s32[6,128]{1,0:T(8,128)} %bitcast.25, bf16[6,128]{1,0:T(8,128)(2,1)} %bitcast.28, bf16[128,2048]{1,0:T(8,128)(2,1)} %grad_hbm.1), custom_call_target="tpu_custom_call" | custom-call | tf_op jit(solution)/shard_map/pack/pallas_call | solution.py:340
  5.5 1.6 %collective-permute-start.1 = (bf16[128,1152]{1,0:T(8,128)(2,1)}, bf16[128,1152]{1,0:T(8,128)(2,1)S(1)}, u32[]{:S(2)}, u32[]{:S(2)}) collective-permute-start(bf16[128,1152]{1,0:T(8,128)(2,1)} %get-tuple-element.46.refs_0_.slots_ref), channel_id=1, source_target_pairs={{0,2},{1,3},{2,0},{3,1},{4,6},{5,7},{6,4},{7,5},{8,10},{9,11},{10,... | collective-permute-start | bytes 884744 | tf_op jit(solution)/shard_map/ppermute | solution.py:328
  7.1 1.6 %collective-permute-start = (bf16[128,1152]{1,0:T(8,128)(2,1)}, bf16[128,1152]{1,0:T(8,128)(2,1)S(1)}, u32[]{:S(2)}, u32[]{:S(2)}) collective-permute-start(bf16[128,1152]{1,0:T(8,128)(2,1)} %get-tuple-element.46.refs_0_.slots_ref), channel_id=1, source_target_pairs={{0,4},{1,5},{2,6},{3,7},{4,12},{5,13},{6,14},{7,15},{12,8},{13,9},... | collective-permute-start | bytes 884744 | tf_op jit(solution)/shard_map/ppermute | solution.py:322
  8.7 5.6 %collective-permute-done.1.refs_1_ = bf16[128,1152]{1,0:T(8,128)(2,1)S(1)} collective-permute-done((bf16[128,1152]{1,0:T(8,128)(2,1)}, bf16[128,1152]{1,0:T(8,128)(2,1)S(1)}, u32[]{:S(2)}, u32[]{:S(2)}) %collective-permute-start.1) | collective-permute-done | bytes 294944 | tf_op jit(solution)/shard_map/ppermute | solution.py:328
  14.3 2.2 %collective-permute-done.refs_2_ = bf16[128,1152]{1,0:T(8,128)(2,1)S(1)} collective-permute-done((bf16[128,1152]{1,0:T(8,128)(2,1)}, bf16[128,1152]{1,0:T(8,128)(2,1)S(1)}, u32[]{:S(2)}, u32[]{:S(2)}) %collective-permute-start) | collective-permute-done | bytes 294944 | tf_op jit(solution)/shard_map/ppermute | solution.py:322
  17.8 5.9 %collective-permute-done.3.refs_3_ = bf16[128,1152]{1,0:T(8,128)(2,1)S(1)} collective-permute-done((bf16[128,1152]{1,0:T(8,128)(2,1)S(1)}, bf16[128,1152]{1,0:T(8,128)(2,1)S(1)}, u32[]{:S(2)}, u32[]{:S(2)}) %collective-permute-start.3) | collective-permute-done | bytes 294944 | tf_op jit(solution)/shard_map/ppermute | solution.py:328
  27.9 3.9 %collective-permute-done.4.refs_6_ = bf16[128,1152]{1,0:T(8,128)(2,1)S(1)} collective-permute-done((bf16[128,1152]{1,0:T(8,128)(2,1)}, bf16[128,1152]{1,0:T(8,128)(2,1)S(1)}, u32[]{:S(2)}, u32[]{:S(2)}) %collective-permute-start.4) | collective-permute-done | bytes 294944 | tf_op jit(solution)/shard_map/ppermute | solution.py:325
  31.8 2.3 %collective-permute-done.5.refs_5_ = bf16[128,1152]{1,0:T(8,128)(2,1)S(1)} collective-permute-done((bf16[128,1152]{1,0:T(8,128)(2,1)S(1)}, bf16[128,1152]{1,0:T(8,128)(2,1)S(1)}, u32[]{:S(2)}, u32[]{:S(2)}) %collective-permute-start.5) | collective-permute-done | bytes 294944 | tf_op jit(solution)/shard_map/ppermute | solution.py:328
  35.6 3.1 %collective-permute-start.12 = (bf16[128,1024]{1,0:T(8,128)(2,1)}, bf16[128,1024]{1,0:T(8,128)(2,1)S(1)}, u32[]{:S(2)}, u32[]{:S(2)}) collective-permute-start(bf16[128,1024]{1,0:T(8,128)(2,1)} %get-tuple-element.50.refs_0_), channel_id=1, source_target_pairs={{0,8},{1,9},{2,10},{3,11},{4,0},{5,1},{6,2},{7,3},{12,4},{13,5},{1... | collective-permute-start | bytes 786440 | tf_op jit(solution)/shard_map/ppermute | solution.py:325
  38.8 2.1 %collective-permute-done.6.refs_7_ = bf16[128,1152]{1,0:T(8,128)(2,1)S(1)} collective-permute-done((bf16[128,1152]{1,0:T(8,128)(2,1)S(1)}, bf16[128,1152]{1,0:T(8,128)(2,1)S(1)}, u32[]{:S(2)}, u32[]{:S(2)}) %collective-permute-start.6) | collective-permute-done | bytes 294944 | tf_op jit(solution)/shard_map/ppermute | solution.py:328
  41.8 1.6 %first_pick.1 = (bf16[512,1024]{1,0:T(8,128)(2,1)S(1)}, bf16[528,1024]{1,0:T(8,128)(2,1)S(1)}, bf16[1024,128]{1,0:T(8,128)(2,1)S(1)}, f32[8,128]{1,0:T(8,128)S(1)}) custom-call(bf16[128,1152]{1,0:T(8,128)(2,1)S(1)} %copy-done.14, bf16[128,1152]{1,0:T(8,128)(2,1)S(1)} %collective-permute-done.1.refs_1_, bf16[128,1152]{1,0:T(8,128)(2,1)S(1)} %collective-permute-done.refs_2_, ...), custom_call_target="tpu_custom_call" | custom-call | flops 3000000000 | bytes 9437184 | tf_op jit(solution)/shard_map/first_pick/pallas_call | solution.py:358
  43.7 3.2 %hidden_weight.1.forward_ref = bf16[1024,1024]{1,0:T(8,128)(2,1)S(1)} custom-call(bf16[352,2048]{1,0:T(8,128)(2,1)S(1)} %bitcast.17, bf16[352,2048]{1,0:T(8,128)(2,1)S(1)} %collective-permute-done.11.refs_0_, bf16[704,1024]{1,0:T(8,128)(2,1)S(1)} %bitcast.19), custom_call_target="tpu_custom_call" | custom-call | flops 3000000000 | bytes 9437184 | tf_op jit(solution)/shard_map/hidden_weight/pallas_call | solution.py:447
  49.7 1.7 %first_products.1 = (f32[1,1024]{1,0:T(1,128)S(1)}, bf16[704,1024]{1,0:T(8,128)(2,1)S(1)}, bf16[1024,512]{1,0:T(8,128)(2,1)S(1)}, bf16[352,512]{1,0:T(8,128)(2,1)S(1)}, bf16[352,512]{1,0:T(8,128)(2,1)S(1)}) custom-call(bf16[512,1024]{1,0:T(8,128)(2,1)S(1)} %get-tuple-element.53.mine_ref, bf16[528,1024]{1,0:T(8,128)(2,1)S(1)} %collective-permute-done.13.got_ref, ...), custom_call_target="tpu_custom_call" | custom-call | flops 2000000000 | bytes 6291456 | tf_op jit(solution)/shard_map/first_products/pallas_call | solution.py:390
  53.3 1.6 %collective-permute-start.18 = (bf16[352,512]{1,0:T(8,128)(2,1)S(1)}, bf16[352,512]{1,0:T(8,128)(2,1)S(1)}, u32[]{:S(2)}, u32[]{:S(2)}) collective-permute-start(bf16[352,512]{1,0:T(8,128)(2,1)S(1)} %get-tuple-element.71), channel_id=1, source_target_pairs={{0,16},{16,0},{1,17},{17,1},{2,18},{18,2},{3,19},{19,3},{4,20},{20... | collective-permute-start | bytes 1081352 | tf_op jit(solution)/shard_map/ppermute | solution.py:334
  54.9 1.5 %collective-permute-start.9 = (bf16[128,1024]{1,0:T(8,128)(2,1)S(1)}, bf16[128,1024]{1,0:T(8,128)(2,1)S(1)}, u32[]{:S(2)}, u32[]{:S(2)}) collective-permute-start(bf16[128,1024]{1,0:T(8,128)(2,1)S(1)} %collective-permute-done.8.refs_2_), channel_id=1, source_target_pairs={{0,2},{1,3},{2,0},{3,1},{4,6},{5,7},{6,4},{7,5},{8,10},{9,11},{10,... | collective-permute-start | bytes 786440 | tf_op jit(solution)/shard_map/ppermute | solution.py:328
  57.1 1.5 %collective-permute-start.14 = (bf16[128,1024]{1,0:T(8,128)(2,1)S(1)}, bf16[128,1024]{1,0:T(8,128)(2,1)S(1)}, u32[]{:S(2)}, u32[]{:S(2)}) collective-permute-start(bf16[128,1024]{1,0:T(8,128)(2,1)S(1)} %collective-permute-done.10.refs_4_), channel_id=1, source_target_pairs={{0,2},{1,3},{2,0},{3,1},{4,6},{5,7},{6,4},{7,5},{8,10},{9,11},{10,... | collective-permute-start | bytes 786440 | tf_op jit(solution)/shard_map/ppermute | solution.py:328
  58.6 1.7 %collective-permute-start.15 = (bf16[128,1024]{1,0:T(8,128)(2,1)S(1)}, bf16[128,1024]{1,0:T(8,128)(2,1)S(1)}, u32[]{:S(2)}, u32[]{:S(2)}) collective-permute-start(bf16[128,1024]{1,0:T(8,128)(2,1)S(1)} %collective-permute-done.7.refs_1_), channel_id=1, source_target_pairs={{0,8},{1,9},{2,10},{3,11},{4,0},{5,1},{6,2},{7,3},{12,4},{13,5},{1... | collective-permute-start | bytes 786440 | tf_op jit(solution)/shard_map/ppermute | solution.py:325
  60.4 2.8 %raw_part.1 = (f32[704,1024]{1,0:T(8,128)S(1)}, f32[16,64]{1,0:T(8,128)S(1)}) custom-call(bf16[1024,512]{1,0:T(8,128)(2,1)S(1)} %get-tuple-element.57.first_ref, bf16[1024,512]{1,0:T(8,128)(2,1)S(1)} %get-tuple-element.59.second_ref, bf16[352,2048]{1,0:T(8,128)(2,1)S(1)} %bitcast.18, bf16[352,2048]{1,0:T(8,128)(2,1)S(1)} %collective-permute-done.11.refs_0_, ...), custom_call_target="tpu_custom_call" | custom-call | flops 3000000000 | bytes 9437184 | tf_op jit(solution)/shard_map/raw_part/pallas_call | solution.py:415
  64.1 4.2 %collective-permute-done.14.refs_5_ = bf16[128,1024]{1,0:T(8,128)(2,1)S(1)} collective-permute-done((bf16[128,1024]{1,0:T(8,128)(2,1)S(1)}, bf16[128,1024]{1,0:T(8,128)(2,1)S(1)}, u32[]{:S(2)}, u32[]{:S(2)}) %collective-permute-start.14) | collective-permute-done | bytes 262176 | tf_op jit(solution)/shard_map/ppermute | solution.py:328
  70.8 1.9 %products.4 = (bf16[1024,512]{1,0:T(8,128)(2,1)S(1)}, bf16[352,512]{1,0:T(8,128)(2,1)}, bf16[352,512]{1,0:T(8,128)(2,1)S(1)}) custom-call(bf16[512,512]{1,0:T(8,128)(2,1)S(1)} %get-tuple-element.65.mine_ref, bf16[512,512]{1,0:T(8,128)(2,1)S(1)} %collective-permute-done.16.got_ref, bf16[704,1024]{1,0:T(8,128)(2,1)S(1)} %get-tuple-element.58.hs_ref), custom_call_target="tpu_custom_call" | custom-call | tf_op jit(solution)/shard_map/products/pallas_call | solution.py:401
  73.3 1.9 %products.5 = (bf16[1024,512]{1,0:T(8,128)(2,1)S(1)}, bf16[352,512]{1,0:T(8,128)(2,1)}, bf16[352,512]{1,0:T(8,128)(2,1)S(1)}) custom-call(bf16[512,512]{1,0:T(8,128)(2,1)S(1)} %get-tuple-element.68.mine_ref, bf16[512,512]{1,0:T(8,128)(2,1)S(1)} %collective-permute-done.19.got_ref, bf16[704,1024]{1,0:T(8,128)(2,1)S(1)} %get-tuple-element.58.hs_ref), custom_call_target="tpu_custom_call" | custom-call | tf_op jit(solution)/shard_map/products/pallas_call | solution.py:401
  78.0 5.5 %all-to-all-start = ((f32[16,1,64]{2,1,0:T(1,128)}), f32[16,1,64]{2,1,0:T(1,128)S(1)}, u32[]{:S(2)}, u32[]{:S(2)}) async-start(f32[16,1,64]{2,1,0:T(1,128)} %bitcast.10), calls=%async_computation | async-start | bytes 16384 | tf_op jit(solution)/shard_map/all_to_all | solution.py:513
  83.6 6.5 %raw.1 = bf16[704,1024]{1,0:T(8,128)(2,1)} custom-call(bf16[1024,512]{1,0:T(8,128)(2,1)} %copy-done, bf16[1024,512]{1,0:T(8,128)(2,1)} %copy-done.1, bf16[352,2048]{1,0:T(8,128)(2,1)} %bitcast.16, bf16[352,2048]{1,0:T(8,128)(2,1)} %copy-done.4, f32[704,1024]{1,0:T(8,128)} %copy-done.2, f32[1,1024]{1,0:T(1,128)} %copy-done.15), custom_call_target="tpu_custom_call" | custom-call | tf_op jit(solution)/shard_map/raw/pallas_call | solution.py:431
  (73 shorter events, 24.4 us)
Async XLA Ops:
  0.6 40.2 %collective-permute-start.11 = (bf16[352,2048]{1,0:T(8,128)(2,1)}, bf16[352,2048]{1,0:T(8,128)(2,1)S(1)}, u32[]{:S(2)}, u32[]{:S(2)}) collective-permute-start(bf16[352,2048]{1,0:T(8,128)(2,1)} %bitcast.15), channel_id=1, source_target_pairs={{0,16},{16,0},{1,17},{17,1},{2,18},{18,2},{3,19},{19,3},{4,20},{20... | collective-permute-start | bytes 4325384 | tf_op jit(solution)/shard_map/ppermute | solution.py:334
  5.5 8.7 %collective-permute-start.1 = (bf16[128,1152]{1,0:T(8,128)(2,1)}, bf16[128,1152]{1,0:T(8,128)(2,1)S(1)}, u32[]{:S(2)}, u32[]{:S(2)}) collective-permute-start(bf16[128,1152]{1,0:T(8,128)(2,1)} %get-tuple-element.46.refs_0_.slots_ref), channel_id=1, source_target_pairs={{0,2},{1,3},{2,0},{3,1},{4,6},{5,7},{6,4},{7,5},{8,10},{9,11},{10,... | collective-permute-start | bytes 884744 | tf_op jit(solution)/shard_map/ppermute | solution.py:328
  7.1 9.3 %collective-permute-start = (bf16[128,1152]{1,0:T(8,128)(2,1)}, bf16[128,1152]{1,0:T(8,128)(2,1)S(1)}, u32[]{:S(2)}, u32[]{:S(2)}) collective-permute-start(bf16[128,1152]{1,0:T(8,128)(2,1)} %get-tuple-element.46.refs_0_.slots_ref), channel_id=1, source_target_pairs={{0,4},{1,5},{2,6},{3,7},{4,12},{5,13},{6,14},{7,15},{12,8},{13,9},... | collective-permute-start | bytes 884744 | tf_op jit(solution)/shard_map/ppermute | solution.py:322
  16.4 7.3 %collective-permute-start.3 = (bf16[128,1152]{1,0:T(8,128)(2,1)S(1)}, bf16[128,1152]{1,0:T(8,128)(2,1)S(1)}, u32[]{:S(2)}, u32[]{:S(2)}) collective-permute-start(bf16[128,1152]{1,0:T(8,128)(2,1)S(1)} %collective-permute-done.refs_2_), channel_id=1, source_target_pairs={{0,2},{1,3},{2,0},{3,1},{4,6},{5,7},{6,4},{7,5},{8,10},{9,11},{10,... | collective-permute-start | bytes 884744 | tf_op jit(solution)/shard_map/ppermute | solution.py:328
  16.9 7.9 %collective-permute-start.2 = (bf16[128,1152]{1,0:T(8,128)(2,1)S(1)}, bf16[128,1152]{1,0:T(8,128)(2,1)S(1)}, u32[]{:S(2)}, u32[]{:S(2)}) collective-permute-start(bf16[128,1152]{1,0:T(8,128)(2,1)S(1)} %collective-permute-done.refs_2_), channel_id=1, source_target_pairs={{0,4},{1,5},{2,6},{3,7},{4,12},{5,13},{6,14},{7,15},{12,8},{13,9},... | collective-permute-start | bytes 884744 | tf_op jit(solution)/shard_map/ppermute | solution.py:322
  24.8 6.9 %collective-permute-start.4 = (bf16[128,1152]{1,0:T(8,128)(2,1)}, bf16[128,1152]{1,0:T(8,128)(2,1)S(1)}, u32[]{:S(2)}, u32[]{:S(2)}) collective-permute-start(bf16[128,1152]{1,0:T(8,128)(2,1)} %get-tuple-element.46.refs_0_.slots_ref), channel_id=1, source_target_pairs={{0,8},{1,9},{2,10},{3,11},{4,0},{5,1},{6,2},{7,3},{12,4},{13,5},{1... | collective-permute-start | bytes 884744 | tf_op jit(solution)/shard_map/ppermute | solution.py:325
  26.3 7.8 %collective-permute-start.5 = (bf16[128,1152]{1,0:T(8,128)(2,1)S(1)}, bf16[128,1152]{1,0:T(8,128)(2,1)S(1)}, u32[]{:S(2)}, u32[]{:S(2)}) collective-permute-start(bf16[128,1152]{1,0:T(8,128)(2,1)S(1)} %collective-permute-done.2.refs_4_), channel_id=1, source_target_pairs={{0,2},{1,3},{2,0},{3,1},{4,6},{5,7},{6,4},{7,5},{8,10},{9,11},{10,... | collective-permute-start | bytes 884744 | tf_op jit(solution)/shard_map/ppermute | solution.py:328
  34.1 6.7 %collective-permute-start.6 = (bf16[128,1152]{1,0:T(8,128)(2,1)S(1)}, bf16[128,1152]{1,0:T(8,128)(2,1)S(1)}, u32[]{:S(2)}, u32[]{:S(2)}) collective-permute-start(bf16[128,1152]{1,0:T(8,128)(2,1)S(1)} %collective-permute-done.4.refs_6_), channel_id=1, source_target_pairs={{0,2},{1,3},{2,0},{3,1},{4,6},{5,7},{6,4},{7,5},{8,10},{9,11},{10,... | collective-permute-start | bytes 884744 | tf_op jit(solution)/shard_map/ppermute | solution.py:328
  35.6 11.3 %collective-permute-start.12 = (bf16[128,1024]{1,0:T(8,128)(2,1)}, bf16[128,1024]{1,0:T(8,128)(2,1)S(1)}, u32[]{:S(2)}, u32[]{:S(2)}) collective-permute-start(bf16[128,1024]{1,0:T(8,128)(2,1)} %get-tuple-element.50.refs_0_), channel_id=1, source_target_pairs={{0,8},{1,9},{2,10},{3,11},{4,0},{5,1},{6,2},{7,3},{12,4},{13,5},{1... | collective-permute-start | bytes 786440 | tf_op jit(solution)/shard_map/ppermute | solution.py:325
  38.8 8.1 %collective-permute-start.8 = (bf16[128,1024]{1,0:T(8,128)(2,1)}, bf16[128,1024]{1,0:T(8,128)(2,1)S(1)}, u32[]{:S(2)}, u32[]{:S(2)}) collective-permute-start(bf16[128,1024]{1,0:T(8,128)(2,1)} %get-tuple-element.50.refs_0_), channel_id=1, source_target_pairs={{0,4},{1,5},{2,6},{3,7},{4,12},{5,13},{6,14},{7,15},{12,8},{13,9},... | collective-permute-start | bytes 786440 | tf_op jit(solution)/shard_map/ppermute | solution.py:322
  41.8 18.6 %copy-start.4 = (bf16[352,2048]{1,0:T(8,128)(2,1)}, bf16[352,2048]{1,0:T(8,128)(2,1)S(1)}, u32[]{:S(2)}) copy-start(bf16[352,2048]{1,0:T(8,128)(2,1)S(1)} %collective-permute-done.11.refs_0_) | copy-start | bytes 4325380
  46.9 2.8 %collective-permute-start.13 = (bf16[528,1024]{1,0:T(8,128)(2,1)S(1)}, bf16[528,1024]{1,0:T(8,128)(2,1)S(1)}, u32[]{:S(2)}, u32[]{:S(2)}) collective-permute-start(bf16[528,1024]{1,0:T(8,128)(2,1)S(1)} %get-tuple-element.55), channel_id=1, source_target_pairs={{0,1},{1,0},{2,3},{3,2},{4,5},{5,4},{6,7},{7,6},{8,9},{9,8},{10,11... | collective-permute-start | bytes 3244040 | tf_op jit(solution)/shard_map/ppermute | solution.py:331
  47.0 10.1 %collective-permute-start.10 = (bf16[128,1024]{1,0:T(8,128)(2,1)S(1)}, bf16[128,1024]{1,0:T(8,128)(2,1)S(1)}, u32[]{:S(2)}, u32[]{:S(2)}) collective-permute-start(bf16[128,1024]{1,0:T(8,128)(2,1)S(1)} %collective-permute-done.8.refs_2_), channel_id=1, source_target_pairs={{0,4},{1,5},{2,6},{3,7},{4,12},{5,13},{6,14},{7,15},{12,8},{13,9},... | collective-permute-start | bytes 786440 | tf_op jit(solution)/shard_map/ppermute | solution.py:322
  48.2 8.9 %collective-permute-start.7 = (bf16[128,1024]{1,0:T(8,128)(2,1)S(1)}, bf16[128,1024]{1,0:T(8,128)(2,1)S(1)}, u32[]{:S(2)}, u32[]{:S(2)}) collective-permute-start(bf16[128,1024]{1,0:T(8,128)(2,1)S(1)} %copy-done.5), channel_id=1, source_target_pairs={{0,2},{1,3},{2,0},{3,1},{4,6},{5,7},{6,4},{7,5},{8,10},{9,11},{10,... | collective-permute-start | bytes 786440 | tf_op jit(solution)/shard_map/ppermute | solution.py:328
  51.4 18.1 %collective-permute-start.17 = (bf16[352,512]{1,0:T(8,128)(2,1)S(1)}, bf16[352,512]{1,0:T(8,128)(2,1)S(1)}, u32[]{:S(2)}, u32[]{:S(2)}) collective-permute-start(bf16[352,512]{1,0:T(8,128)(2,1)S(1)} %get-tuple-element.70), channel_id=1, source_target_pairs={{0,16},{16,0},{1,17},{17,1},{2,18},{18,2},{3,19},{19,3},{4,20},{20... | collective-permute-start | bytes 1081352 | tf_op jit(solution)/shard_map/ppermute | solution.py:334
  53.3 16.4 %collective-permute-start.18 = (bf16[352,512]{1,0:T(8,128)(2,1)S(1)}, bf16[352,512]{1,0:T(8,128)(2,1)S(1)}, u32[]{:S(2)}, u32[]{:S(2)}) collective-permute-start(bf16[352,512]{1,0:T(8,128)(2,1)S(1)} %get-tuple-element.71), channel_id=1, source_target_pairs={{0,16},{16,0},{1,17},{17,1},{2,18},{18,2},{3,19},{19,3},{4,20},{20... | collective-permute-start | bytes 1081352 | tf_op jit(solution)/shard_map/ppermute | solution.py:334
  54.9 9.2 %collective-permute-start.9 = (bf16[128,1024]{1,0:T(8,128)(2,1)S(1)}, bf16[128,1024]{1,0:T(8,128)(2,1)S(1)}, u32[]{:S(2)}, u32[]{:S(2)}) collective-permute-start(bf16[128,1024]{1,0:T(8,128)(2,1)S(1)} %collective-permute-done.8.refs_2_), channel_id=1, source_target_pairs={{0,2},{1,3},{2,0},{3,1},{4,6},{5,7},{6,4},{7,5},{8,10},{9,11},{10,... | collective-permute-start | bytes 786440 | tf_op jit(solution)/shard_map/ppermute | solution.py:328
  57.1 11.2 %collective-permute-start.14 = (bf16[128,1024]{1,0:T(8,128)(2,1)S(1)}, bf16[128,1024]{1,0:T(8,128)(2,1)S(1)}, u32[]{:S(2)}, u32[]{:S(2)}) collective-permute-start(bf16[128,1024]{1,0:T(8,128)(2,1)S(1)} %collective-permute-done.10.refs_4_), channel_id=1, source_target_pairs={{0,2},{1,3},{2,0},{3,1},{4,6},{5,7},{6,4},{7,5},{8,10},{9,11},{10,... | collective-permute-start | bytes 786440 | tf_op jit(solution)/shard_map/ppermute | solution.py:328
  58.6 9.6 %collective-permute-start.15 = (bf16[128,1024]{1,0:T(8,128)(2,1)S(1)}, bf16[128,1024]{1,0:T(8,128)(2,1)S(1)}, u32[]{:S(2)}, u32[]{:S(2)}) collective-permute-start(bf16[128,1024]{1,0:T(8,128)(2,1)S(1)} %collective-permute-done.7.refs_1_), channel_id=1, source_target_pairs={{0,8},{1,9},{2,10},{3,11},{4,0},{5,1},{6,2},{7,3},{12,4},{13,5},{1... | collective-permute-start | bytes 786440 | tf_op jit(solution)/shard_map/ppermute | solution.py:325
  68.9 2.0 %collective-permute-start.16 = (bf16[512,512]{1,0:T(8,128)(2,1)S(1)}, bf16[512,512]{1,0:T(8,128)(2,1)S(1)}, u32[]{:S(2)}, u32[]{:S(2)}) collective-permute-start(bf16[512,512]{1,0:T(8,128)(2,1)S(1)} %get-tuple-element.66), channel_id=1, source_target_pairs={{0,1},{1,0},{2,3},{3,2},{4,5},{5,4},{6,7},{7,6},{8,9},{9,8},{10,11... | collective-permute-start | bytes 1572872 | tf_op jit(solution)/shard_map/ppermute | solution.py:331
  69.7 3.6 %collective-permute-start.19 = (bf16[512,512]{1,0:T(8,128)(2,1)S(1)}, bf16[512,512]{1,0:T(8,128)(2,1)S(1)}, u32[]{:S(2)}, u32[]{:S(2)}) collective-permute-start(bf16[512,512]{1,0:T(8,128)(2,1)S(1)} %get-tuple-element.72), channel_id=1, source_target_pairs={{0,1},{1,0},{2,3},{3,2},{4,5},{5,4},{6,7},{7,6},{8,9},{9,8},{10,11... | collective-permute-start | bytes 1572872 | tf_op jit(solution)/shard_map/ppermute | solution.py:331
  72.7 20.4 %collective-permute-start.20 = (bf16[352,512]{1,0:T(8,128)(2,1)}, bf16[352,512]{1,0:T(8,128)(2,1)S(1)}, u32[]{:S(2)}, u32[]{:S(2)}) collective-permute-start(bf16[352,512]{1,0:T(8,128)(2,1)} %get-tuple-element.74), channel_id=1, source_target_pairs={{0,16},{16,0},{1,17},{17,1},{2,18},{18,2},{3,19},{19,3},{4,20},{20... | collective-permute-start | bytes 1081352 | tf_op jit(solution)/shard_map/ppermute | solution.py:334
  75.2 17.9 %collective-permute-start.21 = (bf16[352,512]{1,0:T(8,128)(2,1)}, bf16[352,512]{1,0:T(8,128)(2,1)S(1)}, u32[]{:S(2)}, u32[]{:S(2)}) collective-permute-start(bf16[352,512]{1,0:T(8,128)(2,1)} %get-tuple-element.75), channel_id=1, source_target_pairs={{0,16},{16,0},{1,17},{17,1},{2,18},{18,2},{3,19},{19,3},{4,20},{20... | collective-permute-start | bytes 1081352 | tf_op jit(solution)/shard_map/ppermute | solution.py:334
  78.0 13.0 %all-to-all-start = ((f32[16,1,64]{2,1,0:T(1,128)}), f32[16,1,64]{2,1,0:T(1,128)S(1)}, u32[]{:S(2)}, u32[]{:S(2)}) async-start(f32[16,1,64]{2,1,0:T(1,128)} %bitcast.10), calls=%async_computation | async-start | bytes 16384 | tf_op jit(solution)/shard_map/all_to_all | solution.py:513
  (17 other events, 79.1 us)

commit v19 on v18

--- a/solution.py
+++ b/solution.py
@@ -490,13 +490,13 @@
         [x0, y0, f0, yf0, ff0, yff0, r0, behind(yr0, w[0])]
     )
     ff1, yf1, y1 = forward(f1), across(behind(f1, yr0)), across(behind(x1, yr0))
-    forwarded = forward_columns(w)
-    got = sibling(behind(theirs0, f1, r1, forwarded))
+    got = sibling(behind(theirs0, f1, r1))
     slot_gates, hs, rows_a, send_a, own_a = first_products(mine0, got, gslot)
     rows_b, send_b, own_b = later_products(piece, mine0, got, hs)
     rows0, send0, own0 = [rows_a, rows_b], [send_a, send_b], [own_a, own_b]
     got0 = [swap(part) for part in send0]
     yff1, ry1 = across(behind(ff1, *rows0)), backward(behind(y1, ff1, *rows0))
+    forwarded = forward_columns(w)
     raw, part = raw_part(rows0, w)
     blocks = [x1, y1, f1, yf1, ff1, yff1, r1, ry1]
     rows1, own1, got1 = [], [], []

time: 94.5 us -> 92 us (0.974)
  starting transfers between devices: 32.1 us -> 28.5 us
  waiting for transfers between devices: 30.5 us -> 32 us
    ppermute x4, waiting for transfers between devices: 4 us -> 6.12 us  [forward(): return lax.ppermute(x, 'expert', ring_pairs(1))]
    all_to_all x1, starting transfers between devices: 5.48 us -> 3.49 us  [ring_shards(): lax.all_to_all(back, 'expert', split_axis=0, concat_axis=0, tiled=True)]
    ppermute x7, starting transfers between devices: 8.78 us -> 7.73 us  [across(): return lax.ppermute(x, 'expert', swap_pairs(2))]
  transfers between devices with their start and end apart: 23 -> 23, of which waited for: 13 -> 11; matrix products, arithmetic and copies ran while one was open for 0% -> 0% of each run, Pallas kernels for 29% -> 30%
where the time goes in v19:
time: 92 us; the launch traced here: 91.7 us
  waiting for transfers between devices  32 us (35%)
  Pallas kernels  28.7 us (31%)
  starting transfers between devices  28.5 us (31%)
  local copies, waits for them, and re-layouts  1.62 us (2%)
    ppermute x7, waiting for transfers between devices, across(): return lax.ppermute(x, 'expert', swap_pairs(2))  20.7 us
    ppermute x7, starting transfers between devices, across(): return lax.ppermute(x, 'expert', swap_pairs(2))  7.73 us
    ppermute x5, starting transfers between devices, swap(): return lax.ppermute(x, 'dp', [(0, 1), (1, 0)])  7.18 us
    pallas_call x1, Pallas kernels, raw_rest(): pl.pallas_call(functools.partial(raw_kernel, half, halves), grid=(slots /...  6.46 us
    ppermute x4, waiting for transfers between devices, forward(): return lax.ppermute(x, 'expert', ring_pairs(1))  6.12 us
    ppermute x3, starting transfers between devices, backward(): return lax.ppermute(x, 'expert', ring_pairs(-1))  5.6 us
    pallas_call x3, Pallas kernels, later_products(): pl.pallas_call(functools.partial(products, low, half, capacity), out_shap...  5.04 us
    ppermute x4, starting transfers between devices, forward(): return lax.ppermute(x, 'expert', ring_pairs(1))  4.41 us
  transfers between devices with their start and end apart: 23, of which 11 were waited for; matrix products, arithmetic and copies ran while one was open for 0% of the time, Pallas kernels for 30%

profile of v19, /device:TPU:0, one launch (start us, length us, event | category | flops | bytes accessed | tf_op | source)
XLA Modules:
  0.0 91.7 jit_solution(4052139069207727343)
XLA Ops:
  0.6 3.0 %collective-permute-start.11 = (bf16[352,2048]{1,0:T(8,128)(2,1)}, bf16[352,2048]{1,0:T(8,128)(2,1)S(1)}, u32[]{:S(2)}, u32[]{:S(2)}) collective-permute-start(bf16[352,2048]{1,0:T(8,128)(2,1)} %bitcast.15), channel_id=1, source_target_pairs={{0,16},{16,0},{1,17},{17,1},{2,18},{18,2},{3,19},{19,3},{4,20},{20... | collective-permute-start | bytes 4325384 | tf_op jit(solution)/shard_map/ppermute | solution.py:334
  3.6 1.9 %pack.1 = (bf16[128,1152]{1,0:T(8,128)(2,1)}, bf16[128,1024]{1,0:T(8,128)(2,1)}) custom-call(s32[6,128]{1,0:T(8,128)} %bitcast.25, bf16[6,128]{1,0:T(8,128)(2,1)} %bitcast.28, bf16[128,2048]{1,0:T(8,128)(2,1)} %grad_hbm.1), custom_call_target="tpu_custom_call" | custom-call | tf_op jit(solution)/shard_map/pack/pallas_call | solution.py:340
  5.5 1.6 %collective-permute-start.1 = (bf16[128,1152]{1,0:T(8,128)(2,1)}, bf16[128,1152]{1,0:T(8,128)(2,1)S(1)}, u32[]{:S(2)}, u32[]{:S(2)}) collective-permute-start(bf16[128,1152]{1,0:T(8,128)(2,1)} %get-tuple-element.46.refs_0_.slots_ref), channel_id=1, source_target_pairs={{0,2},{1,3},{2,0},{3,1},{4,6},{5,7},{6,4},{7,5},{8,10},{9,11},{10,... | collective-permute-start | bytes 884744 | tf_op jit(solution)/shard_map/ppermute | solution.py:328
  7.1 1.6 %collective-permute-start = (bf16[128,1152]{1,0:T(8,128)(2,1)}, bf16[128,1152]{1,0:T(8,128)(2,1)S(1)}, u32[]{:S(2)}, u32[]{:S(2)}) collective-permute-start(bf16[128,1152]{1,0:T(8,128)(2,1)} %get-tuple-element.46.refs_0_.slots_ref), channel_id=1, source_target_pairs={{0,4},{1,5},{2,6},{3,7},{4,12},{5,13},{6,14},{7,15},{12,8},{13,9},... | collective-permute-start | bytes 884744 | tf_op jit(solution)/shard_map/ppermute | solution.py:322
  8.7 5.6 %collective-permute-done.1.refs_1_ = bf16[128,1152]{1,0:T(8,128)(2,1)S(1)} collective-permute-done((bf16[128,1152]{1,0:T(8,128)(2,1)}, bf16[128,1152]{1,0:T(8,128)(2,1)S(1)}, u32[]{:S(2)}, u32[]{:S(2)}) %collective-permute-start.1) | collective-permute-done | bytes 294944 | tf_op jit(solution)/shard_map/ppermute | solution.py:328
  14.3 2.2 %collective-permute-done.refs_2_ = bf16[128,1152]{1,0:T(8,128)(2,1)S(1)} collective-permute-done((bf16[128,1152]{1,0:T(8,128)(2,1)}, bf16[128,1152]{1,0:T(8,128)(2,1)S(1)}, u32[]{:S(2)}, u32[]{:S(2)}) %collective-permute-start) | collective-permute-done | bytes 294944 | tf_op jit(solution)/shard_map/ppermute | solution.py:322
  17.8 5.9 %collective-permute-done.3.refs_3_ = bf16[128,1152]{1,0:T(8,128)(2,1)S(1)} collective-permute-done((bf16[128,1152]{1,0:T(8,128)(2,1)S(1)}, bf16[128,1152]{1,0:T(8,128)(2,1)S(1)}, u32[]{:S(2)}, u32[]{:S(2)}) %collective-permute-start.3) | collective-permute-done | bytes 294944 | tf_op jit(solution)/shard_map/ppermute | solution.py:328
  26.3 1.5 %collective-permute-start.5 = (bf16[128,1152]{1,0:T(8,128)(2,1)S(1)}, bf16[128,1152]{1,0:T(8,128)(2,1)S(1)}, u32[]{:S(2)}, u32[]{:S(2)}) collective-permute-start(bf16[128,1152]{1,0:T(8,128)(2,1)S(1)} %collective-permute-done.2.refs_4_), channel_id=1, source_target_pairs={{0,2},{1,3},{2,0},{3,1},{4,6},{5,7},{6,4},{7,5},{8,10},{9,11},{10,... | collective-permute-start | bytes 884744 | tf_op jit(solution)/shard_map/ppermute | solution.py:328
  27.9 3.9 %collective-permute-done.4.refs_6_ = bf16[128,1152]{1,0:T(8,128)(2,1)S(1)} collective-permute-done((bf16[128,1152]{1,0:T(8,128)(2,1)}, bf16[128,1152]{1,0:T(8,128)(2,1)S(1)}, u32[]{:S(2)}, u32[]{:S(2)}) %collective-permute-start.4) | collective-permute-done | bytes 294944 | tf_op jit(solution)/shard_map/ppermute | solution.py:325
  31.8 2.3 %collective-permute-done.5.refs_5_ = bf16[128,1152]{1,0:T(8,128)(2,1)S(1)} collective-permute-done((bf16[128,1152]{1,0:T(8,128)(2,1)S(1)}, bf16[128,1152]{1,0:T(8,128)(2,1)S(1)}, u32[]{:S(2)}, u32[]{:S(2)}) %collective-permute-start.5) | collective-permute-done | bytes 294944 | tf_op jit(solution)/shard_map/ppermute | solution.py:328
  35.6 3.1 %collective-permute-start.12 = (bf16[128,1024]{1,0:T(8,128)(2,1)}, bf16[128,1024]{1,0:T(8,128)(2,1)S(1)}, u32[]{:S(2)}, u32[]{:S(2)}) collective-permute-start(bf16[128,1024]{1,0:T(8,128)(2,1)} %get-tuple-element.50.refs_0_), channel_id=1, source_target_pairs={{0,8},{1,9},{2,10},{3,11},{4,0},{5,1},{6,2},{7,3},{12,4},{13,5},{1... | collective-permute-start | bytes 786440 | tf_op jit(solution)/shard_map/ppermute | solution.py:325
  38.8 2.1 %collective-permute-done.6.refs_7_ = bf16[128,1152]{1,0:T(8,128)(2,1)S(1)} collective-permute-done((bf16[128,1152]{1,0:T(8,128)(2,1)S(1)}, bf16[128,1152]{1,0:T(8,128)(2,1)S(1)}, u32[]{:S(2)}, u32[]{:S(2)}) %collective-permute-start.6) | collective-permute-done | bytes 294944 | tf_op jit(solution)/shard_map/ppermute | solution.py:328
  41.8 1.6 %first_pick.1 = (bf16[512,1024]{1,0:T(8,128)(2,1)S(1)}, bf16[528,1024]{1,0:T(8,128)(2,1)S(1)}, bf16[1024,128]{1,0:T(8,128)(2,1)S(1)}, f32[8,128]{1,0:T(8,128)S(1)}) custom-call(bf16[128,1152]{1,0:T(8,128)(2,1)S(1)} %copy-done.14, bf16[128,1152]{1,0:T(8,128)(2,1)S(1)} %collective-permute-done.1.refs_1_, bf16[128,1152]{1,0:T(8,128)(2,1)S(1)} %collective-permute-done.refs_2_, ...), custom_call_target="tpu_custom_call" | custom-call | flops 3000000000 | bytes 9437184 | tf_op jit(solution)/shard_map/first_pick/pallas_call | solution.py:358
  43.4 2.8 %collective-permute-done.8.refs_2_ = bf16[128,1024]{1,0:T(8,128)(2,1)S(1)} collective-permute-done((bf16[128,1024]{1,0:T(8,128)(2,1)}, bf16[128,1024]{1,0:T(8,128)(2,1)S(1)}, u32[]{:S(2)}, u32[]{:S(2)}) %collective-permute-start.8) | collective-permute-done | bytes 262176 | tf_op jit(solution)/shard_map/ppermute | solution.py:322
  46.3 2.0 %collective-permute-start.10 = (bf16[128,1024]{1,0:T(8,128)(2,1)S(1)}, bf16[128,1024]{1,0:T(8,128)(2,1)S(1)}, u32[]{:S(2)}, u32[]{:S(2)}) collective-permute-start(bf16[128,1024]{1,0:T(8,128)(2,1)S(1)} %collective-permute-done.8.refs_2_), channel_id=1, source_target_pairs={{0,4},{1,5},{2,6},{3,7},{4,12},{5,13},{6,14},{7,15},{12,8},{13,9},... | collective-permute-start | bytes 786440 | tf_op jit(solution)/shard_map/ppermute | solution.py:322
  50.2 1.7 %first_products.1 = (f32[1,1024]{1,0:T(1,128)S(1)}, bf16[704,1024]{1,0:T(8,128)(2,1)S(1)}, bf16[1024,512]{1,0:T(8,128)(2,1)S(1)}, bf16[352,512]{1,0:T(8,128)(2,1)S(1)}, bf16[352,512]{1,0:T(8,128)(2,1)S(1)}) custom-call(bf16[512,1024]{1,0:T(8,128)(2,1)S(1)} %get-tuple-element.53.mine_ref, bf16[528,1024]{1,0:T(8,128)(2,1)S(1)} %collective-permute-done.13.got_ref, ...), custom_call_target="tpu_custom_call" | custom-call | flops 2000000000 | bytes 6291456 | tf_op jit(solution)/shard_map/first_products/pallas_call | solution.py:390
  53.9 1.6 %collective-permute-start.18 = (bf16[352,512]{1,0:T(8,128)(2,1)S(1)}, bf16[352,512]{1,0:T(8,128)(2,1)S(1)}, u32[]{:S(2)}, u32[]{:S(2)}) collective-permute-start(bf16[352,512]{1,0:T(8,128)(2,1)S(1)} %get-tuple-element.71), channel_id=1, source_target_pairs={{0,16},{16,0},{1,17},{17,1},{2,18},{18,2},{3,19},{19,3},{4,20},{20... | collective-permute-start | bytes 1081352 | tf_op jit(solution)/shard_map/ppermute | solution.py:334
  55.4 3.2 %hidden_weight.1.forward_ref = bf16[1024,1024]{1,0:T(8,128)(2,1)S(1)} custom-call(bf16[352,2048]{1,0:T(8,128)(2,1)S(1)} %bitcast.17, bf16[352,2048]{1,0:T(8,128)(2,1)S(1)} %collective-permute-done.11.refs_0_, bf16[704,1024]{1,0:T(8,128)(2,1)S(1)} %bitcast.20), custom_call_target="tpu_custom_call" | custom-call | flops 3000000000 | bytes 9437184 | tf_op jit(solution)/shard_map/hidden_weight/pallas_call | solution.py:447
  60.2 2.8 %raw_part.1 = (f32[704,1024]{1,0:T(8,128)S(1)}, f32[16,64]{1,0:T(8,128)S(1)}) custom-call(bf16[1024,512]{1,0:T(8,128)(2,1)S(1)} %get-tuple-element.57.first_ref, bf16[1024,512]{1,0:T(8,128)(2,1)S(1)} %get-tuple-element.59.second_ref, bf16[352,2048]{1,0:T(8,128)(2,1)S(1)} %bitcast.18, bf16[352,2048]{1,0:T(8,128)(2,1)S(1)} %collective-permute-done.11.refs_0_, ...), custom_call_target="tpu_custom_call" | custom-call | flops 3000000000 | bytes 9437184 | tf_op jit(solution)/shard_map/raw_part/pallas_call | solution.py:415
  63.1 4.8 %collective-permute-done.14.refs_5_ = bf16[128,1024]{1,0:T(8,128)(2,1)S(1)} collective-permute-done((bf16[128,1024]{1,0:T(8,128)(2,1)S(1)}, bf16[128,1024]{1,0:T(8,128)(2,1)S(1)}, u32[]{:S(2)}, u32[]{:S(2)}) %collective-permute-start.14) | collective-permute-done | bytes 262176 | tf_op jit(solution)/shard_map/ppermute | solution.py:328
  70.5 1.9 %products.4 = (bf16[1024,512]{1,0:T(8,128)(2,1)S(1)}, bf16[352,512]{1,0:T(8,128)(2,1)}, bf16[352,512]{1,0:T(8,128)(2,1)S(1)}) custom-call(bf16[512,512]{1,0:T(8,128)(2,1)S(1)} %get-tuple-element.65.mine_ref, bf16[512,512]{1,0:T(8,128)(2,1)S(1)} %collective-permute-done.16.got_ref, bf16[704,1024]{1,0:T(8,128)(2,1)S(1)} %get-tuple-element.58.hs_ref), custom_call_target="tpu_custom_call" | custom-call | tf_op jit(solution)/shard_map/products/pallas_call | solution.py:401
  72.9 1.9 %products.5 = (bf16[1024,512]{1,0:T(8,128)(2,1)S(1)}, bf16[352,512]{1,0:T(8,128)(2,1)}, bf16[352,512]{1,0:T(8,128)(2,1)S(1)}) custom-call(bf16[512,512]{1,0:T(8,128)(2,1)S(1)} %get-tuple-element.68.mine_ref, bf16[512,512]{1,0:T(8,128)(2,1)S(1)} %collective-permute-done.19.got_ref, bf16[704,1024]{1,0:T(8,128)(2,1)S(1)} %get-tuple-element.58.hs_ref), custom_call_target="tpu_custom_call" | custom-call | tf_op jit(solution)/shard_map/products/pallas_call | solution.py:401
  77.7 3.5 %all-to-all-start = ((f32[16,1,64]{2,1,0:T(1,128)}), f32[16,1,64]{2,1,0:T(1,128)S(1)}, u32[]{:S(2)}, u32[]{:S(2)}) async-start(f32[16,1,64]{2,1,0:T(1,128)} %bitcast.10), calls=%async_computation | async-start | bytes 16384 | tf_op jit(solution)/shard_map/all_to_all | solution.py:513
  81.2 6.5 %raw.1 = bf16[704,1024]{1,0:T(8,128)(2,1)} custom-call(bf16[1024,512]{1,0:T(8,128)(2,1)} %copy-done, bf16[1024,512]{1,0:T(8,128)(2,1)} %copy-done.1, bf16[352,2048]{1,0:T(8,128)(2,1)} %bitcast.16, bf16[352,2048]{1,0:T(8,128)(2,1)} %copy-done.4, f32[704,1024]{1,0:T(8,128)} %copy-done.2, f32[1,1024]{1,0:T(1,128)} %copy-done.15), custom_call_target="tpu_custom_call" | custom-call | tf_op jit(solution)/shard_map/raw/pallas_call | solution.py:431
  (73 shorter events, 21.8 us)
Async XLA Ops:
  0.6 40.2 %collective-permute-start.11 = (bf16[352,2048]{1,0:T(8,128)(2,1)}, bf16[352,2048]{1,0:T(8,128)(2,1)S(1)}, u32[]{:S(2)}, u32[]{:S(2)}) collective-permute-start(bf16[352,2048]{1,0:T(8,128)(2,1)} %bitcast.15), channel_id=1, source_target_pairs={{0,16},{16,0},{1,17},{17,1},{2,18},{18,2},{3,19},{19,3},{4,20},{20... | collective-permute-start | bytes 4325384 | tf_op jit(solution)/shard_map/ppermute | solution.py:334
  5.5 8.7 %collective-permute-start.1 = (bf16[128,1152]{1,0:T(8,128)(2,1)}, bf16[128,1152]{1,0:T(8,128)(2,1)S(1)}, u32[]{:S(2)}, u32[]{:S(2)}) collective-permute-start(bf16[128,1152]{1,0:T(8,128)(2,1)} %get-tuple-element.46.refs_0_.slots_ref), channel_id=1, source_target_pairs={{0,2},{1,3},{2,0},{3,1},{4,6},{5,7},{6,4},{7,5},{8,10},{9,11},{10,... | collective-permute-start | bytes 884744 | tf_op jit(solution)/shard_map/ppermute | solution.py:328
  7.1 9.3 %collective-permute-start = (bf16[128,1152]{1,0:T(8,128)(2,1)}, bf16[128,1152]{1,0:T(8,128)(2,1)S(1)}, u32[]{:S(2)}, u32[]{:S(2)}) collective-permute-start(bf16[128,1152]{1,0:T(8,128)(2,1)} %get-tuple-element.46.refs_0_.slots_ref), channel_id=1, source_target_pairs={{0,4},{1,5},{2,6},{3,7},{4,12},{5,13},{6,14},{7,15},{12,8},{13,9},... | collective-permute-start | bytes 884744 | tf_op jit(solution)/shard_map/ppermute | solution.py:322
  16.4 7.3 %collective-permute-start.3 = (bf16[128,1152]{1,0:T(8,128)(2,1)S(1)}, bf16[128,1152]{1,0:T(8,128)(2,1)S(1)}, u32[]{:S(2)}, u32[]{:S(2)}) collective-permute-start(bf16[128,1152]{1,0:T(8,128)(2,1)S(1)} %collective-permute-done.refs_2_), channel_id=1, source_target_pairs={{0,2},{1,3},{2,0},{3,1},{4,6},{5,7},{6,4},{7,5},{8,10},{9,11},{10,... | collective-permute-start | bytes 884744 | tf_op jit(solution)/shard_map/ppermute | solution.py:328
  16.9 7.9 %collective-permute-start.2 = (bf16[128,1152]{1,0:T(8,128)(2,1)S(1)}, bf16[128,1152]{1,0:T(8,128)(2,1)S(1)}, u32[]{:S(2)}, u32[]{:S(2)}) collective-permute-start(bf16[128,1152]{1,0:T(8,128)(2,1)S(1)} %collective-permute-done.refs_2_), channel_id=1, source_target_pairs={{0,4},{1,5},{2,6},{3,7},{4,12},{5,13},{6,14},{7,15},{12,8},{13,9},... | collective-permute-start | bytes 884744 | tf_op jit(solution)/shard_map/ppermute | solution.py:322
  24.8 6.9 %collective-permute-start.4 = (bf16[128,1152]{1,0:T(8,128)(2,1)}, bf16[128,1152]{1,0:T(8,128)(2,1)S(1)}, u32[]{:S(2)}, u32[]{:S(2)}) collective-permute-start(bf16[128,1152]{1,0:T(8,128)(2,1)} %get-tuple-element.46.refs_0_.slots_ref), channel_id=1, source_target_pairs={{0,8},{1,9},{2,10},{3,11},{4,0},{5,1},{6,2},{7,3},{12,4},{13,5},{1... | collective-permute-start | bytes 884744 | tf_op jit(solution)/shard_map/ppermute | solution.py:325
  26.3 7.8 %collective-permute-start.5 = (bf16[128,1152]{1,0:T(8,128)(2,1)S(1)}, bf16[128,1152]{1,0:T(8,128)(2,1)S(1)}, u32[]{:S(2)}, u32[]{:S(2)}) collective-permute-start(bf16[128,1152]{1,0:T(8,128)(2,1)S(1)} %collective-permute-done.2.refs_4_), channel_id=1, source_target_pairs={{0,2},{1,3},{2,0},{3,1},{4,6},{5,7},{6,4},{7,5},{8,10},{9,11},{10,... | collective-permute-start | bytes 884744 | tf_op jit(solution)/shard_map/ppermute | solution.py:328
  34.1 6.7 %collective-permute-start.6 = (bf16[128,1152]{1,0:T(8,128)(2,1)S(1)}, bf16[128,1152]{1,0:T(8,128)(2,1)S(1)}, u32[]{:S(2)}, u32[]{:S(2)}) collective-permute-start(bf16[128,1152]{1,0:T(8,128)(2,1)S(1)} %collective-permute-done.4.refs_6_), channel_id=1, source_target_pairs={{0,2},{1,3},{2,0},{3,1},{4,6},{5,7},{6,4},{7,5},{8,10},{9,11},{10,... | collective-permute-start | bytes 884744 | tf_op jit(solution)/shard_map/ppermute | solution.py:328
  35.6 7.8 %collective-permute-start.12 = (bf16[128,1024]{1,0:T(8,128)(2,1)}, bf16[128,1024]{1,0:T(8,128)(2,1)S(1)}, u32[]{:S(2)}, u32[]{:S(2)}) collective-permute-start(bf16[128,1024]{1,0:T(8,128)(2,1)} %get-tuple-element.50.refs_0_), channel_id=1, source_target_pairs={{0,8},{1,9},{2,10},{3,11},{4,0},{5,1},{6,2},{7,3},{12,4},{13,5},{1... | collective-permute-start | bytes 786440 | tf_op jit(solution)/shard_map/ppermute | solution.py:325
  38.8 7.5 %collective-permute-start.8 = (bf16[128,1024]{1,0:T(8,128)(2,1)}, bf16[128,1024]{1,0:T(8,128)(2,1)S(1)}, u32[]{:S(2)}, u32[]{:S(2)}) collective-permute-start(bf16[128,1024]{1,0:T(8,128)(2,1)} %get-tuple-element.50.refs_0_), channel_id=1, source_target_pairs={{0,4},{1,5},{2,6},{3,7},{4,12},{5,13},{6,14},{7,15},{12,8},{13,9},... | collective-permute-start | bytes 786440 | tf_op jit(solution)/shard_map/ppermute | solution.py:322
  41.8 18.4 %copy-start.4 = (bf16[352,2048]{1,0:T(8,128)(2,1)}, bf16[352,2048]{1,0:T(8,128)(2,1)S(1)}, u32[]{:S(2)}) copy-start(bf16[352,2048]{1,0:T(8,128)(2,1)S(1)} %collective-permute-done.11.refs_0_) | copy-start | bytes 4325380
  46.2 4.0 %collective-permute-start.13 = (bf16[528,1024]{1,0:T(8,128)(2,1)S(1)}, bf16[528,1024]{1,0:T(8,128)(2,1)S(1)}, u32[]{:S(2)}, u32[]{:S(2)}) collective-permute-start(bf16[528,1024]{1,0:T(8,128)(2,1)S(1)} %get-tuple-element.55), channel_id=1, source_target_pairs={{0,1},{1,0},{2,3},{3,2},{4,5},{5,4},{6,7},{7,6},{8,9},{9,8},{10,11... | collective-permute-start | bytes 3244040 | tf_op jit(solution)/shard_map/ppermute | solution.py:331
  46.3 12.4 %collective-permute-start.10 = (bf16[128,1024]{1,0:T(8,128)(2,1)S(1)}, bf16[128,1024]{1,0:T(8,128)(2,1)S(1)}, u32[]{:S(2)}, u32[]{:S(2)}) collective-permute-start(bf16[128,1024]{1,0:T(8,128)(2,1)S(1)} %collective-permute-done.8.refs_2_), channel_id=1, source_target_pairs={{0,4},{1,5},{2,6},{3,7},{4,12},{5,13},{6,14},{7,15},{12,8},{13,9},... | collective-permute-start | bytes 786440 | tf_op jit(solution)/shard_map/ppermute | solution.py:322
  48.2 10.5 %collective-permute-start.7 = (bf16[128,1024]{1,0:T(8,128)(2,1)S(1)}, bf16[128,1024]{1,0:T(8,128)(2,1)S(1)}, u32[]{:S(2)}, u32[]{:S(2)}) collective-permute-start(bf16[128,1024]{1,0:T(8,128)(2,1)S(1)} %copy-done.5), channel_id=1, source_target_pairs={{0,2},{1,3},{2,0},{3,1},{4,6},{5,7},{6,4},{7,5},{8,10},{9,11},{10,... | collective-permute-start | bytes 786440 | tf_op jit(solution)/shard_map/ppermute | solution.py:328
  48.7 14.4 %collective-permute-start.9 = (bf16[128,1024]{1,0:T(8,128)(2,1)S(1)}, bf16[128,1024]{1,0:T(8,128)(2,1)S(1)}, u32[]{:S(2)}, u32[]{:S(2)}) collective-permute-start(bf16[128,1024]{1,0:T(8,128)(2,1)S(1)} %collective-permute-done.8.refs_2_), channel_id=1, source_target_pairs={{0,2},{1,3},{2,0},{3,1},{4,6},{5,7},{6,4},{7,5},{8,10},{9,11},{10,... | collective-permute-start | bytes 786440 | tf_op jit(solution)/shard_map/ppermute | solution.py:328
  52.0 17.2 %collective-permute-start.17 = (bf16[352,512]{1,0:T(8,128)(2,1)S(1)}, bf16[352,512]{1,0:T(8,128)(2,1)S(1)}, u32[]{:S(2)}, u32[]{:S(2)}) collective-permute-start(bf16[352,512]{1,0:T(8,128)(2,1)S(1)} %get-tuple-element.70), channel_id=1, source_target_pairs={{0,16},{16,0},{1,17},{17,1},{2,18},{18,2},{3,19},{19,3},{4,20},{20... | collective-permute-start | bytes 1081352 | tf_op jit(solution)/shard_map/ppermute | solution.py:334
  53.9 15.9 %collective-permute-start.18 = (bf16[352,512]{1,0:T(8,128)(2,1)S(1)}, bf16[352,512]{1,0:T(8,128)(2,1)S(1)}, u32[]{:S(2)}, u32[]{:S(2)}) collective-permute-start(bf16[352,512]{1,0:T(8,128)(2,1)S(1)} %get-tuple-element.71), channel_id=1, source_target_pairs={{0,16},{16,0},{1,17},{17,1},{2,18},{18,2},{3,19},{19,3},{4,20},{20... | collective-permute-start | bytes 1081352 | tf_op jit(solution)/shard_map/ppermute | solution.py:334
  58.7 9.2 %collective-permute-start.14 = (bf16[128,1024]{1,0:T(8,128)(2,1)S(1)}, bf16[128,1024]{1,0:T(8,128)(2,1)S(1)}, u32[]{:S(2)}, u32[]{:S(2)}) collective-permute-start(bf16[128,1024]{1,0:T(8,128)(2,1)S(1)} %collective-permute-done.10.refs_4_), channel_id=1, source_target_pairs={{0,2},{1,3},{2,0},{3,1},{4,6},{5,7},{6,4},{7,5},{8,10},{9,11},{10,... | collective-permute-start | bytes 786440 | tf_op jit(solution)/shard_map/ppermute | solution.py:328
  59.2 8.6 %collective-permute-start.15 = (bf16[128,1024]{1,0:T(8,128)(2,1)S(1)}, bf16[128,1024]{1,0:T(8,128)(2,1)S(1)}, u32[]{:S(2)}, u32[]{:S(2)}) collective-permute-start(bf16[128,1024]{1,0:T(8,128)(2,1)S(1)} %collective-permute-done.7.refs_1_), channel_id=1, source_target_pairs={{0,8},{1,9},{2,10},{3,11},{4,0},{5,1},{6,2},{7,3},{12,4},{13,5},{1... | collective-permute-start | bytes 786440 | tf_op jit(solution)/shard_map/ppermute | solution.py:325
  68.5 2.0 %collective-permute-start.16 = (bf16[512,512]{1,0:T(8,128)(2,1)S(1)}, bf16[512,512]{1,0:T(8,128)(2,1)S(1)}, u32[]{:S(2)}, u32[]{:S(2)}) collective-permute-start(bf16[512,512]{1,0:T(8,128)(2,1)S(1)} %get-tuple-element.66), channel_id=1, source_target_pairs={{0,1},{1,0},{2,3},{3,2},{4,5},{5,4},{6,7},{7,6},{8,9},{9,8},{10,11... | collective-permute-start | bytes 1572872 | tf_op jit(solution)/shard_map/ppermute | solution.py:331
  69.8 3.1 %collective-permute-start.19 = (bf16[512,512]{1,0:T(8,128)(2,1)S(1)}, bf16[512,512]{1,0:T(8,128)(2,1)S(1)}, u32[]{:S(2)}, u32[]{:S(2)}) collective-permute-start(bf16[512,512]{1,0:T(8,128)(2,1)S(1)} %get-tuple-element.72), channel_id=1, source_target_pairs={{0,1},{1,0},{2,3},{3,2},{4,5},{5,4},{6,7},{7,6},{8,9},{9,8},{10,11... | collective-permute-start | bytes 1572872 | tf_op jit(solution)/shard_map/ppermute | solution.py:331
  72.4 18.4 %collective-permute-start.20 = (bf16[352,512]{1,0:T(8,128)(2,1)}, bf16[352,512]{1,0:T(8,128)(2,1)S(1)}, u32[]{:S(2)}, u32[]{:S(2)}) collective-permute-start(bf16[352,512]{1,0:T(8,128)(2,1)} %get-tuple-element.74), channel_id=1, source_target_pairs={{0,16},{16,0},{1,17},{17,1},{2,18},{18,2},{3,19},{19,3},{4,20},{20... | collective-permute-start | bytes 1081352 | tf_op jit(solution)/shard_map/ppermute | solution.py:334
  74.8 15.9 %collective-permute-start.21 = (bf16[352,512]{1,0:T(8,128)(2,1)}, bf16[352,512]{1,0:T(8,128)(2,1)S(1)}, u32[]{:S(2)}, u32[]{:S(2)}) collective-permute-start(bf16[352,512]{1,0:T(8,128)(2,1)} %get-tuple-element.75), channel_id=1, source_target_pairs={{0,16},{16,0},{1,17},{17,1},{2,18},{18,2},{3,19},{19,3},{4,20},{20... | collective-permute-start | bytes 1081352 | tf_op jit(solution)/shard_map/ppermute | solution.py:334
  77.7 11.0 %all-to-all-start = ((f32[16,1,64]{2,1,0:T(1,128)}), f32[16,1,64]{2,1,0:T(1,128)S(1)}, u32[]{:S(2)}, u32[]{:S(2)}) async-start(f32[16,1,64]{2,1,0:T(1,128)} %bitcast.10), calls=%async_computation | async-start | bytes 16384 | tf_op jit(solution)/shard_map/all_to_all | solution.py:513
  (17 other events, 82.9 us)
